TPU v7x, 32 devices: a whole 2x2x4 slice. The times are simulated.
32 devices in a mesh: prow: 4 (over z), pcol: 8 (over y, x, core).
Axes of the slice: x: 2, y: 2, z: 4, core: 2. Of those that a mesh axis runs over, the one named last changes fastest.
Arguments:
- matrix: bfloat16 [3, 2048, 1, 4096], P(None, 'prow', None, 'pcol'), may hold values from -6 to 6
- pattern: int32 [12, 8], replicated, may hold values 0 or 1
- inverses: bfloat16 [2, 512, 512], replicated, may hold values from -0.01171875 to 0.01171875
- pivots: int32 [2, 3], replicated, may hold values from 0 to 11, as said below
Outputs:
- factored: bfloat16 [3, 2048, 1, 4096], P(None, 'prow', None, 'pcol')
Inputs may be any that keep to these rules, and one draw needn't show every extreme that they name: pivots[s] = (a, b, c) with a and b block rows in 0 .. 11 and c a block column in 0 .. 7; the 4 numbers a and b over all steps are all different, and so are the 2 numbers c; b mod 4 = (a + 2) mod 4 for every step; block row 0 and block row 11 are among the b, and block column 7 is among the c.
All inputs are finite; a program needn't handle non-finite values.
Results may differ from a plain program's by a relative error of at most 0.0068.
Values may be sent and summed in bfloat16 or wider, within the bound.
No kernel may reach another device: no remote copies, remote signals or barrier semaphores. Data moves between devices by JAX's collectives and lax.ppermute only.
A program may use at most 64 MiB of HBM per device.

v0:
```python
import jax
import jax.numpy as jnp
from jax import lax
from jax.sharding import PartitionSpec as P


def partner(value, axis, bit):
    mask = 2**bit
    pairs = [(source, source ^ mask) for source in range(lax.axis_size(axis))]
    return lax.ppermute(value, axis, pairs)


def broadcast(block, axis, source):
    block = jnp.where(lax.axis_index(axis) == source, block, jnp.zeros_like(block))
    return lax.psum(block, axis)


def local(matrix, pattern, inverses, pivots):
    nrow = lax.axis_size("prow")
    ncol = lax.axis_size("pcol")
    my_row = lax.axis_index("prow")
    my_col = lax.axis_index("pcol")
    half_bit = nrow.bit_length() - 2
    row_blocks = matrix.shape[0]
    width = matrix.shape[1]
    col_blocks = matrix.shape[2]
    global_rows = jnp.arange(row_blocks, dtype=jnp.int32) * nrow + my_row
    global_cols = jnp.arange(col_blocks, dtype=jnp.int32) * ncol + my_col
    pick_rows = (
        jnp.arange(pattern.shape[0], dtype=jnp.int32)[None, :] == global_rows[:, None]
    ).astype(jnp.float32)
    pick_cols = (
        jnp.arange(pattern.shape[1], dtype=jnp.int32)[None, :] == global_cols[:, None]
    ).astype(jnp.float32)
    local_pattern = jnp.dot(jnp.dot(pick_rows, pattern.astype(jnp.float32)), pick_cols.T)
    work = matrix * local_pattern.astype(matrix.dtype)[:, None, :, None]
    for step in range(inverses.shape[0]):
        first = pivots[step, 0]
        second = pivots[step, 1]
        column_id = pivots[step, 2]
        owner_first = first % nrow
        slot_first = first // nrow
        owner_second = second % nrow
        slot_second = second // nrow
        row_first = lax.dynamic_index_in_dim(work, slot_first, 0, keepdims=False)
        row_second = lax.dynamic_index_in_dim(work, slot_second, 0, keepdims=False)
        outgoing = jnp.where(my_row == owner_first, row_first, row_second)
        incoming = partner(outgoing, "prow", half_bit)
        work = lax.dynamic_update_index_in_dim(
            work, jnp.where(my_row == owner_first, incoming, row_first), slot_first, 0
        )
        current = lax.dynamic_index_in_dim(work, slot_second, 0, keepdims=False)
        work = lax.dynamic_update_index_in_dim(
            work, jnp.where(my_row == owner_second, incoming, current), slot_second, 0
        )
        pivot_now = lax.dynamic_index_in_dim(work, slot_first, 0, keepdims=False)
        upper = broadcast(pivot_now, "prow", owner_first)
        column = lax.dynamic_index_in_dim(work, column_id // ncol, 2, keepdims=False)
        panel = broadcast(column, "pcol", column_id % ncol)
        multipliers = jnp.dot(
            panel.reshape(row_blocks * width, width),
            inverses[step],
            preferred_element_type=jnp.float32,
        )
        multipliers = multipliers.astype(matrix.dtype)
        product = jnp.dot(
            multipliers,
            upper.reshape(width, col_blocks * width),
            preferred_element_type=jnp.float32,
        )
        product = product.reshape(row_blocks, width, col_blocks, width)
        fresh = (work.astype(jnp.float32) - product).astype(matrix.dtype)
        live_rows = jnp.all(global_rows[:, None] != pivots[None, : step + 1, 0], axis=1)
        live_cols = jnp.all(global_cols[:, None] != pivots[None, : step + 1, 2], axis=1)
        is_column = global_cols == column_id
        left_blocks = multipliers.reshape(row_blocks, width, 1, width)
        mixed = jnp.where(
            live_cols[None, None, :, None],
            fresh,
            jnp.where(is_column[None, None, :, None], left_blocks, work),
        )
        work = jnp.where(live_rows[:, None, None, None], mixed, work)
    return work


def solution(mesh):
    placed = (P(None, "prow", None, "pcol"), P(), P(), P())
    return jax.shard_map(
        local, mesh=mesh, in_specs=placed, out_specs=P(None, "prow", None, "pcol"), check_vma=False
    )
```

profile of v0, /device:TPU:0, one launch (start us, length us, event | category | flops | bytes accessed | tf_op | source)
XLA Modules:
  0.0 284.1 jit_solution(1781171688596516655)
XLA Ops:
  6.5 1.6 fusion.25
  13.5 1.0 fusion.8
  14.5 1.6 broadcast_multiply_fusion
  16.1 4.1 %collective-permute-start = (bf16[512,1,512]{2,0,1:T(8,128)(2,1)S(1)}, bf16[512,1,512]{2,0,1:T(8,128)(2,1)S(1)}, u32[]{:S(2)}, u32[]{:S(2)}) collective-permute-start(bf16[512,1,512]{2,0,1:T(8,128)(2,1)S(1)} %bitcast_select_fusion.4), channel_id=1, source_target_pairs={{0,16},{8,24},{16,0},{24,8},{1,17},{9,25},{17,1},{25,9},{2,18},{10... | collective-permute-start | bytes 1572872 | tf_op jit(solution)/shard_map/ppermute | solution.py:10
  22.0 21.4 %collective-permute-done = bf16[512,1,512]{2,0,1:T(8,128)(2,1)S(1)} collective-permute-done((bf16[512,1,512]{2,0,1:T(8,128)(2,1)S(1)}, bf16[512,1,512]{2,0,1:T(8,128)(2,1)S(1)}, u32[]{:S(2)}, u32[]{:S(2)}) %collective-permute-start) | collective-permute-done | bytes 524320 | tf_op jit(solution)/shard_map/ppermute | solution.py:10
  43.6 0.1 bitcast_dynamic-update-slice_fusion.2
  43.7 1.2 broadcast_select_fusion.1
  45.0 0.8 select_bitcast_fusion.1
  52.7 0.7 broadcast_compare_fusion
  53.3 52.0 %all-reduce.5.cloned.1.call-done = bf16[1536,512]{1,0:T(8,128)(2,1)} async-done(((bf16[1536,512]{1,0:T(8,128)(2,1)}), bf16[1536,512]{1,0:T(8,128)(2,1)}) %all-reduce.5.cloned.1.call-update) | async-done | bytes 1572880 | tf_op jit(solution)/shard_map/psum | solution.py:15
  105.3 3.5 %convolution_convert_fusion.1 = bf16[1536,512]{1,0:T(8,128)(2,1)} fusion(bf16[1536,512]{1,0:T(8,128)(2,1)} %all-reduce.5.cloned.1.call-done, bf16[2,512,512]{2,1,0:T(8,128)(2,1)S(1)} %copy-done.1), kind=kOutput, calls=%fused_computation.5 | convolution fusion | flops 806092800 | bytes 3670016 | tf_op jit(solution)/shard_map/dot_general | solution.py:60
  108.9 36.6 %all-reduce.7.cloned.1.call-done = bf16[512,512]{1,0:T(8,128)(2,1)} async-done(((bf16[512,512]{1,0:T(8,128)(2,1)}), bf16[512,512]{1,0:T(8,128)(2,1)}) %all-reduce.7.cloned.1.call-update) | async-done | bytes 524304 | tf_op jit(solution)/shard_map/psum | solution.py:15
  145.5 2.6 select_select_fusion.1
  148.1 2.1 collective-permute-start.1
  152.3 20.8 %collective-permute-done.1 = bf16[512,1,512]{2,0,1:T(8,128)(2,1)S(1)} collective-permute-done((bf16[512,1,512]{2,0,1:T(8,128)(2,1)S(1)}, bf16[512,1,512]{2,0,1:T(8,128)(2,1)S(1)}, u32[]{:S(2)}, u32[]{:S(2)}) %collective-permute-start.1) | collective-permute-done | bytes 524320 | tf_op jit(solution)/shard_map/ppermute | solution.py:10
  173.2 0.1 bitcast_dynamic-update-slice_fusion
  173.4 1.2 broadcast_select_fusion
  175.4 0.8 compare_reduce_fusion
  176.2 0.8 select_bitcast_fusion
  177.2 0.2 compare_reduce_fusion.1
  177.4 56.0 %all-reduce.9.cloned.1.call-done = bf16[1536,512]{1,0:T(8,128)(2,1)} async-done(((bf16[1536,512]{1,0:T(8,128)(2,1)}), bf16[1536,512]{1,0:T(8,128)(2,1)}) %all-reduce.9.cloned.1.call-update) | async-done | bytes 1572880 | tf_op jit(solution)/shard_map/psum | solution.py:15
  233.4 3.5 %convolution_convert_fusion = bf16[1536,512]{1,0:T(8,128)(2,1)} fusion(bf16[1536,512]{1,0:T(8,128)(2,1)} %all-reduce.9.cloned.1.call-done, bf16[2,512,512]{2,1,0:T(8,128)(2,1)S(1)} %copy-done.2), kind=kOutput, calls=%fused_computation.4 | convolution fusion | flops 806092800 | bytes 3670016 | tf_op jit(solution)/shard_map/dot_general | solution.py:60
  236.9 36.3 %all-reduce.11.cloned.1.call-done = bf16[512,512]{1,0:T(8,128)(2,1)} async-done(((bf16[512,512]{1,0:T(8,128)(2,1)}), bf16[512,512]{1,0:T(8,128)(2,1)}) %all-reduce.11.cloned.1.call-update) | async-done | bytes 524304 | tf_op jit(solution)/shard_map/psum | solution.py:15
  273.2 4.4 %select_select_fusion = bf16[3,512,1,512]{3,1,2,0:T(8,128)(2,1)} fusion(bf16[3,512,1,512]{3,1,2,0:T(8,128)(2,1)S(1)} %bitcast_dynamic-update-slice_fusion, bf16[3,512,1,512]{3,1,2,0:T(8,128)(2,1)} %bitcast.94, pred[3]{0:T(512)(128)(4,1)S(1)} %compare_reduce_fusion.1, pred[]{:T(512)} %bitcast.38, pred[]{:T(512)} %compare_reduce_fusion, ...), kind=kOutput, calls=%fused_computation.6 | convolution fusion | flops 810024960 | bytes 6815749 | tf_op jit(solution)/shard_map/dot_general | solution.py:66
  (24 shorter events, 0.9 us)
Async XLA Ops:
  6.5 98.8 %all-reduce.5.cloned.1.call-start = ((), (), s32[]{:S(2)}) async-start(), calls=%async_computation | async-start | bytes 3145728 | tf_op jit(solution)/shard_map/psum | solution.py:15
  16.1 27.3 %collective-permute-start = (bf16[512,1,512]{2,0,1:T(8,128)(2,1)S(1)}, bf16[512,1,512]{2,0,1:T(8,128)(2,1)S(1)}, u32[]{:S(2)}, u32[]{:S(2)}) collective-permute-start(bf16[512,1,512]{2,0,1:T(8,128)(2,1)S(1)} %bitcast_select_fusion.4), channel_id=1, source_target_pairs={{0,16},{8,24},{16,0},{24,8},{1,17},{9,25},{17,1},{25,9},{2,18},{10... | collective-permute-start | bytes 1572872 | tf_op jit(solution)/shard_map/ppermute | solution.py:10
  45.0 60.4 %copy-start.1 = (bf16[2,512,512]{2,1,0:T(8,128)(2,1)S(1)}, bf16[2,512,512]{2,1,0:T(8,128)(2,1)}, u32[]{:S(2)}) copy-start(bf16[2,512,512]{2,1,0:T(8,128)(2,1)} %param.6) | copy-start | bytes 3145732
  45.0 100.5 %all-reduce.7.cloned.1.call-start = ((), (), s32[]{:S(2)}) async-start(), calls=%async_computation.1 | async-start | bytes 1048576 | tf_op jit(solution)/shard_map/psum | solution.py:15
  45.9 187.5 %all-reduce.9.cloned.1.call-start = ((), (), s32[]{:S(2)}) async-start(), calls=%async_computation.2 | async-start | bytes 3145728 | tf_op jit(solution)/shard_map/psum | solution.py:15
  148.1 24.9 %collective-permute-start.1 = (bf16[512,1,512]{2,0,1:T(8,128)(2,1)S(1)}, bf16[512,1,512]{2,0,1:T(8,128)(2,1)S(1)}, u32[]{:S(2)}, u32[]{:S(2)}) collective-permute-start(bf16[512,1,512]{2,0,1:T(8,128)(2,1)S(1)} %bitcast_select_fusion.1), channel_id=1, source_target_pairs={{0,16},{8,24},{16,0},{24,8},{1,17},{9,25},{17,1},{25,9},{2,18},{10... | collective-permute-start | bytes 1572872 | tf_op jit(solution)/shard_map/ppermute | solution.py:10
  174.6 0.8 copy-start
  174.6 58.8 %copy-start.2 = (bf16[2,512,512]{2,1,0:T(8,128)(2,1)S(1)}, bf16[2,512,512]{2,1,0:T(8,128)(2,1)}, u32[]{:S(2)}) copy-start(bf16[2,512,512]{2,1,0:T(8,128)(2,1)} %param.6) | copy-start | bytes 3145732
  174.6 98.6 %all-reduce.11.cloned.1.call-start = ((), (), s32[]{:S(2)}) async-start(), calls=%async_computation.3 | async-start | bytes 1048576 | tf_op jit(solution)/shard_map/psum | solution.py:15
Sparse Core Ops, SparseCore 0:
  45.1 60.1 all-reduce.4
  107.8 37.6 all-reduce.6
  174.8 58.5 all-reduce.8
  235.6 37.6 all-reduce.10
where the time goes:
time: 285 us; the launch traced here: 284 us
  waiting for transfers between devices  223 us (78%)
  between operations  29.6 us (10%)
  matrix products  15 us (5%)
  other arithmetic  8.07 us (3%)
  starting transfers between devices  6.36 us (2%)
    psum x4, waiting for transfers between devices, broadcast(): return lax.psum(block, axis)  181 us
    ppermute x2, waiting for transfers between devices, partner(): return lax.ppermute(value, axis, pairs)  42.2 us
    dot_general x2, matrix products, local(): jnp.dot(panel.reshape(row_blocks * width, width), inverses[step], preferr...  7.06 us
    dot_general x2, matrix products, local(): jnp.dot(multipliers, upper.reshape(width, col_blocks * width), preferred_...  6.96 us
    ppermute x2, starting transfers between devices, partner(): return lax.ppermute(value, axis, pairs)  6.23 us
  transfers between devices with their start and end apart: 6, of which 6 were waited for; matrix products, arithmetic and copies ran while one was open for 4% of the time, Pallas kernels for 0%

commit v1 on v0

v1 whole, which is shorter than its diff:
```python
import jax
import jax.numpy as jnp
from jax import lax
from jax.sharding import PartitionSpec as P


def ring_order(chips):
    side = round(chips**0.5)
    if side * side != chips or side % 2:
        return list(range(chips))
    walk = []
    for i in range(side):
        cols = list(range(1, side))
        walk += [i * side + k for k in (cols if i % 2 == 0 else cols[::-1])]
    return walk + [i * side for i in range(side - 1, -1, -1)]


def lookup(table, index):
    total = jnp.int32(0)
    for i, value in enumerate(table):
        total = jnp.where(index == i, jnp.int32(value), total)
    return total


def local(matrix, pattern, inverses, pivots):
    n = lax.axis_size("prow")
    m = lax.axis_size("pcol")
    r = lax.axis_index("prow")
    j = lax.axis_index("pcol")
    rb, width = matrix.shape[0], matrix.shape[1]
    half = width // 2
    chips = m // 2
    chip, core = j // 2, j % 2
    dt = matrix.dtype

    low_first = pivots[0, 1] == 0
    a_low = jnp.where(low_first, pivots[0, 0], pivots[1, 0])
    a_high = jnp.where(low_first, pivots[1, 0], pivots[0, 0])
    c0, c1 = pivots[0, 2], pivots[1, 2]
    is_low, is_high = r == n // 2, r == n // 2 - 1
    is_end = (r == 0) | (r == n - 1)
    out = jnp.where(
        r == 0, 0, jnp.where(is_low, a_low // n, jnp.where(is_high, a_high // n, rb - 1))
    )
    slots = [(out + 1 + k) % rb for k in range(rb)]

    blocks = matrix.reshape(rb, width, width)
    mine = lax.dynamic_slice(pattern.reshape(rb, n, m), (0, r, j), (rb, 1, 1)).reshape(rb)

    def block(slot):
        keep = lax.dynamic_index_in_dim(mine, slot, 0, keepdims=False) != 0
        one = lax.dynamic_index_in_dim(blocks, slot, 0, keepdims=False)
        return jnp.where(keep, one, jnp.zeros_like(one))

    raw = [block(s) for s in slots]
    leaving = raw[-1]

    def along(pairs, value):
        return lax.ppermute(value, "prow", pairs)

    first_hop = [(0, 1), (n - 1, n - 2), (n // 2, 0), (n // 2 - 1, n - 1)]
    za = along(first_hop, leaving)
    low = jnp.where(r == 0, leaving, za)
    high = jnp.where(r == n - 1, leaving, za)
    parts_low, parts_high = [], []
    for p in range(2):
        cut = slice(p * half, (p + 1) * half)
        got = za[cut]
        lo, hi = low[cut], high[cut]
        for h in range(1, n - 1):
            got = along([(h, h + 1), (n - 1 - h, n - 2 - h)], got)
            lo = jnp.where(r == h + 1, got, lo)
            hi = jnp.where(r == n - 2 - h, got, hi)
        parts_low.append(lo)
        parts_high.append(hi)
    row_low = jnp.concatenate(parts_low)
    row_high = jnp.concatenate(parts_high)
    upper = jnp.where(low_first, row_low, row_high)
    later = jnp.where(low_first, row_high, row_low)

    swap = [(i, i ^ 1) for i in range(m)]

    def sibling(value):
        return lax.ppermute(value, "pcol", swap)

    def own_half(value):
        return lax.dynamic_slice_in_dim(value, core * half, half, value.ndim - 2)

    def other_half(value):
        return lax.dynamic_slice_in_dim(value, (1 - core) * half, half, value.ndim - 2)

    def whole(own, other):
        top = jnp.where(core == 0, own, other)
        low_part = jnp.where(core == 0, other, own)
        return jnp.concatenate([top, low_part], axis=-2)

    order = ring_order(chips)
    place = [order.index(k) for k in range(chips)]
    around = []
    for i in range(chips):
        around.append((2 * order[i], 2 * order[(i + 1) % chips]))
        around.append((2 * order[i] + 1, 2 * order[(i - 1) % chips] + 1))

    def distance(column):
        gap = lookup(place, chip) - lookup(place, column // 2)
        return jnp.where(core == 0, gap, -gap) % chips

    early = jnp.stack(raw)
    early_own = own_half(early)
    early_sib = sibling(other_half(early))
    in_own = own_half(za)
    in_sib = sibling(other_half(za))

    def held(column, k):
        hit = column % 2 == core
        if k < rb - 1:
            return jnp.where(hit, early_own[k], early_sib[k])
        own = jnp.where(is_end, in_own, early_own[k])
        sib = jnp.where(is_end, in_sib, early_sib[k])
        return jnp.where(hit, own, sib)

    column_x = jnp.where((r == 0) == low_first, c1, c0)
    dist_x = distance(column_x)
    x = jnp.where(column_x % 2 == core, early_own[-1], early_sib[-1])
    for hop in range(chips - 1):
        got = lax.ppermute(x, "pcol", around)
        x = jnp.where(dist_x == hop + 1, got, x)
    x_low, x_high = x, x
    stride = n // 2
    while stride:
        pairs = []
        for i in range(0, n, 2 * stride):
            pairs += [(i, i + stride), (n - 1 - i, n - 1 - i - stride)]
        send = jnp.where(r % (2 * stride) == 0, x_low, x_high)
        got = along(pairs, send)
        x_low = jnp.where(r % (2 * stride) == stride, got, x_low)
        x_high = jnp.where((n - 1 - r) % (2 * stride) == stride, got, x_high)
        stride //= 2
    v_half = jnp.where(low_first, x_low, x_high)
    l_half = jnp.where(low_first, x_high, x_low)

    def product(left, right):
        return jnp.dot(left, right, preferred_element_type=jnp.float32)

    l_half = product(l_half, inverses[0]).astype(dt)
    vl_half = jnp.stack([v_half, l_half])
    vl = whole(vl_half, sibling(vl_half))
    v, left_later = vl[0], vl[1]

    columns = [c0, c1]
    dists = [distance(c) for c in columns]
    got = None
    gots = []
    for t in range(rb + chips - 2):
        send = []
        for q in range(2):
            own = held(columns[q], min(t, rb - 1))
            send.append(own if t == 0 else jnp.where(dists[q] == 0, own, got[q]))
        got = lax.ppermute(jnp.stack(send), "pcol", around)
        gots.append(got)

    def panel(q, k):
        value = held(columns[q], k)
        for d in range(1, chips):
            value = jnp.where(dists[q] == d, gots[k + d - 1][q], value)
        return value

    lefts = []
    for k in range(rb):
        m0 = product(panel(0, k), inverses[0]).astype(dt)
        p1 = (panel(1, k).astype(jnp.float32) - product(m0, v)).astype(dt)
        m1 = product(p1, inverses[1]).astype(dt)
        mm = jnp.stack([m0, m1])
        lefts.append(whole(mm, sibling(mm)))

    next_upper = (later.astype(jnp.float32) - product(left_later, upper)).astype(dt)
    raw[-1] = jnp.where(is_end, za, leaving)
    done = []
    for k in range(rb):
        m0, m1 = lefts[k][0], lefts[k][1]
        w = (raw[k].astype(jnp.float32) - product(m0, upper)).astype(dt)
        w = (w.astype(jnp.float32) - product(m1, next_upper)).astype(dt)
        done.append(jnp.where(j == c0, m0, jnp.where(j == c1, m1, w)))
    pivot_first = (is_low & low_first) | (is_high & ~low_first)
    pivot_later = (is_low & ~low_first) | (is_high & low_first)
    frozen = jnp.where(j == c0, left_later, next_upper)
    done[-1] = jnp.where(pivot_first, upper, jnp.where(pivot_later, frozen, done[-1]))
    result = jnp.stack(done)
    result = jnp.stack(
        [
            lax.dynamic_index_in_dim(result, (slot - out - 1) % rb, 0, keepdims=False)
            for slot in range(rb)
        ]
    )
    return result.reshape(matrix.shape)


def solution(mesh):
    placed = (P(None, "prow", None, "pcol"), P(), P(), P())
    return jax.shard_map(
        local, mesh=mesh, in_specs=placed, out_specs=P(None, "prow", None, "pcol"), check_vma=False
    )
```

time: 285 us -> 118 us (0.41)
  waiting for transfers between devices: 223 us -> 31.7 us
  starting transfers between devices: 6.36 us -> 29 us
  between operations: 29.6 us -> 13.5 us
  other arithmetic: 8.07 us -> 18.6 us
  local copies, waits for them, and re-layouts: 1.87 us -> 6 us
  matrix products: 15 us -> 18.4 us
    psum x4 -> x0, waiting for transfers between devices: 181 us -> none  [broadcast(): return lax.psum(block, axis)]
    ppermute x2 -> x21, starting transfers between devices: 6.23 us -> 29 us  [the longest x7 13.5 us: along(): return lax.ppermute(value, 'prow', pairs)]
    ppermute x2 -> x21, waiting for transfers between devices: 42.2 us -> 31.7 us  [the longest x7 21.8 us: along(): return lax.ppermute(value, 'prow', pairs)]
    another operation x0 -> x15, other arithmetic: none -> 8.7 us  [the longest x8 4.5 us: local(): got = lax.ppermute(jnp.stack(send), 'pcol', around)]
    select_n x4 -> x12, other arithmetic: 2.63 us -> 8.63 us  [the longest x2 2.54 us: whole(): top = jnp.where(core == 0, own, other)]
    dot_general x5 -> x14, matrix products: 15 us -> 18.4 us  [product(): return jnp.dot(left, right, preferred_element_type=jnp.float32)]
    unnamed x6 -> x49, local copies, waits for them, and re-layouts: 0.01 us -> 2.96 us
  transfers between devices with their start and end apart: 6 -> 21, of which waited for: 6 -> 10; matrix products, arithmetic and copies ran while one was open for 4% -> 18% of each run, Pallas kernels for 0% -> 0%
where the time goes in v1:
time: 118 us; the launch traced here: 117 us
  waiting for transfers between devices  31.7 us (27%)
  starting transfers between devices  29 us (25%)
  other arithmetic  18.6 us (16%)
  matrix products  18.4 us (16%)
  between operations  13.5 us (11%)
  local copies, waits for them, and re-layouts  6 us (5%)
    ppermute x7, waiting for transfers between devices, along(): return lax.ppermute(value, 'prow', pairs)  21.8 us
    dot_general x14, matrix products, product(): return jnp.dot(left, right, preferred_element_type=jnp.float32)  18.4 us
    ppermute x7, starting transfers between devices, along(): return lax.ppermute(value, 'prow', pairs)  13.5 us
    ppermute x5, starting transfers between devices, local(): got = lax.ppermute(jnp.stack(send), 'pcol', around)  8.28 us
    ppermute x5, waiting for transfers between devices, local(): got = lax.ppermute(jnp.stack(send), 'pcol', around)  7.53 us
    ppermute x3, starting transfers between devices, local(): got = lax.ppermute(x, 'pcol', around)  6.08 us
    another operation x8, other arithmetic, local(): got = lax.ppermute(jnp.stack(send), 'pcol', around)  4.5 us
    another operation x3, other arithmetic, local(): mm = jnp.stack([m0, m1])  3.75 us
  transfers between devices with their start and end apart: 21, of which 10 were waited for; matrix products, arithmetic and copies ran while one was open for 18% of the time, Pallas kernels for 0%

profile of v1, /device:TPU:0, one launch (start us, length us, event | category | flops | bytes accessed | tf_op | source)
XLA Modules:
  0.0 117.3 jit_solution(10731827066667029683)
XLA Ops:
  16.0 2.5 %collective-permute-start.3 = (bf16[2,256,512]{2,1,0:T(8,128)(2,1)}, bf16[2,256,512]{2,1,0:T(8,128)(2,1)S(1)}, u32[]{:S(2)}, u32[]{:S(2)}) collective-permute-start(bf16[2,256,512]{2,1,0:T(8,128)(2,1)} %pad_maximum_fusion.6), channel_id=1, source_target_pairs={{2,6},{3,1},{6,4},{7,3},{4,0},{5,7},{0,2},{1,5},{10,14},{11,9},{14... | collective-permute-start | bytes 1572872 | tf_op jit(solution)/shard_map/ppermute | solution.py:159
  21.4 4.4 %collective-permute-done.3 = bf16[2,256,512]{2,1,0:T(8,128)(2,1)S(1)} collective-permute-done((bf16[2,256,512]{2,1,0:T(8,128)(2,1)}, bf16[2,256,512]{2,1,0:T(8,128)(2,1)S(1)}, u32[]{:S(2)}, u32[]{:S(2)}) %collective-permute-start.3) | collective-permute-done | bytes 524320 | tf_op jit(solution)/shard_map/ppermute | solution.py:159
  28.0 2.0 %collective-permute-start.4 = (bf16[2,256,512]{2,1,0:T(8,128)(2,1)}, bf16[2,256,512]{2,1,0:T(8,128)(2,1)}, u32[]{:S(2)}, u32[]{:S(2)}) collective-permute-start(bf16[2,256,512]{2,1,0:T(8,128)(2,1)} %pad_maximum_fusion.7), channel_id=1, source_target_pairs={{2,6},{3,1},{6,4},{7,3},{4,0},{5,7},{0,2},{1,5},{10,14},{11,9},{14... | collective-permute-start | bytes 1572872 | tf_op jit(solution)/shard_map/ppermute | solution.py:159
  30.0 3.5 %collective-permute-done = bf16[512,512]{1,0:T(8,128)(2,1)S(1)} collective-permute-done((bf16[512,512]{1,0:T(8,128)(2,1)S(1)}, bf16[512,512]{1,0:T(8,128)(2,1)S(1)}, u32[]{:S(2)}, u32[]{:S(2)}) %collective-permute-start) | collective-permute-done | bytes 524320 | tf_op jit(solution)/shard_map/ppermute | solution.py:59
  37.5 2.4 %fusion.76 = (bf16[1,256,512]{2,1,0:T(8,128)(2,1)}, bf16[256,512]{1,0:T(8,128)(2,1)S(1)}, bf16[1,256,512]{2,1,0:T(8,128)(2,1)}, bf16[256,512]{1,0:T(8,128)(2,1)S...) fusion(pred[]{:T(512)S(6)} %eq.248, ...), kind=kLoop, calls=%fused_computation.142 | loop fusion | flops 917504 | bytes 3932174 | tf_op jit(solution)/shard_map/stack | solution.py:159
  39.9 2.0 %collective-permute-start.6 = (bf16[256,512]{1,0:T(8,128)(2,1)}, bf16[256,512]{1,0:T(8,128)(2,1)}, u32[]{:S(2)}, u32[]{:S(2)}) collective-permute-start(bf16[256,512]{1,0:T(8,128)(2,1)} %get-tuple-element.15), channel_id=1, source_target_pairs={{2,6},{3,1},{6,4},{7,3},{4,0},{5,7},{0,2},{1,5},{10,14},{11,9},{14... | collective-permute-start | bytes 786440 | tf_op jit(solution)/shard_map/ppermute | solution.py:126
  44.9 1.7 %collective-permute-done.6 = bf16[256,512]{1,0:T(8,128)(2,1)} collective-permute-done((bf16[256,512]{1,0:T(8,128)(2,1)}, bf16[256,512]{1,0:T(8,128)(2,1)}, u32[]{:S(2)}, u32[]{:S(2)}) %collective-permute-start.6) | collective-permute-done | bytes 262176 | tf_op jit(solution)/shard_map/ppermute | solution.py:126
  47.6 2.0 %collective-permute-start.7 = (bf16[256,512]{1,0:T(8,128)(2,1)S(1)}, bf16[256,512]{1,0:T(8,128)(2,1)S(1)}, u32[]{:S(2)}, u32[]{:S(2)}) collective-permute-start(bf16[256,512]{1,0:T(8,128)(2,1)S(1)} %broadcast_select_fusion.14), channel_id=1, source_target_pairs={{2,6},{3,1},{6,4},{7,3},{4,0},{5,7},{0,2},{1,5},{10,14},{11,9},{14... | collective-permute-start | bytes 786440 | tf_op jit(solution)/shard_map/ppermute | solution.py:126
  54.0 2.0 %collective-permute-start.8 = (bf16[256,512]{1,0:T(8,128)(2,1)S(1)}, bf16[256,512]{1,0:T(8,128)(2,1)S(1)}, u32[]{:S(2)}, u32[]{:S(2)}) collective-permute-start(bf16[256,512]{1,0:T(8,128)(2,1)S(1)} %broadcast_select_fusion.15), channel_id=1, source_target_pairs={{2,6},{3,1},{6,4},{7,3},{4,0},{5,7},{0,2},{1,5},{10,14},{11,9},{14... | collective-permute-start | bytes 786440 | tf_op jit(solution)/shard_map/ppermute | solution.py:126
  56.1 8.5 %collective-permute-done.16 = bf16[256,512]{1,0:T(8,128)(2,1)S(1)} collective-permute-done((bf16[256,512]{1,0:T(8,128)(2,1)S(1)}, bf16[256,512]{1,0:T(8,128)(2,1)S(1)}, u32[]{:S(2)}, u32[]{:S(2)}) %collective-permute-start.16) | collective-permute-done | bytes 262176 | tf_op jit(solution)/shard_map/ppermute | solution.py:59
  64.6 3.0 %collective-permute-done.14 = bf16[256,512]{1,0:T(8,128)(2,1)S(1)} collective-permute-done((bf16[256,512]{1,0:T(8,128)(2,1)S(1)}, bf16[256,512]{1,0:T(8,128)(2,1)S(1)}, u32[]{:S(2)}, u32[]{:S(2)}) %collective-permute-start.14) | collective-permute-done | bytes 262176 | tf_op jit(solution)/shard_map/ppermute | solution.py:59
  69.3 6.6 %collective-permute-start.9 = (bf16[256,512]{1,0:T(8,128)(2,1)S(1)}, bf16[256,512]{1,0:T(8,128)(2,1)S(1)}, u32[]{:S(2)}, u32[]{:S(2)}) collective-permute-start(bf16[256,512]{1,0:T(8,128)(2,1)S(1)} %broadcast_select_fusion.16), channel_id=1, source_target_pairs={{0,16},{24,8},{1,17},{25,9},{2,18},{26,10},{3,19},{27,11},{4,20},{... | collective-permute-start | bytes 786440 | tf_op jit(solution)/shard_map/ppermute | solution.py:59
  75.9 1.9 %convolution_convert_fusion.6 = bf16[256,512]{1,0:T(8,128)(2,1)} fusion(bf16[2,512,512]{2,1,0:T(8,128)(2,1)S(1)} %copy-done.22, bf16[1,256,512]{2,1,0:T(8,128)(2,1)S(1)} %copy-done.2, pred[]{:T(512)S(6)} %eq.263, pred[]{:T(512)S(6)} %eq.262, pred[]{:T(512)S(6)} %eq.247, bf16[2,256,512]{2,1,0:T(8,128)(2,1)S(1)} %copy-done.15, ...), kind=kOutput, calls=%fused_computation.32 | convolution fusion | flops 134742016 | bytes 1835011 | tf_op jit(solution)/shard_map/dot_general | solution.py:143
  77.9 3.6 %collective-permute-done.9 = bf16[256,512]{1,0:T(8,128)(2,1)S(1)} collective-permute-done((bf16[256,512]{1,0:T(8,128)(2,1)S(1)}, bf16[256,512]{1,0:T(8,128)(2,1)S(1)}, u32[]{:S(2)}, u32[]{:S(2)}) %collective-permute-start.9) | collective-permute-done | bytes 262176 | tf_op jit(solution)/shard_map/ppermute | solution.py:59
  83.0 1.7 %collective-permute-start.19 = (bf16[2,256,512]{2,1,0:T(8,128)(2,1)S(1)}, bf16[2,256,512]{2,1,0:T(8,128)(2,1)S(1)}, u32[]{:S(2)}, u32[]{:S(2)}) collective-permute-start(bf16[2,256,512]{2,1,0:T(8,128)(2,1)S(1)} %pad_maximum_fusion.15), channel_id=1, source_target_pairs={{2,6},{3,1},{6,4},{7,3},{4,0},{5,7},{0,2},{1,5},{10,14},{11,9},{14... | collective-permute-start | bytes 1572872 | tf_op jit(solution)/shard_map/ppermute | solution.py:159
  84.7 3.3 %collective-permute-done.10 = bf16[256,512]{1,0:T(8,128)(2,1)S(1)} collective-permute-done((bf16[256,512]{1,0:T(8,128)(2,1)S(1)}, bf16[256,512]{1,0:T(8,128)(2,1)S(1)}, u32[]{:S(2)}, u32[]{:S(2)}) %collective-permute-start.10) | collective-permute-done | bytes 262176 | tf_op jit(solution)/shard_map/ppermute | solution.py:59
  88.5 2.1 %convolution_convert_fusion.3 = bf16[256,512]{1,0:T(8,128)(2,1)} fusion(bf16[2,512,512]{2,1,0:T(8,128)(2,1)S(1)} %copy-done.22, pred[]{:T(512)S(6)} %eq.263, pred[]{:T(512)S(6)} %eq.262, pred[]{:T(512)S(6)} %eq.247, bf16[2,256,512]{2,1,0:T(8,128)(2,1)S(1)} %collective-permute-done.17, bf16[2,256,512]{2,1,0:T(8,128)(2,1)} %collective-permute-done.4, ...), kind=kOutput, calls=%fused_computation.29 | convolution fusion | flops 134873088 | bytes 2097164 | tf_op jit(solution)/shard_map/dot_general | solution.py:143
  90.5 1.7 %collective-permute-done.19 = bf16[2,256,512]{2,1,0:T(8,128)(2,1)S(1)} collective-permute-done((bf16[2,256,512]{2,1,0:T(8,128)(2,1)S(1)}, bf16[2,256,512]{2,1,0:T(8,128)(2,1)S(1)}, u32[]{:S(2)}, u32[]{:S(2)}) %collective-permute-start.19) | collective-permute-done | bytes 524320 | tf_op jit(solution)/shard_map/ppermute | solution.py:159
  94.3 2.8 %fusion.21 = bf16[1,256,512]{2,1,0:T(8,128)(2,1)} fusion(bf16[2,512,512]{2,1,0:T(8,128)(2,1)} %param.6, bf16[2,256,512]{2,1,0:T(8,128)(2,1)} %copy-done.23, bf16[256,512]{1,0:T(8,128)(2,1)S(1)} %get-tuple-element.12, pred[]{:T(512)S(6)} %eq.266, pred[]{:T(512)S(6)} %eq.265, pred[]{:T(512)S(6)} %eq.264, bf16[2,256,512]{2,1,0:T(8,128)(2,1)} %copy-done.17, ...), kind=kOutput, calls=%fused_computation.36 | convolution fusion | flops 270401536 | bytes 3145731 | tf_op jit(solution)/shard_map/dot_general | solution.py:143
  97.1 1.9 %pad_maximum_fusion.16 = bf16[2,256,512]{2,1,0:T(8,128)(2,1)} fusion(bf16[1,256,512]{2,1,0:T(8,128)(2,1)} %fusion.21, bf16[1,256,512]{2,1,0:T(8,128)(2,1)} %bitcast.255), kind=kLoop, calls=%fused_computation.74 | loop fusion | flops 262144 | bytes 1048576 | tf_op jit(solution)/shard_map/stack | solution.py:173
  99.0 2.7 %fusion.19 = bf16[1,256,512]{2,1,0:T(8,128)(2,1)} fusion(bf16[2,512,512]{2,1,0:T(8,128)(2,1)} %param.6, bf16[1,256,512]{2,1,0:T(8,128)(2,1)S(1)} %get-tuple-element.17, pred[]{:T(512)S(6)} %eq.266, pred[]{:T(512)S(6)} %eq.265, pred[]{:T(512)S(6)} %eq.264, bf16[2,256,512]{2,1,0:T(8,128)(2,1)} %copy-done.14, bf16[2,256,512]{2,1,0:T(8,128)(2,1)} %collective-permute-done.4, ...), kind=kOutput, calls=%fused_computation.34 | convolution fusion | flops 270401536 | bytes 3145731 | tf_op jit(solution)/shard_map/dot_general | solution.py:143
  101.7 1.8 %pad_maximum_fusion.10 = bf16[2,256,512]{2,1,0:T(8,128)(2,1)} fusion(bf16[1,256,512]{2,1,0:T(8,128)(2,1)} %fusion.19, bf16[1,256,512]{2,1,0:T(8,128)(2,1)S(1)} %bitcast.251), kind=kLoop, calls=%fused_computation.68 | loop fusion | flops 262144 | bytes 1048576 | tf_op jit(solution)/shard_map/stack | solution.py:173
  104.0 2.1 %fusion.20 = bf16[1,256,512]{2,1,0:T(8,128)(2,1)S(1)} fusion(bf16[2,512,512]{2,1,0:T(8,128)(2,1)} %param.6, pred[]{:T(512)S(6)} %eq.266, pred[]{:T(512)S(6)} %eq.265, pred[]{:T(512)S(6)} %eq.264, bf16[2,256,512]{2,1,0:T(8,128)(2,1)} %collective-permute-done.4, bf16[2,256,512]{2,1,0:T(8,128)(2,1)} %copy-done.17, bf16[2,256,512]{2,1,0:T(8,128)(2,1)} %copy-done.16, ...), kind=kOutput, calls=%fused_computation.35 | convolution fusion | flops 270532608 | bytes 3407884 | tf_op jit(solution)/shard_map/dot_general | solution.py:143
  106.8 2.2 %subtract_convert_fusion = bf16[512,512]{1,0:T(8,128)(2,1)S(1)} fusion(pred[]{:T(512)} %bitcast.1, bf16[256,512]{1,0:T(8,128)(2,1)} %get-tuple-element.43, bf16[256,512]{1,0:T(8,128)(2,1)} %get-tuple-element.44, bf16[256,512]{1,0:T(8,128)(2,1)} %get-tuple-element.42, bf16[256,512]{1,0:T(8,128)(2,1)} %get-tuple-element.41, ...), kind=kOutput, calls=%fused_computation.45 | convolution fusion | flops 274989056 | bytes 2621441 | tf_op jit(solution)/shard_map/dot_general | solution.py:143
  (115 shorter events, 35.4 us)
Async XLA Ops:
  9.7 4.4 %collective-permute-start.2 = (bf16[3,256,512]{2,1,0:T(8,128)(2,1)S(1)}, bf16[3,256,512]{2,1,0:T(8,128)(2,1)}, u32[]{:S(2)}, u32[]{:S(2)}) collective-permute-start(bf16[3,256,512]{2,1,0:T(8,128)(2,1)S(1)} %constant_dynamic-slice_fusion.3), channel_id=1, source_target_pairs={{0,1},{1,0},{2,3},{3,2},{4,5},{5,4},{6,7},{7,6},{8,9},{9,8},{10,11... | collective-permute-start | bytes 2359304 | tf_op jit(solution)/shard_map/ppermute | solution.py:84
  16.0 9.9 %collective-permute-start.3 = (bf16[2,256,512]{2,1,0:T(8,128)(2,1)}, bf16[2,256,512]{2,1,0:T(8,128)(2,1)S(1)}, u32[]{:S(2)}, u32[]{:S(2)}) collective-permute-start(bf16[2,256,512]{2,1,0:T(8,128)(2,1)} %pad_maximum_fusion.6), channel_id=1, source_target_pairs={{2,6},{3,1},{6,4},{7,3},{4,0},{5,7},{0,2},{1,5},{10,14},{11,9},{14... | collective-permute-start | bytes 1572872 | tf_op jit(solution)/shard_map/ppermute | solution.py:159
  18.5 15.0 %collective-permute-start = (bf16[512,512]{1,0:T(8,128)(2,1)S(1)}, bf16[512,512]{1,0:T(8,128)(2,1)S(1)}, u32[]{:S(2)}, u32[]{:S(2)}) collective-permute-start(bf16[512,512]{1,0:T(8,128)(2,1)S(1)} %get-tuple-element.23), channel_id=1, source_target_pairs={{0,8},{24,16},{16,0},{8,24},{1,9},{25,17},{17,1},{9,25},{2,10},{26... | collective-permute-start | bytes 1572872 | tf_op jit(solution)/shard_map/ppermute | solution.py:59
  28.0 9.5 %collective-permute-start.4 = (bf16[2,256,512]{2,1,0:T(8,128)(2,1)}, bf16[2,256,512]{2,1,0:T(8,128)(2,1)}, u32[]{:S(2)}, u32[]{:S(2)}) collective-permute-start(bf16[2,256,512]{2,1,0:T(8,128)(2,1)} %pad_maximum_fusion.7), channel_id=1, source_target_pairs={{2,6},{3,1},{6,4},{7,3},{4,0},{5,7},{0,2},{1,5},{10,14},{11,9},{14... | collective-permute-start | bytes 1572872 | tf_op jit(solution)/shard_map/ppermute | solution.py:159
  34.2 1.9 %collective-permute-start.1 = (bf16[256,512]{1,0:T(8,128)(2,1)}, bf16[256,512]{1,0:T(8,128)(2,1)}, u32[]{:S(2)}, u32[]{:S(2)}) collective-permute-start(bf16[256,512]{1,0:T(8,128)(2,1)} %constant_dynamic-slice_fusion.4), channel_id=1, source_target_pairs={{0,1},{1,0},{2,3},{3,2},{4,5},{5,4},{6,7},{7,6},{8,9},{9,8},{10,11... | collective-permute-start | bytes 786440 | tf_op jit(solution)/shard_map/ppermute | solution.py:84
  39.9 6.7 %collective-permute-start.6 = (bf16[256,512]{1,0:T(8,128)(2,1)}, bf16[256,512]{1,0:T(8,128)(2,1)}, u32[]{:S(2)}, u32[]{:S(2)}) collective-permute-start(bf16[256,512]{1,0:T(8,128)(2,1)} %get-tuple-element.15), channel_id=1, source_target_pairs={{2,6},{3,1},{6,4},{7,3},{4,0},{5,7},{0,2},{1,5},{10,14},{11,9},{14... | collective-permute-start | bytes 786440 | tf_op jit(solution)/shard_map/ppermute | solution.py:126
  43.4 9.0 %copy-start.3 = (bf16[1,256,512]{2,1,0:T(8,128)(2,1)S(1)}, bf16[1,256,512]{2,1,0:T(8,128)(2,1)}, u32[]{:S(2)}) copy-start(bf16[1,256,512]{2,1,0:T(8,128)(2,1)} %get-tuple-element.5) | copy-start | bytes 786436
  43.4 6.3 %collective-permute-start.15 = (bf16[256,512]{1,0:T(8,128)(2,1)}, bf16[256,512]{1,0:T(8,128)(2,1)S(1)}, u32[]{:S(2)}, u32[]{:S(2)}) collective-permute-start(bf16[256,512]{1,0:T(8,128)(2,1)} %get-tuple-element.39), channel_id=1, source_target_pairs={{8,16},{16,8},{9,17},{17,9},{10,18},{18,10},{11,19},{19,11},{12,20... | collective-permute-start | bytes 786440 | tf_op jit(solution)/shard_map/ppermute | solution.py:59
  44.2 6.8 %collective-permute-start.13 = (bf16[256,512]{1,0:T(8,128)(2,1)}, bf16[256,512]{1,0:T(8,128)(2,1)S(1)}, u32[]{:S(2)}, u32[]{:S(2)}) collective-permute-start(bf16[256,512]{1,0:T(8,128)(2,1)} %get-tuple-element.40), channel_id=1, source_target_pairs={{8,16},{16,8},{9,17},{17,9},{10,18},{18,10},{11,19},{19,11},{12,20... | collective-permute-start | bytes 786440 | tf_op jit(solution)/shard_map/ppermute | solution.py:59
  47.6 6.4 %collective-permute-start.7 = (bf16[256,512]{1,0:T(8,128)(2,1)S(1)}, bf16[256,512]{1,0:T(8,128)(2,1)S(1)}, u32[]{:S(2)}, u32[]{:S(2)}) collective-permute-start(bf16[256,512]{1,0:T(8,128)(2,1)S(1)} %broadcast_select_fusion.14), channel_id=1, source_target_pairs={{2,6},{3,1},{6,4},{7,3},{4,0},{5,7},{0,2},{1,5},{10,14},{11,9},{14... | collective-permute-start | bytes 786440 | tf_op jit(solution)/shard_map/ppermute | solution.py:126
  49.7 14.8 %collective-permute-start.16 = (bf16[256,512]{1,0:T(8,128)(2,1)S(1)}, bf16[256,512]{1,0:T(8,128)(2,1)S(1)}, u32[]{:S(2)}, u32[]{:S(2)}) collective-permute-start(bf16[256,512]{1,0:T(8,128)(2,1)S(1)} %collective-permute-done.15), channel_id=1, source_target_pairs={{16,24},{8,0},{17,25},{9,1},{18,26},{10,2},{19,27},{11,3},{20,28},... | collective-permute-start | bytes 786440 | tf_op jit(solution)/shard_map/ppermute | solution.py:59
  51.0 16.5 %collective-permute-start.14 = (bf16[256,512]{1,0:T(8,128)(2,1)S(1)}, bf16[256,512]{1,0:T(8,128)(2,1)S(1)}, u32[]{:S(2)}, u32[]{:S(2)}) collective-permute-start(bf16[256,512]{1,0:T(8,128)(2,1)S(1)} %collective-permute-done.13), channel_id=1, source_target_pairs={{16,24},{8,0},{17,25},{9,1},{18,26},{10,2},{19,27},{11,3},{20,28},... | collective-permute-start | bytes 786440 | tf_op jit(solution)/shard_map/ppermute | solution.py:59
  52.4 16.2 %collective-permute-start.5 = (bf16[2,256,512]{2,1,0:T(8,128)(2,1)S(1)}, bf16[2,256,512]{2,1,0:T(8,128)(2,1)S(1)}, u32[]{:S(2)}, u32[]{:S(2)}) collective-permute-start(bf16[2,256,512]{2,1,0:T(8,128)(2,1)S(1)} %pad_maximum_fusion.8), channel_id=1, source_target_pairs={{2,6},{3,1},{6,4},{7,3},{4,0},{5,7},{0,2},{1,5},{10,14},{11,9},{14... | collective-permute-start | bytes 1572872 | tf_op jit(solution)/shard_map/ppermute | solution.py:159
  54.0 15.2 %collective-permute-start.8 = (bf16[256,512]{1,0:T(8,128)(2,1)S(1)}, bf16[256,512]{1,0:T(8,128)(2,1)S(1)}, u32[]{:S(2)}, u32[]{:S(2)}) collective-permute-start(bf16[256,512]{1,0:T(8,128)(2,1)S(1)} %broadcast_select_fusion.15), channel_id=1, source_target_pairs={{2,6},{3,1},{6,4},{7,3},{4,0},{5,7},{0,2},{1,5},{10,14},{11,9},{14... | collective-permute-start | bytes 786440 | tf_op jit(solution)/shard_map/ppermute | solution.py:126
  68.6 23.6 %copy-start.16 = (bf16[2,256,512]{2,1,0:T(8,128)(2,1)}, bf16[2,256,512]{2,1,0:T(8,128)(2,1)S(1)}, u32[]{:S(2)}) copy-start(bf16[2,256,512]{2,1,0:T(8,128)(2,1)S(1)} %collective-permute-done.5) | copy-start | bytes 1572868
  68.8 14.1 %collective-permute-start.17 = (bf16[2,256,512]{2,1,0:T(8,128)(2,1)S(1)}, bf16[2,256,512]{2,1,0:T(8,128)(2,1)S(1)}, u32[]{:S(2)}, u32[]{:S(2)}) collective-permute-start(bf16[2,256,512]{2,1,0:T(8,128)(2,1)S(1)} %pad_maximum_fusion.13), channel_id=1, source_target_pairs={{2,6},{3,1},{6,4},{7,3},{4,0},{5,7},{0,2},{1,5},{10,14},{11,9},{14... | collective-permute-start | bytes 1572872 | tf_op jit(solution)/shard_map/ppermute | solution.py:159
  69.3 12.2 %collective-permute-start.9 = (bf16[256,512]{1,0:T(8,128)(2,1)S(1)}, bf16[256,512]{1,0:T(8,128)(2,1)S(1)}, u32[]{:S(2)}, u32[]{:S(2)}) collective-permute-start(bf16[256,512]{1,0:T(8,128)(2,1)S(1)} %broadcast_select_fusion.16), channel_id=1, source_target_pairs={{0,16},{24,8},{1,17},{25,9},{2,18},{26,10},{3,19},{27,11},{4,20},{... | collective-permute-start | bytes 786440 | tf_op jit(solution)/shard_map/ppermute | solution.py:59
  81.5 6.4 %collective-permute-start.10 = (bf16[256,512]{1,0:T(8,128)(2,1)S(1)}, bf16[256,512]{1,0:T(8,128)(2,1)S(1)}, u32[]{:S(2)}, u32[]{:S(2)}) collective-permute-start(bf16[256,512]{1,0:T(8,128)(2,1)S(1)} %get-tuple-element.9), channel_id=1, source_target_pairs={{0,8},{24,16},{16,24},{8,0},{1,9},{25,17},{17,25},{9,1},{2,10},{26... | collective-permute-start | bytes 786440 | tf_op jit(solution)/shard_map/ppermute | solution.py:59
  82.8 9.4 %copy-start.17 = (bf16[2,256,512]{2,1,0:T(8,128)(2,1)}, bf16[2,256,512]{2,1,0:T(8,128)(2,1)S(1)}, u32[]{:S(2)}) copy-start(bf16[2,256,512]{2,1,0:T(8,128)(2,1)S(1)} %collective-permute-done.17) | copy-start | bytes 1572868
  83.0 9.2 %collective-permute-start.19 = (bf16[2,256,512]{2,1,0:T(8,128)(2,1)S(1)}, bf16[2,256,512]{2,1,0:T(8,128)(2,1)S(1)}, u32[]{:S(2)}, u32[]{:S(2)}) collective-permute-start(bf16[2,256,512]{2,1,0:T(8,128)(2,1)S(1)} %pad_maximum_fusion.15), channel_id=1, source_target_pairs={{2,6},{3,1},{6,4},{7,3},{4,0},{5,7},{0,2},{1,5},{10,14},{11,9},{14... | collective-permute-start | bytes 1572872 | tf_op jit(solution)/shard_map/ppermute | solution.py:159
  88.4 4.9 %collective-permute-start.11 = (bf16[2,256,512]{2,1,0:T(8,128)(2,1)S(1)}, bf16[2,256,512]{2,1,0:T(8,128)(2,1)S(1)}, u32[]{:S(2)}, u32[]{:S(2)}) collective-permute-start(bf16[2,256,512]{2,1,0:T(8,128)(2,1)S(1)} %pad_maximum_fusion.9), channel_id=1, source_target_pairs={{0,1},{1,0},{2,3},{3,2},{4,5},{5,4},{6,7},{7,6},{8,9},{9,8},{10,11... | collective-permute-start | bytes 1572872 | tf_op jit(solution)/shard_map/ppermute | solution.py:84
  99.0 10.1 %collective-permute-start.20 = (bf16[2,256,512]{2,1,0:T(8,128)(2,1)}, bf16[2,256,512]{2,1,0:T(8,128)(2,1)}, u32[]{:S(2)}, u32[]{:S(2)}) collective-permute-start(bf16[2,256,512]{2,1,0:T(8,128)(2,1)} %pad_maximum_fusion.16), channel_id=1, source_target_pairs={{0,1},{1,0},{2,3},{3,2},{4,5},{5,4},{6,7},{7,6},{8,9},{9,8},{10,11... | collective-permute-start | bytes 1572872 | tf_op jit(solution)/shard_map/ppermute | solution.py:84
  103.5 5.5 %collective-permute-start.12 = (bf16[2,256,512]{2,1,0:T(8,128)(2,1)}, bf16[2,256,512]{2,1,0:T(8,128)(2,1)}, u32[]{:S(2)}, u32[]{:S(2)}) collective-permute-start(bf16[2,256,512]{2,1,0:T(8,128)(2,1)} %pad_maximum_fusion.10), channel_id=1, source_target_pairs={{0,1},{1,0},{2,3},{3,2},{4,5},{5,4},{6,7},{7,6},{8,9},{9,8},{10,11... | collective-permute-start | bytes 1572872 | tf_op jit(solution)/shard_map/ppermute | solution.py:84
  106.1 5.3 %collective-permute-start.18 = (bf16[2,256,512]{2,1,0:T(8,128)(2,1)S(1)}, bf16[2,256,512]{2,1,0:T(8,128)(2,1)S(1)}, u32[]{:S(2)}, u32[]{:S(2)}) collective-permute-start(bf16[2,256,512]{2,1,0:T(8,128)(2,1)S(1)} %pad_maximum_fusion.14), channel_id=1, source_target_pairs={{0,1},{1,0},{2,3},{3,2},{4,5},{5,4},{6,7},{7,6},{8,9},{9,8},{10,11... | collective-permute-start | bytes 1572872 | tf_op jit(solution)/shard_map/ppermute | solution.py:84
  (21 other events, 73.1 us)

commit v2 on v0

v2 whole, which is shorter than its diff:
```python
import functools

import jax
import jax.numpy as jnp
from jax import lax
from jax.experimental import pallas as pl
from jax.experimental.pallas import tpu as pltpu
from jax.sharding import PartitionSpec as P

SMEM = pl.BlockSpec(memory_space=pltpu.SMEM)
VMEM = pl.BlockSpec(memory_space=pltpu.VMEM)
ANY = pl.BlockSpec(memory_space=pl.ANY)
GRANT = pltpu.CompilerParams(vmem_limit_bytes=24 * 2**20)


def facts(n, m, rb, pivots):
    f = {}
    r = f["r"] = lax.axis_index("prow").astype(jnp.int32)
    j = f["j"] = lax.axis_index("pcol").astype(jnp.int32)
    f["core"] = j & 1
    f["chip"] = j >> 1
    low_first = f["low_first"] = pivots[0, 1] == 0
    shift = n.bit_length() - 1
    a_low = jnp.where(low_first, pivots[0, 0], pivots[1, 0]) >> shift
    a_high = jnp.where(low_first, pivots[1, 0], pivots[0, 0]) >> shift
    f["c"] = [pivots[0, 2], pivots[1, 2]]
    is_low, is_high = r == n // 2, r == n // 2 - 1
    f["is_low"], f["is_high"] = is_low, is_high
    f["is_end"] = jnp.logical_or(r == 0, r == n - 1)
    out = jnp.where(is_low, a_low, jnp.where(is_high, a_high, jnp.where(r == 0, 0, rb - 1)))
    f["slots"] = []
    for k in range(rb):
        slot = out + (1 + k)
        f["slots"].append(jnp.where(slot >= rb, slot - rb, slot))
    f["cx"] = jnp.where((r == 0) == low_first, pivots[1, 2], pivots[0, 2])
    return f


def either(cond, out_ref, yes, no):
    @pl.when(cond)
    def _():
        out_ref[...] = yes()

    @pl.when(jnp.logical_not(cond))
    def _():
        out_ref[...] = no()


def rows(part, half):
    return pl.ds(pl.multiple_of(part * half, half), half)


def prepare(n, m, piv, pat, mat, raw, leaving, other):
    rb, width = mat.shape[0], mat.shape[1]
    f = facts(n, m, rb, piv)
    cut = rows(1 - f["core"], width // 2)
    for k in reversed(range(rb)):
        slot = f["slots"][k]
        keep = pat[slot * n + f["r"], f["j"]] != 0
        zero = lambda: jnp.zeros((width, width), mat.dtype)
        either(keep, raw.at[k], lambda: mat[slot], zero)
        if k == rb - 1:
            leaving[...] = raw[k]
        other[k] = raw[k, cut, :]


def pick(n, m, piv, raw, sib, panel, extra):
    rb, width = raw.shape[0], raw.shape[1]
    f = facts(n, m, rb, piv)
    cut = rows(f["core"], width // 2)
    for q in range(2):
        hit = (f["c"][q] & 1) == f["core"]
        for k in range(rb - 1):
            either(hit, panel.at[q, k], lambda: raw[k, cut, :], lambda: sib[k])
    hit = (f["cx"] & 1) == f["core"]
    either(hit, extra, lambda: raw[rb - 1, cut, :], lambda: sib[rb - 1])


def pick_third(n, m, piv, raw, sib, moved, sib_moved, panel):
    rb, width = raw.shape[0], raw.shape[1]
    f = facts(n, m, rb, piv)
    cut = rows(f["core"], width // 2)
    for q in range(2):
        hit = (f["c"][q] & 1) == f["core"]

        @pl.when(f["is_end"])
        def _():
            either(hit, panel.at[q], lambda: moved[cut, :], lambda: sib_moved[cut, :])

        @pl.when(jnp.logical_not(f["is_end"]))
        def _():
            either(hit, panel.at[q], lambda: raw[rb - 1, cut, :], lambda: sib[rb - 1])


def bit_of(f, column, stage, stages):
    apart = f["chip"] ^ (column >> 1)
    bit = jnp.where(f["core"] == 0, stage, stages - 1 - stage)
    return ((apart >> bit) & 1) == 1


def forward(n, m, stage, stages, piv, had, got, panel):
    f = facts(n, m, 2, piv)
    for q in range(2):
        take = bit_of(f, f["c"][q], stage, stages)
        either(take, panel.at[q], lambda: got[q], lambda: had[q])


def forward_extra(n, m, stage, stages, piv, had, got, extra):
    f = facts(n, m, 2, piv)
    take = bit_of(f, f["cx"], stage, stages)
    either(take, extra, lambda: got[...], lambda: had[...])


def hand_on(n, m, stride, had, got, extra):
    r = lax.axis_index("prow").astype(jnp.int32)
    low = (r & (2 * stride - 1)) == stride
    high = ((n - 1 - r) & (2 * stride - 1)) == stride
    either(jnp.logical_or(low, high), extra, lambda: got[...], lambda: had[...])


def dot(left, right):
    return jnp.dot(left, right, preferred_element_type=jnp.float32)


def settle_extra(n, m, piv, inv, *refs):
    had, out = refs[:-1], refs[-1]
    f = facts(n, m, 2, piv)
    r = f["r"]
    stages = len(had) - 1
    for which in range(2):
        place = r if which == 0 else n - 1 - r
        low_is_v = f["low_first"] if which == 0 else jnp.logical_not(f["low_first"])
        for s in range(stages + 1):
            if s == 0:
                here = place == 0
            else:
                here = (place & (2 * (n >> s) - 1)) == (n >> s)

            @pl.when(jnp.logical_and(here, low_is_v))
            def _():
                out[0] = had[s][...]

            @pl.when(jnp.logical_and(here, jnp.logical_not(low_is_v)))
            def _():
                out[1] = had[s][...]

    out[1] = dot(out[1], inv[0]).astype(out.dtype)


def multiply(n, m, stages, blocks, piv, inv, vl, sib_vl, had, got, out, v):
    f = facts(n, m, 2, piv)
    half = vl.shape[1]
    v[rows(f["core"], half), :] = vl[0]
    v[rows(1 - f["core"], half), :] = sib_vl[0]
    take = [bit_of(f, f["c"][q], stages - 1, stages) for q in range(2)]
    for q in range(2):
        either(take[q], out.at[q], lambda: got[q], lambda: had[q])
    for k in range(blocks):
        where = (lambda q: (q, k)) if blocks > 1 else (lambda q: (q,))
        m0 = dot(out[where(0)], inv[0]).astype(out.dtype)
        p1 = (out[where(1)].astype(jnp.float32) - dot(m0, v[...])).astype(out.dtype)
        out[where(0)] = m0
        out[where(1)] = dot(p1, inv[1]).astype(out.dtype)


def settle_rows(n, m, piv, vl, sib_vl, leaving, moved, *refs):
    hops, upper, lefts = refs[:-2], refs[-2], refs[-1]
    width = leaving.shape[0]
    half = width // 2
    f = facts(n, m, 2, piv)
    r = f["r"]
    for which in range(2):
        place = r if which == 0 else n - 1 - r
        slot = jnp.where(f["low_first"], which, 1 - which)
        for h in range(n):

            @pl.when(place == h)
            def _():
                if h == 0:
                    upper[slot] = leaving[...]
                elif h == 1:
                    upper[slot] = moved[...]
                else:
                    upper[slot, :half, :] = hops[2 * (h - 2)][...]
                    upper[slot, half:, :] = hops[2 * (h - 2) + 1][...]

    lefts[rows(f["core"], half), :] = vl[1]
    lefts[rows(1 - f["core"], half), :] = sib_vl[1]
    for p in range(2):
        cut = slice(p * half, (p + 1) * half)
        fresh = upper[1, cut, :].astype(jnp.float32) - dot(lefts[cut, :], upper[0])
        upper[1, cut, :] = fresh.astype(upper.dtype)


def update(f, upper, mine, sib, at, old, new):
    half = old.shape[0] // 2
    for p in range(2):
        part = jnp.where(f["core"] == p, 0, 1)
        cut = slice(p * half, (p + 1) * half)

        def left(q):
            return jnp.where(part == 0, mine[(q, *at)], sib[(q, *at)])

        m0, m1 = left(0), left(1)

        @pl.when(f["j"] == f["c"][0])
        def _():
            new[cut, :] = m0

        @pl.when(f["j"] == f["c"][1])
        def _():
            new[cut, :] = m1

        @pl.when(jnp.logical_and(f["j"] != f["c"][0], f["j"] != f["c"][1]))
        def _():
            w = (old[cut, :].astype(jnp.float32) - dot(m0, upper[0])).astype(new.dtype)
            w = w.astype(jnp.float32) - dot(m1, upper[1])
            new[cut, :] = w.astype(new.dtype)


def update_stays(n, m, piv, upper, mine, sib, raw, out, new, sems):
    rb = raw.shape[0]
    f = facts(n, m, rb, piv)
    copies = []
    for k in range(rb - 1):
        update(f, upper, mine, sib, (k,), raw.at[k], new.at[k])
        copies.append(pltpu.make_async_copy(new.at[k], out.at[f["slots"][k]], sems.at[k]))
        copies[-1].start()
    for copy in copies:
        copy.wait()


def update_third(n, m, piv, upper, lefts, mine, sib, raw, moved, so_far, out, old, new, sem):
    del so_far
    rb = raw.shape[0]
    f = facts(n, m, rb, piv)
    low_first = f["low_first"]
    first = jnp.where(low_first, f["is_low"], f["is_high"])
    second = jnp.where(low_first, f["is_high"], f["is_low"])

    @pl.when(first)
    def _():
        new[...] = upper[0]

    @pl.when(second)
    def _():
        either(f["j"] == f["c"][0], new, lambda: lefts[...], lambda: upper[1])

    @pl.when(jnp.logical_not(jnp.logical_or(first, second)))
    def _():
        either(f["is_end"], old, lambda: moved[...], lambda: raw[rb - 1])
        update(f, upper, mine, sib, (), old, new)

    copy = pltpu.make_async_copy(new, out.at[f["slots"][rb - 1]], sem)
    copy.start()
    copy.wait()


def local(matrix, pattern, inverses, pivots):
    n = lax.axis_size("prow")
    m = lax.axis_size("pcol")
    rb, width = matrix.shape[0], matrix.shape[1]
    half = width // 2
    chips = m // 2
    stages = chips.bit_length() - 1
    dt = matrix.dtype
    blocks = matrix.reshape(rb, width, width)

    def call(kernel, shapes, specs, *operands, scratch=(), aliases=None, products=0, place=VMEM):
        outs = [jax.ShapeDtypeStruct(s, dt) for s in shapes]
        moved = sum(a.size * a.dtype.itemsize for a in operands)
        result = pl.pallas_call(
            kernel,
            out_shape=outs,
            in_specs=[SMEM if s == "s" else VMEM for s in specs] + [VMEM] * (len(operands) - len(specs) - len(aliases or {}))
            + [place] * len(aliases or {}),
            out_specs=[place] * len(outs),
            scratch_shapes=[pltpu.VMEM(s, dt) if isinstance(s, tuple) else s for s in scratch],
            input_output_aliases=aliases or {},
            compiler_params=GRANT,
            cost_estimate=pl.CostEstimate(
                flops=int(products * 2 * width**3), bytes_accessed=moved, transcendentals=0
            ),
        )(*operands)
        return result if len(result) > 1 else result[0]

    bind = lambda kernel, *args: functools.partial(kernel, n, m, *args)

    def along(pairs, value):
        return lax.ppermute(value, "prow", pairs)

    def sibling(value):
        return lax.ppermute(value, "pcol", [(i, i ^ 1) for i in range(m)])

    def across(stage, value):
        pairs = []
        for i in range(m):
            bit = stage if i % 2 == 0 else stages - 1 - stage
            pairs.append((i, i ^ (2 << bit)))
        return lax.ppermute(value, "pcol", pairs)

    raw, leaving, other = call(
        bind(prepare),
        [(rb, width, width), (width, width), (rb, half, width)],
        "ss",
        pivots,
        pattern,
        blocks,
    )
    early = sibling(other)
    moved = along([(0, 1), (n - 1, n - 2), (n // 2, 0), (n // 2 - 1, n - 1)], leaving)

    panel, extra = call(
        bind(pick), [(2, rb - 1, half, width), (half, width)], "s", pivots, raw, early
    )
    for s in range(stages):
        got = across(s, extra)
        extra = call(bind(forward_extra, s, stages), [(half, width)], "s", pivots, extra, got)
    for s in range(stages):
        got = across(s, panel)
        if s < stages - 1:
            panel = call(bind(forward, s, stages), [panel.shape], "s", pivots, panel, got)
    stays = (panel, got)

    came = [extra]
    send = extra
    stride = n // 2
    while stride:
        pairs = []
        for i in range(0, n, 2 * stride):
            pairs += [(i, i + stride), (n - 1 - i, n - 1 - i - stride)]
        got = along(pairs, send)
        came.append(got)
        if stride > 1:
            send = call(bind(hand_on, stride), [(half, width)], "", send, got)
        stride //= 2
    vl = call(bind(settle_extra), [(2, half, width)], "s", pivots, inverses, *came, products=0.5)
    sib_vl = sibling(vl)

    hops = []
    parts = [moved[:half], moved[half:]]
    for h in range(1, n - 1):
        parts = [along([(h, h + 1), (n - 1 - h, n - 2 - h)], part) for part in parts]
        hops += parts

    sib_moved = sibling(moved)
    third = call(
        bind(pick_third), [(2, half, width)], "s", pivots, raw, early, moved, sib_moved
    )
    for s in range(stages):
        got = across(s, third)
        if s < stages - 1:
            third = call(bind(forward, s, stages), [third.shape], "s", pivots, third, got)

    square = (width, width)
    mine = call(
        bind(multiply, stages, rb - 1),
        [(2, rb - 1, half, width)],
        "s",
        pivots,
        inverses,
        vl,
        sib_vl,
        *stays,
        scratch=[square],
        products=3 * (rb - 1) / 2,
    )
    sib_mine = sibling(mine)
    mine_third = call(
        bind(multiply, stages, 1),
        [(2, half, width)],
        "s",
        pivots,
        inverses,
        vl,
        sib_vl,
        third,
        got,
        scratch=[square],
        products=1.5,
    )
    sib_third = sibling(mine_third)
    upper, lefts = call(
        bind(settle_rows),
        [(2, width, width), square],
        "s",
        pivots,
        vl,
        sib_vl,
        leaving,
        moved,
        *hops,
        products=1,
    )
    result = call(
        bind(update_stays),
        [blocks.shape],
        "s",
        pivots,
        upper,
        mine,
        sib_mine,
        raw,
        scratch=[(rb - 1, width, width), pltpu.SemaphoreType.DMA((rb - 1,))],
        products=2 * (rb - 1),
        place=ANY,
    )
    result = call(
        bind(update_third),
        [blocks.shape],
        "s",
        pivots,
        upper,
        lefts,
        mine_third,
        sib_third,
        raw,
        moved,
        result,
        scratch=[square, square, pltpu.SemaphoreType.DMA],
        aliases={7: 0},
        products=2,
        place=ANY,
    )
    return result.reshape(matrix.shape)


def solution(mesh):
    placed = (P(None, "prow", None, "pcol"), P(), P(), P())
    return jax.shard_map(
        local, mesh=mesh, in_specs=placed, out_specs=P(None, "prow", None, "pcol"), check_vma=False
    )
```

time: 285 us -> 94.2 us (0.33)
  waiting for transfers between devices: 223 us -> 51.7 us
  between operations: 29.6 us -> 0.23 us
  starting transfers between devices: 6.36 us -> 24 us
  Pallas kernels: 0 us -> 15.8 us
  matrix products: 15 us -> 0 us
  other arithmetic: 8.07 us -> 0 us
    psum x4 -> x0, waiting for transfers between devices: 181 us -> none  [broadcast(): return lax.psum(block, axis)]
    ppermute x2 -> x18, starting transfers between devices: 6.23 us -> 24 us  [the longest x7 13.5 us: along(): return lax.ppermute(value, 'prow', pairs)]
    pallas_call x0 -> x14, Pallas kernels: none -> 15.8 us  [call(): pl.pallas_call(kernel, out_shape=outs, in_specs=[SMEM if s == 's' else VM...]
    dot_general x5 -> x0, matrix products: 15 us -> none  [the longest x2 7.06 us: local(): jnp.dot(panel.reshape(row_blocks * width, width), inverses[step], preferr...]
    ppermute x2 -> x18, waiting for transfers between devices: 42.2 us -> 51.7 us  [the longest x6 29.9 us: across(): return lax.ppermute(value, 'pcol', pairs)]
  transfers between devices with their start and end apart: 6 -> 18, of which waited for: 6 -> 10; matrix products, arithmetic and copies ran while one was open for 4% -> 0% of each run, Pallas kernels for 0% -> 12%
where the time goes in v2:
time: 94.2 us; the launch traced here: 94.6 us
  waiting for transfers between devices  51.7 us (55%)
  starting transfers between devices  24 us (25%)
  Pallas kernels  15.8 us (17%)
  local copies, waits for them, and re-layouts  2.9 us (3%)
    ppermute x6, waiting for transfers between devices, across(): return lax.ppermute(value, 'pcol', pairs)  29.9 us
    ppermute x7, waiting for transfers between devices, along(): return lax.ppermute(value, 'prow', pairs)  19.9 us
    pallas_call x14, Pallas kernels, call(): pl.pallas_call(kernel, out_shape=outs, in_specs=[SMEM if s == 's' else VM...  15.8 us
    ppermute x7, starting transfers between devices, along(): return lax.ppermute(value, 'prow', pairs)  13.5 us
    ppermute x6, starting transfers between devices, across(): return lax.ppermute(value, 'pcol', pairs)  9.71 us
    unnamed x7, local copies, waits for them, and re-layouts  2.86 us
    ppermute x5, waiting for transfers between devices, sibling(): return lax.ppermute(value, 'pcol', [(i, i ^ 1) for i in range(m)])  1.92 us
  transfers between devices with their start and end apart: 18, of which 10 were waited for; matrix products, arithmetic and copies ran while one was open for 0% of the time, Pallas kernels for 12%

profile of v2, /device:TPU:0, one launch (start us, length us, event | category | flops | bytes accessed | tf_op | source)
XLA Modules:
  0.0 94.6 jit_solution(18237877862550004692)
XLA Ops:
  0.8 1.4 %copy-done.1 = bf16[3,512,1,512]{3,1,2,0:T(8,128)(2,1)S(1)} copy-done((bf16[3,512,1,512]{3,1,2,0:T(8,128)(2,1)S(1)}, bf16[3,512,1,512]{3,1,2,0:T(8,128)(2,1)}, u32[]{:S(2)}) %copy-start.1) | copy-done | bytes 1572888
  4.3 1.9 %collective-permute-done.sib = bf16[3,256,512]{2,1,0:T(8,128)(2,1)S(1)} collective-permute-done((bf16[3,256,512]{2,1,0:T(8,128)(2,1)S(1)}, bf16[3,256,512]{2,1,0:T(8,128)(2,1)S(1)}, u32[]{:S(2)}, u32[]{:S(2)}) %collective-permute-start) | collective-permute-done | bytes 786464 | tf_op jit(solution)/shard_map/ppermute | solution.py:293
  6.9 2.9 %collective-permute-start.15 = (bf16[2,2,256,512]{3,2,1,0:T(8,128)(2,1)S(1)}, bf16[2,2,256,512]{3,2,1,0:T(8,128)(2,1)S(1)}, u32[]{:S(2)}, u32[]{:S(2)}) collective-permute-start(bf16[2,2,256,512]{3,2,1,0:T(8,128)(2,1)S(1)} %get-tuple-element.18.had), channel_id=1, source_target_pairs={{0,2},{1,5},{2,0},{3,7},{4,6},{5,1},{6,4},{7,3},{8,10},{9,13},{10,... | collective-permute-start | bytes 3145736 | tf_op jit(solution)/shard_map/ppermute | solution.py:300
  9.9 2.0 %collective-permute-start.6 = (bf16[512,512]{1,0:T(8,128)(2,1)S(1)}, bf16[512,512]{1,0:T(8,128)(2,1)S(1)}, u32[]{:S(2)}, u32[]{:S(2)}) collective-permute-start(bf16[512,512]{1,0:T(8,128)(2,1)S(1)} %get-tuple-element.15.leaving), channel_id=1, source_target_pairs={{0,8},{24,16},{16,0},{8,24},{1,9},{25,17},{17,1},{9,25},{2,10},{26... | collective-permute-start | bytes 1572872 | tf_op jit(solution)/shard_map/ppermute | solution.py:290
  11.9 13.5 %collective-permute-done.1.got = bf16[256,512]{1,0:T(8,128)(2,1)S(1)} collective-permute-done((bf16[256,512]{1,0:T(8,128)(2,1)S(1)}, bf16[256,512]{1,0:T(8,128)(2,1)S(1)}, u32[]{:S(2)}, u32[]{:S(2)}) %collective-permute-start.1) | collective-permute-done | bytes 262176 | tf_op jit(solution)/shard_map/ppermute | solution.py:300
  26.0 2.1 %collective-permute-start.2 = (bf16[256,512]{1,0:T(8,128)(2,1)S(1)}, bf16[256,512]{1,0:T(8,128)(2,1)S(1)}, u32[]{:S(2)}, u32[]{:S(2)}) collective-permute-start(bf16[256,512]{1,0:T(8,128)(2,1)S(1)} %shard_map.48.had), channel_id=1, source_target_pairs={{0,4},{1,3},{2,6},{3,1},{4,0},{5,7},{6,2},{7,5},{8,12},{9,11},{10,... | collective-permute-start | bytes 786440 | tf_op jit(solution)/shard_map/ppermute | solution.py:300
  28.1 4.4 %collective-permute-done.2.got = bf16[256,512]{1,0:T(8,128)(2,1)S(1)} collective-permute-done((bf16[256,512]{1,0:T(8,128)(2,1)S(1)}, bf16[256,512]{1,0:T(8,128)(2,1)S(1)}, u32[]{:S(2)}, u32[]{:S(2)}) %collective-permute-start.2) | collective-permute-done | bytes 262176 | tf_op jit(solution)/shard_map/ppermute | solution.py:300
  33.1 5.1 %collective-permute-start.3 = (bf16[256,512]{1,0:T(8,128)(2,1)S(1)}, bf16[256,512]{1,0:T(8,128)(2,1)S(1)}, u32[]{:S(2)}, u32[]{:S(2)}) collective-permute-start(bf16[256,512]{1,0:T(8,128)(2,1)S(1)} %shard_map.49.had.refs_0_), channel_id=1, source_target_pairs={{0,16},{24,8},{1,17},{25,9},{2,18},{26,10},{3,19},{27,11},{4,20},{... | collective-permute-start | bytes 786440 | tf_op jit(solution)/shard_map/ppermute | solution.py:290
  38.9 1.6 %collective-permute-start.16 = (bf16[2,2,256,512]{3,2,1,0:T(8,128)(2,1)S(1)}, bf16[2,2,256,512]{3,2,1,0:T(8,128)(2,1)S(1)}, u32[]{:S(2)}, u32[]{:S(2)}) collective-permute-start(bf16[2,2,256,512]{3,2,1,0:T(8,128)(2,1)S(1)} %shard_map.56.had), channel_id=1, source_target_pairs={{0,4},{1,3},{2,6},{3,1},{4,0},{5,7},{6,2},{7,5},{8,12},{9,11},{10,... | collective-permute-start | bytes 3145736 | tf_op jit(solution)/shard_map/ppermute | solution.py:300
  40.4 1.9 %collective-permute-done.3.got.refs_1_ = bf16[256,512]{1,0:T(8,128)(2,1)S(1)} collective-permute-done((bf16[256,512]{1,0:T(8,128)(2,1)S(1)}, bf16[256,512]{1,0:T(8,128)(2,1)S(1)}, u32[]{:S(2)}, u32[]{:S(2)}) %collective-permute-start.3) | collective-permute-done | bytes 262176 | tf_op jit(solution)/shard_map/ppermute | solution.py:290
  42.3 2.4 %collective-permute-start.4 = (bf16[256,512]{1,0:T(8,128)(2,1)S(1)}, bf16[256,512]{1,0:T(8,128)(2,1)S(1)}, u32[]{:S(2)}, u32[]{:S(2)}) collective-permute-start(bf16[256,512]{1,0:T(8,128)(2,1)S(1)} %shard_map.50), channel_id=1, source_target_pairs={{0,8},{24,16},{16,24},{8,0},{1,9},{25,17},{17,25},{9,1},{2,10},{26... | collective-permute-start | bytes 786440 | tf_op jit(solution)/shard_map/ppermute | solution.py:290
  44.8 4.5 %collective-permute-done.4.refs_2_ = bf16[256,512]{1,0:T(8,128)(2,1)S(1)} collective-permute-done((bf16[256,512]{1,0:T(8,128)(2,1)S(1)}, bf16[256,512]{1,0:T(8,128)(2,1)S(1)}, u32[]{:S(2)}, u32[]{:S(2)}) %collective-permute-start.4) | collective-permute-done | bytes 262176 | tf_op jit(solution)/shard_map/ppermute | solution.py:290
  50.9 1.6 %collective-permute-start.12 = (bf16[2,256,512]{2,1,0:T(8,128)(2,1)S(1)}, bf16[2,256,512]{2,1,0:T(8,128)(2,1)S(1)}, u32[]{:S(2)}, u32[]{:S(2)}) collective-permute-start(bf16[2,256,512]{2,1,0:T(8,128)(2,1)S(1)} %shard_map.53.had), channel_id=1, source_target_pairs={{0,2},{1,5},{2,0},{3,7},{4,6},{5,1},{6,4},{7,3},{8,10},{9,13},{10,... | collective-permute-start | bytes 1572872 | tf_op jit(solution)/shard_map/ppermute | solution.py:300
  53.7 2.0 %shard_map.57.mine = bf16[2,2,256,512]{3,2,1,0:T(8,128)(2,1)S(1)} custom-call(s32[2,3]{1,0:T(2,128)S(1)} %copy-done.2, bf16[2,512,512]{2,1,0:T(8,128)(2,1)S(1)} %copy-done, bf16[2,256,512]{2,1,0:T(8,128)(2,1)S(1)} %shard_map.51.vl, bf16[2,256,512]{2,1,0:T(8,128)(2,1)S(1)} %collective-permute-done.5.sib_vl, bf16[2,2,256,512]{3,2,1,0:T(8,128)(2,1)S(1)} %shard_map.56.had, ...), custom_call_target="tpu_custom_call" | custom-call | flops 805306368 | bytes 4194328 | tf_op jit(solution)/shard_map/pallas_call | solution.py:272
  55.8 4.4 %collective-permute-done.12.got = bf16[2,256,512]{2,1,0:T(8,128)(2,1)S(1)} collective-permute-done((bf16[2,256,512]{2,1,0:T(8,128)(2,1)S(1)}, bf16[2,256,512]{2,1,0:T(8,128)(2,1)S(1)}, u32[]{:S(2)}, u32[]{:S(2)}) %collective-permute-start.12) | collective-permute-done | bytes 524320 | tf_op jit(solution)/shard_map/ppermute | solution.py:300
  60.8 1.5 %collective-permute-start.13 = (bf16[2,256,512]{2,1,0:T(8,128)(2,1)S(1)}, bf16[2,256,512]{2,1,0:T(8,128)(2,1)S(1)}, u32[]{:S(2)}, u32[]{:S(2)}) collective-permute-start(bf16[2,256,512]{2,1,0:T(8,128)(2,1)S(1)} %shard_map.54.had), channel_id=1, source_target_pairs={{0,4},{1,3},{2,6},{3,1},{4,0},{5,7},{6,2},{7,5},{8,12},{9,11},{10,... | collective-permute-start | bytes 1572872 | tf_op jit(solution)/shard_map/ppermute | solution.py:300
  63.6 6.4 %collective-permute-done.13.got = bf16[2,256,512]{2,1,0:T(8,128)(2,1)S(1)} collective-permute-done((bf16[2,256,512]{2,1,0:T(8,128)(2,1)S(1)}, bf16[2,256,512]{2,1,0:T(8,128)(2,1)S(1)}, u32[]{:S(2)}, u32[]{:S(2)}) %collective-permute-start.13) | collective-permute-done | bytes 524320 | tf_op jit(solution)/shard_map/ppermute | solution.py:300
  70.0 1.4 %shard_map.55.mine = bf16[2,256,512]{2,1,0:T(8,128)(2,1)S(1)} custom-call(s32[2,3]{1,0:T(2,128)S(1)} %copy-done.2, bf16[2,512,512]{2,1,0:T(8,128)(2,1)S(1)} %copy-done, bf16[2,256,512]{2,1,0:T(8,128)(2,1)S(1)} %shard_map.51.vl, bf16[2,256,512]{2,1,0:T(8,128)(2,1)S(1)} %collective-permute-done.5.sib_vl, bf16[2,256,512]{2,1,0:T(8,128)(2,1)S(1)} %shard_map.54.had, ...), custom_call_target="tpu_custom_call" | custom-call | flops 402653184 | bytes 3145752 | tf_op jit(solution)/shard_map/pallas_call | solution.py:272
  71.5 1.3 %collective-permute-start.10 = (bf16[256,512]{1,0:T(8,128)(2,1)S(1)}, bf16[256,512]{1,0:T(8,128)(2,1)S(1)}, u32[]{:S(2)}, u32[]{:S(2)}) collective-permute-start(bf16[256,512]{1,0:T(8,128)(2,1)S(1)} %collective-permute-done.8.refs_1_), channel_id=1, source_target_pairs={{16,24},{8,0},{17,25},{9,1},{18,26},{10,2},{19,27},{11,3},{20,28},... | collective-permute-start | bytes 786440 | tf_op jit(solution)/shard_map/ppermute | solution.py:290
  72.8 1.3 %collective-permute-start.9 = (bf16[256,512]{1,0:T(8,128)(2,1)S(1)}, bf16[256,512]{1,0:T(8,128)(2,1)S(1)}, u32[]{:S(2)}, u32[]{:S(2)}) collective-permute-start(bf16[256,512]{1,0:T(8,128)(2,1)S(1)} %collective-permute-done.7.refs_0_), channel_id=1, source_target_pairs={{16,24},{8,0},{17,25},{9,1},{18,26},{10,2},{19,27},{11,3},{20,28},... | collective-permute-start | bytes 786440 | tf_op jit(solution)/shard_map/ppermute | solution.py:290
  74.1 9.8 %collective-permute-done.10.refs_3_ = bf16[256,512]{1,0:T(8,128)(2,1)S(1)} collective-permute-done((bf16[256,512]{1,0:T(8,128)(2,1)S(1)}, bf16[256,512]{1,0:T(8,128)(2,1)S(1)}, u32[]{:S(2)}, u32[]{:S(2)}) %collective-permute-start.10) | collective-permute-done | bytes 262176 | tf_op jit(solution)/shard_map/ppermute | solution.py:290
  83.9 3.8 %collective-permute-done.9.refs_2_ = bf16[256,512]{1,0:T(8,128)(2,1)S(1)} collective-permute-done((bf16[256,512]{1,0:T(8,128)(2,1)S(1)}, bf16[256,512]{1,0:T(8,128)(2,1)S(1)}, u32[]{:S(2)}, u32[]{:S(2)}) %collective-permute-start.9) | collective-permute-done | bytes 262176 | tf_op jit(solution)/shard_map/ppermute | solution.py:290
  88.8 3.4 %shard_map.58.so_far = bf16[3,512,512]{2,1,0:T(8,128)(2,1)} custom-call(s32[2,3]{1,0:T(2,128)S(1)} %copy-done.2, bf16[2,512,512]{2,1,0:T(8,128)(2,1)S(1)} %get-tuple-element.16.upper, bf16[2,2,256,512]{3,2,1,0:T(8,128)(2,1)S(1)} %shard_map.57.mine, bf16[2,2,256,512]{3,2,1,0:T(8,128)(2,1)S(1)} %collective-permute-done.17.sib, ...), custom_call_target="tpu_custom_call" | custom-call | flops 1073741824 | bytes 4718616 | tf_op jit(solution)/shard_map/pallas_call | solution.py:272
  92.2 2.4 %shard_map.59 = bf16[3,512,512]{2,1,0:T(8,128)(2,1)} custom-call(s32[2,3]{1,0:T(2,128)S(1)} %copy-done.2, bf16[2,512,512]{2,1,0:T(8,128)(2,1)S(1)} %get-tuple-element.16.upper, bf16[512,512]{1,0:T(8,128)(2,1)S(1)} %get-tuple-element.17.lefts, bf16[2,256,512]{2,1,0:T(8,128)(2,1)S(1)} %shard_map.55.mine, ...), custom_call_target="tpu_custom_call", output_to_operand_aliasing={{}: (7, {})} | custom-call | flops 536870912 | bytes 6291480 | tf_op jit(solution)/shard_map/pallas_call | solution.py:272
  (34 shorter events, 11.6 us)
Async XLA Ops:
  0.8 1.4 %copy-start.1 = (bf16[3,512,1,512]{3,1,2,0:T(8,128)(2,1)S(1)}, bf16[3,512,1,512]{3,1,2,0:T(8,128)(2,1)}, u32[]{:S(2)}) copy-start(bf16[3,512,1,512]{3,1,2,0:T(8,128)(2,1)} %param.4) | copy-start | bytes 4718596
  2.2 0.7 copy-start.2
  3.8 2.4 %collective-permute-start = (bf16[3,256,512]{2,1,0:T(8,128)(2,1)S(1)}, bf16[3,256,512]{2,1,0:T(8,128)(2,1)S(1)}, u32[]{:S(2)}, u32[]{:S(2)}) collective-permute-start(bf16[3,256,512]{2,1,0:T(8,128)(2,1)S(1)} %get-tuple-element.13), channel_id=1, source_target_pairs={{0,1},{1,0},{2,3},{3,2},{4,5},{5,4},{6,7},{7,6},{8,9},{9,8},{10,11... | collective-permute-start | bytes 2359304 | tf_op jit(solution)/shard_map/ppermute | solution.py:293
  6.9 31.3 %collective-permute-start.15 = (bf16[2,2,256,512]{3,2,1,0:T(8,128)(2,1)S(1)}, bf16[2,2,256,512]{3,2,1,0:T(8,128)(2,1)S(1)}, u32[]{:S(2)}, u32[]{:S(2)}) collective-permute-start(bf16[2,2,256,512]{3,2,1,0:T(8,128)(2,1)S(1)} %get-tuple-element.18.had), channel_id=1, source_target_pairs={{0,2},{1,5},{2,0},{3,7},{4,6},{5,1},{6,4},{7,3},{8,10},{9,13},{10,... | collective-permute-start | bytes 3145736 | tf_op jit(solution)/shard_map/ppermute | solution.py:300
  9.8 15.6 %collective-permute-start.1 = (bf16[256,512]{1,0:T(8,128)(2,1)S(1)}, bf16[256,512]{1,0:T(8,128)(2,1)S(1)}, u32[]{:S(2)}, u32[]{:S(2)}) collective-permute-start(bf16[256,512]{1,0:T(8,128)(2,1)S(1)} %get-tuple-element.14.had), channel_id=1, source_target_pairs={{0,2},{1,5},{2,0},{3,7},{4,6},{5,1},{6,4},{7,3},{8,10},{9,13},{10,... | collective-permute-start | bytes 786440 | tf_op jit(solution)/shard_map/ppermute | solution.py:300
  9.9 30.6 %collective-permute-start.6 = (bf16[512,512]{1,0:T(8,128)(2,1)S(1)}, bf16[512,512]{1,0:T(8,128)(2,1)S(1)}, u32[]{:S(2)}, u32[]{:S(2)}) collective-permute-start(bf16[512,512]{1,0:T(8,128)(2,1)S(1)} %get-tuple-element.15.leaving), channel_id=1, source_target_pairs={{0,8},{24,16},{16,0},{8,24},{1,9},{25,17},{17,1},{9,25},{2,10},{26... | collective-permute-start | bytes 1572872 | tf_op jit(solution)/shard_map/ppermute | solution.py:290
  26.0 6.5 %collective-permute-start.2 = (bf16[256,512]{1,0:T(8,128)(2,1)S(1)}, bf16[256,512]{1,0:T(8,128)(2,1)S(1)}, u32[]{:S(2)}, u32[]{:S(2)}) collective-permute-start(bf16[256,512]{1,0:T(8,128)(2,1)S(1)} %shard_map.48.had), channel_id=1, source_target_pairs={{0,4},{1,3},{2,6},{3,1},{4,0},{5,7},{6,2},{7,5},{8,12},{9,11},{10,... | collective-permute-start | bytes 786440 | tf_op jit(solution)/shard_map/ppermute | solution.py:300
  33.0 16.2 %copy-start = (bf16[2,512,512]{2,1,0:T(8,128)(2,1)S(1)}, bf16[2,512,512]{2,1,0:T(8,128)(2,1)}, u32[]{:S(2)}) copy-start(bf16[2,512,512]{2,1,0:T(8,128)(2,1)} %inv.5) | copy-start | bytes 3145732
  33.1 9.3 %collective-permute-start.3 = (bf16[256,512]{1,0:T(8,128)(2,1)S(1)}, bf16[256,512]{1,0:T(8,128)(2,1)S(1)}, u32[]{:S(2)}, u32[]{:S(2)}) collective-permute-start(bf16[256,512]{1,0:T(8,128)(2,1)S(1)} %shard_map.49.had.refs_0_), channel_id=1, source_target_pairs={{0,16},{24,8},{1,17},{25,9},{2,18},{26,10},{3,19},{27,11},{4,20},{... | collective-permute-start | bytes 786440 | tf_op jit(solution)/shard_map/ppermute | solution.py:290
  38.9 14.9 %collective-permute-start.16 = (bf16[2,2,256,512]{3,2,1,0:T(8,128)(2,1)S(1)}, bf16[2,2,256,512]{3,2,1,0:T(8,128)(2,1)S(1)}, u32[]{:S(2)}, u32[]{:S(2)}) collective-permute-start(bf16[2,2,256,512]{3,2,1,0:T(8,128)(2,1)S(1)} %shard_map.56.had), channel_id=1, source_target_pairs={{0,4},{1,3},{2,6},{3,1},{4,0},{5,7},{6,2},{7,5},{8,12},{9,11},{10,... | collective-permute-start | bytes 3145736 | tf_op jit(solution)/shard_map/ppermute | solution.py:300
  40.4 9.8 %collective-permute-start.11 = (bf16[512,512]{1,0:T(8,128)(2,1)S(1)}, bf16[512,512]{1,0:T(8,128)(2,1)S(1)}, u32[]{:S(2)}, u32[]{:S(2)}) collective-permute-start(bf16[512,512]{1,0:T(8,128)(2,1)S(1)} %collective-permute-done.6.moved), channel_id=1, source_target_pairs={{0,1},{1,0},{2,3},{3,2},{4,5},{5,4},{6,7},{7,6},{8,9},{9,8},{10,11... | collective-permute-start | bytes 1572872 | tf_op jit(solution)/shard_map/ppermute | solution.py:293
  42.3 6.9 %collective-permute-start.4 = (bf16[256,512]{1,0:T(8,128)(2,1)S(1)}, bf16[256,512]{1,0:T(8,128)(2,1)S(1)}, u32[]{:S(2)}, u32[]{:S(2)}) collective-permute-start(bf16[256,512]{1,0:T(8,128)(2,1)S(1)} %shard_map.50), channel_id=1, source_target_pairs={{0,8},{24,16},{16,24},{8,0},{1,9},{25,17},{17,25},{9,1},{2,10},{26... | collective-permute-start | bytes 786440 | tf_op jit(solution)/shard_map/ppermute | solution.py:290
  50.2 2.3 %collective-permute-start.5 = (bf16[2,256,512]{2,1,0:T(8,128)(2,1)S(1)}, bf16[2,256,512]{2,1,0:T(8,128)(2,1)S(1)}, u32[]{:S(2)}, u32[]{:S(2)}) collective-permute-start(bf16[2,256,512]{2,1,0:T(8,128)(2,1)S(1)} %shard_map.51.vl), channel_id=1, source_target_pairs={{0,1},{1,0},{2,3},{3,2},{4,5},{5,4},{6,7},{7,6},{8,9},{9,8},{10,11... | collective-permute-start | bytes 1572872 | tf_op jit(solution)/shard_map/ppermute | solution.py:293
  50.9 9.2 %collective-permute-start.12 = (bf16[2,256,512]{2,1,0:T(8,128)(2,1)S(1)}, bf16[2,256,512]{2,1,0:T(8,128)(2,1)S(1)}, u32[]{:S(2)}, u32[]{:S(2)}) collective-permute-start(bf16[2,256,512]{2,1,0:T(8,128)(2,1)S(1)} %shard_map.53.had), channel_id=1, source_target_pairs={{0,2},{1,5},{2,0},{3,7},{4,6},{5,1},{6,4},{7,3},{8,10},{9,13},{10,... | collective-permute-start | bytes 1572872 | tf_op jit(solution)/shard_map/ppermute | solution.py:300
  55.7 33.1 %collective-permute-start.17 = (bf16[2,2,256,512]{3,2,1,0:T(8,128)(2,1)S(1)}, bf16[2,2,256,512]{3,2,1,0:T(8,128)(2,1)S(1)}, u32[]{:S(2)}, u32[]{:S(2)}) collective-permute-start(bf16[2,2,256,512]{3,2,1,0:T(8,128)(2,1)S(1)} %shard_map.57.mine), channel_id=1, source_target_pairs={{0,1},{1,0},{2,3},{3,2},{4,5},{5,4},{6,7},{7,6},{8,9},{9,8},{10,11... | collective-permute-start | bytes 3145736 | tf_op jit(solution)/shard_map/ppermute | solution.py:293
  60.8 9.2 %collective-permute-start.13 = (bf16[2,256,512]{2,1,0:T(8,128)(2,1)S(1)}, bf16[2,256,512]{2,1,0:T(8,128)(2,1)S(1)}, u32[]{:S(2)}, u32[]{:S(2)}) collective-permute-start(bf16[2,256,512]{2,1,0:T(8,128)(2,1)S(1)} %shard_map.54.had), channel_id=1, source_target_pairs={{0,4},{1,3},{2,6},{3,1},{4,0},{5,7},{6,2},{7,5},{8,12},{9,11},{10,... | collective-permute-start | bytes 1572872 | tf_op jit(solution)/shard_map/ppermute | solution.py:300
  62.3 9.2 %collective-permute-start.8 = (bf16[256,512]{1,0:T(8,128)(2,1)S(1)}, bf16[256,512]{1,0:T(8,128)(2,1)S(1)}, u32[]{:S(2)}, u32[]{:S(2)}) collective-permute-start(bf16[256,512]{1,0:T(8,128)(2,1)S(1)} %get-tuple-element.19), channel_id=1, source_target_pairs={{8,16},{16,8},{9,17},{17,9},{10,18},{18,10},{11,19},{19,11},{12,20... | collective-permute-start | bytes 786440 | tf_op jit(solution)/shard_map/ppermute | solution.py:290
  63.0 9.8 %collective-permute-start.7 = (bf16[256,512]{1,0:T(8,128)(2,1)S(1)}, bf16[256,512]{1,0:T(8,128)(2,1)S(1)}, u32[]{:S(2)}, u32[]{:S(2)}) collective-permute-start(bf16[256,512]{1,0:T(8,128)(2,1)S(1)} %get-tuple-element.20), channel_id=1, source_target_pairs={{8,16},{16,8},{9,17},{17,9},{10,18},{18,10},{11,19},{19,11},{12,20... | collective-permute-start | bytes 786440 | tf_op jit(solution)/shard_map/ppermute | solution.py:290
  71.4 20.8 %collective-permute-start.14 = (bf16[2,256,512]{2,1,0:T(8,128)(2,1)S(1)}, bf16[2,256,512]{2,1,0:T(8,128)(2,1)S(1)}, u32[]{:S(2)}, u32[]{:S(2)}) collective-permute-start(bf16[2,256,512]{2,1,0:T(8,128)(2,1)S(1)} %shard_map.55.mine), channel_id=1, source_target_pairs={{0,1},{1,0},{2,3},{3,2},{4,5},{5,4},{6,7},{7,6},{8,9},{9,8},{10,11... | collective-permute-start | bytes 1572872 | tf_op jit(solution)/shard_map/ppermute | solution.py:293
  71.5 12.4 %collective-permute-start.10 = (bf16[256,512]{1,0:T(8,128)(2,1)S(1)}, bf16[256,512]{1,0:T(8,128)(2,1)S(1)}, u32[]{:S(2)}, u32[]{:S(2)}) collective-permute-start(bf16[256,512]{1,0:T(8,128)(2,1)S(1)} %collective-permute-done.8.refs_1_), channel_id=1, source_target_pairs={{16,24},{8,0},{17,25},{9,1},{18,26},{10,2},{19,27},{11,3},{20,28},... | collective-permute-start | bytes 786440 | tf_op jit(solution)/shard_map/ppermute | solution.py:290
  72.8 14.9 %collective-permute-start.9 = (bf16[256,512]{1,0:T(8,128)(2,1)S(1)}, bf16[256,512]{1,0:T(8,128)(2,1)S(1)}, u32[]{:S(2)}, u32[]{:S(2)}) collective-permute-start(bf16[256,512]{1,0:T(8,128)(2,1)S(1)} %collective-permute-done.7.refs_0_), channel_id=1, source_target_pairs={{16,24},{8,0},{17,25},{9,1},{18,26},{10,2},{19,27},{11,3},{20,28},... | collective-permute-start | bytes 786440 | tf_op jit(solution)/shard_map/ppermute | solution.py:290

commit v3 on v2

--- a/solution.py
+++ b/solution.py
@@ -32,6 +32,8 @@
     for k in range(rb):
         slot = out + (1 + k)
         f["slots"].append(jnp.where(slot >= rb, slot - rb, slot))
+    f["fixed_step"] = jnp.where(pivots[0, 2] == m - 1, 0, 1)
+    f["free"] = pivots[0, 2] + pivots[1, 2] - (m - 1)
     f["cx"] = jnp.where((r == 0) == low_first, pivots[1, 2], pivots[0, 2])
     return f
 
@@ -56,7 +58,7 @@
     cut = rows(1 - f["core"], width // 2)
     for k in reversed(range(rb)):
         slot = f["slots"][k]
-        keep = pat[slot * n + f["r"], f["j"]] != 0
+        keep = pat[f["j"], slot * n + f["r"]] != 0
         zero = lambda: jnp.zeros((width, width), mat.dtype)
         either(keep, raw.at[k], lambda: mat[slot], zero)
         if k == rb - 1:
@@ -64,32 +66,38 @@
         other[k] = raw[k, cut, :]
 
 
-def pick(n, m, piv, raw, sib, panel, extra):
+def pick_extra(n, m, piv, raw, sib, extra):
     rb, width = raw.shape[0], raw.shape[1]
     f = facts(n, m, rb, piv)
     cut = rows(f["core"], width // 2)
-    for q in range(2):
-        hit = (f["c"][q] & 1) == f["core"]
-        for k in range(rb - 1):
-            either(hit, panel.at[q, k], lambda: raw[k, cut, :], lambda: sib[k])
     hit = (f["cx"] & 1) == f["core"]
     either(hit, extra, lambda: raw[rb - 1, cut, :], lambda: sib[rb - 1])
 
 
-def pick_third(n, m, piv, raw, sib, moved, sib_moved, panel):
+def pick(n, m, piv, raw, sib, fixed, free):
     rb, width = raw.shape[0], raw.shape[1]
     f = facts(n, m, rb, piv)
     cut = rows(f["core"], width // 2)
-    for q in range(2):
-        hit = (f["c"][q] & 1) == f["core"]
+    for panel, column in ((fixed, m - 1), (free, f["free"])):
+        hit = (column & 1) == f["core"]
+        for k in range(rb - 1):
+            either(hit, panel.at[k], lambda: raw[k, cut, :], lambda: sib[k])
+
+
+def pick_third(n, m, piv, raw, sib, moved, sib_moved, fixed, free):
+    rb, width = raw.shape[0], raw.shape[1]
+    f = facts(n, m, rb, piv)
+    cut = rows(f["core"], width // 2)
+    for panel, column in ((fixed, m - 1), (free, f["free"])):
+        hit = (column & 1) == f["core"]
 
         @pl.when(f["is_end"])
         def _():
-            either(hit, panel.at[q], lambda: moved[cut, :], lambda: sib_moved[cut, :])
+            either(hit, panel.at[0], lambda: moved[cut, :], lambda: sib_moved[cut, :])
 
         @pl.when(jnp.logical_not(f["is_end"]))
         def _():
-            either(hit, panel.at[q], lambda: raw[rb - 1, cut, :], lambda: sib[rb - 1])
+            either(hit, panel.at[0], lambda: raw[rb - 1, cut, :], lambda: sib[rb - 1])
 
 
 def bit_of(f, column, stage, stages):
@@ -98,17 +106,33 @@
     return ((apart >> bit) & 1) == 1
 
 
-def forward(n, m, stage, stages, piv, had, got, panel):
+def forward(n, m, key, stage, stages, piv, had, got, out):
     f = facts(n, m, 2, piv)
-    for q in range(2):
-        take = bit_of(f, f["c"][q], stage, stages)
-        either(take, panel.at[q], lambda: got[q], lambda: had[q])
-
-
-def forward_extra(n, m, stage, stages, piv, had, got, extra):
-    f = facts(n, m, 2, piv)
-    take = bit_of(f, f["cx"], stage, stages)
-    either(take, extra, lambda: got[...], lambda: had[...])
+    take = bit_of(f, f[key], stage, stages)
+    either(take, out, lambda: got[...], lambda: had[...])
+
+
+def ring_order(chips):
+    side = round(chips**0.5)
+    if side * side != chips or side % 2:
+        return list(range(chips))
+    walk = []
+    for i in range(side):
+        across = list(range(1, side))
+        walk += [i * side + k for k in (across if i % 2 == 0 else across[::-1])]
+    return walk + [i * side for i in range(side - 1, -1, -1)]
+
+
+def ring_hops(chips):
+    order = ring_order(chips)
+    start = order.index(chips - 1)
+    one = [order[(start + k) % chips] for k in range(chips)]
+    two = [order[(start - k) % chips] for k in range(chips)]
+    hops = [
+        [(2 * one[h], 2 * one[h + 1]), (2 * two[h] + 1, 2 * two[h + 1] + 1)]
+        for h in range(chips - 1)
+    ]
+    return one, two, hops
 
 
 def hand_on(n, m, stride, had, got, extra):
@@ -147,20 +171,31 @@
     out[1] = dot(out[1], inv[0]).astype(out.dtype)
 
 
-def multiply(n, m, stages, blocks, piv, inv, vl, sib_vl, had, got, out, v):
+def multiply(n, m, stages, piv, inv, vl, sib_vl, free, free_got, *refs):
+    fixed, out, v = refs[:-2], refs[-2], refs[-1]
     f = facts(n, m, 2, piv)
     half = vl.shape[1]
     v[rows(f["core"], half), :] = vl[0]
     v[rows(1 - f["core"], half), :] = sib_vl[0]
-    take = [bit_of(f, f["c"][q], stages - 1, stages) for q in range(2)]
-    for q in range(2):
-        either(take[q], out.at[q], lambda: got[q], lambda: had[q])
-    for k in range(blocks):
-        where = (lambda q: (q, k)) if blocks > 1 else (lambda q: (q,))
-        m0 = dot(out[where(0)], inv[0]).astype(out.dtype)
-        p1 = (out[where(1)].astype(jnp.float32) - dot(m0, v[...])).astype(out.dtype)
-        out[where(0)] = m0
-        out[where(1)] = dot(p1, inv[1]).astype(out.dtype)
+    chips = m // 2
+    one, two, _ = ring_hops(chips)
+    hop = jnp.int32(0)
+    for chip in range(chips):
+        here = jnp.where(f["core"] == 0, one.index(chip), two.index(chip))
+        hop = jnp.where(f["chip"] == chip, here, hop)
+    for h in range(chips):
+
+        @pl.when(hop == h)
+        def _():
+            out[f["fixed_step"]] = fixed[h][...]
+
+    take = bit_of(f, f["free"], stages - 1, stages)
+    either(take, out.at[1 - f["fixed_step"]], lambda: free_got[...], lambda: free[...])
+    for k in range(free.shape[0]):
+        m0 = dot(out[0, k], inv[0]).astype(out.dtype)
+        p1 = (out[1, k].astype(jnp.float32) - dot(m0, v[...])).astype(out.dtype)
+        out[0, k] = m0
+        out[1, k] = dot(p1, inv[1]).astype(out.dtype)
 
 
 def settle_rows(n, m, piv, vl, sib_vl, leaving, moved, *refs):
@@ -249,7 +284,7 @@
     @pl.when(jnp.logical_not(jnp.logical_or(first, second)))
     def _():
         either(f["is_end"], old, lambda: moved[...], lambda: raw[rb - 1])
-        update(f, upper, mine, sib, (), old, new)
+        update(f, upper, mine, sib, (0,), old, new)
 
     copy = pltpu.make_async_copy(new, out.at[f["slots"][rb - 1]], sem)
     copy.start()
@@ -266,123 +301,137 @@
     dt = matrix.dtype
     blocks = matrix.reshape(rb, width, width)
 
-    def call(kernel, shapes, specs, *operands, scratch=(), aliases=None, products=0, place=VMEM):
+    def call(kernel, shapes, specs, *operands, scratch=(), aliases=(), products=0, place=VMEM, after=(), name=None):
         outs = [jax.ShapeDtypeStruct(s, dt) for s in shapes]
-        moved = sum(a.size * a.dtype.itemsize for a in operands)
+        count = len(operands)
+        scratch = [pltpu.VMEM(s, dt) if isinstance(s, tuple) else s for s in scratch]
+
+        def body(*refs):
+            kernel(n, m, *refs[:count], *refs[count + len(after) :])
+
+        kinds = {"s": SMEM, "v": VMEM, "a": ANY}
+        specs = [kinds[k] for k in specs.ljust(count, "v")] + [ANY] * len(after)
         result = pl.pallas_call(
-            kernel,
+            body,
             out_shape=outs,
-            in_specs=[SMEM if s == "s" else VMEM for s in specs] + [VMEM] * (len(operands) - len(specs) - len(aliases or {}))
-            + [place] * len(aliases or {}),
+            in_specs=specs,
             out_specs=[place] * len(outs),
-            scratch_shapes=[pltpu.VMEM(s, dt) if isinstance(s, tuple) else s for s in scratch],
-            input_output_aliases=aliases or {},
+            scratch_shapes=scratch,
+            input_output_aliases=dict(aliases),
             compiler_params=GRANT,
+            name=name or kernel.__name__,
             cost_estimate=pl.CostEstimate(
-                flops=int(products * 2 * width**3), bytes_accessed=moved, transcendentals=0
+                flops=int(products * 2 * width**3),
+                bytes_accessed=sum(a.size * a.dtype.itemsize for a in operands),
+                transcendentals=0,
             ),
-        )(*operands)
+        )(*operands, *after)
         return result if len(result) > 1 else result[0]
 
-    bind = lambda kernel, *args: functools.partial(kernel, n, m, *args)
-
-    def along(pairs, value):
-        return lax.ppermute(value, "prow", pairs)
-
-    def sibling(value):
-        return lax.ppermute(value, "pcol", [(i, i ^ 1) for i in range(m)])
-
-    def across(stage, value):
+    def along(name, pairs, value):
+        with jax.named_scope(name):
+            return lax.ppermute(value, "prow", pairs)
+
+    def sibling(name, value):
+        with jax.named_scope(name):
+            return lax.ppermute(value, "pcol", [(i, i ^ 1) for i in range(m)])
+
+    def across(name, stage, value):
         pairs = []
         for i in range(m):
             bit = stage if i % 2 == 0 else stages - 1 - stage
             pairs.append((i, i ^ (2 << bit)))
-        return lax.ppermute(value, "pcol", pairs)
-
+        with jax.named_scope(name):
+            return lax.ppermute(value, "pcol", pairs)
+
+    def ring(name, value):
+        came = [value]
+        for h, pairs in enumerate(ring_hops(chips)[2]):
+            with jax.named_scope(name + str(h)):
+                came.append(lax.ppermute(came[-1], "pcol", pairs))
+        return came
+
+    def passing(name, key, value, after=()):
+        for s in range(stages):
+            got = across(name + str(s), s, value)
+            if s < stages - 1:
+                kernel = functools.partial(forward, n, m, key, s, stages)
+                step = lambda _n, _m, *refs: kernel(*refs)
+                value = call(step, [value.shape], "s", pivots, value, got, after=after, name="forward_" + name)
+        return value, got
+
+    square, strip = (width, width), (half, width)
     raw, leaving, other = call(
-        bind(prepare),
-        [(rb, width, width), (width, width), (rb, half, width)],
+        prepare,
+        [(rb, *square), square, (rb, *strip)],
         "ss",
         pivots,
-        pattern,
+        pattern.T,
         blocks,
     )
-    early = sibling(other)
-    moved = along([(0, 1), (n - 1, n - 2), (n // 2, 0), (n // 2 - 1, n - 1)], leaving)
-
-    panel, extra = call(
-        bind(pick), [(2, rb - 1, half, width), (half, width)], "s", pivots, raw, early
-    )
-    for s in range(stages):
-        got = across(s, extra)
-        extra = call(bind(forward_extra, s, stages), [(half, width)], "s", pivots, extra, got)
-    for s in range(stages):
-        got = across(s, panel)
-        if s < stages - 1:
-            panel = call(bind(forward, s, stages), [panel.shape], "s", pivots, panel, got)
-    stays = (panel, got)
-
-    came = [extra]
-    send = extra
+    moved = along("swap", [(0, 1), (n - 1, n - 2), (n // 2, 0), (n // 2 - 1, n - 1)], leaving)
+    early = sibling("sib_early", other)
+
+    extra = call(pick_extra, [strip], "s", pivots, raw, early)
+    had, got = passing("extra", "cx", extra)
+    step = lambda _n, _m, *refs: forward(n, m, "cx", stages - 1, stages, *refs)
+    extra_here = call(step, [strip], "s", pivots, had, got, after=[moved], name="extra_here")
+    fixed, free = call(
+        pick, [(rb - 1, *strip)] * 2, "s", pivots, raw, early, after=[extra]
+    )
+    free_stays = passing("free", "free", free)
+    fixed_stays = ring("fixed", fixed)
+
+    hops = []
+    parts = [moved[:half], moved[half:]]
+    for h in range(1, n - 1):
+        pairs = [(h, h + 1), (n - 1 - h, n - 2 - h)]
+        parts = [along("row" + str(h), pairs, part) for part in parts]
+        hops += parts
+
+    sib_moved = sibling("sib_moved", moved)
+    fixed, free = call(
+        pick_third, [(1, *strip)] * 2, "s", pivots, raw, early, moved, sib_moved
+    )
+
+    came = [extra_here]
+    send = extra_here
     stride = n // 2
     while stride:
         pairs = []
         for i in range(0, n, 2 * stride):
             pairs += [(i, i + stride), (n - 1 - i, n - 1 - i - stride)]
-        got = along(pairs, send)
+        got = along("extra_z", pairs, send)
         came.append(got)
         if stride > 1:
-            send = call(bind(hand_on, stride), [(half, width)], "", send, got)
+            step = lambda _n, _m, *refs: hand_on(n, m, stride, *refs)
+            send = call(step, [strip], "", send, got, name="hand_on", after=[free])
         stride //= 2
-    vl = call(bind(settle_extra), [(2, half, width)], "s", pivots, inverses, *came, products=0.5)
-    sib_vl = sibling(vl)
-
-    hops = []
-    parts = [moved[:half], moved[half:]]
-    for h in range(1, n - 1):
-        parts = [along([(h, h + 1), (n - 1 - h, n - 2 - h)], part) for part in parts]
-        hops += parts
-
-    sib_moved = sibling(moved)
-    third = call(
-        bind(pick_third), [(2, half, width)], "s", pivots, raw, early, moved, sib_moved
-    )
-    for s in range(stages):
-        got = across(s, third)
-        if s < stages - 1:
-            third = call(bind(forward, s, stages), [third.shape], "s", pivots, third, got)
-
-    square = (width, width)
+    vl = call(settle_extra, [(2, *strip)], "s", pivots, inverses, *came, products=0.5, after=hops[:2])
+    sib_vl = sibling("sib_vl", vl)
+
+    free_third = passing("free_third", "free", free)
+    fixed_third = ring("fixed_third", fixed)
+
+    step = lambda _n, _m, *refs: multiply(n, m, stages, *refs)
     mine = call(
-        bind(multiply, stages, rb - 1),
-        [(2, rb - 1, half, width)],
+        step,
+        [(2, rb - 1, *strip)],
         "s",
         pivots,
         inverses,
         vl,
         sib_vl,
-        *stays,
+        *free_stays,
+        *fixed_stays,
         scratch=[square],
         products=3 * (rb - 1) / 2,
-    )
-    sib_mine = sibling(mine)
-    mine_third = call(
-        bind(multiply, stages, 1),
-        [(2, half, width)],
-        "s",
-        pivots,
-        inverses,
-        vl,
-        sib_vl,
-        third,
-        got,
-        scratch=[square],
-        products=1.5,
-    )
-    sib_third = sibling(mine_third)
+        name="multiply_stays",
+    )
+    sib_mine = sibling("sib_mine", mine)
     upper, lefts = call(
-        bind(settle_rows),
-        [(2, width, width), square],
+        settle_rows,
+        [(2, *square), square],
         "s",
         pivots,
         vl,
@@ -392,8 +441,24 @@
         *hops,
         products=1,
     )
+    mine_third = call(
+        step,
+        [(2, 1, *strip)],
+        "s",
+        pivots,
+        inverses,
+        vl,
+        sib_vl,
+        *free_third,
+        *fixed_third,
+        scratch=[square],
+        products=1.5,
+        after=[upper],
+        name="multiply_third",
+    )
+    sib_third = sibling("sib_third", mine_third)
     result = call(
-        bind(update_stays),
+        update_stays,
         [blocks.shape],
         "s",
         pivots,
@@ -401,14 +466,14 @@
         mine,
         sib_mine,
         raw,
-        scratch=[(rb - 1, width, width), pltpu.SemaphoreType.DMA((rb - 1,))],
+        scratch=[(rb - 1, *square), pltpu.SemaphoreType.DMA((rb - 1,))],
         products=2 * (rb - 1),
         place=ANY,
     )
     result = call(
-        bind(update_third),
+        update_third,
         [blocks.shape],
-        "s",
+        "svvvvvva",
         pivots,
         upper,
         lefts,

time: 94.2 us -> 90.9 us (0.965)
  waiting for transfers between devices: 51.7 us -> 35.5 us
  starting transfers between devices: 24 us -> 35.7 us
    ppermute x6, waiting for transfers between devices: 29.9 us -> 6.76 us  [across(): return lax.ppermute(value, 'pcol', pairs)]
    ppermute x0 -> x6, starting transfers between devices: none -> 9.09 us  [ring(): came.append(lax.ppermute(came[-1], 'pcol', pairs))]
    ppermute x0 -> x6, waiting for transfers between devices: none -> 6.07 us  [ring(): came.append(lax.ppermute(came[-1], 'pcol', pairs))]
    ppermute x7, waiting for transfers between devices: 19.9 us -> 22.7 us  [along(): return lax.ppermute(value, 'prow', pairs)]
    ppermute x6, starting transfers between devices: 9.71 us -> 11.9 us  [across(): return lax.ppermute(value, 'pcol', pairs)]
    ppermute x5, waiting for transfers between devices: 1.92 us -> 0.01 us  [sibling(): return lax.ppermute(value, 'pcol', [(i, i ^ 1) for i in range(m)])]
    ppermute x5, starting transfers between devices: 0.73 us -> 1.72 us  [sibling(): return lax.ppermute(value, 'pcol', [(i, i ^ 1) for i in range(m)])]
    pallas_call x14 -> x15, Pallas kernels: 15.8 us -> 16.2 us  [call(): pl.pallas_call(body, out_shape=outs, in_specs=specs, out_specs=[place] *...]
  transfers between devices with their start and end apart: 18 -> 24, of which waited for: 10 -> 10; matrix products, arithmetic and copies ran while one was open for 0% -> 0% of each run, Pallas kernels for 12% -> 14%
where the time goes in v3:
time: 90.9 us; the launch traced here: 90.5 us
  starting transfers between devices  35.7 us (39%)
  waiting for transfers between devices  35.5 us (39%)
  Pallas kernels  16.2 us (18%)
  local copies, waits for them, and re-layouts  2.81 us (3%)
    ppermute x7, waiting for transfers between devices, along(): return lax.ppermute(value, 'prow', pairs)  22.7 us
    pallas_call x15, Pallas kernels, call(): pl.pallas_call(body, out_shape=outs, in_specs=specs, out_specs=[place] *...  16.2 us
    ppermute x7, starting transfers between devices, along(): return lax.ppermute(value, 'prow', pairs)  13 us
    ppermute x6, starting transfers between devices, across(): return lax.ppermute(value, 'pcol', pairs)  11.9 us
    ppermute x6, starting transfers between devices, ring(): came.append(lax.ppermute(came[-1], 'pcol', pairs))  9.09 us
    ppermute x6, waiting for transfers between devices, across(): return lax.ppermute(value, 'pcol', pairs)  6.76 us
    ppermute x6, waiting for transfers between devices, ring(): came.append(lax.ppermute(came[-1], 'pcol', pairs))  6.07 us
    unnamed x8, local copies, waits for them, and re-layouts  2.78 us
  transfers between devices with their start and end apart: 24, of which 10 were waited for; matrix products, arithmetic and copies ran while one was open for 0% of the time, Pallas kernels for 14%

profile of v3, /device:TPU:0, one launch (start us, length us, event | category | flops | bytes accessed | tf_op | source)
XLA Modules:
  0.0 90.5 jit_solution(12027884145722506552)
XLA Ops:
  0.0 1.4 %copy-done.1 = bf16[3,512,1,512]{3,1,2,0:T(8,128)(2,1)S(1)} copy-done((bf16[3,512,1,512]{3,1,2,0:T(8,128)(2,1)S(1)}, bf16[3,512,1,512]{3,1,2,0:T(8,128)(2,1)}, u32[]{:S(2)}) %copy-start.1) | copy-done | bytes 1572888
  4.1 2.6 %collective-permute-start.3 = (bf16[512,512]{1,0:T(8,128)(2,1)S(1)}, bf16[512,512]{1,0:T(8,128)(2,1)S(1)}, u32[]{:S(2)}, u32[]{:S(2)}) collective-permute-start(bf16[512,512]{1,0:T(8,128)(2,1)S(1)} %get-tuple-element.16.refs_3_), channel_id=1, source_target_pairs={{0,8},{24,16},{16,0},{8,24},{1,9},{25,17},{17,1},{9,25},{2,10},{26... | collective-permute-start | bytes 1572872 | tf_op jit(solution)/shard_map/swap/ppermute | solution.py:333
  7.4 2.2 %collective-permute-start.1 = (bf16[256,512]{1,0:T(8,128)(2,1)S(1)}, bf16[256,512]{1,0:T(8,128)(2,1)S(1)}, u32[]{:S(2)}, u32[]{:S(2)}) collective-permute-start(bf16[256,512]{1,0:T(8,128)(2,1)S(1)} %pick_extra.1.refs_1_.refs_3_), channel_id=1, source_target_pairs={{0,2},{1,5},{2,0},{3,7},{4,6},{5,1},{6,4},{7,3},{8,10},{9,13},{10,... | collective-permute-start | bytes 786440 | tf_op jit(solution)/shard_map/extra0/ppermute | solution.py:345
  10.9 9.4 %collective-permute-done.3.refs_3_.refs_4_.refs_6_ = bf16[512,512]{1,0:T(8,128)(2,1)S(1)} collective-permute-done((bf16[512,512]{1,0:T(8,128)(2,1)S(1)}, bf16[512,512]{1,0:T(8,128)(2,1)S(1)}, u32[]{:S(2)}, u32[]{:S(2)}) %collective-permute-start.3) | collective-permute-done | bytes 524320 | tf_op jit(solution)/shard_map/swap/ppermute | solution.py:333
  20.9 1.6 %collective-permute-start.2 = (bf16[256,512]{1,0:T(8,128)(2,1)S(1)}, bf16[256,512]{1,0:T(8,128)(2,1)S(1)}, u32[]{:S(2)}, u32[]{:S(2)}) collective-permute-start(bf16[256,512]{1,0:T(8,128)(2,1)S(1)} %forward_extra.1.refs_1_), channel_id=1, source_target_pairs={{0,4},{1,3},{2,6},{3,1},{4,0},{5,7},{6,2},{7,5},{8,12},{9,11},{10,... | collective-permute-start | bytes 786440 | tf_op jit(solution)/shard_map/extra1/ppermute | solution.py:345
  22.6 1.5 %collective-permute-start.18 = (bf16[2,256,512]{2,1,0:T(8,128)(2,1)S(1)}, bf16[2,256,512]{2,1,0:T(8,128)(2,1)S(1)}, u32[]{:S(2)}, u32[]{:S(2)}) collective-permute-start(bf16[2,256,512]{2,1,0:T(8,128)(2,1)S(1)} %get-tuple-element.21.refs_1_), channel_id=1, source_target_pairs={{0,2},{1,5},{2,0},{3,7},{4,6},{5,1},{6,4},{7,3},{8,10},{9,13},{10,... | collective-permute-start | bytes 1572872 | tf_op jit(solution)/shard_map/free0/ppermute | solution.py:345
  24.0 5.3 %collective-permute-done.2.refs_2_ = bf16[256,512]{1,0:T(8,128)(2,1)S(1)} collective-permute-done((bf16[256,512]{1,0:T(8,128)(2,1)S(1)}, bf16[256,512]{1,0:T(8,128)(2,1)S(1)}, u32[]{:S(2)}, u32[]{:S(2)}) %collective-permute-start.2) | collective-permute-done | bytes 262176 | tf_op jit(solution)/shard_map/extra1/ppermute | solution.py:345
  30.0 3.7 %collective-permute-start.4 = (bf16[256,512]{1,0:T(8,128)(2,1)S(1)}, bf16[256,512]{1,0:T(8,128)(2,1)S(1)}, u32[]{:S(2)}, u32[]{:S(2)}) collective-permute-start(bf16[256,512]{1,0:T(8,128)(2,1)S(1)} %extra_here.1.refs_0_.refs_2_), channel_id=1, source_target_pairs={{0,16},{24,8},{1,17},{25,9},{2,18},{26,10},{3,19},{27,11},{4,20},{... | collective-permute-start | bytes 786440 | tf_op jit(solution)/shard_map/extra_z/ppermute | solution.py:333
  33.7 1.3 %collective-permute-start.21 = (bf16[2,256,512]{2,1,0:T(8,128)(2,1)S(1)}, bf16[2,256,512]{2,1,0:T(8,128)(2,1)S(1)}, u32[]{:S(2)}, u32[]{:S(2)}) collective-permute-start(bf16[2,256,512]{2,1,0:T(8,128)(2,1)S(1)} %collective-permute-done.20.refs_7_), channel_id=1, source_target_pairs={{4,0},{3,1},{12,8},{11,9},{20,16},{19,17},{28,24},{27,25}} | collective-permute-start | bytes 1572872 | tf_op jit(solution)/shard_map/fixed1/ppermute | solution.py:351
  37.8 2.7 %collective-permute-start.6 = (bf16[256,512]{1,0:T(8,128)(2,1)S(1)}, bf16[256,512]{1,0:T(8,128)(2,1)S(1)}, u32[]{:S(2)}, u32[]{:S(2)}) collective-permute-start(bf16[256,512]{1,0:T(8,128)(2,1)S(1)} %hand_on.1), channel_id=1, source_target_pairs={{0,8},{24,16},{16,24},{8,0},{1,9},{25,17},{17,25},{9,1},{2,10},{26... | collective-permute-start | bytes 786440 | tf_op jit(solution)/shard_map/extra_z/ppermute | solution.py:333
  41.1 2.7 %collective-permute-start.19 = (bf16[2,256,512]{2,1,0:T(8,128)(2,1)S(1)}, bf16[2,256,512]{2,1,0:T(8,128)(2,1)S(1)}, u32[]{:S(2)}, u32[]{:S(2)}) collective-permute-start(bf16[2,256,512]{2,1,0:T(8,128)(2,1)S(1)} %forward_free.1.refs_4_), channel_id=1, source_target_pairs={{0,4},{1,3},{2,6},{3,1},{4,0},{5,7},{6,2},{7,5},{8,12},{9,11},{10,... | collective-permute-start | bytes 1572872 | tf_op jit(solution)/shard_map/free1/ppermute | solution.py:345
  45.9 3.8 %collective-permute-start.22 = (bf16[2,256,512]{2,1,0:T(8,128)(2,1)S(1)}, bf16[2,256,512]{2,1,0:T(8,128)(2,1)S(1)}, u32[]{:S(2)}, u32[]{:S(2)}) collective-permute-start(bf16[2,256,512]{2,1,0:T(8,128)(2,1)S(1)} %collective-permute-done.21.refs_8_), channel_id=1, source_target_pairs={{0,2},{1,5},{8,10},{9,13},{16,18},{17,21},{24,26},{25,29}} | collective-permute-start | bytes 1572872 | tf_op jit(solution)/shard_map/fixed2/ppermute | solution.py:351
  51.0 5.4 %collective-permute-done.22.refs_9_ = bf16[2,256,512]{2,1,0:T(8,128)(2,1)S(1)} collective-permute-done((bf16[2,256,512]{2,1,0:T(8,128)(2,1)S(1)}, bf16[2,256,512]{2,1,0:T(8,128)(2,1)S(1)}, u32[]{:S(2)}, u32[]{:S(2)}) %collective-permute-start.22) | collective-permute-done | bytes 524320 | tf_op jit(solution)/shard_map/fixed2/ppermute | solution.py:351
  56.4 2.0 %multiply_stays.1.refs_2_ = bf16[2,2,256,512]{3,2,1,0:T(8,128)(2,1)S(1)} custom-call(s32[2,3]{1,0:T(2,128)S(1)} %copy-done.2, bf16[2,512,512]{2,1,0:T(8,128)(2,1)S(1)} %copy-done, bf16[2,256,512]{2,1,0:T(8,128)(2,1)S(1)} %settle_extra.1.refs_1_.refs_2_, bf16[2,256,512]{2,1,0:T(8,128)(2,1)S(1)} %collective-permute-done.9.refs_2_.refs_3_, ...), custom_call_target="tpu_custom_call" | custom-call | flops 805306368 | bytes 5242904 | tf_op jit(solution)/shard_map/multiply_stays/pallas_call | solution.py:314
  59.4 1.6 %collective-permute-start.12 = (bf16[1,256,512]{2,1,0:T(8,128)(2,1)S(1)}, bf16[1,256,512]{2,1,0:T(8,128)(2,1)S(1)}, u32[]{:S(2)}, u32[]{:S(2)}) collective-permute-start(bf16[1,256,512]{2,1,0:T(8,128)(2,1)S(1)} %get-tuple-element.17.refs_2_.refs_1_), channel_id=1, source_target_pairs={{0,2},{1,5},{2,0},{3,7},{4,6},{5,1},{6,4},{7,3},{8,10},{9,13},{10,... | collective-permute-start | bytes 786440 | tf_op jit(solution)/shard_map/free_third0/ppermute | solution.py:345
  62.3 1.3 %collective-permute-start.10 = (bf16[256,512]{1,0:T(8,128)(2,1)S(1)}, bf16[256,512]{1,0:T(8,128)(2,1)S(1)}, u32[]{:S(2)}, u32[]{:S(2)}) collective-permute-start(bf16[256,512]{1,0:T(8,128)(2,1)S(1)} %collective-permute-done.7.refs_5_), channel_id=1, source_target_pairs={{16,24},{8,0},{17,25},{9,1},{18,26},{10,2},{19,27},{11,3},{20,28},... | collective-permute-start | bytes 786440 | tf_op jit(solution)/shard_map/row2/ppermute | solution.py:333
  63.6 1.3 %collective-permute-start.11 = (bf16[256,512]{1,0:T(8,128)(2,1)S(1)}, bf16[256,512]{1,0:T(8,128)(2,1)S(1)}, u32[]{:S(2)}, u32[]{:S(2)}) collective-permute-start(bf16[256,512]{1,0:T(8,128)(2,1)S(1)} %collective-permute-done.8.refs_6_), channel_id=1, source_target_pairs={{16,24},{8,0},{17,25},{9,1},{18,26},{10,2},{19,27},{11,3},{20,28},... | collective-permute-start | bytes 786440 | tf_op jit(solution)/shard_map/row2/ppermute | solution.py:333
  66.4 2.3 %collective-permute-start.13 = (bf16[1,256,512]{2,1,0:T(8,128)(2,1)S(1)}, bf16[1,256,512]{2,1,0:T(8,128)(2,1)S(1)}, u32[]{:S(2)}, u32[]{:S(2)}) collective-permute-start(bf16[1,256,512]{2,1,0:T(8,128)(2,1)S(1)} %forward_free_third.1.refs_4_), channel_id=1, source_target_pairs={{0,4},{1,3},{2,6},{3,1},{4,0},{5,7},{6,2},{7,5},{8,12},{9,11},{10,... | collective-permute-start | bytes 786440 | tf_op jit(solution)/shard_map/free_third1/ppermute | solution.py:345
  69.3 1.3 %collective-permute-start.16 = (bf16[1,256,512]{2,1,0:T(8,128)(2,1)S(1)}, bf16[1,256,512]{2,1,0:T(8,128)(2,1)S(1)}, u32[]{:S(2)}, u32[]{:S(2)}) collective-permute-start(bf16[1,256,512]{2,1,0:T(8,128)(2,1)S(1)} %collective-permute-done.15.refs_8_), channel_id=1, source_target_pairs={{0,2},{1,5},{8,10},{9,13},{16,18},{17,21},{24,26},{25,29}} | collective-permute-start | bytes 786440 | tf_op jit(solution)/shard_map/fixed_third2/ppermute | solution.py:351
  70.6 6.4 %collective-permute-done.10.refs_7_ = bf16[256,512]{1,0:T(8,128)(2,1)S(1)} collective-permute-done((bf16[256,512]{1,0:T(8,128)(2,1)S(1)}, bf16[256,512]{1,0:T(8,128)(2,1)S(1)}, u32[]{:S(2)}, u32[]{:S(2)}) %collective-permute-start.10) | collective-permute-done | bytes 262176 | tf_op jit(solution)/shard_map/row2/ppermute | solution.py:333
  77.0 5.2 %collective-permute-done.11.refs_8_ = bf16[256,512]{1,0:T(8,128)(2,1)S(1)} collective-permute-done((bf16[256,512]{1,0:T(8,128)(2,1)S(1)}, bf16[256,512]{1,0:T(8,128)(2,1)S(1)}, u32[]{:S(2)}, u32[]{:S(2)}) %collective-permute-start.11) | collective-permute-done | bytes 262176 | tf_op jit(solution)/shard_map/row2/ppermute | solution.py:333
  83.3 1.4 %multiply_third.1.refs_3_ = bf16[2,1,256,512]{3,2,1,0:T(8,128)(2,1)S(1)} custom-call(s32[2,3]{1,0:T(2,128)S(1)} %copy-done.2, bf16[2,512,512]{2,1,0:T(8,128)(2,1)S(1)} %copy-done, bf16[2,256,512]{2,1,0:T(8,128)(2,1)S(1)} %settle_extra.1.refs_1_.refs_2_, bf16[2,256,512]{2,1,0:T(8,128)(2,1)S(1)} %collective-permute-done.9.refs_2_.refs_3_, ...), custom_call_target="tpu_custom_call" | custom-call | flops 402653184 | bytes 3670040 | tf_op jit(solution)/shard_map/multiply_third/pallas_call | solution.py:314
  84.8 3.4 %update_stays.1.refs_7_ = bf16[3,512,512]{2,1,0:T(8,128)(2,1)} custom-call(s32[2,3]{1,0:T(2,128)S(1)} %copy-done.2, bf16[2,512,512]{2,1,0:T(8,128)(2,1)S(1)} %get-tuple-element.18.refs_10_.refs_1_, bf16[2,2,256,512]{3,2,1,0:T(8,128)(2,1)S(1)} %multiply_stays.1.refs_2_, bf16[2,2,256,512]{3,2,1,0:T(8,128)(2,1)S(1)} %collective-permute-done.23.refs_3_, ...), custom_call_target="tpu_custom_call" | custom-call | flops 1073741824 | bytes 4718616 | tf_op jit(solution)/shard_map/update_stays/pallas_call | solution.py:314
  88.1 2.4 %update_third.1 = bf16[3,512,512]{2,1,0:T(8,128)(2,1)} custom-call(s32[2,3]{1,0:T(2,128)S(1)} %copy-done.2, bf16[2,512,512]{2,1,0:T(8,128)(2,1)S(1)} %get-tuple-element.18.refs_10_.refs_1_, bf16[512,512]{1,0:T(8,128)(2,1)S(1)} %get-tuple-element.19.refs_2_, bf16[2,1,256,512]{3,2,1,0:T(8,128)(2,1)S(1)} %multiply_third.1.refs_3_, ...), custom_call_target="tpu_custom_call", output_to_operand_aliasing={{}: (7, {})} | custom-call | flops 536870912 | bytes 6291480 | tf_op jit(solution)/shard_map/update_third/pallas_call | solution.py:314
  (48 shorter events, 18.0 us)
Async XLA Ops:
  3.6 3.2 %collective-permute-start = (bf16[3,256,512]{2,1,0:T(8,128)(2,1)S(1)}, bf16[3,256,512]{2,1,0:T(8,128)(2,1)S(1)}, u32[]{:S(2)}, u32[]{:S(2)}) collective-permute-start(bf16[3,256,512]{2,1,0:T(8,128)(2,1)S(1)} %get-tuple-element.15), channel_id=1, source_target_pairs={{0,1},{1,0},{2,3},{3,2},{4,5},{5,4},{6,7},{7,6},{8,9},{9,8},{10,11... | collective-permute-start | bytes 2359304 | tf_op jit(solution)/shard_map/sib_early/ppermute | solution.py:337
  4.1 16.2 %collective-permute-start.3 = (bf16[512,512]{1,0:T(8,128)(2,1)S(1)}, bf16[512,512]{1,0:T(8,128)(2,1)S(1)}, u32[]{:S(2)}, u32[]{:S(2)}) collective-permute-start(bf16[512,512]{1,0:T(8,128)(2,1)S(1)} %get-tuple-element.16.refs_3_), channel_id=1, source_target_pairs={{0,8},{24,16},{16,0},{8,24},{1,9},{25,17},{17,1},{9,25},{2,10},{26... | collective-permute-start | bytes 1572872 | tf_op jit(solution)/shard_map/swap/ppermute | solution.py:333
  7.4 13.0 %collective-permute-start.1 = (bf16[256,512]{1,0:T(8,128)(2,1)S(1)}, bf16[256,512]{1,0:T(8,128)(2,1)S(1)}, u32[]{:S(2)}, u32[]{:S(2)}) collective-permute-start(bf16[256,512]{1,0:T(8,128)(2,1)S(1)} %pick_extra.1.refs_1_.refs_3_), channel_id=1, source_target_pairs={{0,2},{1,5},{2,0},{3,7},{4,6},{5,1},{6,4},{7,3},{8,10},{9,13},{10,... | collective-permute-start | bytes 786440 | tf_op jit(solution)/shard_map/extra0/ppermute | solution.py:345
  10.2 23.5 %collective-permute-start.20 = (bf16[2,256,512]{2,1,0:T(8,128)(2,1)S(1)}, bf16[2,256,512]{2,1,0:T(8,128)(2,1)S(1)}, u32[]{:S(2)}, u32[]{:S(2)}) collective-permute-start(bf16[2,256,512]{2,1,0:T(8,128)(2,1)S(1)} %get-tuple-element.22.refs_6_), channel_id=1, source_target_pairs={{6,4},{7,3},{14,12},{15,11},{22,20},{23,19},{30,28},{31,27}} | collective-permute-start | bytes 1572872 | tf_op jit(solution)/shard_map/fixed0/ppermute | solution.py:351
  20.3 15.4 %collective-permute-start.5 = (bf16[512,512]{1,0:T(8,128)(2,1)S(1)}, bf16[512,512]{1,0:T(8,128)(2,1)S(1)}, u32[]{:S(2)}, u32[]{:S(2)}) collective-permute-start(bf16[512,512]{1,0:T(8,128)(2,1)S(1)} %collective-permute-done.3.refs_3_.refs_4_.refs_6_), channel_id=1, source_target_pairs={{0,1},{1,0},{2,3},{3,2},{4,5},{5,4},{6,7},{7,6},{8,9},{9,8},{10,11... | collective-permute-start | bytes 1572872 | tf_op jit(solution)/shard_map/sib_moved/ppermute | solution.py:337
  20.9 8.5 %collective-permute-start.2 = (bf16[256,512]{1,0:T(8,128)(2,1)S(1)}, bf16[256,512]{1,0:T(8,128)(2,1)S(1)}, u32[]{:S(2)}, u32[]{:S(2)}) collective-permute-start(bf16[256,512]{1,0:T(8,128)(2,1)S(1)} %forward_extra.1.refs_1_), channel_id=1, source_target_pairs={{0,4},{1,3},{2,6},{3,1},{4,0},{5,7},{6,2},{7,5},{8,12},{9,11},{10,... | collective-permute-start | bytes 786440 | tf_op jit(solution)/shard_map/extra1/ppermute | solution.py:345
  22.6 18.0 %collective-permute-start.18 = (bf16[2,256,512]{2,1,0:T(8,128)(2,1)S(1)}, bf16[2,256,512]{2,1,0:T(8,128)(2,1)S(1)}, u32[]{:S(2)}, u32[]{:S(2)}) collective-permute-start(bf16[2,256,512]{2,1,0:T(8,128)(2,1)S(1)} %get-tuple-element.21.refs_1_), channel_id=1, source_target_pairs={{0,2},{1,5},{2,0},{3,7},{4,6},{5,1},{6,4},{7,3},{8,10},{9,13},{10,... | collective-permute-start | bytes 1572872 | tf_op jit(solution)/shard_map/free0/ppermute | solution.py:345
  30.0 7.8 %collective-permute-start.4 = (bf16[256,512]{1,0:T(8,128)(2,1)S(1)}, bf16[256,512]{1,0:T(8,128)(2,1)S(1)}, u32[]{:S(2)}, u32[]{:S(2)}) collective-permute-start(bf16[256,512]{1,0:T(8,128)(2,1)S(1)} %extra_here.1.refs_0_.refs_2_), channel_id=1, source_target_pairs={{0,16},{24,8},{1,17},{25,9},{2,18},{26,10},{3,19},{27,11},{4,20},{... | collective-permute-start | bytes 786440 | tf_op jit(solution)/shard_map/extra_z/ppermute | solution.py:333
  33.7 12.2 %collective-permute-start.21 = (bf16[2,256,512]{2,1,0:T(8,128)(2,1)S(1)}, bf16[2,256,512]{2,1,0:T(8,128)(2,1)S(1)}, u32[]{:S(2)}, u32[]{:S(2)}) collective-permute-start(bf16[2,256,512]{2,1,0:T(8,128)(2,1)S(1)} %collective-permute-done.20.refs_7_), channel_id=1, source_target_pairs={{4,0},{3,1},{12,8},{11,9},{20,16},{19,17},{28,24},{27,25}} | collective-permute-start | bytes 1572872 | tf_op jit(solution)/shard_map/fixed1/ppermute | solution.py:351
  35.1 8.7 %collective-permute-start.7 = (bf16[256,512]{1,0:T(8,128)(2,1)S(1)}, bf16[256,512]{1,0:T(8,128)(2,1)S(1)}, u32[]{:S(2)}, u32[]{:S(2)}) collective-permute-start(bf16[256,512]{1,0:T(8,128)(2,1)S(1)} %get-tuple-element.24), channel_id=1, source_target_pairs={{8,16},{16,8},{9,17},{17,9},{10,18},{18,10},{11,19},{19,11},{12,20... | collective-permute-start | bytes 786440 | tf_op jit(solution)/shard_map/row1/ppermute | solution.py:333
  35.8 8.0 %collective-permute-start.8 = (bf16[256,512]{1,0:T(8,128)(2,1)S(1)}, bf16[256,512]{1,0:T(8,128)(2,1)S(1)}, u32[]{:S(2)}, u32[]{:S(2)}) collective-permute-start(bf16[256,512]{1,0:T(8,128)(2,1)S(1)} %get-tuple-element.23), channel_id=1, source_target_pairs={{8,16},{16,8},{9,17},{17,9},{10,18},{18,10},{11,19},{19,11},{12,20... | collective-permute-start | bytes 786440 | tf_op jit(solution)/shard_map/row1/ppermute | solution.py:333
  37.8 7.1 %collective-permute-start.6 = (bf16[256,512]{1,0:T(8,128)(2,1)S(1)}, bf16[256,512]{1,0:T(8,128)(2,1)S(1)}, u32[]{:S(2)}, u32[]{:S(2)}) collective-permute-start(bf16[256,512]{1,0:T(8,128)(2,1)S(1)} %hand_on.1), channel_id=1, source_target_pairs={{0,8},{24,16},{16,24},{8,0},{1,9},{25,17},{17,25},{9,1},{2,10},{26... | collective-permute-start | bytes 786440 | tf_op jit(solution)/shard_map/extra_z/ppermute | solution.py:333
  41.1 9.8 %collective-permute-start.19 = (bf16[2,256,512]{2,1,0:T(8,128)(2,1)S(1)}, bf16[2,256,512]{2,1,0:T(8,128)(2,1)S(1)}, u32[]{:S(2)}, u32[]{:S(2)}) collective-permute-start(bf16[2,256,512]{2,1,0:T(8,128)(2,1)S(1)} %forward_free.1.refs_4_), channel_id=1, source_target_pairs={{0,4},{1,3},{2,6},{3,1},{4,0},{5,7},{6,2},{7,5},{8,12},{9,11},{10,... | collective-permute-start | bytes 1572872 | tf_op jit(solution)/shard_map/free1/ppermute | solution.py:345
  45.8 5.1 %collective-permute-start.9 = (bf16[2,256,512]{2,1,0:T(8,128)(2,1)S(1)}, bf16[2,256,512]{2,1,0:T(8,128)(2,1)S(1)}, u32[]{:S(2)}, u32[]{:S(2)}) collective-permute-start(bf16[2,256,512]{2,1,0:T(8,128)(2,1)S(1)} %settle_extra.1.refs_1_.refs_2_), channel_id=1, source_target_pairs={{0,1},{1,0},{2,3},{3,2},{4,5},{5,4},{6,7},{7,6},{8,9},{9,8},{10,11... | collective-permute-start | bytes 1572872 | tf_op jit(solution)/shard_map/sib_vl/ppermute | solution.py:337
  45.9 10.5 %collective-permute-start.22 = (bf16[2,256,512]{2,1,0:T(8,128)(2,1)S(1)}, bf16[2,256,512]{2,1,0:T(8,128)(2,1)S(1)}, u32[]{:S(2)}, u32[]{:S(2)}) collective-permute-start(bf16[2,256,512]{2,1,0:T(8,128)(2,1)S(1)} %collective-permute-done.21.refs_8_), channel_id=1, source_target_pairs={{0,2},{1,5},{8,10},{9,13},{16,18},{17,21},{24,26},{25,29}} | collective-permute-start | bytes 1572872 | tf_op jit(solution)/shard_map/fixed2/ppermute | solution.py:351
  49.8 11.3 %collective-permute-start.14 = (bf16[1,256,512]{2,1,0:T(8,128)(2,1)S(1)}, bf16[1,256,512]{2,1,0:T(8,128)(2,1)S(1)}, u32[]{:S(2)}, u32[]{:S(2)}) collective-permute-start(bf16[1,256,512]{2,1,0:T(8,128)(2,1)S(1)} %get-tuple-element.20.refs_6_), channel_id=1, source_target_pairs={{6,4},{7,3},{14,12},{15,11},{22,20},{23,19},{30,28},{31,27}} | collective-permute-start | bytes 786440 | tf_op jit(solution)/shard_map/fixed_third0/ppermute | solution.py:351
  58.4 26.4 %collective-permute-start.23 = (bf16[2,2,256,512]{3,2,1,0:T(8,128)(2,1)S(1)}, bf16[2,2,256,512]{3,2,1,0:T(8,128)(2,1)S(1)}, u32[]{:S(2)}, u32[]{:S(2)}) collective-permute-start(bf16[2,2,256,512]{3,2,1,0:T(8,128)(2,1)S(1)} %multiply_stays.1.refs_2_), channel_id=1, source_target_pairs={{0,1},{1,0},{2,3},{3,2},{4,5},{5,4},{6,7},{7,6},{8,9},{9,8},{10,11... | collective-permute-start | bytes 3145736 | tf_op jit(solution)/shard_map/sib_mine/ppermute | solution.py:337
  59.4 6.4 %collective-permute-start.12 = (bf16[1,256,512]{2,1,0:T(8,128)(2,1)S(1)}, bf16[1,256,512]{2,1,0:T(8,128)(2,1)S(1)}, u32[]{:S(2)}, u32[]{:S(2)}) collective-permute-start(bf16[1,256,512]{2,1,0:T(8,128)(2,1)S(1)} %get-tuple-element.17.refs_2_.refs_1_), channel_id=1, source_target_pairs={{0,2},{1,5},{2,0},{3,7},{4,6},{5,1},{6,4},{7,3},{8,10},{9,13},{10,... | collective-permute-start | bytes 786440 | tf_op jit(solution)/shard_map/free_third0/ppermute | solution.py:345
  61.0 8.3 %collective-permute-start.15 = (bf16[1,256,512]{2,1,0:T(8,128)(2,1)S(1)}, bf16[1,256,512]{2,1,0:T(8,128)(2,1)S(1)}, u32[]{:S(2)}, u32[]{:S(2)}) collective-permute-start(bf16[1,256,512]{2,1,0:T(8,128)(2,1)S(1)} %collective-permute-done.14.refs_7_), channel_id=1, source_target_pairs={{4,0},{3,1},{12,8},{11,9},{20,16},{19,17},{28,24},{27,25}} | collective-permute-start | bytes 786440 | tf_op jit(solution)/shard_map/fixed_third1/ppermute | solution.py:351
  62.3 14.6 %collective-permute-start.10 = (bf16[256,512]{1,0:T(8,128)(2,1)S(1)}, bf16[256,512]{1,0:T(8,128)(2,1)S(1)}, u32[]{:S(2)}, u32[]{:S(2)}) collective-permute-start(bf16[256,512]{1,0:T(8,128)(2,1)S(1)} %collective-permute-done.7.refs_5_), channel_id=1, source_target_pairs={{16,24},{8,0},{17,25},{9,1},{18,26},{10,2},{19,27},{11,3},{20,28},... | collective-permute-start | bytes 786440 | tf_op jit(solution)/shard_map/row2/ppermute | solution.py:333
  63.6 18.5 %collective-permute-start.11 = (bf16[256,512]{1,0:T(8,128)(2,1)S(1)}, bf16[256,512]{1,0:T(8,128)(2,1)S(1)}, u32[]{:S(2)}, u32[]{:S(2)}) collective-permute-start(bf16[256,512]{1,0:T(8,128)(2,1)S(1)} %collective-permute-done.8.refs_6_), channel_id=1, source_target_pairs={{16,24},{8,0},{17,25},{9,1},{18,26},{10,2},{19,27},{11,3},{20,28},... | collective-permute-start | bytes 786440 | tf_op jit(solution)/shard_map/row2/ppermute | solution.py:333
  66.4 16.9 %collective-permute-start.13 = (bf16[1,256,512]{2,1,0:T(8,128)(2,1)S(1)}, bf16[1,256,512]{2,1,0:T(8,128)(2,1)S(1)}, u32[]{:S(2)}, u32[]{:S(2)}) collective-permute-start(bf16[1,256,512]{2,1,0:T(8,128)(2,1)S(1)} %forward_free_third.1.refs_4_), channel_id=1, source_target_pairs={{0,4},{1,3},{2,6},{3,1},{4,0},{5,7},{6,2},{7,5},{8,12},{9,11},{10,... | collective-permute-start | bytes 786440 | tf_op jit(solution)/shard_map/free_third1/ppermute | solution.py:345
  69.3 14.0 %collective-permute-start.16 = (bf16[1,256,512]{2,1,0:T(8,128)(2,1)S(1)}, bf16[1,256,512]{2,1,0:T(8,128)(2,1)S(1)}, u32[]{:S(2)}, u32[]{:S(2)}) collective-permute-start(bf16[1,256,512]{2,1,0:T(8,128)(2,1)S(1)} %collective-permute-done.15.refs_8_), channel_id=1, source_target_pairs={{0,2},{1,5},{8,10},{9,13},{16,18},{17,21},{24,26},{25,29}} | collective-permute-start | bytes 786440 | tf_op jit(solution)/shard_map/fixed_third2/ppermute | solution.py:351
  84.7 3.5 %collective-permute-start.17 = (bf16[2,1,256,512]{3,2,1,0:T(8,128)(2,1)S(1)}, bf16[2,1,256,512]{3,2,1,0:T(8,128)(2,1)S(1)}, u32[]{:S(2)}, u32[]{:S(2)}) collective-permute-start(bf16[2,1,256,512]{3,2,1,0:T(8,128)(2,1)S(1)} %multiply_third.1.refs_3_), channel_id=1, source_target_pairs={{0,1},{1,0},{2,3},{3,2},{4,5},{5,4},{6,7},{7,6},{8,9},{9,8},{10,11... | collective-permute-start | bytes 1572872 | tf_op jit(solution)/shard_map/sib_third/ppermute | solution.py:337
  (4 other events, 10.6 us)

commit v4 on v3

--- a/solution.py
+++ b/solution.py
@@ -112,6 +112,11 @@
     either(take, out, lambda: got[...], lambda: had[...])
 
 
+def forward_both(n, m, key, stage, stages, piv, had, got, moved, out, moved_out):
+    forward(n, m, key, stage, stages, piv, had, got, out)
+    moved_out[...] = moved[...]
+
+
 def ring_order(chips):
     side = round(chips**0.5)
     if side * side != chips or side % 2:
@@ -301,7 +306,7 @@
     dt = matrix.dtype
     blocks = matrix.reshape(rb, width, width)
 
-    def call(kernel, shapes, specs, *operands, scratch=(), aliases=(), products=0, place=VMEM, after=(), name=None):
+    def call(kernel, shapes, specs, *operands, scratch=(), aliases=(), products=0, place=VMEM, after=(), name=None, weight=0):
         outs = [jax.ShapeDtypeStruct(s, dt) for s in shapes]
         count = len(operands)
         scratch = [pltpu.VMEM(s, dt) if isinstance(s, tuple) else s for s in scratch]
@@ -322,7 +327,7 @@
             name=name or kernel.__name__,
             cost_estimate=pl.CostEstimate(
                 flops=int(products * 2 * width**3),
-                bytes_accessed=sum(a.size * a.dtype.itemsize for a in operands),
+                bytes_accessed=weight + sum(a.size * a.dtype.itemsize for a in operands),
                 transcendentals=0,
             ),
         )(*operands, *after)
@@ -351,13 +356,16 @@
                 came.append(lax.ppermute(came[-1], "pcol", pairs))
         return came
 
-    def passing(name, key, value, after=()):
+    def passing(name, key, value, after=(), weight=0):
         for s in range(stages):
             got = across(name + str(s), s, value)
             if s < stages - 1:
                 kernel = functools.partial(forward, n, m, key, s, stages)
                 step = lambda _n, _m, *refs: kernel(*refs)
-                value = call(step, [value.shape], "s", pivots, value, got, after=after, name="forward_" + name)
+                label = "forward_" + name
+                value = call(
+                    step, [value.shape], "s", pivots, value, got, after=after, name=label, weight=weight
+                )
         return value, got
 
     square, strip = (width, width), (half, width)
@@ -373,14 +381,35 @@
     early = sibling("sib_early", other)
 
     extra = call(pick_extra, [strip], "s", pivots, raw, early)
-    had, got = passing("extra", "cx", extra)
-    step = lambda _n, _m, *refs: forward(n, m, "cx", stages - 1, stages, *refs)
-    extra_here = call(step, [strip], "s", pivots, had, got, after=[moved], name="extra_here")
     fixed, free = call(
         pick, [(rb - 1, *strip)] * 2, "s", pivots, raw, early, after=[extra]
     )
-    free_stays = passing("free", "free", free)
+    had, got = passing("extra", "cx", extra, after=[fixed], weight=16 * 2**20)
     fixed_stays = ring("fixed", fixed)
+    free_got = across("free0", 0, free)
+    if stages > 1:
+        step = lambda _n, _m, *refs: forward_both(n, m, "free", 0, stages, *refs)
+        free, moved = call(
+            step,
+            [free.shape, square],
+            "s",
+            pivots,
+            free,
+            free_got,
+            moved,
+            after=[had, fixed_stays[1]],
+            name="forward_free",
+        )
+        free_got = across("free1", 1, free)
+    for s in range(2, stages):
+        step = lambda _n, _m, *refs: forward(n, m, "free", s - 1, stages, *refs)
+        free = call(step, [free.shape], "s", pivots, free, free_got, name="forward_free")
+        free_got = across("free" + str(s), s, free)
+    free_stays = free, free_got
+    step = lambda _n, _m, *refs: forward(n, m, "cx", stages - 1, stages, *refs)
+    extra_here = call(
+        step, [strip], "s", pivots, had, got, after=[free], name="extra_here"
+    )
 
     hops = []
     parts = [moved[:half], moved[half:]]
@@ -391,8 +420,18 @@
 
     sib_moved = sibling("sib_moved", moved)
     fixed, free = call(
-        pick_third, [(1, *strip)] * 2, "s", pivots, raw, early, moved, sib_moved
-    )
+        pick_third,
+        [(1, *strip)] * 2,
+        "s",
+        pivots,
+        raw,
+        early,
+        moved,
+        sib_moved,
+        after=[extra_here],
+    )
+    fixed_third = ring("fixed_third", fixed)
+    free_third = passing("free_third", "free", free, after=[fixed_stays[2], free_got])
 
     came = [extra_here]
     send = extra_here
@@ -405,13 +444,27 @@
         came.append(got)
         if stride > 1:
             step = lambda _n, _m, *refs: hand_on(n, m, stride, *refs)
-            send = call(step, [strip], "", send, got, name="hand_on", after=[free])
+            send = call(
+                step,
+                [strip],
+                "",
+                send,
+                got,
+                name="hand_on",
+                after=[hops[0], fixed_third[1], free_third[0]],
+            )
         stride //= 2
-    vl = call(settle_extra, [(2, *strip)], "s", pivots, inverses, *came, products=0.5, after=hops[:2])
+    vl = call(
+        settle_extra,
+        [(2, *strip)],
+        "s",
+        pivots,
+        inverses,
+        *came,
+        products=0.5,
+        after=[hops[1], fixed_stays[3], fixed_third[2], free_third[1]],
+    )
     sib_vl = sibling("sib_vl", vl)
-
-    free_third = passing("free_third", "free", free)
-    fixed_third = ring("fixed_third", fixed)
 
     step = lambda _n, _m, *refs: multiply(n, m, stages, *refs)
     mine = call(
@@ -427,6 +480,7 @@
         scratch=[square],
         products=3 * (rb - 1) / 2,
         name="multiply_stays",
+        after=[fixed_third[-1], hops[2]],
     )
     sib_mine = sibling("sib_mine", mine)
     upper, lefts = call(
@@ -440,6 +494,7 @@
         moved,
         *hops,
         products=1,
+        after=[mine],
     )
     mine_third = call(
         step,

time: 90.9 us -> 108 us (1.19)
  waiting for transfers between devices: 35.5 us -> 45.7 us
  starting transfers between devices: 35.7 us -> 42.6 us
    ppermute x6, waiting for transfers between devices: 6.76 us -> 21.5 us  [across(): return lax.ppermute(value, 'pcol', pairs)]
    ppermute x7, starting transfers between devices: 13 us -> 17 us  [along(): return lax.ppermute(value, 'prow', pairs)]
    ppermute x6, starting transfers between devices: 11.9 us -> 15.6 us  [across(): return lax.ppermute(value, 'pcol', pairs)]
    ppermute x6, waiting for transfers between devices: 6.07 us -> 3.53 us  [ring(): came.append(lax.ppermute(came[-1], 'pcol', pairs))]
    ppermute x7, waiting for transfers between devices: 22.7 us -> 20.7 us  [along(): return lax.ppermute(value, 'prow', pairs)]
  transfers between devices with their start and end apart: 24 -> 24, of which waited for: 10 -> 6; matrix products, arithmetic and copies ran while one was open for 0% -> 0% of each run, Pallas kernels for 14% -> 9%
where the time goes in v4:
time: 108 us
  waiting for transfers between devices  45.7 us (42%)
  starting transfers between devices  42.6 us (39%)
  Pallas kernels  16.3 us (15%)
  local copies, waits for them, and re-layouts  2.81 us (3%)
    ppermute x6, waiting for transfers between devices, across(): return lax.ppermute(value, 'pcol', pairs)  21.5 us
    ppermute x7, waiting for transfers between devices, along(): return lax.ppermute(value, 'prow', pairs)  20.7 us
    ppermute x7, starting transfers between devices, along(): return lax.ppermute(value, 'prow', pairs)  17 us
    pallas_call x15, Pallas kernels, call(): pl.pallas_call(body, out_shape=outs, in_specs=specs, out_specs=[place] *...  16.3 us
    ppermute x6, starting transfers between devices, across(): return lax.ppermute(value, 'pcol', pairs)  15.6 us
    ppermute x6, starting transfers between devices, ring(): came.append(lax.ppermute(came[-1], 'pcol', pairs))  9.17 us
    ppermute x6, waiting for transfers between devices, ring(): came.append(lax.ppermute(came[-1], 'pcol', pairs))  3.53 us
    unnamed x8, local copies, waits for them, and re-layouts  2.78 us
  transfers between devices with their start and end apart: 24, of which 6 were waited for; matrix products, arithmetic and copies ran while one was open for 0% of the time, Pallas kernels for 9%

profile of v4, /device:TPU:0, one launch (start us, length us, event | category | flops | bytes accessed | tf_op | source)
XLA Modules:
  0.0 107.8 jit_solution(1006366726626808938)
XLA Ops:
  0.0 1.4 %copy-done.1 = bf16[3,512,1,512]{3,1,2,0:T(8,128)(2,1)S(1)} copy-done((bf16[3,512,1,512]{3,1,2,0:T(8,128)(2,1)S(1)}, bf16[3,512,1,512]{3,1,2,0:T(8,128)(2,1)}, u32[]{:S(2)}) %copy-start.1) | copy-done | bytes 1572888
  4.1 2.6 %collective-permute-start.4 = (bf16[512,512]{1,0:T(8,128)(2,1)S(1)}, bf16[512,512]{1,0:T(8,128)(2,1)S(1)}, u32[]{:S(2)}, u32[]{:S(2)}) collective-permute-start(bf16[512,512]{1,0:T(8,128)(2,1)S(1)} %get-tuple-element.20.refs_3_), channel_id=1, source_target_pairs={{0,8},{24,16},{16,0},{8,24},{1,9},{25,17},{17,1},{9,25},{2,10},{26... | collective-permute-start | bytes 1572872 | tf_op jit(solution)/shard_map/swap/ppermute | solution.py:338
  8.7 2.2 %collective-permute-start.3 = (bf16[2,256,512]{2,1,0:T(8,128)(2,1)S(1)}, bf16[2,256,512]{2,1,0:T(8,128)(2,1)S(1)}, u32[]{:S(2)}, u32[]{:S(2)}) collective-permute-start(bf16[2,256,512]{2,1,0:T(8,128)(2,1)S(1)} %get-tuple-element.19.refs_1_), channel_id=1, source_target_pairs={{0,2},{1,5},{2,0},{3,7},{4,6},{5,1},{6,4},{7,3},{8,10},{9,13},{10,... | collective-permute-start | bytes 1572872 | tf_op jit(solution)/shard_map/free0/ppermute | solution.py:350
  11.0 9.9 %collective-permute-done.1.refs_2_ = bf16[256,512]{1,0:T(8,128)(2,1)S(1)} collective-permute-done((bf16[256,512]{1,0:T(8,128)(2,1)S(1)}, bf16[256,512]{1,0:T(8,128)(2,1)S(1)}, u32[]{:S(2)}, u32[]{:S(2)}) %collective-permute-start.1) | collective-permute-done | bytes 262176 | tf_op jit(solution)/shard_map/extra0/ppermute | solution.py:350
  22.2 8.9 %collective-permute-start.12 = (bf16[2,256,512]{2,1,0:T(8,128)(2,1)S(1)}, bf16[2,256,512]{2,1,0:T(8,128)(2,1)S(1)}, u32[]{:S(2)}, u32[]{:S(2)}) collective-permute-start(bf16[2,256,512]{2,1,0:T(8,128)(2,1)S(1)} %get-tuple-element.21.refs_3_.refs_4_), channel_id=1, source_target_pairs={{0,4},{1,3},{2,6},{3,1},{4,0},{5,7},{6,2},{7,5},{8,12},{9,11},{10,... | collective-permute-start | bytes 1572872 | tf_op jit(solution)/shard_map/free1/ppermute | solution.py:350
  31.1 1.3 %collective-permute-start.11 = (bf16[2,256,512]{2,1,0:T(8,128)(2,1)S(1)}, bf16[2,256,512]{2,1,0:T(8,128)(2,1)S(1)}, u32[]{:S(2)}, u32[]{:S(2)}) collective-permute-start(bf16[2,256,512]{2,1,0:T(8,128)(2,1)S(1)} %collective-permute-done.5.refs_5_.refs_7_), channel_id=1, source_target_pairs={{4,0},{3,1},{12,8},{11,9},{20,16},{19,17},{28,24},{27,25}} | collective-permute-start | bytes 1572872 | tf_op jit(solution)/shard_map/fixed1/ppermute | solution.py:356
  32.4 2.7 %collective-permute-start.2 = (bf16[256,512]{1,0:T(8,128)(2,1)S(1)}, bf16[256,512]{1,0:T(8,128)(2,1)S(1)}, u32[]{:S(2)}, u32[]{:S(2)}) collective-permute-start(bf16[256,512]{1,0:T(8,128)(2,1)S(1)} %forward_extra.1.refs_4_.refs_1_), channel_id=1, source_target_pairs={{0,4},{1,3},{2,6},{3,1},{4,0},{5,7},{6,2},{7,5},{8,12},{9,11},{10,... | collective-permute-start | bytes 786440 | tf_op jit(solution)/shard_map/extra1/ppermute | solution.py:350
  35.1 11.6 %collective-permute-done.2.refs_2_ = bf16[256,512]{1,0:T(8,128)(2,1)S(1)} collective-permute-done((bf16[256,512]{1,0:T(8,128)(2,1)S(1)}, bf16[256,512]{1,0:T(8,128)(2,1)S(1)}, u32[]{:S(2)}, u32[]{:S(2)}) %collective-permute-start.2) | collective-permute-done | bytes 262176 | tf_op jit(solution)/shard_map/extra1/ppermute | solution.py:350
  48.0 4.5 %collective-permute-start.6 = (bf16[256,512]{1,0:T(8,128)(2,1)S(1)}, bf16[256,512]{1,0:T(8,128)(2,1)S(1)}, u32[]{:S(2)}, u32[]{:S(2)}) collective-permute-start(bf16[256,512]{1,0:T(8,128)(2,1)S(1)} %extra_here.1.refs_5_.refs_0_.refs_2_), channel_id=1, source_target_pairs={{0,16},{24,8},{1,17},{25,9},{2,18},{26,10},{3,19},{27,11},{4,20},{... | collective-permute-start | bytes 786440 | tf_op jit(solution)/shard_map/extra_z/ppermute | solution.py:338
  53.9 3.9 %collective-permute-start.15 = (bf16[2,256,512]{2,1,0:T(8,128)(2,1)S(1)}, bf16[2,256,512]{2,1,0:T(8,128)(2,1)S(1)}, u32[]{:S(2)}, u32[]{:S(2)}) collective-permute-start(bf16[2,256,512]{2,1,0:T(8,128)(2,1)S(1)} %collective-permute-done.11.refs_3_.refs_8_), channel_id=1, source_target_pairs={{0,2},{1,5},{8,10},{9,13},{16,18},{17,21},{24,26},{25,29}} | collective-permute-start | bytes 1572872 | tf_op jit(solution)/shard_map/fixed2/ppermute | solution.py:356
  59.4 5.8 %collective-permute-start.13 = (bf16[256,512]{1,0:T(8,128)(2,1)S(1)}, bf16[256,512]{1,0:T(8,128)(2,1)S(1)}, u32[]{:S(2)}, u32[]{:S(2)}) collective-permute-start(bf16[256,512]{1,0:T(8,128)(2,1)S(1)} %hand_on.1), channel_id=1, source_target_pairs={{0,8},{24,16},{16,24},{8,0},{1,9},{25,17},{17,25},{9,1},{2,10},{26... | collective-permute-start | bytes 786440 | tf_op jit(solution)/shard_map/extra_z/ppermute | solution.py:338
  65.2 1.7 %collective-permute-start.17 = (bf16[1,256,512]{2,1,0:T(8,128)(2,1)S(1)}, bf16[1,256,512]{2,1,0:T(8,128)(2,1)S(1)}, u32[]{:S(2)}, u32[]{:S(2)}) collective-permute-start(bf16[1,256,512]{2,1,0:T(8,128)(2,1)S(1)} %forward_free_third.1.refs_4_), channel_id=1, source_target_pairs={{0,4},{1,3},{2,6},{3,1},{4,0},{5,7},{6,2},{7,5},{8,12},{9,11},{10,... | collective-permute-start | bytes 786440 | tf_op jit(solution)/shard_map/free_third1/ppermute | solution.py:350
  66.9 1.3 %collective-permute-start.16 = (bf16[1,256,512]{2,1,0:T(8,128)(2,1)S(1)}, bf16[1,256,512]{2,1,0:T(8,128)(2,1)S(1)}, u32[]{:S(2)}, u32[]{:S(2)}) collective-permute-start(bf16[1,256,512]{2,1,0:T(8,128)(2,1)S(1)} %collective-permute-done.9.refs_3_.refs_7_), channel_id=1, source_target_pairs={{4,0},{3,1},{12,8},{11,9},{20,16},{19,17},{28,24},{27,25}} | collective-permute-start | bytes 786440 | tf_op jit(solution)/shard_map/fixed_third1/ppermute | solution.py:356
  68.2 3.4 %collective-permute-done.13.refs_4_ = bf16[256,512]{1,0:T(8,128)(2,1)S(1)} collective-permute-done((bf16[256,512]{1,0:T(8,128)(2,1)S(1)}, bf16[256,512]{1,0:T(8,128)(2,1)S(1)}, u32[]{:S(2)}, u32[]{:S(2)}) %collective-permute-start.13) | collective-permute-done | bytes 262176 | tf_op jit(solution)/shard_map/extra_z/ppermute | solution.py:338
  71.6 3.5 %collective-permute-done.16.refs_7_.refs_8_ = bf16[1,256,512]{2,1,0:T(8,128)(2,1)S(1)} collective-permute-done((bf16[1,256,512]{2,1,0:T(8,128)(2,1)S(1)}, bf16[1,256,512]{2,1,0:T(8,128)(2,1)S(1)}, u32[]{:S(2)}, u32[]{:S(2)}) %collective-permute-start.16) | collective-permute-done | bytes 262176 | tf_op jit(solution)/shard_map/fixed_third1/ppermute | solution.py:356
  76.2 1.3 %collective-permute-start.19 = (bf16[256,512]{1,0:T(8,128)(2,1)S(1)}, bf16[256,512]{1,0:T(8,128)(2,1)S(1)}, u32[]{:S(2)}, u32[]{:S(2)}) collective-permute-start(bf16[256,512]{1,0:T(8,128)(2,1)S(1)} %collective-permute-done.7.refs_2_.refs_5_), channel_id=1, source_target_pairs={{16,24},{8,0},{17,25},{9,1},{18,26},{10,2},{19,27},{11,3},{20,28},... | collective-permute-start | bytes 786440 | tf_op jit(solution)/shard_map/row2/ppermute | solution.py:338
  77.5 1.3 %collective-permute-start.21 = (bf16[1,256,512]{2,1,0:T(8,128)(2,1)S(1)}, bf16[1,256,512]{2,1,0:T(8,128)(2,1)S(1)}, u32[]{:S(2)}, u32[]{:S(2)}) collective-permute-start(bf16[1,256,512]{2,1,0:T(8,128)(2,1)S(1)} %collective-permute-done.16.refs_7_.refs_8_), channel_id=1, source_target_pairs={{0,2},{1,5},{8,10},{9,13},{16,18},{17,21},{24,26},{25,29}} | collective-permute-start | bytes 786440 | tf_op jit(solution)/shard_map/fixed_third2/ppermute | solution.py:356
  78.8 8.0 %collective-permute-done.19.refs_11_.refs_7_ = bf16[256,512]{1,0:T(8,128)(2,1)S(1)} collective-permute-done((bf16[256,512]{1,0:T(8,128)(2,1)S(1)}, bf16[256,512]{1,0:T(8,128)(2,1)S(1)}, u32[]{:S(2)}, u32[]{:S(2)}) %collective-permute-start.19) | collective-permute-done | bytes 262176 | tf_op jit(solution)/shard_map/row2/ppermute | solution.py:338
  86.8 2.0 %multiply_stays.1.refs_9_.refs_2_ = bf16[2,2,256,512]{3,2,1,0:T(8,128)(2,1)S(1)} custom-call(s32[2,3]{1,0:T(2,128)S(1)} %copy-done.2, bf16[2,512,512]{2,1,0:T(8,128)(2,1)S(1)} %copy-done, bf16[2,256,512]{2,1,0:T(8,128)(2,1)S(1)} %settle_extra.1.refs_2_.refs_1_, bf16[2,256,512]{2,1,0:T(8,128)(2,1)S(1)} %collective-permute-done.18.refs_3_.refs_2_, ...), custom_call_target="tpu_custom_call" | custom-call | flops 805306368 | bytes 5242904 | tf_op jit(solution)/shard_map/multiply_stays/pallas_call | solution.py:319
  88.8 1.3 %collective-permute-start.20 = (bf16[256,512]{1,0:T(8,128)(2,1)S(1)}, bf16[256,512]{1,0:T(8,128)(2,1)S(1)}, u32[]{:S(2)}, u32[]{:S(2)}) collective-permute-start(bf16[256,512]{1,0:T(8,128)(2,1)S(1)} %collective-permute-done.14.refs_5_.refs_6_), channel_id=1, source_target_pairs={{16,24},{8,0},{17,25},{9,1},{18,26},{10,2},{19,27},{11,3},{20,28},... | collective-permute-start | bytes 786440 | tf_op jit(solution)/shard_map/row2/ppermute | solution.py:338
  90.1 9.3 %collective-permute-done.20.refs_8_ = bf16[256,512]{1,0:T(8,128)(2,1)S(1)} collective-permute-done((bf16[256,512]{1,0:T(8,128)(2,1)S(1)}, bf16[256,512]{1,0:T(8,128)(2,1)S(1)}, u32[]{:S(2)}, u32[]{:S(2)}) %collective-permute-start.20) | collective-permute-done | bytes 262176 | tf_op jit(solution)/shard_map/row2/ppermute | solution.py:338
  100.5 1.4 %multiply_third.1.refs_3_ = bf16[2,1,256,512]{3,2,1,0:T(8,128)(2,1)S(1)} custom-call(s32[2,3]{1,0:T(2,128)S(1)} %copy-done.2, bf16[2,512,512]{2,1,0:T(8,128)(2,1)S(1)} %copy-done, bf16[2,256,512]{2,1,0:T(8,128)(2,1)S(1)} %settle_extra.1.refs_2_.refs_1_, bf16[2,256,512]{2,1,0:T(8,128)(2,1)S(1)} %collective-permute-done.18.refs_3_.refs_2_, ...), custom_call_target="tpu_custom_call" | custom-call | flops 402653184 | bytes 3670040 | tf_op jit(solution)/shard_map/multiply_third/pallas_call | solution.py:319
  102.0 3.4 %update_stays.1.refs_7_ = bf16[3,512,512]{2,1,0:T(8,128)(2,1)} custom-call(s32[2,3]{1,0:T(2,128)S(1)} %copy-done.2, bf16[2,512,512]{2,1,0:T(8,128)(2,1)S(1)} %get-tuple-element.25.refs_10_.refs_1_, bf16[2,2,256,512]{3,2,1,0:T(8,128)(2,1)S(1)} %multiply_stays.1.refs_9_.refs_2_, bf16[2,2,256,512]{3,2,1,0:T(8,128)(2,1)S(1)} %collective-permute-done.23.refs_3_, ...), custom_call_target="tpu_custom_call" | custom-call | flops 1073741824 | bytes 4718616 | tf_op jit(solution)/shard_map/update_stays/pallas_call | solution.py:319
  105.4 2.4 %update_third.1 = bf16[3,512,512]{2,1,0:T(8,128)(2,1)} custom-call(s32[2,3]{1,0:T(2,128)S(1)} %copy-done.2, bf16[2,512,512]{2,1,0:T(8,128)(2,1)S(1)} %get-tuple-element.25.refs_10_.refs_1_, bf16[512,512]{1,0:T(8,128)(2,1)S(1)} %get-tuple-element.26.refs_2_, bf16[2,1,256,512]{3,2,1,0:T(8,128)(2,1)S(1)} %multiply_third.1.refs_3_, ...), custom_call_target="tpu_custom_call", output_to_operand_aliasing={{}: (7, {})} | custom-call | flops 536870912 | bytes 6291480 | tf_op jit(solution)/shard_map/update_third/pallas_call | solution.py:319
  (48 shorter events, 12.4 us)
Async XLA Ops:
  3.6 3.2 %collective-permute-start = (bf16[3,256,512]{2,1,0:T(8,128)(2,1)S(1)}, bf16[3,256,512]{2,1,0:T(8,128)(2,1)S(1)}, u32[]{:S(2)}, u32[]{:S(2)}) collective-permute-start(bf16[3,256,512]{2,1,0:T(8,128)(2,1)S(1)} %get-tuple-element.17), channel_id=1, source_target_pairs={{0,1},{1,0},{2,3},{3,2},{4,5},{5,4},{6,7},{7,6},{8,9},{9,8},{10,11... | collective-permute-start | bytes 2359304 | tf_op jit(solution)/shard_map/sib_early/ppermute | solution.py:342
  4.1 17.3 %collective-permute-start.4 = (bf16[512,512]{1,0:T(8,128)(2,1)S(1)}, bf16[512,512]{1,0:T(8,128)(2,1)S(1)}, u32[]{:S(2)}, u32[]{:S(2)}) collective-permute-start(bf16[512,512]{1,0:T(8,128)(2,1)S(1)} %get-tuple-element.20.refs_3_), channel_id=1, source_target_pairs={{0,8},{24,16},{16,0},{8,24},{1,9},{25,17},{17,1},{9,25},{2,10},{26... | collective-permute-start | bytes 1572872 | tf_op jit(solution)/shard_map/swap/ppermute | solution.py:338
  8.0 13.5 %collective-permute-start.5 = (bf16[2,256,512]{2,1,0:T(8,128)(2,1)S(1)}, bf16[2,256,512]{2,1,0:T(8,128)(2,1)S(1)}, u32[]{:S(2)}, u32[]{:S(2)}) collective-permute-start(bf16[2,256,512]{2,1,0:T(8,128)(2,1)S(1)} %get-tuple-element.18.refs_3_.refs_6_), channel_id=1, source_target_pairs={{6,4},{7,3},{14,12},{15,11},{22,20},{23,19},{30,28},{31,27}} | collective-permute-start | bytes 1572872 | tf_op jit(solution)/shard_map/fixed0/ppermute | solution.py:356
  8.7 12.8 %collective-permute-start.3 = (bf16[2,256,512]{2,1,0:T(8,128)(2,1)S(1)}, bf16[2,256,512]{2,1,0:T(8,128)(2,1)S(1)}, u32[]{:S(2)}, u32[]{:S(2)}) collective-permute-start(bf16[2,256,512]{2,1,0:T(8,128)(2,1)S(1)} %get-tuple-element.19.refs_1_), channel_id=1, source_target_pairs={{0,2},{1,5},{2,0},{3,7},{4,6},{5,1},{6,4},{7,3},{8,10},{9,13},{10,... | collective-permute-start | bytes 1572872 | tf_op jit(solution)/shard_map/free0/ppermute | solution.py:350
  10.9 10.0 %collective-permute-start.1 = (bf16[256,512]{1,0:T(8,128)(2,1)S(1)}, bf16[256,512]{1,0:T(8,128)(2,1)S(1)}, u32[]{:S(2)}, u32[]{:S(2)}) collective-permute-start(bf16[256,512]{1,0:T(8,128)(2,1)S(1)} %pick_extra.1.refs_3_.refs_1_), channel_id=1, source_target_pairs={{0,2},{1,5},{2,0},{3,7},{4,6},{5,1},{6,4},{7,3},{8,10},{9,13},{10,... | collective-permute-start | bytes 786440 | tf_op jit(solution)/shard_map/extra0/ppermute | solution.py:350
  22.2 25.2 %collective-permute-start.8 = (bf16[512,512]{1,0:T(8,128)(2,1)S(1)}, bf16[512,512]{1,0:T(8,128)(2,1)S(1)}, u32[]{:S(2)}, u32[]{:S(2)}) collective-permute-start(bf16[512,512]{1,0:T(8,128)(2,1)S(1)} %get-tuple-element.22.refs_3_.refs_4_.refs_6_), channel_id=1, source_target_pairs={{0,1},{1,0},{2,3},{3,2},{4,5},{5,4},{6,7},{7,6},{8,9},{9,8},{10,11... | collective-permute-start | bytes 1572872 | tf_op jit(solution)/shard_map/sib_moved/ppermute | solution.py:342
  22.2 31.0 %collective-permute-start.12 = (bf16[2,256,512]{2,1,0:T(8,128)(2,1)S(1)}, bf16[2,256,512]{2,1,0:T(8,128)(2,1)S(1)}, u32[]{:S(2)}, u32[]{:S(2)}) collective-permute-start(bf16[2,256,512]{2,1,0:T(8,128)(2,1)S(1)} %get-tuple-element.21.refs_3_.refs_4_), channel_id=1, source_target_pairs={{0,4},{1,3},{2,6},{3,1},{4,0},{5,7},{6,2},{7,5},{8,12},{9,11},{10,... | collective-permute-start | bytes 1572872 | tf_op jit(solution)/shard_map/free1/ppermute | solution.py:350
  31.1 22.8 %collective-permute-start.11 = (bf16[2,256,512]{2,1,0:T(8,128)(2,1)S(1)}, bf16[2,256,512]{2,1,0:T(8,128)(2,1)S(1)}, u32[]{:S(2)}, u32[]{:S(2)}) collective-permute-start(bf16[2,256,512]{2,1,0:T(8,128)(2,1)S(1)} %collective-permute-done.5.refs_5_.refs_7_), channel_id=1, source_target_pairs={{4,0},{3,1},{12,8},{11,9},{20,16},{19,17},{28,24},{27,25}} | collective-permute-start | bytes 1572872 | tf_op jit(solution)/shard_map/fixed1/ppermute | solution.py:356
  32.4 14.3 %collective-permute-start.2 = (bf16[256,512]{1,0:T(8,128)(2,1)S(1)}, bf16[256,512]{1,0:T(8,128)(2,1)S(1)}, u32[]{:S(2)}, u32[]{:S(2)}) collective-permute-start(bf16[256,512]{1,0:T(8,128)(2,1)S(1)} %forward_extra.1.refs_4_.refs_1_), channel_id=1, source_target_pairs={{0,4},{1,3},{2,6},{3,1},{4,0},{5,7},{6,2},{7,5},{8,12},{9,11},{10,... | collective-permute-start | bytes 786440 | tf_op jit(solution)/shard_map/extra1/ppermute | solution.py:350
  48.0 9.9 %collective-permute-start.10 = (bf16[1,256,512]{2,1,0:T(8,128)(2,1)S(1)}, bf16[1,256,512]{2,1,0:T(8,128)(2,1)S(1)}, u32[]{:S(2)}, u32[]{:S(2)}) collective-permute-start(bf16[1,256,512]{2,1,0:T(8,128)(2,1)S(1)} %get-tuple-element.24.refs_1_), channel_id=1, source_target_pairs={{0,2},{1,5},{2,0},{3,7},{4,6},{5,1},{6,4},{7,3},{8,10},{9,13},{10,... | collective-permute-start | bytes 786440 | tf_op jit(solution)/shard_map/free_third0/ppermute | solution.py:350
  48.0 11.3 %collective-permute-start.6 = (bf16[256,512]{1,0:T(8,128)(2,1)S(1)}, bf16[256,512]{1,0:T(8,128)(2,1)S(1)}, u32[]{:S(2)}, u32[]{:S(2)}) collective-permute-start(bf16[256,512]{1,0:T(8,128)(2,1)S(1)} %extra_here.1.refs_5_.refs_0_.refs_2_), channel_id=1, source_target_pairs={{0,16},{24,8},{1,17},{25,9},{2,18},{26,10},{3,19},{27,11},{4,20},{... | collective-permute-start | bytes 786440 | tf_op jit(solution)/shard_map/extra_z/ppermute | solution.py:338
  52.6 6.8 %collective-permute-start.7 = (bf16[256,512]{1,0:T(8,128)(2,1)S(1)}, bf16[256,512]{1,0:T(8,128)(2,1)S(1)}, u32[]{:S(2)}, u32[]{:S(2)}) collective-permute-start(bf16[256,512]{1,0:T(8,128)(2,1)S(1)} %get-tuple-element.28), channel_id=1, source_target_pairs={{8,16},{16,8},{9,17},{17,9},{10,18},{18,10},{11,19},{19,11},{12,20... | collective-permute-start | bytes 786440 | tf_op jit(solution)/shard_map/row1/ppermute | solution.py:338
  53.2 6.1 %collective-permute-start.9 = (bf16[1,256,512]{2,1,0:T(8,128)(2,1)S(1)}, bf16[1,256,512]{2,1,0:T(8,128)(2,1)S(1)}, u32[]{:S(2)}, u32[]{:S(2)}) collective-permute-start(bf16[1,256,512]{2,1,0:T(8,128)(2,1)S(1)} %get-tuple-element.23.refs_6_), channel_id=1, source_target_pairs={{6,4},{7,3},{14,12},{15,11},{22,20},{23,19},{30,28},{31,27}} | collective-permute-start | bytes 786440 | tf_op jit(solution)/shard_map/fixed_third0/ppermute | solution.py:356
  53.9 21.2 %collective-permute-start.15 = (bf16[2,256,512]{2,1,0:T(8,128)(2,1)S(1)}, bf16[2,256,512]{2,1,0:T(8,128)(2,1)S(1)}, u32[]{:S(2)}, u32[]{:S(2)}) collective-permute-start(bf16[2,256,512]{2,1,0:T(8,128)(2,1)S(1)} %collective-permute-done.11.refs_3_.refs_8_), channel_id=1, source_target_pairs={{0,2},{1,5},{8,10},{9,13},{16,18},{17,21},{24,26},{25,29}} | collective-permute-start | bytes 1572872 | tf_op jit(solution)/shard_map/fixed2/ppermute | solution.py:356
  57.9 10.2 %collective-permute-start.14 = (bf16[256,512]{1,0:T(8,128)(2,1)S(1)}, bf16[256,512]{1,0:T(8,128)(2,1)S(1)}, u32[]{:S(2)}, u32[]{:S(2)}) collective-permute-start(bf16[256,512]{1,0:T(8,128)(2,1)S(1)} %get-tuple-element.27), channel_id=1, source_target_pairs={{8,16},{16,8},{9,17},{17,9},{10,18},{18,10},{11,19},{19,11},{12,20... | collective-permute-start | bytes 786440 | tf_op jit(solution)/shard_map/row1/ppermute | solution.py:338
  59.4 12.2 %collective-permute-start.13 = (bf16[256,512]{1,0:T(8,128)(2,1)S(1)}, bf16[256,512]{1,0:T(8,128)(2,1)S(1)}, u32[]{:S(2)}, u32[]{:S(2)}) collective-permute-start(bf16[256,512]{1,0:T(8,128)(2,1)S(1)} %hand_on.1), channel_id=1, source_target_pairs={{0,8},{24,16},{16,24},{8,0},{1,9},{25,17},{17,25},{9,1},{2,10},{26... | collective-permute-start | bytes 786440 | tf_op jit(solution)/shard_map/extra_z/ppermute | solution.py:338
  65.2 6.4 %collective-permute-start.17 = (bf16[1,256,512]{2,1,0:T(8,128)(2,1)S(1)}, bf16[1,256,512]{2,1,0:T(8,128)(2,1)S(1)}, u32[]{:S(2)}, u32[]{:S(2)}) collective-permute-start(bf16[1,256,512]{2,1,0:T(8,128)(2,1)S(1)} %forward_free_third.1.refs_4_), channel_id=1, source_target_pairs={{0,4},{1,3},{2,6},{3,1},{4,0},{5,7},{6,2},{7,5},{8,12},{9,11},{10,... | collective-permute-start | bytes 786440 | tf_op jit(solution)/shard_map/free_third1/ppermute | solution.py:350
  66.9 8.3 %collective-permute-start.16 = (bf16[1,256,512]{2,1,0:T(8,128)(2,1)S(1)}, bf16[1,256,512]{2,1,0:T(8,128)(2,1)S(1)}, u32[]{:S(2)}, u32[]{:S(2)}) collective-permute-start(bf16[1,256,512]{2,1,0:T(8,128)(2,1)S(1)} %collective-permute-done.9.refs_3_.refs_7_), channel_id=1, source_target_pairs={{4,0},{3,1},{12,8},{11,9},{20,16},{19,17},{28,24},{27,25}} | collective-permute-start | bytes 786440 | tf_op jit(solution)/shard_map/fixed_third1/ppermute | solution.py:356
  76.1 10.7 %collective-permute-start.18 = (bf16[2,256,512]{2,1,0:T(8,128)(2,1)S(1)}, bf16[2,256,512]{2,1,0:T(8,128)(2,1)S(1)}, u32[]{:S(2)}, u32[]{:S(2)}) collective-permute-start(bf16[2,256,512]{2,1,0:T(8,128)(2,1)S(1)} %settle_extra.1.refs_2_.refs_1_), channel_id=1, source_target_pairs={{0,1},{1,0},{2,3},{3,2},{4,5},{5,4},{6,7},{7,6},{8,9},{9,8},{10,11... | collective-permute-start | bytes 1572872 | tf_op jit(solution)/shard_map/sib_vl/ppermute | solution.py:342
  76.2 10.6 %collective-permute-start.19 = (bf16[256,512]{1,0:T(8,128)(2,1)S(1)}, bf16[256,512]{1,0:T(8,128)(2,1)S(1)}, u32[]{:S(2)}, u32[]{:S(2)}) collective-permute-start(bf16[256,512]{1,0:T(8,128)(2,1)S(1)} %collective-permute-done.7.refs_2_.refs_5_), channel_id=1, source_target_pairs={{16,24},{8,0},{17,25},{9,1},{18,26},{10,2},{19,27},{11,3},{20,28},... | collective-permute-start | bytes 786440 | tf_op jit(solution)/shard_map/row2/ppermute | solution.py:338
  77.5 9.3 %collective-permute-start.21 = (bf16[1,256,512]{2,1,0:T(8,128)(2,1)S(1)}, bf16[1,256,512]{2,1,0:T(8,128)(2,1)S(1)}, u32[]{:S(2)}, u32[]{:S(2)}) collective-permute-start(bf16[1,256,512]{2,1,0:T(8,128)(2,1)S(1)} %collective-permute-done.16.refs_7_.refs_8_), channel_id=1, source_target_pairs={{0,2},{1,5},{8,10},{9,13},{16,18},{17,21},{24,26},{25,29}} | collective-permute-start | bytes 786440 | tf_op jit(solution)/shard_map/fixed_third2/ppermute | solution.py:356
  88.7 13.3 %collective-permute-start.23 = (bf16[2,2,256,512]{3,2,1,0:T(8,128)(2,1)S(1)}, bf16[2,2,256,512]{3,2,1,0:T(8,128)(2,1)S(1)}, u32[]{:S(2)}, u32[]{:S(2)}) collective-permute-start(bf16[2,2,256,512]{3,2,1,0:T(8,128)(2,1)S(1)} %multiply_stays.1.refs_9_.refs_2_), channel_id=1, source_target_pairs={{0,1},{1,0},{2,3},{3,2},{4,5},{5,4},{6,7},{7,6},{8,9},{9,8},{10,11... | collective-permute-start | bytes 3145736 | tf_op jit(solution)/shard_map/sib_mine/ppermute | solution.py:342
  88.8 10.6 %collective-permute-start.20 = (bf16[256,512]{1,0:T(8,128)(2,1)S(1)}, bf16[256,512]{1,0:T(8,128)(2,1)S(1)}, u32[]{:S(2)}, u32[]{:S(2)}) collective-permute-start(bf16[256,512]{1,0:T(8,128)(2,1)S(1)} %collective-permute-done.14.refs_5_.refs_6_), channel_id=1, source_target_pairs={{16,24},{8,0},{17,25},{9,1},{18,26},{10,2},{19,27},{11,3},{20,28},... | collective-permute-start | bytes 786440 | tf_op jit(solution)/shard_map/row2/ppermute | solution.py:338
  101.9 3.5 %collective-permute-start.22 = (bf16[2,1,256,512]{3,2,1,0:T(8,128)(2,1)S(1)}, bf16[2,1,256,512]{3,2,1,0:T(8,128)(2,1)S(1)}, u32[]{:S(2)}, u32[]{:S(2)}) collective-permute-start(bf16[2,1,256,512]{3,2,1,0:T(8,128)(2,1)S(1)} %multiply_third.1.refs_3_), channel_id=1, source_target_pairs={{0,1},{1,0},{2,3},{3,2},{4,5},{5,4},{6,7},{7,6},{8,9},{9,8},{10,11... | collective-permute-start | bytes 1572872 | tf_op jit(solution)/shard_map/sib_third/ppermute | solution.py:342
  (4 other events, 20.0 us)

commit v5 on v3

--- a/solution.py
+++ b/solution.py
@@ -32,8 +32,6 @@
     for k in range(rb):
         slot = out + (1 + k)
         f["slots"].append(jnp.where(slot >= rb, slot - rb, slot))
-    f["fixed_step"] = jnp.where(pivots[0, 2] == m - 1, 0, 1)
-    f["free"] = pivots[0, 2] + pivots[1, 2] - (m - 1)
     f["cx"] = jnp.where((r == 0) == low_first, pivots[1, 2], pivots[0, 2])
     return f
 
@@ -74,30 +72,41 @@
     either(hit, extra, lambda: raw[rb - 1, cut, :], lambda: sib[rb - 1])
 
 
-def pick(n, m, piv, raw, sib, fixed, free):
+def pair(refs):
+    return [refs[0].at[q] for q in range(2)] if len(refs) == 1 else list(refs)
+
+
+def pick(n, m, piv, raw, sib, *panel):
     rb, width = raw.shape[0], raw.shape[1]
     f = facts(n, m, rb, piv)
     cut = rows(f["core"], width // 2)
-    for panel, column in ((fixed, m - 1), (free, f["free"])):
-        hit = (column & 1) == f["core"]
+    for q in range(2):
+        hit = (f["c"][q] & 1) == f["core"]
         for k in range(rb - 1):
-            either(hit, panel.at[k], lambda: raw[k, cut, :], lambda: sib[k])
-
-
-def pick_third(n, m, piv, raw, sib, moved, sib_moved, fixed, free):
+            either(hit, pair(panel)[q].at[k], lambda: raw[k, cut, :], lambda: sib[k])
+
+
+def pick_third(n, m, piv, raw, sib, moved, sib_moved, panel):
     rb, width = raw.shape[0], raw.shape[1]
     f = facts(n, m, rb, piv)
     cut = rows(f["core"], width // 2)
-    for panel, column in ((fixed, m - 1), (free, f["free"])):
-        hit = (column & 1) == f["core"]
+    for q in range(2):
+        hit = (f["c"][q] & 1) == f["core"]
 
         @pl.when(f["is_end"])
         def _():
-            either(hit, panel.at[0], lambda: moved[cut, :], lambda: sib_moved[cut, :])
+            either(hit, panel.at[q, 0], lambda: moved[cut, :], lambda: sib_moved[cut, :])
 
         @pl.when(jnp.logical_not(f["is_end"]))
         def _():
-            either(hit, panel.at[0], lambda: raw[rb - 1, cut, :], lambda: sib[rb - 1])
+            either(hit, panel.at[q, 0], lambda: raw[rb - 1, cut, :], lambda: sib[rb - 1])
+
+
+def relay(n, m, moved, out, *halves):
+    out[...] = moved[...]
+    half = moved.shape[0] // 2
+    for p, ref in enumerate(halves):
+        ref[...] = moved[p * half : (p + 1) * half, :]
 
 
 def bit_of(f, column, stage, stages):
@@ -106,33 +115,19 @@
     return ((apart >> bit) & 1) == 1
 
 
-def forward(n, m, key, stage, stages, piv, had, got, out):
+def forward_extra(n, m, stage, stages, piv, had, got, out):
     f = facts(n, m, 2, piv)
-    take = bit_of(f, f[key], stage, stages)
+    take = bit_of(f, f["cx"], stage, stages)
     either(take, out, lambda: got[...], lambda: had[...])
 
 
-def ring_order(chips):
-    side = round(chips**0.5)
-    if side * side != chips or side % 2:
-        return list(range(chips))
-    walk = []
-    for i in range(side):
-        across = list(range(1, side))
-        walk += [i * side + k for k in (across if i % 2 == 0 else across[::-1])]
-    return walk + [i * side for i in range(side - 1, -1, -1)]
-
-
-def ring_hops(chips):
-    order = ring_order(chips)
-    start = order.index(chips - 1)
-    one = [order[(start + k) % chips] for k in range(chips)]
-    two = [order[(start - k) % chips] for k in range(chips)]
-    hops = [
-        [(2 * one[h], 2 * one[h + 1]), (2 * two[h] + 1, 2 * two[h + 1] + 1)]
-        for h in range(chips - 1)
-    ]
-    return one, two, hops
+def forward(n, m, stage, stages, piv, *refs):
+    f = facts(n, m, 2, piv)
+    count = len(refs) // 3
+    had, got, out = (pair(refs[i * count : (i + 1) * count]) for i in range(3))
+    for q in range(2):
+        take = bit_of(f, f["c"][q], stage, stages)
+        either(take, out[q], lambda: got[q][...], lambda: had[q][...])
 
 
 def hand_on(n, m, stride, had, got, extra):
@@ -171,27 +166,18 @@
     out[1] = dot(out[1], inv[0]).astype(out.dtype)
 
 
-def multiply(n, m, stages, piv, inv, vl, sib_vl, free, free_got, *refs):
-    fixed, out, v = refs[:-2], refs[-2], refs[-1]
+def multiply(n, m, stages, piv, inv, vl, sib_vl, *refs):
+    panels, out, v = refs[:-2], refs[-2], refs[-1]
     f = facts(n, m, 2, piv)
     half = vl.shape[1]
     v[rows(f["core"], half), :] = vl[0]
     v[rows(1 - f["core"], half), :] = sib_vl[0]
-    chips = m // 2
-    one, two, _ = ring_hops(chips)
-    hop = jnp.int32(0)
-    for chip in range(chips):
-        here = jnp.where(f["core"] == 0, one.index(chip), two.index(chip))
-        hop = jnp.where(f["chip"] == chip, here, hop)
-    for h in range(chips):
-
-        @pl.when(hop == h)
-        def _():
-            out[f["fixed_step"]] = fixed[h][...]
-
-    take = bit_of(f, f["free"], stages - 1, stages)
-    either(take, out.at[1 - f["fixed_step"]], lambda: free_got[...], lambda: free[...])
-    for k in range(free.shape[0]):
+    count = len(panels) // 2
+    for q in range(2):
+        take = bit_of(f, f["c"][q], stages - 1, stages)
+        had, got = pair(panels[:count])[q], pair(panels[count:])[q]
+        either(take, out.at[q], lambda: got[...], lambda: had[...])
+    for k in range(out.shape[1]):
         m0 = dot(out[0, k], inv[0]).astype(out.dtype)
         p1 = (out[1, k].astype(jnp.float32) - dot(m0, v[...])).astype(out.dtype)
         out[0, k] = m0
@@ -301,7 +287,7 @@
     dt = matrix.dtype
     blocks = matrix.reshape(rb, width, width)
 
-    def call(kernel, shapes, specs, *operands, scratch=(), aliases=(), products=0, place=VMEM, after=(), name=None):
+    def call(kernel, shapes, specs, *operands, scratch=(), aliases=(), products=0, place=VMEM, after=(), name=None, weight=0):
         outs = [jax.ShapeDtypeStruct(s, dt) for s in shapes]
         count = len(operands)
         scratch = [pltpu.VMEM(s, dt) if isinstance(s, tuple) else s for s in scratch]
@@ -322,7 +308,7 @@
             name=name or kernel.__name__,
             cost_estimate=pl.CostEstimate(
                 flops=int(products * 2 * width**3),
-                bytes_accessed=sum(a.size * a.dtype.itemsize for a in operands),
+                bytes_accessed=weight + sum(a.size * a.dtype.itemsize for a in operands),
                 transcendentals=0,
             ),
         )(*operands, *after)
@@ -344,21 +330,19 @@
         with jax.named_scope(name):
             return lax.ppermute(value, "pcol", pairs)
 
-    def ring(name, value):
-        came = [value]
-        for h, pairs in enumerate(ring_hops(chips)[2]):
-            with jax.named_scope(name + str(h)):
-                came.append(lax.ppermute(came[-1], "pcol", pairs))
-        return came
-
-    def passing(name, key, value, after=()):
-        for s in range(stages):
-            got = across(name + str(s), s, value)
-            if s < stages - 1:
-                kernel = functools.partial(forward, n, m, key, s, stages)
-                step = lambda _n, _m, *refs: kernel(*refs)
-                value = call(step, [value.shape], "s", pivots, value, got, after=after, name="forward_" + name)
-        return value, got
+    def cross(name, s, values):
+        return [across(name + str(s) + "ab"[i], s, v) for i, v in enumerate(values)]
+
+    def passing(name, kernel, values, got, after=()):
+        for s in range(stages - 1):
+            step = lambda _n, _m, *refs: kernel(n, m, s, stages, *refs)
+            shapes = [v.shape for v in values]
+            values = call(
+                step, shapes, "s", pivots, *values, *got, after=after, name="pass_" + name
+            )
+            values = [values] if len(shapes) == 1 else list(values)
+            got = cross(name, s + 1, values)
+        return [*values, *got]
 
     square, strip = (width, width), (half, width)
     raw, leaving, other = call(
@@ -373,26 +357,28 @@
     early = sibling("sib_early", other)
 
     extra = call(pick_extra, [strip], "s", pivots, raw, early)
-    had, got = passing("extra", "cx", extra)
-    step = lambda _n, _m, *refs: forward(n, m, "cx", stages - 1, stages, *refs)
-    extra_here = call(step, [strip], "s", pivots, had, got, after=[moved], name="extra_here")
-    fixed, free = call(
-        pick, [(rb - 1, *strip)] * 2, "s", pivots, raw, early, after=[extra]
-    )
-    free_stays = passing("free", "free", free)
-    fixed_stays = ring("fixed", fixed)
+    panel = call(pick, [(rb - 1, *strip)] * 2, "s", pivots, raw, early, after=[extra])
+    got_extra = cross("extra", 0, [extra])
+    got_stays = cross("stays", 0, panel)
+    had, got = passing("extra", forward_extra, [extra], got_extra, after=[panel[0]])
+    step = lambda _n, _m, *refs: forward_extra(n, m, stages - 1, stages, *refs)
+    extra_here = call(
+        step, [strip], "s", pivots, had, got, after=[got_stays[0]], name="extra_here"
+    )
+    moved, *parts = call(relay, [square, strip, strip], "", moved, after=[extra_here])
+
+    sib_moved = sibling("sib_moved", moved)
+    third = call(
+        pick_third, [(2, 1, *strip)], "s", pivots, raw, early, moved, sib_moved
+    )
+    got_third = cross("third", 0, [third])
+    stays = passing("stays", forward, panel, got_stays, after=[third])
 
     hops = []
-    parts = [moved[:half], moved[half:]]
     for h in range(1, n - 1):
         pairs = [(h, h + 1), (n - 1 - h, n - 2 - h)]
-        parts = [along("row" + str(h), pairs, part) for part in parts]
+        parts = [along("row" + str(h) + "ab"[i], pairs, part) for i, part in enumerate(parts)]
         hops += parts
-
-    sib_moved = sibling("sib_moved", moved)
-    fixed, free = call(
-        pick_third, [(1, *strip)] * 2, "s", pivots, raw, early, moved, sib_moved
-    )
 
     came = [extra_here]
     send = extra_here
@@ -401,17 +387,32 @@
         pairs = []
         for i in range(0, n, 2 * stride):
             pairs += [(i, i + stride), (n - 1 - i, n - 1 - i - stride)]
-        got = along("extra_z", pairs, send)
+        got = along("extra_z" + str(stride), pairs, send)
         came.append(got)
         if stride > 1:
             step = lambda _n, _m, *refs: hand_on(n, m, stride, *refs)
-            send = call(step, [strip], "", send, got, name="hand_on", after=[free])
+            send = call(
+                step,
+                [strip],
+                "",
+                send,
+                got,
+                name="hand_on",
+                after=[stays[0]],
+            )
         stride //= 2
-    vl = call(settle_extra, [(2, *strip)], "s", pivots, inverses, *came, products=0.5, after=hops[:2])
+    third = passing("third", forward, [third], got_third, after=[send, hops[0]])
+    vl = call(
+        settle_extra,
+        [(2, *strip)],
+        "s",
+        pivots,
+        inverses,
+        *came,
+        products=0.5,
+        after=[third[0], hops[1]],
+    )
     sib_vl = sibling("sib_vl", vl)
-
-    free_third = passing("free_third", "free", free)
-    fixed_third = ring("fixed_third", fixed)
 
     step = lambda _n, _m, *refs: multiply(n, m, stages, *refs)
     mine = call(
@@ -422,11 +423,11 @@
         inverses,
         vl,
         sib_vl,
-        *free_stays,
-        *fixed_stays,
+        *stays,
         scratch=[square],
         products=3 * (rb - 1) / 2,
         name="multiply_stays",
+        after=[hops[2], third[1]],
     )
     sib_mine = sibling("sib_mine", mine)
     upper, lefts = call(
@@ -440,6 +441,7 @@
         moved,
         *hops,
         products=1,
+        after=[mine],
     )
     mine_third = call(
         step,
@@ -449,8 +451,7 @@
         inverses,
         vl,
         sib_vl,
-        *free_third,
-        *fixed_third,
+        *third,
         scratch=[square],
         products=1.5,
         after=[upper],

time: 90.9 us -> 83.4 us (0.917)
  starting transfers between devices: 35.7 us -> 23.8 us
  waiting for transfers between devices: 35.5 us -> 40 us
    ppermute x6 -> x0, starting transfers between devices: 9.09 us -> none  [ring(): came.append(lax.ppermute(came[-1], 'pcol', pairs))]
    ppermute x7, waiting for transfers between devices: 22.7 us -> 30.5 us  [along(): return lax.ppermute(value, 'prow', pairs)]
    ppermute x6 -> x0, waiting for transfers between devices: 6.07 us -> none  [ring(): came.append(lax.ppermute(came[-1], 'pcol', pairs))]
    ppermute x5, waiting for transfers between devices: 0.01 us -> 2.2 us  [sibling(): return lax.ppermute(value, 'pcol', [(i, i ^ 1) for i in range(m)])]
    ppermute x6 -> x8, starting transfers between devices: 11.9 us -> 10.4 us  [across(): return lax.ppermute(value, 'pcol', pairs)]
    ppermute x6 -> x8, waiting for transfers between devices: 6.76 us -> 7.3 us  [across(): return lax.ppermute(value, 'pcol', pairs)]
    pallas_call x15 -> x16, Pallas kernels: 16.2 us -> 16.3 us  [call(): pl.pallas_call(body, out_shape=outs, in_specs=specs, out_specs=[place] *...]
  transfers between devices with their start and end apart: 24 -> 20, of which waited for: 10 -> 11; matrix products, arithmetic and copies ran while one was open for 0% -> 0% of each run, Pallas kernels for 14% -> 13%
where the time goes in v5:
time: 83.4 us; the launch traced here: 83.1 us
  waiting for transfers between devices  40 us (48%)
  starting transfers between devices  23.8 us (29%)
  Pallas kernels  16.3 us (20%)
  local copies, waits for them, and re-layouts  2.78 us (3%)
    ppermute x7, waiting for transfers between devices, along(): return lax.ppermute(value, 'prow', pairs)  30.5 us
    pallas_call x16, Pallas kernels, call(): pl.pallas_call(body, out_shape=outs, in_specs=specs, out_specs=[place] *...  16.3 us
    ppermute x7, starting transfers between devices, along(): return lax.ppermute(value, 'prow', pairs)  12.3 us
    ppermute x8, starting transfers between devices, across(): return lax.ppermute(value, 'pcol', pairs)  10.4 us
    ppermute x8, waiting for transfers between devices, across(): return lax.ppermute(value, 'pcol', pairs)  7.3 us
    unnamed x8, local copies, waits for them, and re-layouts  2.78 us
    ppermute x5, waiting for transfers between devices, sibling(): return lax.ppermute(value, 'pcol', [(i, i ^ 1) for i in range(m)])  2.2 us
  transfers between devices with their start and end apart: 20, of which 11 were waited for; matrix products, arithmetic and copies ran while one was open for 0% of the time, Pallas kernels for 13%

profile of v5, /device:TPU:0, one launch (start us, length us, event | category | flops | bytes accessed | tf_op | source)
XLA Modules:
  0.0 83.1 jit_solution(13095168156742892732)
XLA Ops:
  0.0 1.4 %copy-done.1 = bf16[3,512,1,512]{3,1,2,0:T(8,128)(2,1)S(1)} copy-done((bf16[3,512,1,512]{3,1,2,0:T(8,128)(2,1)S(1)}, bf16[3,512,1,512]{3,1,2,0:T(8,128)(2,1)}, u32[]{:S(2)}) %copy-start.1) | copy-done | bytes 1572888
  4.1 1.9 %collective-permute-done.refs_2_ = bf16[3,256,512]{2,1,0:T(8,128)(2,1)S(1)} collective-permute-done((bf16[3,256,512]{2,1,0:T(8,128)(2,1)S(1)}, bf16[3,256,512]{2,1,0:T(8,128)(2,1)S(1)}, u32[]{:S(2)}, u32[]{:S(2)}) %collective-permute-start) | collective-permute-done | bytes 786464 | tf_op jit(solution)/shard_map/sib_early/ppermute | solution.py:323
  6.6 2.9 %collective-permute-start.1 = (bf16[256,512]{1,0:T(8,128)(2,1)S(1)}, bf16[256,512]{1,0:T(8,128)(2,1)S(1)}, u32[]{:S(2)}, u32[]{:S(2)}) collective-permute-start(bf16[256,512]{1,0:T(8,128)(2,1)S(1)} %pick_extra.1.refs_3_.refs_1_), channel_id=1, source_target_pairs={{0,2},{1,5},{2,0},{3,7},{4,6},{5,1},{6,4},{7,3},{8,10},{9,13},{10,... | collective-permute-start | bytes 786440 | tf_op jit(solution)/shard_map/extra0a/ppermute | solution.py:331
  10.3 2.1 %collective-permute-start.6 = (bf16[512,512]{1,0:T(8,128)(2,1)S(1)}, bf16[512,512]{1,0:T(8,128)(2,1)S(1)}, u32[]{:S(2)}, u32[]{:S(2)}) collective-permute-start(bf16[512,512]{1,0:T(8,128)(2,1)S(1)} %get-tuple-element.21.refs_3_), channel_id=1, source_target_pairs={{0,8},{24,16},{16,0},{8,24},{1,9},{25,17},{17,1},{9,25},{2,10},{26... | collective-permute-start | bytes 1572872 | tf_op jit(solution)/shard_map/swap/ppermute | solution.py:319
  12.4 1.5 %collective-permute-done.1.refs_2_ = bf16[256,512]{1,0:T(8,128)(2,1)S(1)} collective-permute-done((bf16[256,512]{1,0:T(8,128)(2,1)S(1)}, bf16[256,512]{1,0:T(8,128)(2,1)S(1)}, u32[]{:S(2)}, u32[]{:S(2)}) %collective-permute-start.1) | collective-permute-done | bytes 262176 | tf_op jit(solution)/shard_map/extra0a/ppermute | solution.py:331
  14.5 2.1 %collective-permute-start.2 = (bf16[256,512]{1,0:T(8,128)(2,1)S(1)}, bf16[256,512]{1,0:T(8,128)(2,1)S(1)}, u32[]{:S(2)}, u32[]{:S(2)}) collective-permute-start(bf16[256,512]{1,0:T(8,128)(2,1)S(1)} %pass_extra.1.refs_1_), channel_id=1, source_target_pairs={{0,4},{1,3},{2,6},{3,1},{4,0},{5,7},{6,2},{7,5},{8,12},{9,11},{10,... | collective-permute-start | bytes 786440 | tf_op jit(solution)/shard_map/extra1a/ppermute | solution.py:331
  16.6 5.2 %collective-permute-done.2.refs_2_ = bf16[256,512]{1,0:T(8,128)(2,1)S(1)} collective-permute-done((bf16[256,512]{1,0:T(8,128)(2,1)S(1)}, bf16[256,512]{1,0:T(8,128)(2,1)S(1)}, u32[]{:S(2)}, u32[]{:S(2)}) %collective-permute-start.2) | collective-permute-done | bytes 262176 | tf_op jit(solution)/shard_map/extra1a/ppermute | solution.py:331
  22.8 2.2 %collective-permute-done.6.refs_0_ = bf16[512,512]{1,0:T(8,128)(2,1)S(1)} collective-permute-done((bf16[512,512]{1,0:T(8,128)(2,1)S(1)}, bf16[512,512]{1,0:T(8,128)(2,1)S(1)}, u32[]{:S(2)}, u32[]{:S(2)}) %collective-permute-start.6) | collective-permute-done | bytes 524320 | tf_op jit(solution)/shard_map/swap/ppermute | solution.py:319
  25.2 1.6 %collective-permute-start.5 = (bf16[2,256,512]{2,1,0:T(8,128)(2,1)S(1)}, bf16[2,256,512]{2,1,0:T(8,128)(2,1)S(1)}, u32[]{:S(2)}, u32[]{:S(2)}) collective-permute-start(bf16[2,256,512]{2,1,0:T(8,128)(2,1)S(1)} %get-tuple-element.20.refs_2_), channel_id=1, source_target_pairs={{0,2},{1,5},{2,0},{3,7},{4,6},{5,1},{6,4},{7,3},{8,10},{9,13},{10,... | collective-permute-start | bytes 1572872 | tf_op jit(solution)/shard_map/stays0b/ppermute | solution.py:331
  27.7 1.6 %collective-permute-start.9 = (bf16[2,1,256,512]{3,2,1,0:T(8,128)(2,1)S(1)}, bf16[2,1,256,512]{3,2,1,0:T(8,128)(2,1)S(1)}, u32[]{:S(2)}, u32[]{:S(2)}) collective-permute-start(bf16[2,1,256,512]{3,2,1,0:T(8,128)(2,1)S(1)} %pick_third.1.refs_5_.refs_1_), channel_id=1, source_target_pairs={{0,2},{1,5},{2,0},{3,7},{4,6},{5,1},{6,4},{7,3},{8,10},{9,13},{10,... | collective-permute-start | bytes 1572872 | tf_op jit(solution)/shard_map/third0a/ppermute | solution.py:331
  29.4 3.6 %collective-permute-start.4 = (bf16[256,512]{1,0:T(8,128)(2,1)S(1)}, bf16[256,512]{1,0:T(8,128)(2,1)S(1)}, u32[]{:S(2)}, u32[]{:S(2)}) collective-permute-start(bf16[256,512]{1,0:T(8,128)(2,1)S(1)} %extra_here.1.refs_1_.refs_0_.refs_2_), channel_id=1, source_target_pairs={{0,16},{24,8},{1,17},{25,9},{2,18},{26,10},{3,19},{27,11},{4,20},{... | collective-permute-start | bytes 786440 | tf_op jit(solution)/shard_map/extra_z2/ppermute | solution.py:319
  35.1 3.5 %collective-permute-done.4.refs_1_.refs_3_ = bf16[256,512]{1,0:T(8,128)(2,1)S(1)} collective-permute-done((bf16[256,512]{1,0:T(8,128)(2,1)S(1)}, bf16[256,512]{1,0:T(8,128)(2,1)S(1)}, u32[]{:S(2)}, u32[]{:S(2)}) %collective-permute-start.4) | collective-permute-done | bytes 262176 | tf_op jit(solution)/shard_map/extra_z2/ppermute | solution.py:319
  38.6 2.7 %collective-permute-start.8 = (bf16[256,512]{1,0:T(8,128)(2,1)S(1)}, bf16[256,512]{1,0:T(8,128)(2,1)S(1)}, u32[]{:S(2)}, u32[]{:S(2)}) collective-permute-start(bf16[256,512]{1,0:T(8,128)(2,1)S(1)} %hand_on.1.refs_3_), channel_id=1, source_target_pairs={{0,8},{24,16},{16,24},{8,0},{1,9},{25,17},{17,25},{9,1},{2,10},{26... | collective-permute-start | bytes 786440 | tf_op jit(solution)/shard_map/extra_z1/ppermute | solution.py:319
  41.8 1.5 %collective-permute-start.16 = (bf16[2,256,512]{2,1,0:T(8,128)(2,1)S(1)}, bf16[2,256,512]{2,1,0:T(8,128)(2,1)S(1)}, u32[]{:S(2)}, u32[]{:S(2)}) collective-permute-start(bf16[2,256,512]{2,1,0:T(8,128)(2,1)S(1)} %get-tuple-element.26.refs_5_), channel_id=1, source_target_pairs={{0,4},{1,3},{2,6},{3,1},{4,0},{5,7},{6,2},{7,5},{8,12},{9,11},{10,... | collective-permute-start | bytes 1572872 | tf_op jit(solution)/shard_map/stays1b/ppermute | solution.py:331
  44.0 2.9 %collective-permute-done.8.refs_4_ = bf16[256,512]{1,0:T(8,128)(2,1)S(1)} collective-permute-done((bf16[256,512]{1,0:T(8,128)(2,1)S(1)}, bf16[256,512]{1,0:T(8,128)(2,1)S(1)}, u32[]{:S(2)}, u32[]{:S(2)}) %collective-permute-start.8) | collective-permute-done | bytes 262176 | tf_op jit(solution)/shard_map/extra_z1/ppermute | solution.py:319
  48.0 1.3 %collective-permute-start.13 = (bf16[256,512]{1,0:T(8,128)(2,1)S(1)}, bf16[256,512]{1,0:T(8,128)(2,1)S(1)}, u32[]{:S(2)}, u32[]{:S(2)}) collective-permute-start(bf16[256,512]{1,0:T(8,128)(2,1)S(1)} %collective-permute-done.10.refs_4_.refs_5_), channel_id=1, source_target_pairs={{16,24},{8,0},{17,25},{9,1},{18,26},{10,2},{19,27},{11,3},{20,28},... | collective-permute-start | bytes 786440 | tf_op jit(solution)/shard_map/row2a/ppermute | solution.py:319
  49.3 12.7 %collective-permute-done.13.refs_8_.refs_7_ = bf16[256,512]{1,0:T(8,128)(2,1)S(1)} collective-permute-done((bf16[256,512]{1,0:T(8,128)(2,1)S(1)}, bf16[256,512]{1,0:T(8,128)(2,1)S(1)}, u32[]{:S(2)}, u32[]{:S(2)}) %collective-permute-start.13) | collective-permute-done | bytes 262176 | tf_op jit(solution)/shard_map/row2a/ppermute | solution.py:319
  62.1 2.0 %multiply_stays.1.refs_9_.refs_2_ = bf16[2,2,256,512]{3,2,1,0:T(8,128)(2,1)S(1)} custom-call(s32[2,3]{1,0:T(2,128)S(1)} %copy-done.2, bf16[2,512,512]{2,1,0:T(8,128)(2,1)S(1)} %copy-done, bf16[2,256,512]{2,1,0:T(8,128)(2,1)S(1)} %settle_extra.1.refs_2_.refs_1_, bf16[2,256,512]{2,1,0:T(8,128)(2,1)S(1)} %collective-permute-done.12.refs_3_.refs_2_, ...), custom_call_target="tpu_custom_call" | custom-call | flops 805306368 | bytes 4194328 | tf_op jit(solution)/shard_map/multiply_stays/pallas_call | solution.py:300
  64.3 1.3 %collective-permute-start.14 = (bf16[256,512]{1,0:T(8,128)(2,1)S(1)}, bf16[256,512]{1,0:T(8,128)(2,1)S(1)}, u32[]{:S(2)}, u32[]{:S(2)}) collective-permute-start(bf16[256,512]{1,0:T(8,128)(2,1)S(1)} %collective-permute-done.11.refs_6_), channel_id=1, source_target_pairs={{16,24},{8,0},{17,25},{9,1},{18,26},{10,2},{19,27},{11,3},{20,28},... | collective-permute-start | bytes 786440 | tf_op jit(solution)/shard_map/row2b/ppermute | solution.py:319
  65.6 9.1 %collective-permute-done.14.refs_8_ = bf16[256,512]{1,0:T(8,128)(2,1)S(1)} collective-permute-done((bf16[256,512]{1,0:T(8,128)(2,1)S(1)}, bf16[256,512]{1,0:T(8,128)(2,1)S(1)}, u32[]{:S(2)}, u32[]{:S(2)}) %collective-permute-start.14) | collective-permute-done | bytes 262176 | tf_op jit(solution)/shard_map/row2b/ppermute | solution.py:319
  74.7 1.1 %settle_rows.1 = (bf16[2,512,512]{2,1,0:T(8,128)(2,1)S(1)}, bf16[512,512]{1,0:T(8,128)(2,1)S(1)}) custom-call(s32[2,3]{1,0:T(2,128)S(1)} %copy-done.2, bf16[2,256,512]{2,1,0:T(8,128)(2,1)S(1)} %settle_extra.1.refs_2_.refs_1_, bf16[2,256,512]{2,1,0:T(8,128)(2,1)S(1)} %collective-permute-done.12.refs_3_.refs_2_, ...), custom_call_target="tpu_custom_call" | custom-call | flops 268435456 | bytes 3145752 | tf_op jit(solution)/shard_map/settle_rows/pallas_call | solution.py:300
  75.8 1.4 %multiply_third.1.refs_3_ = bf16[2,1,256,512]{3,2,1,0:T(8,128)(2,1)S(1)} custom-call(s32[2,3]{1,0:T(2,128)S(1)} %copy-done.2, bf16[2,512,512]{2,1,0:T(8,128)(2,1)S(1)} %copy-done, bf16[2,256,512]{2,1,0:T(8,128)(2,1)S(1)} %settle_extra.1.refs_2_.refs_1_, bf16[2,256,512]{2,1,0:T(8,128)(2,1)S(1)} %collective-permute-done.12.refs_3_.refs_2_, ...), custom_call_target="tpu_custom_call" | custom-call | flops 402653184 | bytes 3145752 | tf_op jit(solution)/shard_map/multiply_third/pallas_call | solution.py:300
  77.3 3.4 %update_stays.1.refs_7_ = bf16[3,512,512]{2,1,0:T(8,128)(2,1)} custom-call(s32[2,3]{1,0:T(2,128)S(1)} %copy-done.2, bf16[2,512,512]{2,1,0:T(8,128)(2,1)S(1)} %get-tuple-element.27.refs_6_.refs_1_, bf16[2,2,256,512]{3,2,1,0:T(8,128)(2,1)S(1)} %multiply_stays.1.refs_9_.refs_2_, bf16[2,2,256,512]{3,2,1,0:T(8,128)(2,1)S(1)} %collective-permute-done.19.refs_3_, ...), custom_call_target="tpu_custom_call" | custom-call | flops 1073741824 | bytes 4718616 | tf_op jit(solution)/shard_map/update_stays/pallas_call | solution.py:300
  80.7 2.4 %update_third.1 = bf16[3,512,512]{2,1,0:T(8,128)(2,1)} custom-call(s32[2,3]{1,0:T(2,128)S(1)} %copy-done.2, bf16[2,512,512]{2,1,0:T(8,128)(2,1)S(1)} %get-tuple-element.27.refs_6_.refs_1_, bf16[512,512]{1,0:T(8,128)(2,1)S(1)} %get-tuple-element.28.refs_2_, bf16[2,1,256,512]{3,2,1,0:T(8,128)(2,1)S(1)} %multiply_third.1.refs_3_, ...), custom_call_target="tpu_custom_call", output_to_operand_aliasing={{}: (7, {})} | custom-call | flops 536870912 | bytes 6291480 | tf_op jit(solution)/shard_map/update_third/pallas_call | solution.py:300
  (40 shorter events, 11.4 us)
Async XLA Ops:
  0.0 1.4 %copy-start.1 = (bf16[3,512,1,512]{3,1,2,0:T(8,128)(2,1)S(1)}, bf16[3,512,1,512]{3,1,2,0:T(8,128)(2,1)}, u32[]{:S(2)}) copy-start(bf16[3,512,1,512]{3,1,2,0:T(8,128)(2,1)} %param.4) | copy-start | bytes 4718596
  1.4 0.7 copy-start.2
  2.1 0.7 copy-start.3
  3.6 2.4 %collective-permute-start = (bf16[3,256,512]{2,1,0:T(8,128)(2,1)S(1)}, bf16[3,256,512]{2,1,0:T(8,128)(2,1)S(1)}, u32[]{:S(2)}, u32[]{:S(2)}) collective-permute-start(bf16[3,256,512]{2,1,0:T(8,128)(2,1)S(1)} %get-tuple-element.18), channel_id=1, source_target_pairs={{0,1},{1,0},{2,3},{3,2},{4,5},{5,4},{6,7},{7,6},{8,9},{9,8},{10,11... | collective-permute-start | bytes 2359304 | tf_op jit(solution)/shard_map/sib_early/ppermute | solution.py:323
  6.6 7.3 %collective-permute-start.1 = (bf16[256,512]{1,0:T(8,128)(2,1)S(1)}, bf16[256,512]{1,0:T(8,128)(2,1)S(1)}, u32[]{:S(2)}, u32[]{:S(2)}) collective-permute-start(bf16[256,512]{1,0:T(8,128)(2,1)S(1)} %pick_extra.1.refs_3_.refs_1_), channel_id=1, source_target_pairs={{0,2},{1,5},{2,0},{3,7},{4,6},{5,1},{6,4},{7,3},{8,10},{9,13},{10,... | collective-permute-start | bytes 786440 | tf_op jit(solution)/shard_map/extra0a/ppermute | solution.py:331
  10.2 12.0 %collective-permute-start.3 = (bf16[2,256,512]{2,1,0:T(8,128)(2,1)S(1)}, bf16[2,256,512]{2,1,0:T(8,128)(2,1)S(1)}, u32[]{:S(2)}, u32[]{:S(2)}) collective-permute-start(bf16[2,256,512]{2,1,0:T(8,128)(2,1)S(1)} %get-tuple-element.19.refs_3_.refs_1_), channel_id=1, source_target_pairs={{0,2},{1,5},{2,0},{3,7},{4,6},{5,1},{6,4},{7,3},{8,10},{9,13},{10,... | collective-permute-start | bytes 1572872 | tf_op jit(solution)/shard_map/stays0a/ppermute | solution.py:331
  10.3 14.8 %collective-permute-start.6 = (bf16[512,512]{1,0:T(8,128)(2,1)S(1)}, bf16[512,512]{1,0:T(8,128)(2,1)S(1)}, u32[]{:S(2)}, u32[]{:S(2)}) collective-permute-start(bf16[512,512]{1,0:T(8,128)(2,1)S(1)} %get-tuple-element.21.refs_3_), channel_id=1, source_target_pairs={{0,8},{24,16},{16,0},{8,24},{1,9},{25,17},{17,1},{9,25},{2,10},{26... | collective-permute-start | bytes 1572872 | tf_op jit(solution)/shard_map/swap/ppermute | solution.py:319
  14.5 7.3 %collective-permute-start.2 = (bf16[256,512]{1,0:T(8,128)(2,1)S(1)}, bf16[256,512]{1,0:T(8,128)(2,1)S(1)}, u32[]{:S(2)}, u32[]{:S(2)}) collective-permute-start(bf16[256,512]{1,0:T(8,128)(2,1)S(1)} %pass_extra.1.refs_1_), channel_id=1, source_target_pairs={{0,4},{1,3},{2,6},{3,1},{4,0},{5,7},{6,2},{7,5},{8,12},{9,11},{10,... | collective-permute-start | bytes 786440 | tf_op jit(solution)/shard_map/extra1a/ppermute | solution.py:331
  25.1 2.0 %collective-permute-start.7 = (bf16[512,512]{1,0:T(8,128)(2,1)S(1)}, bf16[512,512]{1,0:T(8,128)(2,1)S(1)}, u32[]{:S(2)}, u32[]{:S(2)}) collective-permute-start(bf16[512,512]{1,0:T(8,128)(2,1)S(1)} %get-tuple-element.22.refs_3_.refs_4_.refs_6_), channel_id=1, source_target_pairs={{0,1},{1,0},{2,3},{3,2},{4,5},{5,4},{6,7},{7,6},{8,9},{9,8},{10,11... | collective-permute-start | bytes 1572872 | tf_op jit(solution)/shard_map/sib_moved/ppermute | solution.py:323
  25.2 9.2 %collective-permute-start.5 = (bf16[2,256,512]{2,1,0:T(8,128)(2,1)S(1)}, bf16[2,256,512]{2,1,0:T(8,128)(2,1)S(1)}, u32[]{:S(2)}, u32[]{:S(2)}) collective-permute-start(bf16[2,256,512]{2,1,0:T(8,128)(2,1)S(1)} %get-tuple-element.20.refs_2_), channel_id=1, source_target_pairs={{0,2},{1,5},{2,0},{3,7},{4,6},{5,1},{6,4},{7,3},{8,10},{9,13},{10,... | collective-permute-start | bytes 1572872 | tf_op jit(solution)/shard_map/stays0b/ppermute | solution.py:331
  27.7 15.6 %collective-permute-start.9 = (bf16[2,1,256,512]{3,2,1,0:T(8,128)(2,1)S(1)}, bf16[2,1,256,512]{3,2,1,0:T(8,128)(2,1)S(1)}, u32[]{:S(2)}, u32[]{:S(2)}) collective-permute-start(bf16[2,1,256,512]{3,2,1,0:T(8,128)(2,1)S(1)} %pick_third.1.refs_5_.refs_1_), channel_id=1, source_target_pairs={{0,2},{1,5},{2,0},{3,7},{4,6},{5,1},{6,4},{7,3},{8,10},{9,13},{10,... | collective-permute-start | bytes 1572872 | tf_op jit(solution)/shard_map/third0a/ppermute | solution.py:331
  29.4 9.2 %collective-permute-start.4 = (bf16[256,512]{1,0:T(8,128)(2,1)S(1)}, bf16[256,512]{1,0:T(8,128)(2,1)S(1)}, u32[]{:S(2)}, u32[]{:S(2)}) collective-permute-start(bf16[256,512]{1,0:T(8,128)(2,1)S(1)} %extra_here.1.refs_1_.refs_0_.refs_2_), channel_id=1, source_target_pairs={{0,16},{24,8},{1,17},{25,9},{2,18},{26,10},{3,19},{27,11},{4,20},{... | collective-permute-start | bytes 786440 | tf_op jit(solution)/shard_map/extra_z2/ppermute | solution.py:319
  33.0 8.9 %collective-permute-start.10 = (bf16[256,512]{1,0:T(8,128)(2,1)S(1)}, bf16[256,512]{1,0:T(8,128)(2,1)S(1)}, u32[]{:S(2)}, u32[]{:S(2)}) collective-permute-start(bf16[256,512]{1,0:T(8,128)(2,1)S(1)} %get-tuple-element.24), channel_id=1, source_target_pairs={{8,16},{16,8},{9,17},{17,9},{10,18},{18,10},{11,19},{19,11},{12,20... | collective-permute-start | bytes 786440 | tf_op jit(solution)/shard_map/row1a/ppermute | solution.py:319
  33.6 10.3 %collective-permute-start.11 = (bf16[256,512]{1,0:T(8,128)(2,1)S(1)}, bf16[256,512]{1,0:T(8,128)(2,1)S(1)}, u32[]{:S(2)}, u32[]{:S(2)}) collective-permute-start(bf16[256,512]{1,0:T(8,128)(2,1)S(1)} %get-tuple-element.25), channel_id=1, source_target_pairs={{8,16},{16,8},{9,17},{17,9},{10,18},{18,10},{11,19},{19,11},{12,20... | collective-permute-start | bytes 786440 | tf_op jit(solution)/shard_map/row1b/ppermute | solution.py:319
  38.6 8.3 %copy-start = (bf16[2,512,512]{2,1,0:T(8,128)(2,1)S(1)}, bf16[2,512,512]{2,1,0:T(8,128)(2,1)}, u32[]{:S(2)}) copy-start(bf16[2,512,512]{2,1,0:T(8,128)(2,1)} %refs_1_.5) | copy-start | bytes 3145732
  38.6 8.3 %collective-permute-start.8 = (bf16[256,512]{1,0:T(8,128)(2,1)S(1)}, bf16[256,512]{1,0:T(8,128)(2,1)S(1)}, u32[]{:S(2)}, u32[]{:S(2)}) collective-permute-start(bf16[256,512]{1,0:T(8,128)(2,1)S(1)} %hand_on.1.refs_3_), channel_id=1, source_target_pairs={{0,8},{24,16},{16,24},{8,0},{1,9},{25,17},{17,25},{9,1},{2,10},{26... | collective-permute-start | bytes 786440 | tf_op jit(solution)/shard_map/extra_z1/ppermute | solution.py:319
  41.3 20.7 %collective-permute-start.15 = (bf16[2,256,512]{2,1,0:T(8,128)(2,1)S(1)}, bf16[2,256,512]{2,1,0:T(8,128)(2,1)S(1)}, u32[]{:S(2)}, u32[]{:S(2)}) collective-permute-start(bf16[2,256,512]{2,1,0:T(8,128)(2,1)S(1)} %get-tuple-element.23.refs_2_.refs_4_), channel_id=1, source_target_pairs={{0,4},{1,3},{2,6},{3,1},{4,0},{5,7},{6,2},{7,5},{8,12},{9,11},{10,... | collective-permute-start | bytes 1572872 | tf_op jit(solution)/shard_map/stays1a/ppermute | solution.py:331
  41.8 20.2 %collective-permute-start.16 = (bf16[2,256,512]{2,1,0:T(8,128)(2,1)S(1)}, bf16[2,256,512]{2,1,0:T(8,128)(2,1)S(1)}, u32[]{:S(2)}, u32[]{:S(2)}) collective-permute-start(bf16[2,256,512]{2,1,0:T(8,128)(2,1)S(1)} %get-tuple-element.26.refs_5_), channel_id=1, source_target_pairs={{0,4},{1,3},{2,6},{3,1},{4,0},{5,7},{6,2},{7,5},{8,12},{9,11},{10,... | collective-permute-start | bytes 1572872 | tf_op jit(solution)/shard_map/stays1b/ppermute | solution.py:331
  47.9 14.2 %collective-permute-start.12 = (bf16[2,256,512]{2,1,0:T(8,128)(2,1)S(1)}, bf16[2,256,512]{2,1,0:T(8,128)(2,1)S(1)}, u32[]{:S(2)}, u32[]{:S(2)}) collective-permute-start(bf16[2,256,512]{2,1,0:T(8,128)(2,1)S(1)} %settle_extra.1.refs_2_.refs_1_), channel_id=1, source_target_pairs={{0,1},{1,0},{2,3},{3,2},{4,5},{5,4},{6,7},{7,6},{8,9},{9,8},{10,11... | collective-permute-start | bytes 1572872 | tf_op jit(solution)/shard_map/sib_vl/ppermute | solution.py:323
  47.9 14.1 %collective-permute-start.17 = (bf16[2,1,256,512]{3,2,1,0:T(8,128)(2,1)S(1)}, bf16[2,1,256,512]{3,2,1,0:T(8,128)(2,1)S(1)}, u32[]{:S(2)}, u32[]{:S(2)}) collective-permute-start(bf16[2,1,256,512]{3,2,1,0:T(8,128)(2,1)S(1)} %pass_third.1.refs_5_.refs_4_), channel_id=1, source_target_pairs={{0,4},{1,3},{2,6},{3,1},{4,0},{5,7},{6,2},{7,5},{8,12},{9,11},{10,... | collective-permute-start | bytes 1572872 | tf_op jit(solution)/shard_map/third1a/ppermute | solution.py:331
  48.0 14.0 %collective-permute-start.13 = (bf16[256,512]{1,0:T(8,128)(2,1)S(1)}, bf16[256,512]{1,0:T(8,128)(2,1)S(1)}, u32[]{:S(2)}, u32[]{:S(2)}) collective-permute-start(bf16[256,512]{1,0:T(8,128)(2,1)S(1)} %collective-permute-done.10.refs_4_.refs_5_), channel_id=1, source_target_pairs={{16,24},{8,0},{17,25},{9,1},{18,26},{10,2},{19,27},{11,3},{20,28},... | collective-permute-start | bytes 786440 | tf_op jit(solution)/shard_map/row2a/ppermute | solution.py:319
  64.0 13.3 %collective-permute-start.19 = (bf16[2,2,256,512]{3,2,1,0:T(8,128)(2,1)S(1)}, bf16[2,2,256,512]{3,2,1,0:T(8,128)(2,1)S(1)}, u32[]{:S(2)}, u32[]{:S(2)}) collective-permute-start(bf16[2,2,256,512]{3,2,1,0:T(8,128)(2,1)S(1)} %multiply_stays.1.refs_9_.refs_2_), channel_id=1, source_target_pairs={{0,1},{1,0},{2,3},{3,2},{4,5},{5,4},{6,7},{7,6},{8,9},{9,8},{10,11... | collective-permute-start | bytes 3145736 | tf_op jit(solution)/shard_map/sib_mine/ppermute | solution.py:323
  64.3 10.4 %collective-permute-start.14 = (bf16[256,512]{1,0:T(8,128)(2,1)S(1)}, bf16[256,512]{1,0:T(8,128)(2,1)S(1)}, u32[]{:S(2)}, u32[]{:S(2)}) collective-permute-start(bf16[256,512]{1,0:T(8,128)(2,1)S(1)} %collective-permute-done.11.refs_6_), channel_id=1, source_target_pairs={{16,24},{8,0},{17,25},{9,1},{18,26},{10,2},{19,27},{11,3},{20,28},... | collective-permute-start | bytes 786440 | tf_op jit(solution)/shard_map/row2b/ppermute | solution.py:319
  77.2 3.5 %collective-permute-start.18 = (bf16[2,1,256,512]{3,2,1,0:T(8,128)(2,1)S(1)}, bf16[2,1,256,512]{3,2,1,0:T(8,128)(2,1)S(1)}, u32[]{:S(2)}, u32[]{:S(2)}) collective-permute-start(bf16[2,1,256,512]{3,2,1,0:T(8,128)(2,1)S(1)} %multiply_third.1.refs_3_), channel_id=1, source_target_pairs={{0,1},{1,0},{2,3},{3,2},{4,5},{5,4},{6,7},{7,6},{8,9},{9,8},{10,11... | collective-permute-start | bytes 1572872 | tf_op jit(solution)/shard_map/sib_third/ppermute | solution.py:323

commit v6 on v5

--- a/solution.py
+++ b/solution.py
@@ -50,7 +50,7 @@
     return pl.ds(pl.multiple_of(part * half, half), half)
 
 
-def prepare(n, m, piv, pat, mat, raw, leaving, other):
+def prepare(n, m, piv, pat, mat, raw, leave_top, leave_low, other):
     rb, width = mat.shape[0], mat.shape[1]
     f = facts(n, m, rb, piv)
     cut = rows(1 - f["core"], width // 2)
@@ -60,7 +60,8 @@
         zero = lambda: jnp.zeros((width, width), mat.dtype)
         either(keep, raw.at[k], lambda: mat[slot], zero)
         if k == rb - 1:
-            leaving[...] = raw[k]
+            leave_top[...] = raw[k, : width // 2, :]
+            leave_low[...] = raw[k, width // 2 :, :]
         other[k] = raw[k, cut, :]
 
 
@@ -86,27 +87,35 @@
             either(hit, pair(panel)[q].at[k], lambda: raw[k, cut, :], lambda: sib[k])
 
 
-def pick_third(n, m, piv, raw, sib, moved, sib_moved, panel):
+def pick_third(n, m, piv, raw, sib, top, low, sib_moved, panel):
     rb, width = raw.shape[0], raw.shape[1]
     f = facts(n, m, rb, piv)
     cut = rows(f["core"], width // 2)
     for q in range(2):
         hit = (f["c"][q] & 1) == f["core"]
-
-        @pl.when(f["is_end"])
-        def _():
-            either(hit, panel.at[q, 0], lambda: moved[cut, :], lambda: sib_moved[cut, :])
+        new = jnp.logical_and(f["is_end"], hit)
+
+        @pl.when(jnp.logical_and(new, f["core"] == 0))
+        def _():
+            panel[q, 0] = top[...]
+
+        @pl.when(jnp.logical_and(new, f["core"] == 1))
+        def _():
+            panel[q, 0] = low[...]
+
+        @pl.when(jnp.logical_and(f["is_end"], jnp.logical_not(hit)))
+        def _():
+            panel[q, 0] = sib_moved[...]
 
         @pl.when(jnp.logical_not(f["is_end"]))
         def _():
             either(hit, panel.at[q, 0], lambda: raw[rb - 1, cut, :], lambda: sib[rb - 1])
 
 
-def relay(n, m, moved, out, *halves):
-    out[...] = moved[...]
-    half = moved.shape[0] // 2
-    for p, ref in enumerate(halves):
-        ref[...] = moved[p * half : (p + 1) * half, :]
+def relay(n, m, stride, leave_low, top, low, other, send):
+    core = lax.axis_index("pcol").astype(jnp.int32) & 1
+    either(core == 0, other, lambda: low[...], lambda: top[...])
+    hand_on(n, m, stride, leave_low, low, send)
 
 
 def bit_of(f, column, stage, stages):
@@ -184,26 +193,22 @@
         out[1, k] = dot(p1, inv[1]).astype(out.dtype)
 
 
-def settle_rows(n, m, piv, vl, sib_vl, leaving, moved, *refs):
-    hops, upper, lefts = refs[:-2], refs[-2], refs[-1]
-    width = leaving.shape[0]
-    half = width // 2
+def settle_rows(n, m, piv, vl, sib_vl, *refs):
+    tops, upper, lefts = refs[:-2], refs[-2], refs[-1]
+    count = len(tops) // 2
+    half, width = tops[0].shape
     f = facts(n, m, 2, piv)
     r = f["r"]
     for which in range(2):
         place = r if which == 0 else n - 1 - r
         slot = jnp.where(f["low_first"], which, 1 - which)
-        for h in range(n):
-
-            @pl.when(place == h)
+        for s in range(count):
+            here = place == 0 if s == 0 else (place & (2 * (n >> s) - 1)) == (n >> s)
+
+            @pl.when(here)
             def _():
-                if h == 0:
-                    upper[slot] = leaving[...]
-                elif h == 1:
-                    upper[slot] = moved[...]
-                else:
-                    upper[slot, :half, :] = hops[2 * (h - 2)][...]
-                    upper[slot, half:, :] = hops[2 * (h - 2) + 1][...]
+                upper[slot, :half, :] = tops[s][...]
+                upper[slot, half:, :] = tops[count + s][...]
 
     lefts[rows(f["core"], half), :] = vl[1]
     lefts[rows(1 - f["core"], half), :] = sib_vl[1]
@@ -251,7 +256,7 @@
         copy.wait()
 
 
-def update_third(n, m, piv, upper, lefts, mine, sib, raw, moved, so_far, out, old, new, sem):
+def update_third(n, m, piv, upper, lefts, mine, sib, raw, top, low, so_far, out, old, new, sem):
     del so_far
     rb = raw.shape[0]
     f = facts(n, m, rb, piv)
@@ -269,7 +274,9 @@
 
     @pl.when(jnp.logical_not(jnp.logical_or(first, second)))
     def _():
-        either(f["is_end"], old, lambda: moved[...], lambda: raw[rb - 1])
+        half = top.shape[0]
+        either(f["is_end"], old.at[:half], lambda: top[...], lambda: raw[rb - 1, :half, :])
+        either(f["is_end"], old.at[half:], lambda: low[...], lambda: raw[rb - 1, half:, :])
         update(f, upper, mine, sib, (0,), old, new)
 
     copy = pltpu.make_async_copy(new, out.at[f["slots"][rb - 1]], sem)
@@ -345,63 +352,69 @@
         return [*values, *got]
 
     square, strip = (width, width), (half, width)
-    raw, leaving, other = call(
+    raw, *leaving, other = call(
         prepare,
-        [(rb, *square), square, (rb, *strip)],
+        [(rb, *square), strip, strip, (rb, *strip)],
         "ss",
         pivots,
         pattern.T,
         blocks,
     )
-    moved = along("swap", [(0, 1), (n - 1, n - 2), (n // 2, 0), (n // 2 - 1, n - 1)], leaving)
     early = sibling("sib_early", other)
+    exchange = [(0, n // 2), (n - 1, n // 2 - 1), (n // 2, 0), (n // 2 - 1, n - 1)]
+    moved = [along("swap" + "ab"[i], exchange, leaving[i]) for i in range(2)]
+
+    def split(stride):
+        pairs = []
+        for i in range(0, n, 2 * stride):
+            pairs += [(i, i + stride), (n - 1 - i, n - 1 - i - stride)]
+        return pairs
 
     extra = call(pick_extra, [strip], "s", pivots, raw, early)
     panel = call(pick, [(rb - 1, *strip)] * 2, "s", pivots, raw, early, after=[extra])
     got_extra = cross("extra", 0, [extra])
     got_stays = cross("stays", 0, panel)
     had, got = passing("extra", forward_extra, [extra], got_extra, after=[panel[0]])
+    hand = lambda stride: lambda _n, _m, *refs: hand_on(n, m, stride, *refs)
+    sends = [
+        call(hand(n // 2), [strip], "", leaving[0], moved[0], name="hand_on_a", after=[had])
+    ]
     step = lambda _n, _m, *refs: forward_extra(n, m, stages - 1, stages, *refs)
-    extra_here = call(
-        step, [strip], "s", pivots, had, got, after=[got_stays[0]], name="extra_here"
-    )
-    moved, *parts = call(relay, [square, strip, strip], "", moved, after=[extra_here])
-
-    sib_moved = sibling("sib_moved", moved)
-    third = call(
-        pick_third, [(2, 1, *strip)], "s", pivots, raw, early, moved, sib_moved
-    )
-    got_third = cross("third", 0, [third])
-    stays = passing("stays", forward, panel, got_stays, after=[third])
-
-    hops = []
-    for h in range(1, n - 1):
-        pairs = [(h, h + 1), (n - 1 - h, n - 2 - h)]
-        parts = [along("row" + str(h) + "ab"[i], pairs, part) for i, part in enumerate(parts)]
-        hops += parts
+    extra_here = call(step, [strip], "s", pivots, had, got, after=[sends[0]], name="extra_here")
+    stays = passing("stays", forward, panel, got_stays, after=[extra_here])
+    step = lambda _n, _m, *refs: relay(n, m, n // 2, *refs)
+    other_moved, send = call(
+        step, [strip] * 2, "", leaving[1], *moved, name="relay", after=[stays[0]]
+    )
+    sends.append(send)
+    after_relay = send
+
+    arrived = [[leaving[i], moved[i]] for i in range(2)]
+    stride = n // 4
+    while stride:
+        for i in range(2):
+            got = along("row" + str(stride) + "ab"[i], split(stride), sends[i])
+            arrived[i].append(got)
+            if stride > 1:
+                sends[i] = call(hand(stride), [strip], "", sends[i], got, name="hand_on_row")
+        stride //= 2
 
     came = [extra_here]
     send = extra_here
     stride = n // 2
     while stride:
-        pairs = []
-        for i in range(0, n, 2 * stride):
-            pairs += [(i, i + stride), (n - 1 - i, n - 1 - i - stride)]
-        got = along("extra_z" + str(stride), pairs, send)
+        got = along("extra_z" + str(stride), split(stride), send)
         came.append(got)
         if stride > 1:
-            step = lambda _n, _m, *refs: hand_on(n, m, stride, *refs)
-            send = call(
-                step,
-                [strip],
-                "",
-                send,
-                got,
-                name="hand_on",
-                after=[stays[0]],
-            )
+            send = call(hand(stride), [strip], "", send, got, name="hand_on", after=[after_relay])
         stride //= 2
-    third = passing("third", forward, [third], got_third, after=[send, hops[0]])
+    sib_moved = sibling("sib_moved", other_moved)
+    third = call(
+        pick_third, [(2, 1, *strip)], "s", pivots, raw, early, *moved, sib_moved, after=[send, stays[2]]
+    )
+    got_third = cross("third", 0, [third])
+
+    third = passing("third", forward, [third], got_third, after=[arrived[0][2], *stays[2:]])
     vl = call(
         settle_extra,
         [(2, *strip)],
@@ -410,10 +423,21 @@
         inverses,
         *came,
         products=0.5,
-        after=[third[0], hops[1]],
+        after=[third[0]],
     )
     sib_vl = sibling("sib_vl", vl)
 
+    upper, lefts = call(
+        settle_rows,
+        [(2, *square), square],
+        "s",
+        pivots,
+        vl,
+        sib_vl,
+        *arrived[0],
+        *arrived[1],
+        products=1,
+    )
     step = lambda _n, _m, *refs: multiply(n, m, stages, *refs)
     mine = call(
         step,
@@ -427,22 +451,9 @@
         scratch=[square],
         products=3 * (rb - 1) / 2,
         name="multiply_stays",
-        after=[hops[2], third[1]],
+        after=[upper],
     )
     sib_mine = sibling("sib_mine", mine)
-    upper, lefts = call(
-        settle_rows,
-        [(2, *square), square],
-        "s",
-        pivots,
-        vl,
-        sib_vl,
-        leaving,
-        moved,
-        *hops,
-        products=1,
-        after=[mine],
-    )
     mine_third = call(
         step,
         [(2, 1, *strip)],
@@ -454,7 +465,7 @@
         *third,
         scratch=[square],
         products=1.5,
-        after=[upper],
+        after=[mine],
         name="multiply_third",
     )
     sib_third = sibling("sib_third", mine_third)
@@ -474,17 +485,17 @@
     result = call(
         update_third,
         [blocks.shape],
-        "svvvvvva",
+        "svvvvvvva",
         pivots,
         upper,
         lefts,
         mine_third,
         sib_third,
         raw,
-        moved,
+        *moved,
         result,
         scratch=[square, square, pltpu.SemaphoreType.DMA],
-        aliases={7: 0},
+        aliases={8: 0},
         products=2,
         place=ANY,
     )

time: 83.4 us -> 88.9 us (1.066)
  waiting for transfers between devices: 40 us -> 47.7 us
  starting transfers between devices: 23.8 us -> 21.7 us
    ppermute x7 -> x6, waiting for transfers between devices: 30.5 us -> 36.3 us  [along(): return lax.ppermute(value, 'prow', pairs)]
    ppermute x8, waiting for transfers between devices: 7.3 us -> 9.44 us  [across(): return lax.ppermute(value, 'pcol', pairs)]
    ppermute x7 -> x6, starting transfers between devices: 12.3 us -> 10.8 us  [along(): return lax.ppermute(value, 'prow', pairs)]
    pallas_call x16 -> x17, Pallas kernels: 16.3 us -> 16.3 us  [call(): pl.pallas_call(body, out_shape=outs, in_specs=specs, out_specs=[place] *...]
  transfers between devices with their start and end apart: 20 -> 19, of which waited for: 11 -> 9; matrix products, arithmetic and copies ran while one was open for 0% -> 0% of each run, Pallas kernels for 13% -> 10%
where the time goes in v6:
time: 88.9 us; the launch traced here: 88.7 us
  waiting for transfers between devices  47.7 us (54%)
  starting transfers between devices  21.7 us (24%)
  Pallas kernels  16.3 us (18%)
  local copies, waits for them, and re-layouts  2.78 us (3%)
    ppermute x6, waiting for transfers between devices, along(): return lax.ppermute(value, 'prow', pairs)  36.3 us
    pallas_call x17, Pallas kernels, call(): pl.pallas_call(body, out_shape=outs, in_specs=specs, out_specs=[place] *...  16.3 us
    ppermute x6, starting transfers between devices, along(): return lax.ppermute(value, 'prow', pairs)  10.8 us
    ppermute x8, starting transfers between devices, across(): return lax.ppermute(value, 'pcol', pairs)  10.1 us
    ppermute x8, waiting for transfers between devices, across(): return lax.ppermute(value, 'pcol', pairs)  9.44 us
    unnamed x8, local copies, waits for them, and re-layouts  2.78 us
    ppermute x5, waiting for transfers between devices, sibling(): return lax.ppermute(value, 'pcol', [(i, i ^ 1) for i in range(m)])  1.92 us
  transfers between devices with their start and end apart: 19, of which 9 were waited for; matrix products, arithmetic and copies ran while one was open for 0% of the time, Pallas kernels for 10%

profile of v6, /device:TPU:0, one launch (start us, length us, event | category | flops | bytes accessed | tf_op | source)
XLA Modules:
  0.0 88.7 jit_solution(17978432710691151338)
XLA Ops:
  0.0 1.4 %copy-done.1 = bf16[3,512,1,512]{3,1,2,0:T(8,128)(2,1)S(1)} copy-done((bf16[3,512,1,512]{3,1,2,0:T(8,128)(2,1)S(1)}, bf16[3,512,1,512]{3,1,2,0:T(8,128)(2,1)}, u32[]{:S(2)}) %copy-start.1) | copy-done | bytes 1572888
  4.1 1.9 %collective-permute-done.refs_2_ = bf16[3,256,512]{2,1,0:T(8,128)(2,1)S(1)} collective-permute-done((bf16[3,256,512]{2,1,0:T(8,128)(2,1)S(1)}, bf16[3,256,512]{2,1,0:T(8,128)(2,1)S(1)}, u32[]{:S(2)}, u32[]{:S(2)}) %collective-permute-start) | collective-permute-done | bytes 786464 | tf_op jit(solution)/shard_map/sib_early/ppermute | solution.py:330
  6.6 2.9 %collective-permute-start.1 = (bf16[256,512]{1,0:T(8,128)(2,1)S(1)}, bf16[256,512]{1,0:T(8,128)(2,1)S(1)}, u32[]{:S(2)}, u32[]{:S(2)}) collective-permute-start(bf16[256,512]{1,0:T(8,128)(2,1)S(1)} %pick_extra.1.refs_3_.refs_1_), channel_id=1, source_target_pairs={{0,2},{1,5},{2,0},{3,7},{4,6},{5,1},{6,4},{7,3},{8,10},{9,13},{10,... | collective-permute-start | bytes 786440 | tf_op jit(solution)/shard_map/extra0a/ppermute | solution.py:338
  10.3 2.0 %collective-permute-start.6 = (bf16[2,256,512]{2,1,0:T(8,128)(2,1)S(1)}, bf16[2,256,512]{2,1,0:T(8,128)(2,1)S(1)}, u32[]{:S(2)}, u32[]{:S(2)}) collective-permute-start(bf16[2,256,512]{2,1,0:T(8,128)(2,1)S(1)} %get-tuple-element.19.refs_3_.refs_1_), channel_id=1, source_target_pairs={{0,2},{1,5},{2,0},{3,7},{4,6},{5,1},{6,4},{7,3},{8,10},{9,13},{10,... | collective-permute-start | bytes 1572872 | tf_op jit(solution)/shard_map/stays0a/ppermute | solution.py:338
  12.3 2.6 %collective-permute-start.3 = (bf16[256,512]{1,0:T(8,128)(2,1)S(1)}, bf16[256,512]{1,0:T(8,128)(2,1)S(1)}, u32[]{:S(2)}, u32[]{:S(2)}) collective-permute-start(bf16[256,512]{1,0:T(8,128)(2,1)S(1)} %get-tuple-element.20.refs_0_.refs_3_), channel_id=1, source_target_pairs={{0,16},{24,8},{16,0},{8,24},{1,17},{25,9},{17,1},{9,25},{2,18},{26... | collective-permute-start | bytes 786440 | tf_op jit(solution)/shard_map/swapa/ppermute | solution.py:326
  15.5 1.6 %collective-permute-start.2 = (bf16[256,512]{1,0:T(8,128)(2,1)S(1)}, bf16[256,512]{1,0:T(8,128)(2,1)S(1)}, u32[]{:S(2)}, u32[]{:S(2)}) collective-permute-start(bf16[256,512]{1,0:T(8,128)(2,1)S(1)} %pass_extra.1.refs_2_.refs_1_), channel_id=1, source_target_pairs={{0,4},{1,3},{2,6},{3,1},{4,0},{5,7},{6,2},{7,5},{8,12},{9,11},{10,... | collective-permute-start | bytes 786440 | tf_op jit(solution)/shard_map/extra1a/ppermute | solution.py:338
  17.1 2.1 %collective-permute-start.5 = (bf16[256,512]{1,0:T(8,128)(2,1)S(1)}, bf16[256,512]{1,0:T(8,128)(2,1)S(1)}, u32[]{:S(2)}, u32[]{:S(2)}) collective-permute-start(bf16[256,512]{1,0:T(8,128)(2,1)S(1)} %get-tuple-element.21.refs_0_.refs_6_), channel_id=1, source_target_pairs={{0,16},{24,8},{16,0},{8,24},{1,17},{25,9},{17,1},{9,25},{2,18},{26... | collective-permute-start | bytes 786440 | tf_op jit(solution)/shard_map/swapb/ppermute | solution.py:326
  19.2 13.9 %collective-permute-done.3.refs_1_.refs_3_.refs_4_.refs_6_ = bf16[256,512]{1,0:T(8,128)(2,1)S(1)} collective-permute-done((bf16[256,512]{1,0:T(8,128)(2,1)S(1)}, bf16[256,512]{1,0:T(8,128)(2,1)S(1)}, u32[]{:S(2)}, u32[]{:S(2)}) %collective-permute-start.3) | collective-permute-done | bytes 262176 | tf_op jit(solution)/shard_map/swapa/ppermute | solution.py:326
  35.0 1.5 %collective-permute-start.4 = (bf16[256,512]{1,0:T(8,128)(2,1)S(1)}, bf16[256,512]{1,0:T(8,128)(2,1)S(1)}, u32[]{:S(2)}, u32[]{:S(2)}) collective-permute-start(bf16[256,512]{1,0:T(8,128)(2,1)S(1)} %extra_here.1.refs_5_.refs_0_.refs_2_), channel_id=1, source_target_pairs={{0,16},{24,8},{1,17},{25,9},{2,18},{26,10},{3,19},{27,11},{4,20},{... | collective-permute-start | bytes 786440 | tf_op jit(solution)/shard_map/extra_z2/ppermute | solution.py:326
  36.5 1.1 %collective-permute-done.5.refs_2_.refs_4_.refs_7_ = bf16[256,512]{1,0:T(8,128)(2,1)S(1)} collective-permute-done((bf16[256,512]{1,0:T(8,128)(2,1)S(1)}, bf16[256,512]{1,0:T(8,128)(2,1)S(1)}, u32[]{:S(2)}, u32[]{:S(2)}) %collective-permute-start.5) | collective-permute-done | bytes 262176 | tf_op jit(solution)/shard_map/swapb/ppermute | solution.py:326
  38.2 3.5 %collective-permute-done.4.refs_1_.refs_3_ = bf16[256,512]{1,0:T(8,128)(2,1)S(1)} collective-permute-done((bf16[256,512]{1,0:T(8,128)(2,1)S(1)}, bf16[256,512]{1,0:T(8,128)(2,1)S(1)}, u32[]{:S(2)}, u32[]{:S(2)}) %collective-permute-start.4) | collective-permute-done | bytes 262176 | tf_op jit(solution)/shard_map/extra_z2/ppermute | solution.py:326
  41.8 1.9 %collective-permute-done.10.refs_7_.refs_4_.refs_6_ = bf16[2,256,512]{2,1,0:T(8,128)(2,1)S(1)} collective-permute-done((bf16[2,256,512]{2,1,0:T(8,128)(2,1)S(1)}, bf16[2,256,512]{2,1,0:T(8,128)(2,1)S(1)}, u32[]{:S(2)}, u32[]{:S(2)}) %collective-permute-start.10) | collective-permute-done | bytes 524320 | tf_op jit(solution)/shard_map/stays1a/ppermute | solution.py:338
  45.0 2.8 %collective-permute-start.12 = (bf16[256,512]{1,0:T(8,128)(2,1)S(1)}, bf16[256,512]{1,0:T(8,128)(2,1)S(1)}, u32[]{:S(2)}, u32[]{:S(2)}) collective-permute-start(bf16[256,512]{1,0:T(8,128)(2,1)S(1)} %hand_on_a.1.refs_3_), channel_id=1, source_target_pairs={{0,8},{24,16},{16,24},{8,0},{1,9},{25,17},{17,25},{9,1},{2,10},{26... | collective-permute-start | bytes 786440 | tf_op jit(solution)/shard_map/row1a/ppermute | solution.py:326
  47.8 7.2 %collective-permute-done.12.refs_3_.refs_5_ = bf16[256,512]{1,0:T(8,128)(2,1)S(1)} collective-permute-done((bf16[256,512]{1,0:T(8,128)(2,1)S(1)}, bf16[256,512]{1,0:T(8,128)(2,1)S(1)}, u32[]{:S(2)}, u32[]{:S(2)}) %collective-permute-start.12) | collective-permute-done | bytes 262176 | tf_op jit(solution)/shard_map/row1a/ppermute | solution.py:326
  55.6 3.7 %collective-permute-done.8.refs_4_ = bf16[256,512]{1,0:T(8,128)(2,1)S(1)} collective-permute-done((bf16[256,512]{1,0:T(8,128)(2,1)S(1)}, bf16[256,512]{1,0:T(8,128)(2,1)S(1)}, u32[]{:S(2)}, u32[]{:S(2)}) %collective-permute-start.8) | collective-permute-done | bytes 262176 | tf_op jit(solution)/shard_map/extra_z1/ppermute | solution.py:326
  60.3 1.8 %collective-permute-start.15 = (bf16[256,512]{1,0:T(8,128)(2,1)S(1)}, bf16[256,512]{1,0:T(8,128)(2,1)S(1)}, u32[]{:S(2)}, u32[]{:S(2)}) collective-permute-start(bf16[256,512]{1,0:T(8,128)(2,1)S(1)} %get-tuple-element.24.refs_2_), channel_id=1, source_target_pairs={{0,8},{24,16},{16,24},{8,0},{1,9},{25,17},{17,25},{9,1},{2,10},{26... | collective-permute-start | bytes 786440 | tf_op jit(solution)/shard_map/row1b/ppermute | solution.py:326
  62.1 6.9 %collective-permute-done.15.refs_8_ = bf16[256,512]{1,0:T(8,128)(2,1)S(1)} collective-permute-done((bf16[256,512]{1,0:T(8,128)(2,1)S(1)}, bf16[256,512]{1,0:T(8,128)(2,1)S(1)}, u32[]{:S(2)}, u32[]{:S(2)}) %collective-permute-start.15) | collective-permute-done | bytes 262176 | tf_op jit(solution)/shard_map/row1b/ppermute | solution.py:326
  69.0 1.1 %settle_rows.1 = (bf16[2,512,512]{2,1,0:T(8,128)(2,1)S(1)}, bf16[512,512]{1,0:T(8,128)(2,1)S(1)}) custom-call(s32[2,3]{1,0:T(2,128)S(1)} %copy-done.2, bf16[2,256,512]{2,1,0:T(8,128)(2,1)S(1)} %settle_extra.1.refs_1_.refs_2_, bf16[2,256,512]{2,1,0:T(8,128)(2,1)S(1)} %collective-permute-done.14.refs_2_.refs_3_, ...), custom_call_target="tpu_custom_call" | custom-call | flops 268435456 | bytes 2621464 | tf_op jit(solution)/shard_map/settle_rows/pallas_call | solution.py:307
  70.1 2.0 %multiply_stays.1.refs_6_.refs_2_ = bf16[2,2,256,512]{3,2,1,0:T(8,128)(2,1)S(1)} custom-call(s32[2,3]{1,0:T(2,128)S(1)} %copy-done.2, bf16[2,512,512]{2,1,0:T(8,128)(2,1)S(1)} %copy-done, bf16[2,256,512]{2,1,0:T(8,128)(2,1)S(1)} %settle_extra.1.refs_1_.refs_2_, bf16[2,256,512]{2,1,0:T(8,128)(2,1)S(1)} %collective-permute-done.14.refs_2_.refs_3_, ...), custom_call_target="tpu_custom_call" | custom-call | flops 805306368 | bytes 4194328 | tf_op jit(solution)/shard_map/multiply_stays/pallas_call | solution.py:307
  72.2 1.7 %collective-permute-start.16 = (bf16[2,1,256,512]{3,2,1,0:T(8,128)(2,1)S(1)}, bf16[2,1,256,512]{3,2,1,0:T(8,128)(2,1)S(1)}, u32[]{:S(2)}, u32[]{:S(2)}) collective-permute-start(bf16[2,1,256,512]{3,2,1,0:T(8,128)(2,1)S(1)} %pass_third.1.refs_5_.refs_4_), channel_id=1, source_target_pairs={{0,4},{1,3},{2,6},{3,1},{4,0},{5,7},{6,2},{7,5},{8,12},{9,11},{10,... | collective-permute-start | bytes 1572872 | tf_op jit(solution)/shard_map/third1a/ppermute | solution.py:338
  73.9 7.5 %collective-permute-done.16.refs_5_ = bf16[2,1,256,512]{3,2,1,0:T(8,128)(2,1)S(1)} collective-permute-done((bf16[2,1,256,512]{3,2,1,0:T(8,128)(2,1)S(1)}, bf16[2,1,256,512]{3,2,1,0:T(8,128)(2,1)S(1)}, u32[]{:S(2)}, u32[]{:S(2)}) %collective-permute-start.16) | collective-permute-done | bytes 524320 | tf_op jit(solution)/shard_map/third1a/ppermute | solution.py:338
  81.4 1.4 %multiply_third.1.refs_3_ = bf16[2,1,256,512]{3,2,1,0:T(8,128)(2,1)S(1)} custom-call(s32[2,3]{1,0:T(2,128)S(1)} %copy-done.2, bf16[2,512,512]{2,1,0:T(8,128)(2,1)S(1)} %copy-done, bf16[2,256,512]{2,1,0:T(8,128)(2,1)S(1)} %settle_extra.1.refs_1_.refs_2_, bf16[2,256,512]{2,1,0:T(8,128)(2,1)S(1)} %collective-permute-done.14.refs_2_.refs_3_, ...), custom_call_target="tpu_custom_call" | custom-call | flops 402653184 | bytes 3145752 | tf_op jit(solution)/shard_map/multiply_third/pallas_call | solution.py:307
  82.9 3.4 %update_stays.1.refs_8_ = bf16[3,512,512]{2,1,0:T(8,128)(2,1)} custom-call(s32[2,3]{1,0:T(2,128)S(1)} %copy-done.2, bf16[2,512,512]{2,1,0:T(8,128)(2,1)S(1)} %get-tuple-element.27.refs_8_.refs_1_, bf16[2,2,256,512]{3,2,1,0:T(8,128)(2,1)S(1)} %multiply_stays.1.refs_6_.refs_2_, bf16[2,2,256,512]{3,2,1,0:T(8,128)(2,1)S(1)} %collective-permute-done.18.refs_3_, ...), custom_call_target="tpu_custom_call" | custom-call | flops 1073741824 | bytes 4718616 | tf_op jit(solution)/shard_map/update_stays/pallas_call | solution.py:307
  86.3 2.4 %update_third.1 = bf16[3,512,512]{2,1,0:T(8,128)(2,1)} custom-call(s32[2,3]{1,0:T(2,128)S(1)} %copy-done.2, bf16[2,512,512]{2,1,0:T(8,128)(2,1)S(1)} %get-tuple-element.27.refs_8_.refs_1_, bf16[512,512]{1,0:T(8,128)(2,1)S(1)} %get-tuple-element.28.refs_2_, bf16[2,1,256,512]{3,2,1,0:T(8,128)(2,1)S(1)} %multiply_third.1.refs_3_, ...), custom_call_target="tpu_custom_call", output_to_operand_aliasing={{}: (8, {})} | custom-call | flops 536870912 | bytes 6291480 | tf_op jit(solution)/shard_map/update_third/pallas_call | solution.py:307
  (39 shorter events, 10.2 us)
Async XLA Ops:
  0.0 1.4 %copy-start.1 = (bf16[3,512,1,512]{3,1,2,0:T(8,128)(2,1)S(1)}, bf16[3,512,1,512]{3,1,2,0:T(8,128)(2,1)}, u32[]{:S(2)}) copy-start(bf16[3,512,1,512]{3,1,2,0:T(8,128)(2,1)} %param.4) | copy-start | bytes 4718596
  1.4 0.7 copy-start.2
  2.1 0.7 copy-start.3
  3.6 2.4 %collective-permute-start = (bf16[3,256,512]{2,1,0:T(8,128)(2,1)S(1)}, bf16[3,256,512]{2,1,0:T(8,128)(2,1)S(1)}, u32[]{:S(2)}, u32[]{:S(2)}) collective-permute-start(bf16[3,256,512]{2,1,0:T(8,128)(2,1)S(1)} %get-tuple-element.18), channel_id=1, source_target_pairs={{0,1},{1,0},{2,3},{3,2},{4,5},{5,4},{6,7},{7,6},{8,9},{9,8},{10,11... | collective-permute-start | bytes 2359304 | tf_op jit(solution)/shard_map/sib_early/ppermute | solution.py:330
  6.6 8.3 %collective-permute-start.1 = (bf16[256,512]{1,0:T(8,128)(2,1)S(1)}, bf16[256,512]{1,0:T(8,128)(2,1)S(1)}, u32[]{:S(2)}, u32[]{:S(2)}) collective-permute-start(bf16[256,512]{1,0:T(8,128)(2,1)S(1)} %pick_extra.1.refs_3_.refs_1_), channel_id=1, source_target_pairs={{0,2},{1,5},{2,0},{3,7},{4,6},{5,1},{6,4},{7,3},{8,10},{9,13},{10,... | collective-permute-start | bytes 786440 | tf_op jit(solution)/shard_map/extra0a/ppermute | solution.py:338
  10.2 23.6 %collective-permute-start.7 = (bf16[2,256,512]{2,1,0:T(8,128)(2,1)S(1)}, bf16[2,256,512]{2,1,0:T(8,128)(2,1)S(1)}, u32[]{:S(2)}, u32[]{:S(2)}) collective-permute-start(bf16[2,256,512]{2,1,0:T(8,128)(2,1)S(1)} %get-tuple-element.22.refs_2_), channel_id=1, source_target_pairs={{0,2},{1,5},{2,0},{3,7},{4,6},{5,1},{6,4},{7,3},{8,10},{9,13},{10,... | collective-permute-start | bytes 1572872 | tf_op jit(solution)/shard_map/stays0b/ppermute | solution.py:338
  10.3 23.5 %collective-permute-start.6 = (bf16[2,256,512]{2,1,0:T(8,128)(2,1)S(1)}, bf16[2,256,512]{2,1,0:T(8,128)(2,1)S(1)}, u32[]{:S(2)}, u32[]{:S(2)}) collective-permute-start(bf16[2,256,512]{2,1,0:T(8,128)(2,1)S(1)} %get-tuple-element.19.refs_3_.refs_1_), channel_id=1, source_target_pairs={{0,2},{1,5},{2,0},{3,7},{4,6},{5,1},{6,4},{7,3},{8,10},{9,13},{10,... | collective-permute-start | bytes 1572872 | tf_op jit(solution)/shard_map/stays0a/ppermute | solution.py:338
  12.3 20.8 %collective-permute-start.3 = (bf16[256,512]{1,0:T(8,128)(2,1)S(1)}, bf16[256,512]{1,0:T(8,128)(2,1)S(1)}, u32[]{:S(2)}, u32[]{:S(2)}) collective-permute-start(bf16[256,512]{1,0:T(8,128)(2,1)S(1)} %get-tuple-element.20.refs_0_.refs_3_), channel_id=1, source_target_pairs={{0,16},{24,8},{16,0},{8,24},{1,17},{25,9},{17,1},{9,25},{2,18},{26... | collective-permute-start | bytes 786440 | tf_op jit(solution)/shard_map/swapa/ppermute | solution.py:326
  15.5 17.7 %collective-permute-start.2 = (bf16[256,512]{1,0:T(8,128)(2,1)S(1)}, bf16[256,512]{1,0:T(8,128)(2,1)S(1)}, u32[]{:S(2)}, u32[]{:S(2)}) collective-permute-start(bf16[256,512]{1,0:T(8,128)(2,1)S(1)} %pass_extra.1.refs_2_.refs_1_), channel_id=1, source_target_pairs={{0,4},{1,3},{2,6},{3,1},{4,0},{5,7},{6,2},{7,5},{8,12},{9,11},{10,... | collective-permute-start | bytes 786440 | tf_op jit(solution)/shard_map/extra1a/ppermute | solution.py:338
  17.1 20.5 %collective-permute-start.5 = (bf16[256,512]{1,0:T(8,128)(2,1)S(1)}, bf16[256,512]{1,0:T(8,128)(2,1)S(1)}, u32[]{:S(2)}, u32[]{:S(2)}) collective-permute-start(bf16[256,512]{1,0:T(8,128)(2,1)S(1)} %get-tuple-element.21.refs_0_.refs_6_), channel_id=1, source_target_pairs={{0,16},{24,8},{16,0},{8,24},{1,17},{25,9},{17,1},{9,25},{2,18},{26... | collective-permute-start | bytes 786440 | tf_op jit(solution)/shard_map/swapb/ppermute | solution.py:326
  34.4 9.2 %collective-permute-start.10 = (bf16[2,256,512]{2,1,0:T(8,128)(2,1)S(1)}, bf16[2,256,512]{2,1,0:T(8,128)(2,1)S(1)}, u32[]{:S(2)}, u32[]{:S(2)}) collective-permute-start(bf16[2,256,512]{2,1,0:T(8,128)(2,1)S(1)} %get-tuple-element.23.refs_3_.refs_4_), channel_id=1, source_target_pairs={{0,4},{1,3},{2,6},{3,1},{4,0},{5,7},{6,2},{7,5},{8,12},{9,11},{10,... | collective-permute-start | bytes 1572872 | tf_op jit(solution)/shard_map/stays1a/ppermute | solution.py:338
  35.0 6.7 %collective-permute-start.4 = (bf16[256,512]{1,0:T(8,128)(2,1)S(1)}, bf16[256,512]{1,0:T(8,128)(2,1)S(1)}, u32[]{:S(2)}, u32[]{:S(2)}) collective-permute-start(bf16[256,512]{1,0:T(8,128)(2,1)S(1)} %extra_here.1.refs_5_.refs_0_.refs_2_), channel_id=1, source_target_pairs={{0,16},{24,8},{1,17},{25,9},{2,18},{26,10},{3,19},{27,11},{4,20},{... | collective-permute-start | bytes 786440 | tf_op jit(solution)/shard_map/extra_z2/ppermute | solution.py:326
  37.6 4.1 %collective-permute-start.9 = (bf16[256,512]{1,0:T(8,128)(2,1)S(1)}, bf16[256,512]{1,0:T(8,128)(2,1)S(1)}, u32[]{:S(2)}, u32[]{:S(2)}) collective-permute-start(bf16[256,512]{1,0:T(8,128)(2,1)S(1)} %get-tuple-element.25), channel_id=1, source_target_pairs={{0,1},{1,0},{2,3},{3,2},{4,5},{5,4},{6,7},{7,6},{8,9},{9,8},{10,11... | collective-permute-start | bytes 786440 | tf_op jit(solution)/shard_map/sib_moved/ppermute | solution.py:330
  37.7 17.2 %collective-permute-start.13 = (bf16[2,256,512]{2,1,0:T(8,128)(2,1)S(1)}, bf16[2,256,512]{2,1,0:T(8,128)(2,1)S(1)}, u32[]{:S(2)}, u32[]{:S(2)}) collective-permute-start(bf16[2,256,512]{2,1,0:T(8,128)(2,1)S(1)} %get-tuple-element.26.refs_5_), channel_id=1, source_target_pairs={{0,4},{1,3},{2,6},{3,1},{4,0},{5,7},{6,2},{7,5},{8,12},{9,11},{10,... | collective-permute-start | bytes 1572872 | tf_op jit(solution)/shard_map/stays1b/ppermute | solution.py:338
  44.3 14.9 %copy-start = (bf16[2,512,512]{2,1,0:T(8,128)(2,1)S(1)}, bf16[2,512,512]{2,1,0:T(8,128)(2,1)}, u32[]{:S(2)}) copy-start(bf16[2,512,512]{2,1,0:T(8,128)(2,1)} %refs_1_.5) | copy-start | bytes 3145732
  44.3 10.6 %collective-permute-start.11 = (bf16[2,1,256,512]{3,2,1,0:T(8,128)(2,1)S(1)}, bf16[2,1,256,512]{3,2,1,0:T(8,128)(2,1)S(1)}, u32[]{:S(2)}, u32[]{:S(2)}) collective-permute-start(bf16[2,1,256,512]{3,2,1,0:T(8,128)(2,1)S(1)} %pick_third.1.refs_1_), channel_id=1, source_target_pairs={{0,2},{1,5},{2,0},{3,7},{4,6},{5,1},{6,4},{7,3},{8,10},{9,13},{10,... | collective-permute-start | bytes 1572872 | tf_op jit(solution)/shard_map/third0a/ppermute | solution.py:338
  45.0 10.0 %collective-permute-start.12 = (bf16[256,512]{1,0:T(8,128)(2,1)S(1)}, bf16[256,512]{1,0:T(8,128)(2,1)S(1)}, u32[]{:S(2)}, u32[]{:S(2)}) collective-permute-start(bf16[256,512]{1,0:T(8,128)(2,1)S(1)} %hand_on_a.1.refs_3_), channel_id=1, source_target_pairs={{0,8},{24,16},{16,24},{8,0},{1,9},{25,17},{17,25},{9,1},{2,10},{26... | collective-permute-start | bytes 786440 | tf_op jit(solution)/shard_map/row1a/ppermute | solution.py:326
  47.8 11.5 %collective-permute-start.8 = (bf16[256,512]{1,0:T(8,128)(2,1)S(1)}, bf16[256,512]{1,0:T(8,128)(2,1)S(1)}, u32[]{:S(2)}, u32[]{:S(2)}) collective-permute-start(bf16[256,512]{1,0:T(8,128)(2,1)S(1)} %hand_on.1.refs_6_), channel_id=1, source_target_pairs={{0,8},{24,16},{16,24},{8,0},{1,9},{25,17},{17,25},{9,1},{2,10},{26... | collective-permute-start | bytes 786440 | tf_op jit(solution)/shard_map/extra_z1/ppermute | solution.py:326
  60.2 8.8 %collective-permute-start.14 = (bf16[2,256,512]{2,1,0:T(8,128)(2,1)S(1)}, bf16[2,256,512]{2,1,0:T(8,128)(2,1)S(1)}, u32[]{:S(2)}, u32[]{:S(2)}) collective-permute-start(bf16[2,256,512]{2,1,0:T(8,128)(2,1)S(1)} %settle_extra.1.refs_1_.refs_2_), channel_id=1, source_target_pairs={{0,1},{1,0},{2,3},{3,2},{4,5},{5,4},{6,7},{7,6},{8,9},{9,8},{10,11... | collective-permute-start | bytes 1572872 | tf_op jit(solution)/shard_map/sib_vl/ppermute | solution.py:330
  60.3 8.7 %collective-permute-start.15 = (bf16[256,512]{1,0:T(8,128)(2,1)S(1)}, bf16[256,512]{1,0:T(8,128)(2,1)S(1)}, u32[]{:S(2)}, u32[]{:S(2)}) collective-permute-start(bf16[256,512]{1,0:T(8,128)(2,1)S(1)} %get-tuple-element.24.refs_2_), channel_id=1, source_target_pairs={{0,8},{24,16},{16,24},{8,0},{1,9},{25,17},{17,25},{9,1},{2,10},{26... | collective-permute-start | bytes 786440 | tf_op jit(solution)/shard_map/row1b/ppermute | solution.py:326
  72.1 10.8 %collective-permute-start.18 = (bf16[2,2,256,512]{3,2,1,0:T(8,128)(2,1)S(1)}, bf16[2,2,256,512]{3,2,1,0:T(8,128)(2,1)S(1)}, u32[]{:S(2)}, u32[]{:S(2)}) collective-permute-start(bf16[2,2,256,512]{3,2,1,0:T(8,128)(2,1)S(1)} %multiply_stays.1.refs_6_.refs_2_), channel_id=1, source_target_pairs={{0,1},{1,0},{2,3},{3,2},{4,5},{5,4},{6,7},{7,6},{8,9},{9,8},{10,11... | collective-permute-start | bytes 3145736 | tf_op jit(solution)/shard_map/sib_mine/ppermute | solution.py:330
  72.2 9.2 %collective-permute-start.16 = (bf16[2,1,256,512]{3,2,1,0:T(8,128)(2,1)S(1)}, bf16[2,1,256,512]{3,2,1,0:T(8,128)(2,1)S(1)}, u32[]{:S(2)}, u32[]{:S(2)}) collective-permute-start(bf16[2,1,256,512]{3,2,1,0:T(8,128)(2,1)S(1)} %pass_third.1.refs_5_.refs_4_), channel_id=1, source_target_pairs={{0,4},{1,3},{2,6},{3,1},{4,0},{5,7},{6,2},{7,5},{8,12},{9,11},{10,... | collective-permute-start | bytes 1572872 | tf_op jit(solution)/shard_map/third1a/ppermute | solution.py:338
  82.8 3.5 %collective-permute-start.17 = (bf16[2,1,256,512]{3,2,1,0:T(8,128)(2,1)S(1)}, bf16[2,1,256,512]{3,2,1,0:T(8,128)(2,1)S(1)}, u32[]{:S(2)}, u32[]{:S(2)}) collective-permute-start(bf16[2,1,256,512]{3,2,1,0:T(8,128)(2,1)S(1)} %multiply_third.1.refs_3_), channel_id=1, source_target_pairs={{0,1},{1,0},{2,3},{3,2},{4,5},{5,4},{6,7},{7,6},{8,9},{9,8},{10,11... | collective-permute-start | bytes 1572872 | tf_op jit(solution)/shard_map/sib_third/ppermute | solution.py:330

commit v7 on v5

--- a/solution.py
+++ b/solution.py
@@ -95,18 +95,17 @@
 
         @pl.when(f["is_end"])
         def _():
-            either(hit, panel.at[q, 0], lambda: moved[cut, :], lambda: sib_moved[cut, :])
+            either(hit, panel.at[q, 0], lambda: moved[cut, :], lambda: sib_moved[...])
 
         @pl.when(jnp.logical_not(f["is_end"]))
         def _():
             either(hit, panel.at[q, 0], lambda: raw[rb - 1, cut, :], lambda: sib[rb - 1])
 
 
-def relay(n, m, moved, out, *halves):
-    out[...] = moved[...]
-    half = moved.shape[0] // 2
-    for p, ref in enumerate(halves):
-        ref[...] = moved[p * half : (p + 1) * half, :]
+def relay(n, m, stride, leaving, moved, other, send):
+    core = lax.axis_index("pcol").astype(jnp.int32) & 1
+    other[...] = moved[rows(1 - core, moved.shape[0] // 2), :]
+    hand_on(n, m, stride, leaving, moved, send)
 
 
 def bit_of(f, column, stage, stages):
@@ -167,43 +166,38 @@
 
 
 def multiply(n, m, stages, piv, inv, vl, sib_vl, *refs):
-    panels, out, v = refs[:-2], refs[-2], refs[-1]
+    panels, third, third_got, out, v = refs[:-4], refs[-4], refs[-3], refs[-2], refs[-1]
     f = facts(n, m, 2, piv)
     half = vl.shape[1]
     v[rows(f["core"], half), :] = vl[0]
     v[rows(1 - f["core"], half), :] = sib_vl[0]
-    count = len(panels) // 2
+    count = out.shape[1] - 1
     for q in range(2):
         take = bit_of(f, f["c"][q], stages - 1, stages)
-        had, got = pair(panels[:count])[q], pair(panels[count:])[q]
-        either(take, out.at[q], lambda: got[...], lambda: had[...])
-    for k in range(out.shape[1]):
+        had, got = panels[q], panels[2 + q]
+        either(take, out.at[q, :count], lambda: got[...], lambda: had[...])
+        either(take, out.at[q, count], lambda: third_got[q, 0], lambda: third[q, 0])
+    for k in range(count + 1):
         m0 = dot(out[0, k], inv[0]).astype(out.dtype)
         p1 = (out[1, k].astype(jnp.float32) - dot(m0, v[...])).astype(out.dtype)
         out[0, k] = m0
         out[1, k] = dot(p1, inv[1]).astype(out.dtype)
 
 
-def settle_rows(n, m, piv, vl, sib_vl, leaving, moved, *refs):
-    hops, upper, lefts = refs[:-2], refs[-2], refs[-1]
-    width = leaving.shape[0]
-    half = width // 2
+def settle_rows(n, m, piv, vl, sib_vl, *refs):
+    came, upper, lefts = refs[:-2], refs[-2], refs[-1]
+    half = came[0].shape[0] // 2
     f = facts(n, m, 2, piv)
     r = f["r"]
     for which in range(2):
         place = r if which == 0 else n - 1 - r
         slot = jnp.where(f["low_first"], which, 1 - which)
-        for h in range(n):
-
-            @pl.when(place == h)
+        for s in range(len(came)):
+            here = place == 0 if s == 0 else (place & (2 * (n >> s) - 1)) == (n >> s)
+
+            @pl.when(here)
             def _():
-                if h == 0:
-                    upper[slot] = leaving[...]
-                elif h == 1:
-                    upper[slot] = moved[...]
-                else:
-                    upper[slot, :half, :] = hops[2 * (h - 2)][...]
-                    upper[slot, half:, :] = hops[2 * (h - 2) + 1][...]
+                upper[slot] = came[s][...]
 
     lefts[rows(f["core"], half), :] = vl[1]
     lefts[rows(1 - f["core"], half), :] = sib_vl[1]
@@ -239,7 +233,7 @@
             new[cut, :] = w.astype(new.dtype)
 
 
-def update_stays(n, m, piv, upper, mine, sib, raw, out, new, sems):
+def finish(n, m, piv, upper, lefts, mine, sib, raw, moved, out, old, new, sems):
     rb = raw.shape[0]
     f = facts(n, m, rb, piv)
     copies = []
@@ -247,34 +241,28 @@
         update(f, upper, mine, sib, (k,), raw.at[k], new.at[k])
         copies.append(pltpu.make_async_copy(new.at[k], out.at[f["slots"][k]], sems.at[k]))
         copies[-1].start()
-    for copy in copies:
-        copy.wait()
-
-
-def update_third(n, m, piv, upper, lefts, mine, sib, raw, moved, so_far, out, old, new, sem):
-    del so_far
-    rb = raw.shape[0]
-    f = facts(n, m, rb, piv)
+    k = rb - 1
     low_first = f["low_first"]
     first = jnp.where(low_first, f["is_low"], f["is_high"])
     second = jnp.where(low_first, f["is_high"], f["is_low"])
 
     @pl.when(first)
     def _():
-        new[...] = upper[0]
+        new[k] = upper[0]
 
     @pl.when(second)
     def _():
-        either(f["j"] == f["c"][0], new, lambda: lefts[...], lambda: upper[1])
+        either(f["j"] == f["c"][0], new.at[k], lambda: lefts[...], lambda: upper[1])
 
     @pl.when(jnp.logical_not(jnp.logical_or(first, second)))
     def _():
-        either(f["is_end"], old, lambda: moved[...], lambda: raw[rb - 1])
-        update(f, upper, mine, sib, (0,), old, new)
-
-    copy = pltpu.make_async_copy(new, out.at[f["slots"][rb - 1]], sem)
-    copy.start()
-    copy.wait()
+        either(f["is_end"], old, lambda: moved[...], lambda: raw[k])
+        update(f, upper, mine, sib, (k,), old, new.at[k])
+
+    copies.append(pltpu.make_async_copy(new.at[k], out.at[f["slots"][k]], sems.at[k]))
+    copies[-1].start()
+    for copy in copies:
+        copy.wait()
 
 
 def local(matrix, pattern, inverses, pivots):
@@ -353,55 +341,55 @@
         pattern.T,
         blocks,
     )
-    moved = along("swap", [(0, 1), (n - 1, n - 2), (n // 2, 0), (n // 2 - 1, n - 1)], leaving)
     early = sibling("sib_early", other)
+    exchange = [(0, n // 2), (n - 1, n // 2 - 1), (n // 2, 0), (n // 2 - 1, n - 1)]
+    moved = along("swap", exchange, leaving)
+
+    def split(stride):
+        pairs = []
+        for i in range(0, n, 2 * stride):
+            pairs += [(i, i + stride), (n - 1 - i, n - 1 - i - stride)]
+        return pairs
 
     extra = call(pick_extra, [strip], "s", pivots, raw, early)
     panel = call(pick, [(rb - 1, *strip)] * 2, "s", pivots, raw, early, after=[extra])
     got_extra = cross("extra", 0, [extra])
     got_stays = cross("stays", 0, panel)
     had, got = passing("extra", forward_extra, [extra], got_extra, after=[panel[0]])
+    hand = lambda stride: lambda _n, _m, *refs: hand_on(n, m, stride, *refs)
     step = lambda _n, _m, *refs: forward_extra(n, m, stages - 1, stages, *refs)
-    extra_here = call(
-        step, [strip], "s", pivots, had, got, after=[got_stays[0]], name="extra_here"
-    )
-    moved, *parts = call(relay, [square, strip, strip], "", moved, after=[extra_here])
-
-    sib_moved = sibling("sib_moved", moved)
+    extra_here = call(step, [strip], "s", pivots, had, got, name="extra_here")
+    stays = passing("stays", forward, panel, got_stays, after=[extra_here])
+
+    step = lambda _n, _m, *refs: relay(n, m, n // 2, *refs)
+    other_moved, send = call(
+        step, [strip, square], "", leaving, moved, name="relay", after=[stays[0]]
+    )
+    sib_moved = sibling("sib_moved", other_moved)
     third = call(
-        pick_third, [(2, 1, *strip)], "s", pivots, raw, early, moved, sib_moved
+        pick_third, [(2, 1, *strip)], "s", pivots, raw, early, moved, sib_moved, after=stays[2:]
     )
     got_third = cross("third", 0, [third])
-    stays = passing("stays", forward, panel, got_stays, after=[third])
-
-    hops = []
-    for h in range(1, n - 1):
-        pairs = [(h, h + 1), (n - 1 - h, n - 2 - h)]
-        parts = [along("row" + str(h) + "ab"[i], pairs, part) for i, part in enumerate(parts)]
-        hops += parts
+
+    arrived = [leaving, moved]
+    stride = n // 4
+    while stride:
+        got = along("row" + str(stride), split(stride), send)
+        arrived.append(got)
+        if stride > 1:
+            send = call(hand(stride), [square], "", send, got, name="hand_on_row")
+        stride //= 2
 
     came = [extra_here]
     send = extra_here
     stride = n // 2
     while stride:
-        pairs = []
-        for i in range(0, n, 2 * stride):
-            pairs += [(i, i + stride), (n - 1 - i, n - 1 - i - stride)]
-        got = along("extra_z" + str(stride), pairs, send)
+        got = along("extra_z" + str(stride), split(stride), send)
         came.append(got)
         if stride > 1:
-            step = lambda _n, _m, *refs: hand_on(n, m, stride, *refs)
-            send = call(
-                step,
-                [strip],
-                "",
-                send,
-                got,
-                name="hand_on",
-                after=[stays[0]],
-            )
+            send = call(hand(stride), [strip], "", send, got, name="hand_on", after=[third])
         stride //= 2
-    third = passing("third", forward, [third], got_third, after=[send, hops[0]])
+    third = passing("third", forward, [third], got_third, after=[send])
     vl = call(
         settle_extra,
         [(2, *strip)],
@@ -410,24 +398,23 @@
         inverses,
         *came,
         products=0.5,
-        after=[third[0], hops[1]],
+        after=[third[0], arrived[2]],
     )
     sib_vl = sibling("sib_vl", vl)
-
     step = lambda _n, _m, *refs: multiply(n, m, stages, *refs)
     mine = call(
         step,
-        [(2, rb - 1, *strip)],
+        [(2, rb, *strip)],
         "s",
         pivots,
         inverses,
         vl,
         sib_vl,
         *stays,
+        *third,
         scratch=[square],
-        products=3 * (rb - 1) / 2,
-        name="multiply_stays",
-        after=[hops[2], third[1]],
+        products=3 * rb / 2,
+        name="multiply",
     )
     sib_mine = sibling("sib_mine", mine)
     upper, lefts = call(
@@ -437,55 +424,23 @@
         pivots,
         vl,
         sib_vl,
-        leaving,
-        moved,
-        *hops,
+        *arrived,
         products=1,
         after=[mine],
     )
-    mine_third = call(
-        step,
-        [(2, 1, *strip)],
-        "s",
-        pivots,
-        inverses,
-        vl,
-        sib_vl,
-        *third,
-        scratch=[square],
-        products=1.5,
-        after=[upper],
-        name="multiply_third",
-    )
-    sib_third = sibling("sib_third", mine_third)
     result = call(
-        update_stays,
+        finish,
         [blocks.shape],
         "s",
         pivots,
         upper,
+        lefts,
         mine,
         sib_mine,
         raw,
-        scratch=[(rb - 1, *square), pltpu.SemaphoreType.DMA((rb - 1,))],
-        products=2 * (rb - 1),
-        place=ANY,
-    )
-    result = call(
-        update_third,
-        [blocks.shape],
-        "svvvvvva",
-        pivots,
-        upper,
-        lefts,
-        mine_third,
-        sib_third,
-        raw,
         moved,
-        result,
-        scratch=[square, square, pltpu.SemaphoreType.DMA],
-        aliases={7: 0},
-        products=2,
+        scratch=[square, (rb, *square), pltpu.SemaphoreType.DMA((rb,))],
+        products=2 * rb,
         place=ANY,
     )
     return result.reshape(matrix.shape)

time: 83.4 us -> 84.8 us (1.017)
  waiting for transfers between devices: 40 us -> 44.2 us
  Pallas kernels: 16.3 us -> 14.2 us
    ppermute x5 -> x4, waiting for transfers between devices: 2.2 us -> 7.46 us  [sibling(): return lax.ppermute(value, 'pcol', [(i, i ^ 1) for i in range(m)])]
    ppermute x7 -> x4, waiting for transfers between devices: 30.5 us -> 26.7 us  [along(): return lax.ppermute(value, 'prow', pairs)]
    ppermute x8, waiting for transfers between devices: 7.3 us -> 10 us  [across(): return lax.ppermute(value, 'pcol', pairs)]
    ppermute x7 -> x4, starting transfers between devices: 12.3 us -> 9.6 us  [along(): return lax.ppermute(value, 'prow', pairs)]
    ppermute x8, starting transfers between devices: 10.4 us -> 13 us  [across(): return lax.ppermute(value, 'pcol', pairs)]
    pallas_call x16 -> x14, Pallas kernels: 16.3 us -> 14.2 us  [call(): pl.pallas_call(body, out_shape=outs, in_specs=specs, out_specs=[place] *...]
  transfers between devices with their start and end apart: 20 -> 16, of which waited for: 11 -> 12; matrix products, arithmetic and copies ran while one was open for 0% -> 0% of each run, Pallas kernels for 13% -> 6%
where the time goes in v7:
time: 84.8 us
  waiting for transfers between devices  44.2 us (52%)
  starting transfers between devices  23.4 us (28%)
  Pallas kernels  14.2 us (17%)
  local copies, waits for them, and re-layouts  2.78 us (3%)
    ppermute x4, waiting for transfers between devices, along(): return lax.ppermute(value, 'prow', pairs)  26.7 us
    pallas_call x14, Pallas kernels, call(): pl.pallas_call(body, out_shape=outs, in_specs=specs, out_specs=[place] *...  14.2 us
    ppermute x8, starting transfers between devices, across(): return lax.ppermute(value, 'pcol', pairs)  13 us
    ppermute x8, waiting for transfers between devices, across(): return lax.ppermute(value, 'pcol', pairs)  10 us
    ppermute x4, starting transfers between devices, along(): return lax.ppermute(value, 'prow', pairs)  9.6 us
    ppermute x4, waiting for transfers between devices, sibling(): return lax.ppermute(value, 'pcol', [(i, i ^ 1) for i in range(m)])  7.46 us
    unnamed x8, local copies, waits for them, and re-layouts  2.78 us
  transfers between devices with their start and end apart: 16, of which 12 were waited for; matrix products, arithmetic and copies ran while one was open for 0% of the time, Pallas kernels for 6%

profile of v7, /device:TPU:0, one launch (start us, length us, event | category | flops | bytes accessed | tf_op | source)
XLA Modules:
  0.0 84.8 jit_solution(18173158933374866957)
XLA Ops:
  0.0 1.4 %copy-done.1 = bf16[3,512,1,512]{3,1,2,0:T(8,128)(2,1)S(1)} copy-done((bf16[3,512,1,512]{3,1,2,0:T(8,128)(2,1)S(1)}, bf16[3,512,1,512]{3,1,2,0:T(8,128)(2,1)}, u32[]{:S(2)}) %copy-start.1) | copy-done | bytes 1572888
  4.1 1.9 %collective-permute-done.refs_2_ = bf16[3,256,512]{2,1,0:T(8,128)(2,1)S(1)} collective-permute-done((bf16[3,256,512]{2,1,0:T(8,128)(2,1)S(1)}, bf16[3,256,512]{2,1,0:T(8,128)(2,1)S(1)}, u32[]{:S(2)}, u32[]{:S(2)}) %collective-permute-start) | collective-permute-done | bytes 786464 | tf_op jit(solution)/shard_map/sib_early/ppermute | solution.py:311
  6.6 2.9 %collective-permute-start.1 = (bf16[256,512]{1,0:T(8,128)(2,1)S(1)}, bf16[256,512]{1,0:T(8,128)(2,1)S(1)}, u32[]{:S(2)}, u32[]{:S(2)}) collective-permute-start(bf16[256,512]{1,0:T(8,128)(2,1)S(1)} %pick_extra.1.refs_3_.refs_1_), channel_id=1, source_target_pairs={{0,2},{1,5},{2,0},{3,7},{4,6},{5,1},{6,4},{7,3},{8,10},{9,13},{10,... | collective-permute-start | bytes 786440 | tf_op jit(solution)/shard_map/extra0a/ppermute | solution.py:319
  10.3 2.0 %collective-permute-start.5 = (bf16[2,256,512]{2,1,0:T(8,128)(2,1)S(1)}, bf16[2,256,512]{2,1,0:T(8,128)(2,1)S(1)}, u32[]{:S(2)}, u32[]{:S(2)}) collective-permute-start(bf16[2,256,512]{2,1,0:T(8,128)(2,1)S(1)} %get-tuple-element.18.refs_3_.refs_1_), channel_id=1, source_target_pairs={{0,2},{1,5},{2,0},{3,7},{4,6},{5,1},{6,4},{7,3},{8,10},{9,13},{10,... | collective-permute-start | bytes 1572872 | tf_op jit(solution)/shard_map/stays0a/ppermute | solution.py:319
  12.3 1.6 %collective-permute-done.1.refs_2_ = bf16[256,512]{1,0:T(8,128)(2,1)S(1)} collective-permute-done((bf16[256,512]{1,0:T(8,128)(2,1)S(1)}, bf16[256,512]{1,0:T(8,128)(2,1)S(1)}, u32[]{:S(2)}, u32[]{:S(2)}) %collective-permute-start.1) | collective-permute-done | bytes 262176 | tf_op jit(solution)/shard_map/extra0a/ppermute | solution.py:319
  14.5 2.1 %collective-permute-start.2 = (bf16[256,512]{1,0:T(8,128)(2,1)S(1)}, bf16[256,512]{1,0:T(8,128)(2,1)S(1)}, u32[]{:S(2)}, u32[]{:S(2)}) collective-permute-start(bf16[256,512]{1,0:T(8,128)(2,1)S(1)} %pass_extra.1.refs_1_), channel_id=1, source_target_pairs={{0,4},{1,3},{2,6},{3,1},{4,0},{5,7},{6,2},{7,5},{8,12},{9,11},{10,... | collective-permute-start | bytes 786440 | tf_op jit(solution)/shard_map/extra1a/ppermute | solution.py:319
  16.6 2.6 %collective-permute-start.4 = (bf16[512,512]{1,0:T(8,128)(2,1)S(1)}, bf16[512,512]{1,0:T(8,128)(2,1)S(1)}, u32[]{:S(2)}, u32[]{:S(2)}) collective-permute-start(bf16[512,512]{1,0:T(8,128)(2,1)S(1)} %get-tuple-element.19.refs_0_.refs_3_), channel_id=1, source_target_pairs={{0,16},{24,8},{16,0},{8,24},{1,17},{25,9},{17,1},{9,25},{2,18},{26... | collective-permute-start | bytes 1572872 | tf_op jit(solution)/shard_map/swap/ppermute | solution.py:307
  19.2 4.6 %collective-permute-done.2.refs_2_ = bf16[256,512]{1,0:T(8,128)(2,1)S(1)} collective-permute-done((bf16[256,512]{1,0:T(8,128)(2,1)S(1)}, bf16[256,512]{1,0:T(8,128)(2,1)S(1)}, u32[]{:S(2)}, u32[]{:S(2)}) %collective-permute-start.2) | collective-permute-done | bytes 262176 | tf_op jit(solution)/shard_map/extra1a/ppermute | solution.py:319
  24.5 3.5 %collective-permute-done.5.refs_3_ = bf16[2,256,512]{2,1,0:T(8,128)(2,1)S(1)} collective-permute-done((bf16[2,256,512]{2,1,0:T(8,128)(2,1)S(1)}, bf16[2,256,512]{2,1,0:T(8,128)(2,1)S(1)}, u32[]{:S(2)}, u32[]{:S(2)}) %collective-permute-start.5) | collective-permute-done | bytes 524320 | tf_op jit(solution)/shard_map/stays0a/ppermute | solution.py:319
  28.6 2.1 %collective-permute-start.9 = (bf16[2,256,512]{2,1,0:T(8,128)(2,1)S(1)}, bf16[2,256,512]{2,1,0:T(8,128)(2,1)S(1)}, u32[]{:S(2)}, u32[]{:S(2)}) collective-permute-start(bf16[2,256,512]{2,1,0:T(8,128)(2,1)S(1)} %get-tuple-element.23.refs_5_), channel_id=1, source_target_pairs={{0,4},{1,3},{2,6},{3,1},{4,0},{5,7},{6,2},{7,5},{8,12},{9,11},{10,... | collective-permute-start | bytes 1572872 | tf_op jit(solution)/shard_map/stays1b/ppermute | solution.py:319
  30.8 10.8 %collective-permute-done.4.refs_1_.refs_3_.refs_4_.refs_6_ = bf16[512,512]{1,0:T(8,128)(2,1)S(1)} collective-permute-done((bf16[512,512]{1,0:T(8,128)(2,1)S(1)}, bf16[512,512]{1,0:T(8,128)(2,1)S(1)}, u32[]{:S(2)}, u32[]{:S(2)}) %collective-permute-start.4) | collective-permute-done | bytes 524320 | tf_op jit(solution)/shard_map/swap/ppermute | solution.py:307
  41.7 1.5 %collective-permute-done.7.refs_4_ = bf16[256,512]{1,0:T(8,128)(2,1)S(1)} collective-permute-done((bf16[256,512]{1,0:T(8,128)(2,1)S(1)}, bf16[256,512]{1,0:T(8,128)(2,1)S(1)}, u32[]{:S(2)}, u32[]{:S(2)}) %collective-permute-start.7) | collective-permute-done | bytes 262176 | tf_op jit(solution)/shard_map/sib_moved/ppermute | solution.py:311
  44.1 2.1 %collective-permute-start.11 = (bf16[2,1,256,512]{3,2,1,0:T(8,128)(2,1)S(1)}, bf16[2,1,256,512]{3,2,1,0:T(8,128)(2,1)S(1)}, u32[]{:S(2)}, u32[]{:S(2)}) collective-permute-start(bf16[2,1,256,512]{3,2,1,0:T(8,128)(2,1)S(1)} %pick_third.1.refs_2_.refs_1_), channel_id=1, source_target_pairs={{0,2},{1,5},{2,0},{3,7},{4,6},{5,1},{6,4},{7,3},{8,10},{9,13},{10,... | collective-permute-start | bytes 1572872 | tf_op jit(solution)/shard_map/third0a/ppermute | solution.py:319
  46.2 4.5 %collective-permute-start.3 = (bf16[256,512]{1,0:T(8,128)(2,1)S(1)}, bf16[256,512]{1,0:T(8,128)(2,1)S(1)}, u32[]{:S(2)}, u32[]{:S(2)}) collective-permute-start(bf16[256,512]{1,0:T(8,128)(2,1)S(1)} %extra_here.1.refs_5_.refs_0_.refs_2_), channel_id=1, source_target_pairs={{0,16},{24,8},{1,17},{25,9},{2,18},{26,10},{3,19},{27,11},{4,20},{... | collective-permute-start | bytes 786440 | tf_op jit(solution)/shard_map/extra_z2/ppermute | solution.py:307
  50.8 6.6 %collective-permute-done.3.refs_1_.refs_3_ = bf16[256,512]{1,0:T(8,128)(2,1)S(1)} collective-permute-done((bf16[256,512]{1,0:T(8,128)(2,1)S(1)}, bf16[256,512]{1,0:T(8,128)(2,1)S(1)}, u32[]{:S(2)}, u32[]{:S(2)}) %collective-permute-start.3) | collective-permute-done | bytes 262176 | tf_op jit(solution)/shard_map/extra_z2/ppermute | solution.py:307
  57.4 2.4 %collective-permute-start.10 = (bf16[256,512]{1,0:T(8,128)(2,1)S(1)}, bf16[256,512]{1,0:T(8,128)(2,1)S(1)}, u32[]{:S(2)}, u32[]{:S(2)}) collective-permute-start(bf16[256,512]{1,0:T(8,128)(2,1)S(1)} %hand_on.1.refs_3_), channel_id=1, source_target_pairs={{0,8},{24,16},{16,24},{8,0},{1,9},{25,17},{17,25},{9,1},{2,10},{26... | collective-permute-start | bytes 786440 | tf_op jit(solution)/shard_map/extra_z1/ppermute | solution.py:307
  60.5 1.6 %collective-permute-start.14 = (bf16[2,1,256,512]{3,2,1,0:T(8,128)(2,1)S(1)}, bf16[2,1,256,512]{3,2,1,0:T(8,128)(2,1)S(1)}, u32[]{:S(2)}, u32[]{:S(2)}) collective-permute-start(bf16[2,1,256,512]{3,2,1,0:T(8,128)(2,1)S(1)} %pass_third.1.refs_5_.refs_8_), channel_id=1, source_target_pairs={{0,4},{1,3},{2,6},{3,1},{4,0},{5,7},{6,2},{7,5},{8,12},{9,11},{10,... | collective-permute-start | bytes 1572872 | tf_op jit(solution)/shard_map/third1a/ppermute | solution.py:319
  62.1 6.6 %collective-permute-done.12.refs_6_.refs_5_ = bf16[512,512]{1,0:T(8,128)(2,1)S(1)} collective-permute-done((bf16[512,512]{1,0:T(8,128)(2,1)S(1)}, bf16[512,512]{1,0:T(8,128)(2,1)S(1)}, u32[]{:S(2)}, u32[]{:S(2)}) %collective-permute-start.12) | collective-permute-done | bytes 524320 | tf_op jit(solution)/shard_map/row1/ppermute | solution.py:307
  68.6 2.8 %collective-permute-done.10.refs_4_ = bf16[256,512]{1,0:T(8,128)(2,1)S(1)} collective-permute-done((bf16[256,512]{1,0:T(8,128)(2,1)S(1)}, bf16[256,512]{1,0:T(8,128)(2,1)S(1)}, u32[]{:S(2)}, u32[]{:S(2)}) %collective-permute-start.10) | collective-permute-done | bytes 262176 | tf_op jit(solution)/shard_map/extra_z1/ppermute | solution.py:307
  72.5 1.9 %collective-permute-done.13.refs_3_.refs_2_ = bf16[2,256,512]{2,1,0:T(8,128)(2,1)S(1)} collective-permute-done((bf16[2,256,512]{2,1,0:T(8,128)(2,1)S(1)}, bf16[2,256,512]{2,1,0:T(8,128)(2,1)S(1)}, u32[]{:S(2)}, u32[]{:S(2)}) %collective-permute-start.13) | collective-permute-done | bytes 524320 | tf_op jit(solution)/shard_map/sib_vl/ppermute | solution.py:311
  74.3 2.6 %multiply.1.refs_6_.refs_3_ = bf16[2,3,256,512]{3,2,1,0:T(8,128)(2,1)S(1)} custom-call(s32[2,3]{1,0:T(2,128)S(1)} %copy-done.2, bf16[2,512,512]{2,1,0:T(8,128)(2,1)S(1)} %copy-done, bf16[2,256,512]{2,1,0:T(8,128)(2,1)S(1)} %settle_extra.1.refs_2_.refs_1_, bf16[2,256,512]{2,1,0:T(8,128)(2,1)S(1)} %collective-permute-done.13.refs_3_.refs_2_, ...), custom_call_target="tpu_custom_call" | custom-call | flops 1207959552 | bytes 5242904 | tf_op jit(solution)/shard_map/multiply/pallas_call | solution.py:288
  77.1 1.1 %settle_rows.1 = (bf16[2,512,512]{2,1,0:T(8,128)(2,1)S(1)}, bf16[512,512]{1,0:T(8,128)(2,1)S(1)}) custom-call(s32[2,3]{1,0:T(2,128)S(1)} %copy-done.2, bf16[2,256,512]{2,1,0:T(8,128)(2,1)S(1)} %settle_extra.1.refs_2_.refs_1_, bf16[2,256,512]{2,1,0:T(8,128)(2,1)S(1)} %collective-permute-done.13.refs_3_.refs_2_, ...), custom_call_target="tpu_custom_call" | custom-call | flops 268435456 | bytes 2621464 | tf_op jit(solution)/shard_map/settle_rows/pallas_call | solution.py:288
  78.2 2.1 %collective-permute-done.15.refs_4_ = bf16[2,3,256,512]{3,2,1,0:T(8,128)(2,1)S(1)} collective-permute-done((bf16[2,3,256,512]{3,2,1,0:T(8,128)(2,1)S(1)}, bf16[2,3,256,512]{3,2,1,0:T(8,128)(2,1)S(1)}, u32[]{:S(2)}, u32[]{:S(2)}) %collective-permute-start.15) | collective-permute-done | bytes 1572896 | tf_op jit(solution)/shard_map/sib_mine/ppermute | solution.py:311
  80.4 4.4 %finish.1 = bf16[3,512,512]{2,1,0:T(8,128)(2,1)} custom-call(s32[2,3]{1,0:T(2,128)S(1)} %copy-done.2, bf16[2,512,512]{2,1,0:T(8,128)(2,1)S(1)} %get-tuple-element.25.refs_1_, bf16[512,512]{1,0:T(8,128)(2,1)S(1)} %get-tuple-element.26.refs_2_, bf16[2,3,256,512]{3,2,1,0:T(8,128)(2,1)S(1)} %multiply.1.refs_6_.refs_3_, ...), custom_call_target="tpu_custom_call" | custom-call | flops 1610612736 | bytes 6815768 | tf_op jit(solution)/shard_map/finish/pallas_call | solution.py:288
  (30 shorter events, 8.9 us)
Async XLA Ops:
  0.0 1.4 %copy-start.1 = (bf16[3,512,1,512]{3,1,2,0:T(8,128)(2,1)S(1)}, bf16[3,512,1,512]{3,1,2,0:T(8,128)(2,1)}, u32[]{:S(2)}) copy-start(bf16[3,512,1,512]{3,1,2,0:T(8,128)(2,1)} %param.4) | copy-start | bytes 4718596
  1.4 0.7 copy-start.2
  2.1 0.7 copy-start.3
  3.6 2.4 %collective-permute-start = (bf16[3,256,512]{2,1,0:T(8,128)(2,1)S(1)}, bf16[3,256,512]{2,1,0:T(8,128)(2,1)S(1)}, u32[]{:S(2)}, u32[]{:S(2)}) collective-permute-start(bf16[3,256,512]{2,1,0:T(8,128)(2,1)S(1)} %get-tuple-element.17), channel_id=1, source_target_pairs={{0,1},{1,0},{2,3},{3,2},{4,5},{5,4},{6,7},{7,6},{8,9},{9,8},{10,11... | collective-permute-start | bytes 2359304 | tf_op jit(solution)/shard_map/sib_early/ppermute | solution.py:311
  6.6 7.3 %collective-permute-start.1 = (bf16[256,512]{1,0:T(8,128)(2,1)S(1)}, bf16[256,512]{1,0:T(8,128)(2,1)S(1)}, u32[]{:S(2)}, u32[]{:S(2)}) collective-permute-start(bf16[256,512]{1,0:T(8,128)(2,1)S(1)} %pick_extra.1.refs_3_.refs_1_), channel_id=1, source_target_pairs={{0,2},{1,5},{2,0},{3,7},{4,6},{5,1},{6,4},{7,3},{8,10},{9,13},{10,... | collective-permute-start | bytes 786440 | tf_op jit(solution)/shard_map/extra0a/ppermute | solution.py:319
  10.2 14.2 %collective-permute-start.6 = (bf16[2,256,512]{2,1,0:T(8,128)(2,1)S(1)}, bf16[2,256,512]{2,1,0:T(8,128)(2,1)S(1)}, u32[]{:S(2)}, u32[]{:S(2)}) collective-permute-start(bf16[2,256,512]{2,1,0:T(8,128)(2,1)S(1)} %get-tuple-element.20.refs_2_), channel_id=1, source_target_pairs={{0,2},{1,5},{2,0},{3,7},{4,6},{5,1},{6,4},{7,3},{8,10},{9,13},{10,... | collective-permute-start | bytes 1572872 | tf_op jit(solution)/shard_map/stays0b/ppermute | solution.py:319
  10.3 17.7 %collective-permute-start.5 = (bf16[2,256,512]{2,1,0:T(8,128)(2,1)S(1)}, bf16[2,256,512]{2,1,0:T(8,128)(2,1)S(1)}, u32[]{:S(2)}, u32[]{:S(2)}) collective-permute-start(bf16[2,256,512]{2,1,0:T(8,128)(2,1)S(1)} %get-tuple-element.18.refs_3_.refs_1_), channel_id=1, source_target_pairs={{0,2},{1,5},{2,0},{3,7},{4,6},{5,1},{6,4},{7,3},{8,10},{9,13},{10,... | collective-permute-start | bytes 1572872 | tf_op jit(solution)/shard_map/stays0a/ppermute | solution.py:319
  14.5 9.3 %collective-permute-start.2 = (bf16[256,512]{1,0:T(8,128)(2,1)S(1)}, bf16[256,512]{1,0:T(8,128)(2,1)S(1)}, u32[]{:S(2)}, u32[]{:S(2)}) collective-permute-start(bf16[256,512]{1,0:T(8,128)(2,1)S(1)} %pass_extra.1.refs_1_), channel_id=1, source_target_pairs={{0,4},{1,3},{2,6},{3,1},{4,0},{5,7},{6,2},{7,5},{8,12},{9,11},{10,... | collective-permute-start | bytes 786440 | tf_op jit(solution)/shard_map/extra1a/ppermute | solution.py:319
  16.6 24.9 %collective-permute-start.4 = (bf16[512,512]{1,0:T(8,128)(2,1)S(1)}, bf16[512,512]{1,0:T(8,128)(2,1)S(1)}, u32[]{:S(2)}, u32[]{:S(2)}) collective-permute-start(bf16[512,512]{1,0:T(8,128)(2,1)S(1)} %get-tuple-element.19.refs_0_.refs_3_), channel_id=1, source_target_pairs={{0,16},{24,8},{16,0},{8,24},{1,17},{25,9},{17,1},{9,25},{2,18},{26... | collective-permute-start | bytes 1572872 | tf_op jit(solution)/shard_map/swap/ppermute | solution.py:307
  28.6 14.6 %collective-permute-start.9 = (bf16[2,256,512]{2,1,0:T(8,128)(2,1)S(1)}, bf16[2,256,512]{2,1,0:T(8,128)(2,1)S(1)}, u32[]{:S(2)}, u32[]{:S(2)}) collective-permute-start(bf16[2,256,512]{2,1,0:T(8,128)(2,1)S(1)} %get-tuple-element.23.refs_5_), channel_id=1, source_target_pairs={{0,4},{1,3},{2,6},{3,1},{4,0},{5,7},{6,2},{7,5},{8,12},{9,11},{10,... | collective-permute-start | bytes 1572872 | tf_op jit(solution)/shard_map/stays1b/ppermute | solution.py:319
  30.7 12.8 %collective-permute-start.8 = (bf16[2,256,512]{2,1,0:T(8,128)(2,1)S(1)}, bf16[2,256,512]{2,1,0:T(8,128)(2,1)S(1)}, u32[]{:S(2)}, u32[]{:S(2)}) collective-permute-start(bf16[2,256,512]{2,1,0:T(8,128)(2,1)S(1)} %get-tuple-element.21.refs_2_.refs_4_), channel_id=1, source_target_pairs={{0,4},{1,3},{2,6},{3,1},{4,0},{5,7},{6,2},{7,5},{8,12},{9,11},{10,... | collective-permute-start | bytes 1572872 | tf_op jit(solution)/shard_map/stays1a/ppermute | solution.py:319
  41.6 1.6 %collective-permute-start.7 = (bf16[256,512]{1,0:T(8,128)(2,1)S(1)}, bf16[256,512]{1,0:T(8,128)(2,1)S(1)}, u32[]{:S(2)}, u32[]{:S(2)}) collective-permute-start(bf16[256,512]{1,0:T(8,128)(2,1)S(1)} %get-tuple-element.22), channel_id=1, source_target_pairs={{0,1},{1,0},{2,3},{3,2},{4,5},{5,4},{6,7},{7,6},{8,9},{9,8},{10,11... | collective-permute-start | bytes 786440 | tf_op jit(solution)/shard_map/sib_moved/ppermute | solution.py:311
  44.1 15.8 %collective-permute-start.11 = (bf16[2,1,256,512]{3,2,1,0:T(8,128)(2,1)S(1)}, bf16[2,1,256,512]{3,2,1,0:T(8,128)(2,1)S(1)}, u32[]{:S(2)}, u32[]{:S(2)}) collective-permute-start(bf16[2,1,256,512]{3,2,1,0:T(8,128)(2,1)S(1)} %pick_third.1.refs_2_.refs_1_), channel_id=1, source_target_pairs={{0,2},{1,5},{2,0},{3,7},{4,6},{5,1},{6,4},{7,3},{8,10},{9,13},{10,... | collective-permute-start | bytes 1572872 | tf_op jit(solution)/shard_map/third0a/ppermute | solution.py:319
  46.2 11.2 %collective-permute-start.3 = (bf16[256,512]{1,0:T(8,128)(2,1)S(1)}, bf16[256,512]{1,0:T(8,128)(2,1)S(1)}, u32[]{:S(2)}, u32[]{:S(2)}) collective-permute-start(bf16[256,512]{1,0:T(8,128)(2,1)S(1)} %extra_here.1.refs_5_.refs_0_.refs_2_), channel_id=1, source_target_pairs={{0,16},{24,8},{1,17},{25,9},{2,18},{26,10},{3,19},{27,11},{4,20},{... | collective-permute-start | bytes 786440 | tf_op jit(solution)/shard_map/extra_z2/ppermute | solution.py:307
  50.7 20.7 %copy-start = (bf16[2,512,512]{2,1,0:T(8,128)(2,1)S(1)}, bf16[2,512,512]{2,1,0:T(8,128)(2,1)}, u32[]{:S(2)}) copy-start(bf16[2,512,512]{2,1,0:T(8,128)(2,1)} %refs_1_.3) | copy-start | bytes 3145732
  50.7 17.9 %collective-permute-start.12 = (bf16[512,512]{1,0:T(8,128)(2,1)S(1)}, bf16[512,512]{1,0:T(8,128)(2,1)S(1)}, u32[]{:S(2)}, u32[]{:S(2)}) collective-permute-start(bf16[512,512]{1,0:T(8,128)(2,1)S(1)} %get-tuple-element.24), channel_id=1, source_target_pairs={{0,8},{24,16},{16,24},{8,0},{1,9},{25,17},{17,25},{9,1},{2,10},{26... | collective-permute-start | bytes 1572872 | tf_op jit(solution)/shard_map/row1/ppermute | solution.py:307
  57.4 14.0 %collective-permute-start.10 = (bf16[256,512]{1,0:T(8,128)(2,1)S(1)}, bf16[256,512]{1,0:T(8,128)(2,1)S(1)}, u32[]{:S(2)}, u32[]{:S(2)}) collective-permute-start(bf16[256,512]{1,0:T(8,128)(2,1)S(1)} %hand_on.1.refs_3_), channel_id=1, source_target_pairs={{0,8},{24,16},{16,24},{8,0},{1,9},{25,17},{17,25},{9,1},{2,10},{26... | collective-permute-start | bytes 786440 | tf_op jit(solution)/shard_map/extra_z1/ppermute | solution.py:307
  60.5 12.0 %collective-permute-start.14 = (bf16[2,1,256,512]{3,2,1,0:T(8,128)(2,1)S(1)}, bf16[2,1,256,512]{3,2,1,0:T(8,128)(2,1)S(1)}, u32[]{:S(2)}, u32[]{:S(2)}) collective-permute-start(bf16[2,1,256,512]{3,2,1,0:T(8,128)(2,1)S(1)} %pass_third.1.refs_5_.refs_8_), channel_id=1, source_target_pairs={{0,4},{1,3},{2,6},{3,1},{4,0},{5,7},{6,2},{7,5},{8,12},{9,11},{10,... | collective-permute-start | bytes 1572872 | tf_op jit(solution)/shard_map/third1a/ppermute | solution.py:319
  72.4 2.0 %collective-permute-start.13 = (bf16[2,256,512]{2,1,0:T(8,128)(2,1)S(1)}, bf16[2,256,512]{2,1,0:T(8,128)(2,1)S(1)}, u32[]{:S(2)}, u32[]{:S(2)}) collective-permute-start(bf16[2,256,512]{2,1,0:T(8,128)(2,1)S(1)} %settle_extra.1.refs_2_.refs_1_), channel_id=1, source_target_pairs={{0,1},{1,0},{2,3},{3,2},{4,5},{5,4},{6,7},{7,6},{8,9},{9,8},{10,11... | collective-permute-start | bytes 1572872 | tf_op jit(solution)/shard_map/sib_vl/ppermute | solution.py:311
  76.9 3.5 %collective-permute-start.15 = (bf16[2,3,256,512]{3,2,1,0:T(8,128)(2,1)S(1)}, bf16[2,3,256,512]{3,2,1,0:T(8,128)(2,1)S(1)}, u32[]{:S(2)}, u32[]{:S(2)}) collective-permute-start(bf16[2,3,256,512]{3,2,1,0:T(8,128)(2,1)S(1)} %multiply.1.refs_6_.refs_3_), channel_id=1, source_target_pairs={{0,1},{1,0},{2,3},{3,2},{4,5},{5,4},{6,7},{7,6},{8,9},{9,8},{10,11... | collective-permute-start | bytes 4718600 | tf_op jit(solution)/shard_map/sib_mine/ppermute | solution.py:311

commit v8 on v7

--- a/solution.py
+++ b/solution.py
@@ -64,26 +64,23 @@
         other[k] = raw[k, cut, :]
 
 
-def pick_extra(n, m, piv, raw, sib, extra):
+def views(refs, rb):
+    if len(refs) == 2:
+        refs = [refs[0].at[k] for k in range(rb)] + [refs[1].at[k] for k in range(rb - 1)]
+    return refs[0], refs[1:rb], refs[rb:]
+
+
+def pick(n, m, piv, raw, sib, *pieces):
     rb, width = raw.shape[0], raw.shape[1]
     f = facts(n, m, rb, piv)
     cut = rows(f["core"], width // 2)
+    extra, *panel = views(pieces, rb)
     hit = (f["cx"] & 1) == f["core"]
     either(hit, extra, lambda: raw[rb - 1, cut, :], lambda: sib[rb - 1])
-
-
-def pair(refs):
-    return [refs[0].at[q] for q in range(2)] if len(refs) == 1 else list(refs)
-
-
-def pick(n, m, piv, raw, sib, *panel):
-    rb, width = raw.shape[0], raw.shape[1]
-    f = facts(n, m, rb, piv)
-    cut = rows(f["core"], width // 2)
     for q in range(2):
         hit = (f["c"][q] & 1) == f["core"]
         for k in range(rb - 1):
-            either(hit, pair(panel)[q].at[k], lambda: raw[k, cut, :], lambda: sib[k])
+            either(hit, panel[q][k], lambda: raw[k, cut, :], lambda: sib[k])
 
 
 def pick_third(n, m, piv, raw, sib, moved, sib_moved, panel):
@@ -117,16 +114,27 @@
 def forward_extra(n, m, stage, stages, piv, had, got, out):
     f = facts(n, m, 2, piv)
     take = bit_of(f, f["cx"], stage, stages)
-    either(take, out, lambda: got[...], lambda: had[...])
-
-
-def forward(n, m, stage, stages, piv, *refs):
-    f = facts(n, m, 2, piv)
-    count = len(refs) // 3
-    had, got, out = (pair(refs[i * count : (i + 1) * count]) for i in range(3))
+    either(take, out, lambda: got[0], lambda: had[0])
+
+
+def forward(n, m, stage, stages, piv, had, got, out):
+    f = facts(n, m, 2, piv)
     for q in range(2):
         take = bit_of(f, f["c"][q], stage, stages)
-        either(take, out[q], lambda: got[q][...], lambda: had[q][...])
+        either(take, out.at[q], lambda: got[q], lambda: had[q])
+
+
+def forward_all(n, m, rb, stage, stages, piv, *refs):
+    f = facts(n, m, 2, piv)
+    count = (len(refs) - 2) // 2
+    had, got = views(refs[:count], rb), views(refs[count:-2], rb)
+    out = views(refs[-2:], rb)
+    take = bit_of(f, f["cx"], stage, stages)
+    either(take, out[0], lambda: got[0][...], lambda: had[0][...])
+    for q in range(2):
+        take = bit_of(f, f["c"][q], stage, stages)
+        for k in range(rb - 1):
+            either(take, out[1 + q][k], lambda: got[1 + q][k][...], lambda: had[1 + q][k][...])
 
 
 def hand_on(n, m, stride, had, got, extra):
@@ -174,8 +182,9 @@
     count = out.shape[1] - 1
     for q in range(2):
         take = bit_of(f, f["c"][q], stages - 1, stages)
-        had, got = panels[q], panels[2 + q]
-        either(take, out.at[q, :count], lambda: got[...], lambda: had[...])
+        had, got = (views(panels[i : i + 2], count + 1)[1 + q] for i in (0, 2))
+        for k in range(count):
+            either(take, out.at[q, k], lambda: got[k][...], lambda: had[k][...])
         either(take, out.at[q, count], lambda: third_got[q, 0], lambda: third[q, 0])
     for k in range(count + 1):
         m0 = dot(out[0, k], inv[0]).astype(out.dtype)
@@ -318,20 +327,6 @@
         with jax.named_scope(name):
             return lax.ppermute(value, "pcol", pairs)
 
-    def cross(name, s, values):
-        return [across(name + str(s) + "ab"[i], s, v) for i, v in enumerate(values)]
-
-    def passing(name, kernel, values, got, after=()):
-        for s in range(stages - 1):
-            step = lambda _n, _m, *refs: kernel(n, m, s, stages, *refs)
-            shapes = [v.shape for v in values]
-            values = call(
-                step, shapes, "s", pivots, *values, *got, after=after, name="pass_" + name
-            )
-            values = [values] if len(shapes) == 1 else list(values)
-            got = cross(name, s + 1, values)
-        return [*values, *got]
-
     square, strip = (width, width), (half, width)
     raw, leaving, other = call(
         prepare,
@@ -351,26 +346,27 @@
             pairs += [(i, i + stride), (n - 1 - i, n - 1 - i - stride)]
         return pairs
 
-    extra = call(pick_extra, [strip], "s", pivots, raw, early)
-    panel = call(pick, [(rb - 1, *strip)] * 2, "s", pivots, raw, early, after=[extra])
-    got_extra = cross("extra", 0, [extra])
-    got_stays = cross("stays", 0, panel)
-    had, got = passing("extra", forward_extra, [extra], got_extra, after=[panel[0]])
     hand = lambda stride: lambda _n, _m, *refs: hand_on(n, m, stride, *refs)
+    panel = call(pick, [strip] * (2 * rb - 1), "s", pivots, raw, early)
+    got = [across("stays0", 0, piece) for piece in panel]
+    for s in range(stages - 1):
+        step = lambda _n, _m, *refs: forward_all(n, m, rb, s, stages, *refs)
+        panel = call(
+            step, [(rb, *strip), (rb - 1, *strip)], "s", pivots, *panel, *got, name="forward_all"
+        )
+        got = [across("stays" + str(s + 1), s + 1, part) for part in panel]
+
     step = lambda _n, _m, *refs: forward_extra(n, m, stages - 1, stages, *refs)
-    extra_here = call(step, [strip], "s", pivots, had, got, name="extra_here")
-    stays = passing("stays", forward, panel, got_stays, after=[extra_here])
+    extra_here = call(
+        step, [strip], "s", pivots, panel[0], got[0], name="extra_here"
+    )
 
     step = lambda _n, _m, *refs: relay(n, m, n // 2, *refs)
     other_moved, send = call(
-        step, [strip, square], "", leaving, moved, name="relay", after=[stays[0]]
+        step, [strip, square], "", leaving, moved, name="relay", after=[extra_here]
     )
     sib_moved = sibling("sib_moved", other_moved)
-    third = call(
-        pick_third, [(2, 1, *strip)], "s", pivots, raw, early, moved, sib_moved, after=stays[2:]
-    )
-    got_third = cross("third", 0, [third])
-
+    stays = [*panel, *got]
     arrived = [leaving, moved]
     stride = n // 4
     while stride:
@@ -387,9 +383,26 @@
         got = along("extra_z" + str(stride), split(stride), send)
         came.append(got)
         if stride > 1:
-            send = call(hand(stride), [strip], "", send, got, name="hand_on", after=[third])
+            send = call(hand(stride), [strip], "", send, got, name="hand_on", after=[other_moved])
         stride //= 2
-    third = passing("third", forward, [third], got_third, after=[send])
+    third = call(
+        pick_third,
+        [(2, 1, *strip)],
+        "s",
+        pivots,
+        raw,
+        early,
+        moved,
+        sib_moved,
+        after=[send, stays[-1]],
+    )
+    third_got = across("third0", 0, third)
+    for s in range(stages - 1):
+        step = lambda _n, _m, *refs: forward(n, m, s, stages, *refs)
+        third = call(
+            step, [third.shape], "s", pivots, third, third_got, name="forward_third"
+        )
+        third_got = across("third" + str(s + 1), s + 1, third)
     vl = call(
         settle_extra,
         [(2, *strip)],
@@ -398,7 +411,7 @@
         inverses,
         *came,
         products=0.5,
-        after=[third[0], arrived[2]],
+        after=[third, arrived[2]],
     )
     sib_vl = sibling("sib_vl", vl)
     step = lambda _n, _m, *refs: multiply(n, m, stages, *refs)
@@ -411,7 +424,8 @@
         vl,
         sib_vl,
         *stays,
-        *third,
+        third,
+        third_got,
         scratch=[square],
         products=3 * rb / 2,
         name="multiply",

time: 84.8 us -> 95.4 us (1.12)
  waiting for transfers between devices: 44.2 us -> 56.9 us
  Pallas kernels: 14.2 us -> 13.1 us
  starting transfers between devices: 23.4 us -> 22.3 us
    ppermute x8 -> x9, waiting for transfers between devices: 10 us -> 25.1 us  [across(): return lax.ppermute(value, 'pcol', pairs)]
    ppermute x4, waiting for transfers between devices: 26.7 us -> 24.4 us  [along(): return lax.ppermute(value, 'prow', pairs)]
    ppermute x8 -> x9, starting transfers between devices: 13 us -> 11.7 us  [across(): return lax.ppermute(value, 'pcol', pairs)]
    pallas_call x14 -> x12, Pallas kernels: 14.2 us -> 13.1 us  [call(): pl.pallas_call(body, out_shape=outs, in_specs=specs, out_specs=[place] *...]
    unnamed x8 -> x10, local copies, waits for them, and re-layouts: 2.78 us -> 2.78 us
  transfers between devices with their start and end apart: 16 -> 17, of which waited for: 12 -> 13; matrix products, arithmetic and copies ran while one was open for 0% -> 0% of each run, Pallas kernels for 6% -> 3%
where the time goes in v8:
time: 95.4 us; the launch traced here: 95.2 us
  waiting for transfers between devices  56.9 us (60%)
  starting transfers between devices  22.3 us (23%)
  Pallas kernels  13.1 us (14%)
  local copies, waits for them, and re-layouts  2.78 us (3%)
    ppermute x9, waiting for transfers between devices, across(): return lax.ppermute(value, 'pcol', pairs)  25.1 us
    ppermute x4, waiting for transfers between devices, along(): return lax.ppermute(value, 'prow', pairs)  24.4 us
    pallas_call x12, Pallas kernels, call(): pl.pallas_call(body, out_shape=outs, in_specs=specs, out_specs=[place] *...  13.1 us
    ppermute x9, starting transfers between devices, across(): return lax.ppermute(value, 'pcol', pairs)  11.7 us
    ppermute x4, starting transfers between devices, along(): return lax.ppermute(value, 'prow', pairs)  9.62 us
    ppermute x4, waiting for transfers between devices, sibling(): return lax.ppermute(value, 'pcol', [(i, i ^ 1) for i in range(m)])  7.37 us
    unnamed x10, local copies, waits for them, and re-layouts  2.78 us
  transfers between devices with their start and end apart: 17, of which 13 were waited for; matrix products, arithmetic and copies ran while one was open for 0% of the time, Pallas kernels for 3%

profile of v8, /device:TPU:0, one launch (start us, length us, event | category | flops | bytes accessed | tf_op | source)
XLA Modules:
  0.0 95.2 jit_solution(6902422104066599857)
XLA Ops:
  0.0 1.4 %copy-done.1 = bf16[3,512,1,512]{3,1,2,0:T(8,128)(2,1)S(1)} copy-done((bf16[3,512,1,512]{3,1,2,0:T(8,128)(2,1)S(1)}, bf16[3,512,1,512]{3,1,2,0:T(8,128)(2,1)}, u32[]{:S(2)}) %copy-start.1) | copy-done | bytes 1572888
  4.1 1.9 %collective-permute-done.refs_2_ = bf16[3,256,512]{2,1,0:T(8,128)(2,1)S(1)} collective-permute-done((bf16[3,256,512]{2,1,0:T(8,128)(2,1)S(1)}, bf16[3,256,512]{2,1,0:T(8,128)(2,1)S(1)}, u32[]{:S(2)}, u32[]{:S(2)}) %collective-permute-start) | collective-permute-done | bytes 786464 | tf_op jit(solution)/shard_map/sib_early/ppermute | solution.py:320
  6.7 2.9 %collective-permute-start.1 = (bf16[256,512]{1,0:T(8,128)(2,1)S(1)}, bf16[256,512]{1,0:T(8,128)(2,1)S(1)}, u32[]{:S(2)}, u32[]{:S(2)}) collective-permute-start(bf16[256,512]{1,0:T(8,128)(2,1)S(1)} %get-tuple-element.21.refs_1_), channel_id=1, source_target_pairs={{0,2},{1,5},{2,0},{3,7},{4,6},{5,1},{6,4},{7,3},{8,10},{9,13},{10,... | collective-permute-start | bytes 786440 | tf_op jit(solution)/shard_map/stays0/ppermute | solution.py:328
  9.7 1.9 %collective-permute-start.3 = (bf16[256,512]{1,0:T(8,128)(2,1)S(1)}, bf16[256,512]{1,0:T(8,128)(2,1)S(1)}, u32[]{:S(2)}, u32[]{:S(2)}) collective-permute-start(bf16[256,512]{1,0:T(8,128)(2,1)S(1)} %get-tuple-element.23.refs_3_), channel_id=1, source_target_pairs={{0,2},{1,5},{2,0},{3,7},{4,6},{5,1},{6,4},{7,3},{8,10},{9,13},{10,... | collective-permute-start | bytes 786440 | tf_op jit(solution)/shard_map/stays0/ppermute | solution.py:328
  11.8 1.9 %collective-permute-start.5 = (bf16[256,512]{1,0:T(8,128)(2,1)S(1)}, bf16[256,512]{1,0:T(8,128)(2,1)S(1)}, u32[]{:S(2)}, u32[]{:S(2)}) collective-permute-start(bf16[256,512]{1,0:T(8,128)(2,1)S(1)} %get-tuple-element.25.refs_5_), channel_id=1, source_target_pairs={{0,2},{1,5},{2,0},{3,7},{4,6},{5,1},{6,4},{7,3},{8,10},{9,13},{10,... | collective-permute-start | bytes 786440 | tf_op jit(solution)/shard_map/stays0/ppermute | solution.py:328
  14.0 2.8 %collective-permute-done.2.refs_7_ = bf16[256,512]{1,0:T(8,128)(2,1)S(1)} collective-permute-done((bf16[256,512]{1,0:T(8,128)(2,1)S(1)}, bf16[256,512]{1,0:T(8,128)(2,1)S(1)}, u32[]{:S(2)}, u32[]{:S(2)}) %collective-permute-start.2) | collective-permute-done | bytes 262176 | tf_op jit(solution)/shard_map/stays0/ppermute | solution.py:328
  16.8 2.8 %collective-permute-done.3.refs_8_ = bf16[256,512]{1,0:T(8,128)(2,1)S(1)} collective-permute-done((bf16[256,512]{1,0:T(8,128)(2,1)S(1)}, bf16[256,512]{1,0:T(8,128)(2,1)S(1)}, u32[]{:S(2)}, u32[]{:S(2)}) %collective-permute-start.3) | collective-permute-done | bytes 262176 | tf_op jit(solution)/shard_map/stays0/ppermute | solution.py:328
  19.6 2.8 %collective-permute-done.4.refs_9_ = bf16[256,512]{1,0:T(8,128)(2,1)S(1)} collective-permute-done((bf16[256,512]{1,0:T(8,128)(2,1)S(1)}, bf16[256,512]{1,0:T(8,128)(2,1)S(1)}, u32[]{:S(2)}, u32[]{:S(2)}) %collective-permute-start.4) | collective-permute-done | bytes 262176 | tf_op jit(solution)/shard_map/stays0/ppermute | solution.py:328
  22.4 2.8 %collective-permute-done.5.refs_10_ = bf16[256,512]{1,0:T(8,128)(2,1)S(1)} collective-permute-done((bf16[256,512]{1,0:T(8,128)(2,1)S(1)}, bf16[256,512]{1,0:T(8,128)(2,1)S(1)}, u32[]{:S(2)}, u32[]{:S(2)}) %collective-permute-start.5) | collective-permute-done | bytes 262176 | tf_op jit(solution)/shard_map/stays0/ppermute | solution.py:328
  25.9 2.1 %collective-permute-start.6 = (bf16[3,256,512]{2,1,0:T(8,128)(2,1)S(1)}, bf16[3,256,512]{2,1,0:T(8,128)(2,1)S(1)}, u32[]{:S(2)}, u32[]{:S(2)}) collective-permute-start(bf16[3,256,512]{2,1,0:T(8,128)(2,1)S(1)} %get-tuple-element.26.refs_1_.refs_4_), channel_id=1, source_target_pairs={{0,4},{1,3},{2,6},{3,1},{4,0},{5,7},{6,2},{7,5},{8,12},{9,11},{10,... | collective-permute-start | bytes 2359304 | tf_op jit(solution)/shard_map/stays1/ppermute | solution.py:328
  28.0 2.6 %collective-permute-start.8 = (bf16[512,512]{1,0:T(8,128)(2,1)S(1)}, bf16[512,512]{1,0:T(8,128)(2,1)S(1)}, u32[]{:S(2)}, u32[]{:S(2)}) collective-permute-start(bf16[512,512]{1,0:T(8,128)(2,1)S(1)} %get-tuple-element.27.refs_0_.refs_3_), channel_id=1, source_target_pairs={{0,16},{24,8},{16,0},{8,24},{1,17},{25,9},{17,1},{9,25},{2,18},{26... | collective-permute-start | bytes 1572872 | tf_op jit(solution)/shard_map/swap/ppermute | solution.py:316
  31.1 6.9 %collective-permute-done.6.refs_2_.refs_6_ = bf16[3,256,512]{2,1,0:T(8,128)(2,1)S(1)} collective-permute-done((bf16[3,256,512]{2,1,0:T(8,128)(2,1)S(1)}, bf16[3,256,512]{2,1,0:T(8,128)(2,1)S(1)}, u32[]{:S(2)}, u32[]{:S(2)}) %collective-permute-start.6) | collective-permute-done | bytes 786464 | tf_op jit(solution)/shard_map/stays1/ppermute | solution.py:328
  38.6 5.0 %collective-permute-start.7 = (bf16[256,512]{1,0:T(8,128)(2,1)S(1)}, bf16[256,512]{1,0:T(8,128)(2,1)S(1)}, u32[]{:S(2)}, u32[]{:S(2)}) collective-permute-start(bf16[256,512]{1,0:T(8,128)(2,1)S(1)} %extra_here.1.refs_2_.refs_0_), channel_id=1, source_target_pairs={{0,16},{24,8},{1,17},{25,9},{2,18},{26,10},{3,19},{27,11},{4,20},{... | collective-permute-start | bytes 786440 | tf_op jit(solution)/shard_map/extra_z2/ppermute | solution.py:316
  43.6 15.0 %collective-permute-done.8.refs_1_.refs_3_.refs_4_.refs_6_ = bf16[512,512]{1,0:T(8,128)(2,1)S(1)} collective-permute-done((bf16[512,512]{1,0:T(8,128)(2,1)S(1)}, bf16[512,512]{1,0:T(8,128)(2,1)S(1)}, u32[]{:S(2)}, u32[]{:S(2)}) %collective-permute-start.8) | collective-permute-done | bytes 524320 | tf_op jit(solution)/shard_map/swap/ppermute | solution.py:316
  58.8 1.5 %collective-permute-done.10.refs_4_ = bf16[256,512]{1,0:T(8,128)(2,1)S(1)} collective-permute-done((bf16[256,512]{1,0:T(8,128)(2,1)S(1)}, bf16[256,512]{1,0:T(8,128)(2,1)S(1)}, u32[]{:S(2)}, u32[]{:S(2)}) %collective-permute-start.10) | collective-permute-done | bytes 262176 | tf_op jit(solution)/shard_map/sib_moved/ppermute | solution.py:320
  62.2 1.3 %collective-permute-start.9 = (bf16[256,512]{1,0:T(8,128)(2,1)S(1)}, bf16[256,512]{1,0:T(8,128)(2,1)S(1)}, u32[]{:S(2)}, u32[]{:S(2)}) collective-permute-start(bf16[256,512]{1,0:T(8,128)(2,1)S(1)} %hand_on.1.refs_5_), channel_id=1, source_target_pairs={{0,8},{24,16},{16,24},{8,0},{1,9},{25,17},{17,25},{9,1},{2,10},{26... | collective-permute-start | bytes 786440 | tf_op jit(solution)/shard_map/extra_z1/ppermute | solution.py:316
  63.5 6.7 %collective-permute-done.12.refs_2_ = bf16[2,1,256,512]{3,2,1,0:T(8,128)(2,1)S(1)} collective-permute-done((bf16[2,1,256,512]{3,2,1,0:T(8,128)(2,1)S(1)}, bf16[2,1,256,512]{3,2,1,0:T(8,128)(2,1)S(1)}, u32[]{:S(2)}, u32[]{:S(2)}) %collective-permute-start.12) | collective-permute-done | bytes 524320 | tf_op jit(solution)/shard_map/third0/ppermute | solution.py:328
  70.7 1.6 %collective-permute-start.15 = (bf16[2,1,256,512]{3,2,1,0:T(8,128)(2,1)S(1)}, bf16[2,1,256,512]{3,2,1,0:T(8,128)(2,1)S(1)}, u32[]{:S(2)}, u32[]{:S(2)}) collective-permute-start(bf16[2,1,256,512]{3,2,1,0:T(8,128)(2,1)S(1)} %forward_third.1.refs_5_.refs_8_), channel_id=1, source_target_pairs={{0,4},{1,3},{2,6},{3,1},{4,0},{5,7},{6,2},{7,5},{8,12},{9,11},{10,... | collective-permute-start | bytes 1572872 | tf_op jit(solution)/shard_map/third1/ppermute | solution.py:328
  72.3 9.4 %collective-permute-done.9.refs_4_ = bf16[256,512]{1,0:T(8,128)(2,1)S(1)} collective-permute-done((bf16[256,512]{1,0:T(8,128)(2,1)S(1)}, bf16[256,512]{1,0:T(8,128)(2,1)S(1)}, u32[]{:S(2)}, u32[]{:S(2)}) %collective-permute-start.9) | collective-permute-done | bytes 262176 | tf_op jit(solution)/shard_map/extra_z1/ppermute | solution.py:316
  82.9 1.9 %collective-permute-done.14.refs_3_.refs_2_ = bf16[2,256,512]{2,1,0:T(8,128)(2,1)S(1)} collective-permute-done((bf16[2,256,512]{2,1,0:T(8,128)(2,1)S(1)}, bf16[2,256,512]{2,1,0:T(8,128)(2,1)S(1)}, u32[]{:S(2)}, u32[]{:S(2)}) %collective-permute-start.14) | collective-permute-done | bytes 524320 | tf_op jit(solution)/shard_map/sib_vl/ppermute | solution.py:320
  84.7 2.6 %multiply.1.refs_6_.refs_3_ = bf16[2,3,256,512]{3,2,1,0:T(8,128)(2,1)S(1)} custom-call(s32[2,3]{1,0:T(2,128)S(1)} %copy-done.3, bf16[2,512,512]{2,1,0:T(8,128)(2,1)S(1)} %copy-done, bf16[2,256,512]{2,1,0:T(8,128)(2,1)S(1)} %settle_extra.1.refs_2_.refs_1_, bf16[2,256,512]{2,1,0:T(8,128)(2,1)S(1)} %collective-permute-done.14.refs_3_.refs_2_, ...), custom_call_target="tpu_custom_call" | custom-call | flops 1207959552 | bytes 5767192 | tf_op jit(solution)/shard_map/multiply/pallas_call | solution.py:297
  87.5 1.1 %settle_rows.1 = (bf16[2,512,512]{2,1,0:T(8,128)(2,1)S(1)}, bf16[512,512]{1,0:T(8,128)(2,1)S(1)}) custom-call(s32[2,3]{1,0:T(2,128)S(1)} %copy-done.3, bf16[2,256,512]{2,1,0:T(8,128)(2,1)S(1)} %settle_extra.1.refs_2_.refs_1_, bf16[2,256,512]{2,1,0:T(8,128)(2,1)S(1)} %collective-permute-done.14.refs_3_.refs_2_, ...), custom_call_target="tpu_custom_call" | custom-call | flops 268435456 | bytes 2621464 | tf_op jit(solution)/shard_map/settle_rows/pallas_call | solution.py:297
  88.6 2.1 %collective-permute-done.16.refs_4_ = bf16[2,3,256,512]{3,2,1,0:T(8,128)(2,1)S(1)} collective-permute-done((bf16[2,3,256,512]{3,2,1,0:T(8,128)(2,1)S(1)}, bf16[2,3,256,512]{3,2,1,0:T(8,128)(2,1)S(1)}, u32[]{:S(2)}, u32[]{:S(2)}) %collective-permute-start.16) | collective-permute-done | bytes 1572896 | tf_op jit(solution)/shard_map/sib_mine/ppermute | solution.py:320
  90.8 4.4 %finish.1 = bf16[3,512,512]{2,1,0:T(8,128)(2,1)} custom-call(s32[2,3]{1,0:T(2,128)S(1)} %copy-done.3, bf16[2,512,512]{2,1,0:T(8,128)(2,1)S(1)} %get-tuple-element.31.refs_1_, bf16[512,512]{1,0:T(8,128)(2,1)S(1)} %get-tuple-element.32.refs_2_, bf16[2,3,256,512]{3,2,1,0:T(8,128)(2,1)S(1)} %multiply.1.refs_6_.refs_3_, ...), custom_call_target="tpu_custom_call" | custom-call | flops 1610612736 | bytes 6815768 | tf_op jit(solution)/shard_map/finish/pallas_call | solution.py:297
  (32 shorter events, 9.5 us)
Async XLA Ops:
  0.0 1.4 %copy-start.1 = (bf16[3,512,1,512]{3,1,2,0:T(8,128)(2,1)S(1)}, bf16[3,512,1,512]{3,1,2,0:T(8,128)(2,1)}, u32[]{:S(2)}) copy-start(bf16[3,512,1,512]{3,1,2,0:T(8,128)(2,1)} %param.4) | copy-start | bytes 4718596
  1.4 0.7 copy-start.2
  2.1 0.7 copy-start.4
  3.6 2.4 %collective-permute-start = (bf16[3,256,512]{2,1,0:T(8,128)(2,1)S(1)}, bf16[3,256,512]{2,1,0:T(8,128)(2,1)S(1)}, u32[]{:S(2)}, u32[]{:S(2)}) collective-permute-start(bf16[3,256,512]{2,1,0:T(8,128)(2,1)S(1)} %get-tuple-element.20), channel_id=1, source_target_pairs={{0,1},{1,0},{2,3},{3,2},{4,5},{5,4},{6,7},{7,6},{8,9},{9,8},{10,11... | collective-permute-start | bytes 2359304 | tf_op jit(solution)/shard_map/sib_early/ppermute | solution.py:320
  6.7 7.3 %collective-permute-start.1 = (bf16[256,512]{1,0:T(8,128)(2,1)S(1)}, bf16[256,512]{1,0:T(8,128)(2,1)S(1)}, u32[]{:S(2)}, u32[]{:S(2)}) collective-permute-start(bf16[256,512]{1,0:T(8,128)(2,1)S(1)} %get-tuple-element.21.refs_1_), channel_id=1, source_target_pairs={{0,2},{1,5},{2,0},{3,7},{4,6},{5,1},{6,4},{7,3},{8,10},{9,13},{10,... | collective-permute-start | bytes 786440 | tf_op jit(solution)/shard_map/stays0/ppermute | solution.py:328
  9.7 7.2 %collective-permute-start.2 = (bf16[256,512]{1,0:T(8,128)(2,1)S(1)}, bf16[256,512]{1,0:T(8,128)(2,1)S(1)}, u32[]{:S(2)}, u32[]{:S(2)}) collective-permute-start(bf16[256,512]{1,0:T(8,128)(2,1)S(1)} %get-tuple-element.22.refs_2_), channel_id=1, source_target_pairs={{0,2},{1,5},{2,0},{3,7},{4,6},{5,1},{6,4},{7,3},{8,10},{9,13},{10,... | collective-permute-start | bytes 786440 | tf_op jit(solution)/shard_map/stays0/ppermute | solution.py:328
  9.7 9.9 %collective-permute-start.3 = (bf16[256,512]{1,0:T(8,128)(2,1)S(1)}, bf16[256,512]{1,0:T(8,128)(2,1)S(1)}, u32[]{:S(2)}, u32[]{:S(2)}) collective-permute-start(bf16[256,512]{1,0:T(8,128)(2,1)S(1)} %get-tuple-element.23.refs_3_), channel_id=1, source_target_pairs={{0,2},{1,5},{2,0},{3,7},{4,6},{5,1},{6,4},{7,3},{8,10},{9,13},{10,... | collective-permute-start | bytes 786440 | tf_op jit(solution)/shard_map/stays0/ppermute | solution.py:328
  11.7 10.8 %collective-permute-start.4 = (bf16[256,512]{1,0:T(8,128)(2,1)S(1)}, bf16[256,512]{1,0:T(8,128)(2,1)S(1)}, u32[]{:S(2)}, u32[]{:S(2)}) collective-permute-start(bf16[256,512]{1,0:T(8,128)(2,1)S(1)} %get-tuple-element.24.refs_4_), channel_id=1, source_target_pairs={{0,2},{1,5},{2,0},{3,7},{4,6},{5,1},{6,4},{7,3},{8,10},{9,13},{10,... | collective-permute-start | bytes 786440 | tf_op jit(solution)/shard_map/stays0/ppermute | solution.py:328
  11.8 13.5 %collective-permute-start.5 = (bf16[256,512]{1,0:T(8,128)(2,1)S(1)}, bf16[256,512]{1,0:T(8,128)(2,1)S(1)}, u32[]{:S(2)}, u32[]{:S(2)}) collective-permute-start(bf16[256,512]{1,0:T(8,128)(2,1)S(1)} %get-tuple-element.25.refs_5_), channel_id=1, source_target_pairs={{0,2},{1,5},{2,0},{3,7},{4,6},{5,1},{6,4},{7,3},{8,10},{9,13},{10,... | collective-permute-start | bytes 786440 | tf_op jit(solution)/shard_map/stays0/ppermute | solution.py:328
  25.9 12.1 %collective-permute-start.6 = (bf16[3,256,512]{2,1,0:T(8,128)(2,1)S(1)}, bf16[3,256,512]{2,1,0:T(8,128)(2,1)S(1)}, u32[]{:S(2)}, u32[]{:S(2)}) collective-permute-start(bf16[3,256,512]{2,1,0:T(8,128)(2,1)S(1)} %get-tuple-element.26.refs_1_.refs_4_), channel_id=1, source_target_pairs={{0,4},{1,3},{2,6},{3,1},{4,0},{5,7},{6,2},{7,5},{8,12},{9,11},{10,... | collective-permute-start | bytes 2359304 | tf_op jit(solution)/shard_map/stays1/ppermute | solution.py:328
  28.0 30.6 %collective-permute-start.8 = (bf16[512,512]{1,0:T(8,128)(2,1)S(1)}, bf16[512,512]{1,0:T(8,128)(2,1)S(1)}, u32[]{:S(2)}, u32[]{:S(2)}) collective-permute-start(bf16[512,512]{1,0:T(8,128)(2,1)S(1)} %get-tuple-element.27.refs_0_.refs_3_), channel_id=1, source_target_pairs={{0,16},{24,8},{16,0},{8,24},{1,17},{25,9},{17,1},{9,25},{2,18},{26... | collective-permute-start | bytes 1572872 | tf_op jit(solution)/shard_map/swap/ppermute | solution.py:316
  30.6 28.2 %collective-permute-start.11 = (bf16[2,256,512]{2,1,0:T(8,128)(2,1)S(1)}, bf16[2,256,512]{2,1,0:T(8,128)(2,1)S(1)}, u32[]{:S(2)}, u32[]{:S(2)}) collective-permute-start(bf16[2,256,512]{2,1,0:T(8,128)(2,1)S(1)} %get-tuple-element.29.refs_5_), channel_id=1, source_target_pairs={{0,4},{1,3},{2,6},{3,1},{4,0},{5,7},{6,2},{7,5},{8,12},{9,11},{10,... | collective-permute-start | bytes 1572872 | tf_op jit(solution)/shard_map/stays1/ppermute | solution.py:328
  38.6 21.7 %copy-start.3 = (s32[2,3]{1,0:T(2,128)S(1)}, s32[2,3]{1,0:T(2,128)}, u32[]{:S(2)}) copy-start(s32[2,3]{1,0:T(2,128)} %refs_0_.19) | copy-start | bytes 76
  38.6 20.1 %collective-permute-start.7 = (bf16[256,512]{1,0:T(8,128)(2,1)S(1)}, bf16[256,512]{1,0:T(8,128)(2,1)S(1)}, u32[]{:S(2)}, u32[]{:S(2)}) collective-permute-start(bf16[256,512]{1,0:T(8,128)(2,1)S(1)} %extra_here.1.refs_2_.refs_0_), channel_id=1, source_target_pairs={{0,16},{24,8},{1,17},{25,9},{2,18},{26,10},{3,19},{27,11},{4,20},{... | collective-permute-start | bytes 786440 | tf_op jit(solution)/shard_map/extra_z2/ppermute | solution.py:316
  58.7 1.6 %collective-permute-start.10 = (bf16[256,512]{1,0:T(8,128)(2,1)S(1)}, bf16[256,512]{1,0:T(8,128)(2,1)S(1)}, u32[]{:S(2)}, u32[]{:S(2)}) collective-permute-start(bf16[256,512]{1,0:T(8,128)(2,1)S(1)} %get-tuple-element.28.refs_2_), channel_id=1, source_target_pairs={{0,1},{1,0},{2,3},{3,2},{4,5},{5,4},{6,7},{7,6},{8,9},{9,8},{10,11... | collective-permute-start | bytes 786440 | tf_op jit(solution)/shard_map/sib_moved/ppermute | solution.py:320
  60.9 20.9 %copy-start = (bf16[2,512,512]{2,1,0:T(8,128)(2,1)S(1)}, bf16[2,512,512]{2,1,0:T(8,128)(2,1)}, u32[]{:S(2)}) copy-start(bf16[2,512,512]{2,1,0:T(8,128)(2,1)} %refs_1_.3) | copy-start | bytes 3145732
  60.9 9.2 %collective-permute-start.12 = (bf16[2,1,256,512]{3,2,1,0:T(8,128)(2,1)S(1)}, bf16[2,1,256,512]{3,2,1,0:T(8,128)(2,1)S(1)}, u32[]{:S(2)}, u32[]{:S(2)}) collective-permute-start(bf16[2,1,256,512]{3,2,1,0:T(8,128)(2,1)S(1)} %pick_third.1.refs_1_), channel_id=1, source_target_pairs={{0,2},{1,5},{2,0},{3,7},{4,6},{5,1},{6,4},{7,3},{8,10},{9,13},{10,... | collective-permute-start | bytes 1572872 | tf_op jit(solution)/shard_map/third0/ppermute | solution.py:328
  61.4 20.4 %collective-permute-start.13 = (bf16[512,512]{1,0:T(8,128)(2,1)S(1)}, bf16[512,512]{1,0:T(8,128)(2,1)S(1)}, u32[]{:S(2)}, u32[]{:S(2)}) collective-permute-start(bf16[512,512]{1,0:T(8,128)(2,1)S(1)} %get-tuple-element.30), channel_id=1, source_target_pairs={{0,8},{24,16},{16,24},{8,0},{1,9},{25,17},{17,25},{9,1},{2,10},{26... | collective-permute-start | bytes 1572872 | tf_op jit(solution)/shard_map/row1/ppermute | solution.py:316
  62.2 19.6 %collective-permute-start.9 = (bf16[256,512]{1,0:T(8,128)(2,1)S(1)}, bf16[256,512]{1,0:T(8,128)(2,1)S(1)}, u32[]{:S(2)}, u32[]{:S(2)}) collective-permute-start(bf16[256,512]{1,0:T(8,128)(2,1)S(1)} %hand_on.1.refs_5_), channel_id=1, source_target_pairs={{0,8},{24,16},{16,24},{8,0},{1,9},{25,17},{17,25},{9,1},{2,10},{26... | collective-permute-start | bytes 786440 | tf_op jit(solution)/shard_map/extra_z1/ppermute | solution.py:316
  70.7 12.1 %collective-permute-start.15 = (bf16[2,1,256,512]{3,2,1,0:T(8,128)(2,1)S(1)}, bf16[2,1,256,512]{3,2,1,0:T(8,128)(2,1)S(1)}, u32[]{:S(2)}, u32[]{:S(2)}) collective-permute-start(bf16[2,1,256,512]{3,2,1,0:T(8,128)(2,1)S(1)} %forward_third.1.refs_5_.refs_8_), channel_id=1, source_target_pairs={{0,4},{1,3},{2,6},{3,1},{4,0},{5,7},{6,2},{7,5},{8,12},{9,11},{10,... | collective-permute-start | bytes 1572872 | tf_op jit(solution)/shard_map/third1/ppermute | solution.py:328
  82.8 2.0 %collective-permute-start.14 = (bf16[2,256,512]{2,1,0:T(8,128)(2,1)S(1)}, bf16[2,256,512]{2,1,0:T(8,128)(2,1)S(1)}, u32[]{:S(2)}, u32[]{:S(2)}) collective-permute-start(bf16[2,256,512]{2,1,0:T(8,128)(2,1)S(1)} %settle_extra.1.refs_2_.refs_1_), channel_id=1, source_target_pairs={{0,1},{1,0},{2,3},{3,2},{4,5},{5,4},{6,7},{7,6},{8,9},{9,8},{10,11... | collective-permute-start | bytes 1572872 | tf_op jit(solution)/shard_map/sib_vl/ppermute | solution.py:320
  87.3 3.5 %collective-permute-start.16 = (bf16[2,3,256,512]{3,2,1,0:T(8,128)(2,1)S(1)}, bf16[2,3,256,512]{3,2,1,0:T(8,128)(2,1)S(1)}, u32[]{:S(2)}, u32[]{:S(2)}) collective-permute-start(bf16[2,3,256,512]{3,2,1,0:T(8,128)(2,1)S(1)} %multiply.1.refs_6_.refs_3_), channel_id=1, source_target_pairs={{0,1},{1,0},{2,3},{3,2},{4,5},{5,4},{6,7},{7,6},{8,9},{9,8},{10,11... | collective-permute-start | bytes 4718600 | tf_op jit(solution)/shard_map/sib_mine/ppermute | solution.py:320

commit v9 on v8

--- a/solution.py
+++ b/solution.py
@@ -149,7 +149,7 @@
 
 
 def settle_extra(n, m, piv, inv, *refs):
-    had, out = refs[:-1], refs[-1]
+    had, out = refs[:-2], refs[-2:]
     f = facts(n, m, 2, piv)
     r = f["r"]
     stages = len(had) - 1
@@ -164,21 +164,21 @@
 
             @pl.when(jnp.logical_and(here, low_is_v))
             def _():
-                out[0] = had[s][...]
+                out[0][...] = had[s][...]
 
             @pl.when(jnp.logical_and(here, jnp.logical_not(low_is_v)))
             def _():
-                out[1] = had[s][...]
-
-    out[1] = dot(out[1], inv[0]).astype(out.dtype)
-
-
-def multiply(n, m, stages, piv, inv, vl, sib_vl, *refs):
+                out[1][...] = had[s][...]
+
+    out[1][...] = dot(out[1][...], inv[0]).astype(out[1].dtype)
+
+
+def multiply(n, m, stages, piv, inv, v_half, sib_v, *refs):
     panels, third, third_got, out, v = refs[:-4], refs[-4], refs[-3], refs[-2], refs[-1]
     f = facts(n, m, 2, piv)
-    half = vl.shape[1]
-    v[rows(f["core"], half), :] = vl[0]
-    v[rows(1 - f["core"], half), :] = sib_vl[0]
+    half = v_half.shape[0]
+    v[rows(f["core"], half), :] = v_half[...]
+    v[rows(1 - f["core"], half), :] = sib_v[...]
     count = out.shape[1] - 1
     for q in range(2):
         take = bit_of(f, f["c"][q], stages - 1, stages)
@@ -193,7 +193,7 @@
         out[1, k] = dot(p1, inv[1]).astype(out.dtype)
 
 
-def settle_rows(n, m, piv, vl, sib_vl, *refs):
+def settle_rows(n, m, piv, l_half, sib_l, *refs):
     came, upper, lefts = refs[:-2], refs[-2], refs[-1]
     half = came[0].shape[0] // 2
     f = facts(n, m, 2, piv)
@@ -208,8 +208,8 @@
             def _():
                 upper[slot] = came[s][...]
 
-    lefts[rows(f["core"], half), :] = vl[1]
-    lefts[rows(1 - f["core"], half), :] = sib_vl[1]
+    lefts[rows(f["core"], half), :] = l_half[...]
+    lefts[rows(1 - f["core"], half), :] = sib_l[...]
     for p in range(2):
         cut = slice(p * half, (p + 1) * half)
         fresh = upper[1, cut, :].astype(jnp.float32) - dot(lefts[cut, :], upper[0])
@@ -284,7 +284,9 @@
     dt = matrix.dtype
     blocks = matrix.reshape(rb, width, width)
 
-    def call(kernel, shapes, specs, *operands, scratch=(), aliases=(), products=0, place=VMEM, after=(), name=None, weight=0):
+    def call(
+        kernel, shapes, specs, *operands, scratch=(), products=0, place=VMEM, after=(), name=None
+    ):
         outs = [jax.ShapeDtypeStruct(s, dt) for s in shapes]
         count = len(operands)
         scratch = [pltpu.VMEM(s, dt) if isinstance(s, tuple) else s for s in scratch]
@@ -300,12 +302,11 @@
             in_specs=specs,
             out_specs=[place] * len(outs),
             scratch_shapes=scratch,
-            input_output_aliases=dict(aliases),
             compiler_params=GRANT,
             name=name or kernel.__name__,
             cost_estimate=pl.CostEstimate(
                 flops=int(products * 2 * width**3),
-                bytes_accessed=weight + sum(a.size * a.dtype.itemsize for a in operands),
+                bytes_accessed=sum(a.size * a.dtype.itemsize for a in operands),
                 transcendentals=0,
             ),
         )(*operands, *after)
@@ -349,24 +350,43 @@
     hand = lambda stride: lambda _n, _m, *refs: hand_on(n, m, stride, *refs)
     panel = call(pick, [strip] * (2 * rb - 1), "s", pivots, raw, early)
     got = [across("stays0", 0, piece) for piece in panel]
+    step = lambda _n, _m, *refs: relay(n, m, n // 2, *refs)
+    other_moved, send = call(
+        step, [strip, square], "", leaving, moved, name="relay", after=got
+    )
     for s in range(stages - 1):
         step = lambda _n, _m, *refs: forward_all(n, m, rb, s, stages, *refs)
         panel = call(
-            step, [(rb, *strip), (rb - 1, *strip)], "s", pivots, *panel, *got, name="forward_all"
+            step,
+            [(rb, *strip), (rb - 1, *strip)],
+            "s",
+            pivots,
+            *panel,
+            *got,
+            name="forward_all",
+            after=[send],
         )
         got = [across("stays" + str(s + 1), s + 1, part) for part in panel]
 
+    sib_moved = sibling("sib_moved", other_moved)
     step = lambda _n, _m, *refs: forward_extra(n, m, stages - 1, stages, *refs)
     extra_here = call(
         step, [strip], "s", pivots, panel[0], got[0], name="extra_here"
     )
-
-    step = lambda _n, _m, *refs: relay(n, m, n // 2, *refs)
-    other_moved, send = call(
-        step, [strip, square], "", leaving, moved, name="relay", after=[extra_here]
-    )
-    sib_moved = sibling("sib_moved", other_moved)
     stays = [*panel, *got]
+    third = call(
+        pick_third,
+        [(2, 1, *strip)],
+        "s",
+        pivots,
+        raw,
+        early,
+        moved,
+        sib_moved,
+        after=[extra_here, stays[-1]],
+    )
+    third_got = across("third0", 0, third)
+
     arrived = [leaving, moved]
     stride = n // 4
     while stride:
@@ -383,29 +403,17 @@
         got = along("extra_z" + str(stride), split(stride), send)
         came.append(got)
         if stride > 1:
-            send = call(hand(stride), [strip], "", send, got, name="hand_on", after=[other_moved])
+            send = call(hand(stride), [strip], "", send, got, name="hand_on", after=[third])
         stride //= 2
-    third = call(
-        pick_third,
-        [(2, 1, *strip)],
-        "s",
-        pivots,
-        raw,
-        early,
-        moved,
-        sib_moved,
-        after=[send, stays[-1]],
-    )
-    third_got = across("third0", 0, third)
     for s in range(stages - 1):
         step = lambda _n, _m, *refs: forward(n, m, s, stages, *refs)
         third = call(
             step, [third.shape], "s", pivots, third, third_got, name="forward_third"
         )
         third_got = across("third" + str(s + 1), s + 1, third)
-    vl = call(
+    v_half, l_half = call(
         settle_extra,
-        [(2, *strip)],
+        [strip] * 2,
         "s",
         pivots,
         inverses,
@@ -413,7 +421,8 @@
         products=0.5,
         after=[third, arrived[2]],
     )
-    sib_vl = sibling("sib_vl", vl)
+    sib_v = sibling("sib_v", v_half)
+    sib_l = sibling("sib_l", l_half)
     step = lambda _n, _m, *refs: multiply(n, m, stages, *refs)
     mine = call(
         step,
@@ -421,14 +430,15 @@
         "s",
         pivots,
         inverses,
-        vl,
-        sib_vl,
+        v_half,
+        sib_v,
         *stays,
         third,
         third_got,
         scratch=[square],
         products=3 * rb / 2,
         name="multiply",
+        after=[sib_l],
     )
     sib_mine = sibling("sib_mine", mine)
     upper, lefts = call(
@@ -436,8 +446,8 @@
         [(2, *square), square],
         "s",
         pivots,
-        vl,
-        sib_vl,
+        l_half,
+        sib_l,
         *arrived,
         products=1,
         after=[mine],

time: 95.4 us -> 94.3 us (0.988)
  waiting for transfers between devices: 56.9 us -> 55.3 us
    ppermute x4, waiting for transfers between devices: 24.4 us -> 31.9 us  [along(): return lax.ppermute(value, 'prow', pairs)]
    ppermute x9, waiting for transfers between devices: 25.1 us -> 19.8 us  [across(): return lax.ppermute(value, 'pcol', pairs)]
    ppermute x4 -> x5, waiting for transfers between devices: 7.37 us -> 3.56 us  [sibling(): return lax.ppermute(value, 'pcol', [(i, i ^ 1) for i in range(m)])]
    unnamed x10 -> x8, local copies, waits for them, and re-layouts: 2.78 us -> 2.78 us
  transfers between devices with their start and end apart: 17 -> 18, of which waited for: 13 -> 10; matrix products, arithmetic and copies ran while one was open for 0% -> 0% of each run, Pallas kernels for 3% -> 4%
where the time goes in v9:
time: 94.3 us; the launch traced here: 93.8 us
  waiting for transfers between devices  55.3 us (59%)
  starting transfers between devices  22.6 us (24%)
  Pallas kernels  13.1 us (14%)
  local copies, waits for them, and re-layouts  2.78 us (3%)
    ppermute x4, waiting for transfers between devices, along(): return lax.ppermute(value, 'prow', pairs)  31.9 us
    ppermute x9, waiting for transfers between devices, across(): return lax.ppermute(value, 'pcol', pairs)  19.8 us
    pallas_call x12, Pallas kernels, call(): pl.pallas_call(body, out_shape=outs, in_specs=specs, out_specs=[place] *...  13.1 us
    ppermute x9, starting transfers between devices, across(): return lax.ppermute(value, 'pcol', pairs)  11 us
    ppermute x4, starting transfers between devices, along(): return lax.ppermute(value, 'prow', pairs)  10.3 us
    ppermute x5, waiting for transfers between devices, sibling(): return lax.ppermute(value, 'pcol', [(i, i ^ 1) for i in range(m)])  3.56 us
    unnamed x8, local copies, waits for them, and re-layouts  2.78 us
  transfers between devices with their start and end apart: 18, of which 10 were waited for; matrix products, arithmetic and copies ran while one was open for 0% of the time, Pallas kernels for 4%

profile of v9, /device:TPU:0, one launch (start us, length us, event | category | flops | bytes accessed | tf_op | source)
XLA Modules:
  0.0 93.8 jit_solution(11769191026119552379)
XLA Ops:
  0.0 1.4 %copy-done.1 = bf16[3,512,1,512]{3,1,2,0:T(8,128)(2,1)S(1)} copy-done((bf16[3,512,1,512]{3,1,2,0:T(8,128)(2,1)S(1)}, bf16[3,512,1,512]{3,1,2,0:T(8,128)(2,1)}, u32[]{:S(2)}) %copy-start.1) | copy-done | bytes 1572888
  2.8 0.8 prepare.1
  4.1 3.7 %collective-permute-start.6 = (bf16[512,512]{1,0:T(8,128)(2,1)S(1)}, bf16[512,512]{1,0:T(8,128)(2,1)S(1)}, u32[]{:S(2)}, u32[]{:S(2)}) collective-permute-start(bf16[512,512]{1,0:T(8,128)(2,1)S(1)} %get-tuple-element.28.refs_0_.refs_3_), channel_id=1, source_target_pairs={{0,16},{24,8},{16,0},{8,24},{1,17},{25,9},{17,1},{9,25},{2,18},{26... | collective-permute-start | bytes 1572872 | tf_op jit(solution)/shard_map/swap/ppermute | solution.py:317
  8.5 1.6 %collective-permute-start.1 = (bf16[256,512]{1,0:T(8,128)(2,1)S(1)}, bf16[256,512]{1,0:T(8,128)(2,1)S(1)}, u32[]{:S(2)}, u32[]{:S(2)}) collective-permute-start(bf16[256,512]{1,0:T(8,128)(2,1)S(1)} %get-tuple-element.23.refs_1_), channel_id=1, source_target_pairs={{0,2},{1,5},{2,0},{3,7},{4,6},{5,1},{6,4},{7,3},{8,10},{9,13},{10,... | collective-permute-start | bytes 786440 | tf_op jit(solution)/shard_map/stays0/ppermute | solution.py:329
  10.6 1.5 %collective-permute-start.3 = (bf16[256,512]{1,0:T(8,128)(2,1)S(1)}, bf16[256,512]{1,0:T(8,128)(2,1)S(1)}, u32[]{:S(2)}, u32[]{:S(2)}) collective-permute-start(bf16[256,512]{1,0:T(8,128)(2,1)S(1)} %get-tuple-element.25.refs_3_), channel_id=1, source_target_pairs={{0,2},{1,5},{2,0},{3,7},{4,6},{5,1},{6,4},{7,3},{8,10},{9,13},{10,... | collective-permute-start | bytes 786440 | tf_op jit(solution)/shard_map/stays0/ppermute | solution.py:329
  12.6 18.9 %collective-permute-done.6.refs_1_.refs_3_.refs_4_.refs_6_ = bf16[512,512]{1,0:T(8,128)(2,1)S(1)} collective-permute-done((bf16[512,512]{1,0:T(8,128)(2,1)S(1)}, bf16[512,512]{1,0:T(8,128)(2,1)S(1)}, u32[]{:S(2)}, u32[]{:S(2)}) %collective-permute-start.6) | collective-permute-done | bytes 524320 | tf_op jit(solution)/shard_map/swap/ppermute | solution.py:317
  31.6 1.6 %collective-permute-start.5 = (bf16[256,512]{1,0:T(8,128)(2,1)S(1)}, bf16[256,512]{1,0:T(8,128)(2,1)S(1)}, u32[]{:S(2)}, u32[]{:S(2)}) collective-permute-start(bf16[256,512]{1,0:T(8,128)(2,1)S(1)} %get-tuple-element.27.refs_5_), channel_id=1, source_target_pairs={{0,2},{1,5},{2,0},{3,7},{4,6},{5,1},{6,4},{7,3},{8,10},{9,13},{10,... | collective-permute-start | bytes 786440 | tf_op jit(solution)/shard_map/stays0/ppermute | solution.py:329
  33.1 4.8 %collective-permute-done.5.refs_6_.refs_10_ = bf16[256,512]{1,0:T(8,128)(2,1)S(1)} collective-permute-done((bf16[256,512]{1,0:T(8,128)(2,1)S(1)}, bf16[256,512]{1,0:T(8,128)(2,1)S(1)}, u32[]{:S(2)}, u32[]{:S(2)}) %collective-permute-start.5) | collective-permute-done | bytes 262176 | tf_op jit(solution)/shard_map/stays0/ppermute | solution.py:329
  38.7 1.7 %collective-permute-start.7 = (bf16[3,256,512]{2,1,0:T(8,128)(2,1)S(1)}, bf16[3,256,512]{2,1,0:T(8,128)(2,1)S(1)}, u32[]{:S(2)}, u32[]{:S(2)}) collective-permute-start(bf16[3,256,512]{2,1,0:T(8,128)(2,1)S(1)} %get-tuple-element.30.refs_1_.refs_4_), channel_id=1, source_target_pairs={{0,4},{1,3},{2,6},{3,1},{4,0},{5,7},{6,2},{7,5},{8,12},{9,11},{10,... | collective-permute-start | bytes 2359304 | tf_op jit(solution)/shard_map/stays1/ppermute | solution.py:329
  40.8 10.0 %collective-permute-done.7.refs_2_.refs_6_ = bf16[3,256,512]{2,1,0:T(8,128)(2,1)S(1)} collective-permute-done((bf16[3,256,512]{2,1,0:T(8,128)(2,1)S(1)}, bf16[3,256,512]{2,1,0:T(8,128)(2,1)S(1)}, u32[]{:S(2)}, u32[]{:S(2)}) %collective-permute-start.7) | collective-permute-done | bytes 786464 | tf_op jit(solution)/shard_map/stays1/ppermute | solution.py:329
  51.3 5.0 %collective-permute-done.10.refs_6_.refs_7_ = bf16[2,256,512]{2,1,0:T(8,128)(2,1)S(1)} collective-permute-done((bf16[2,256,512]{2,1,0:T(8,128)(2,1)S(1)}, bf16[2,256,512]{2,1,0:T(8,128)(2,1)S(1)}, u32[]{:S(2)}, u32[]{:S(2)}) %collective-permute-start.10) | collective-permute-done | bytes 524320 | tf_op jit(solution)/shard_map/stays1/ppermute | solution.py:329
  57.0 1.6 %collective-permute-start.12 = (bf16[2,1,256,512]{3,2,1,0:T(8,128)(2,1)S(1)}, bf16[2,1,256,512]{3,2,1,0:T(8,128)(2,1)S(1)}, u32[]{:S(2)}, u32[]{:S(2)}) collective-permute-start(bf16[2,1,256,512]{3,2,1,0:T(8,128)(2,1)S(1)} %pick_third.1.refs_2_.refs_1_), channel_id=1, source_target_pairs={{0,2},{1,5},{2,0},{3,7},{4,6},{5,1},{6,4},{7,3},{8,10},{9,13},{10,... | collective-permute-start | bytes 1572872 | tf_op jit(solution)/shard_map/third0/ppermute | solution.py:329
  58.6 1.5 %collective-permute-start.8 = (bf16[256,512]{1,0:T(8,128)(2,1)S(1)}, bf16[256,512]{1,0:T(8,128)(2,1)S(1)}, u32[]{:S(2)}, u32[]{:S(2)}) collective-permute-start(bf16[256,512]{1,0:T(8,128)(2,1)S(1)} %extra_here.1.refs_5_.refs_0_.refs_2_), channel_id=1, source_target_pairs={{0,16},{24,8},{1,17},{25,9},{2,18},{26,10},{3,19},{27,11},{4,20},{... | collective-permute-start | bytes 786440 | tf_op jit(solution)/shard_map/extra_z2/ppermute | solution.py:317
  60.6 6.1 %collective-permute-done.8.refs_1_.refs_3_ = bf16[256,512]{1,0:T(8,128)(2,1)S(1)} collective-permute-done((bf16[256,512]{1,0:T(8,128)(2,1)S(1)}, bf16[256,512]{1,0:T(8,128)(2,1)S(1)}, u32[]{:S(2)}, u32[]{:S(2)}) %collective-permute-start.8) | collective-permute-done | bytes 262176 | tf_op jit(solution)/shard_map/extra_z2/ppermute | solution.py:317
  66.8 4.6 %collective-permute-start.11 = (bf16[256,512]{1,0:T(8,128)(2,1)S(1)}, bf16[256,512]{1,0:T(8,128)(2,1)S(1)}, u32[]{:S(2)}, u32[]{:S(2)}) collective-permute-start(bf16[256,512]{1,0:T(8,128)(2,1)S(1)} %hand_on.1), channel_id=1, source_target_pairs={{0,8},{24,16},{16,24},{8,0},{1,9},{25,17},{17,25},{9,1},{2,10},{26... | collective-permute-start | bytes 786440 | tf_op jit(solution)/shard_map/extra_z1/ppermute | solution.py:317
  72.0 1.6 %collective-permute-start.16 = (bf16[2,1,256,512]{3,2,1,0:T(8,128)(2,1)S(1)}, bf16[2,1,256,512]{3,2,1,0:T(8,128)(2,1)S(1)}, u32[]{:S(2)}, u32[]{:S(2)}) collective-permute-start(bf16[2,1,256,512]{3,2,1,0:T(8,128)(2,1)S(1)} %forward_third.1.refs_5_.refs_8_), channel_id=1, source_target_pairs={{0,4},{1,3},{2,6},{3,1},{4,0},{5,7},{6,2},{7,5},{8,12},{9,11},{10,... | collective-permute-start | bytes 1572872 | tf_op jit(solution)/shard_map/third1/ppermute | solution.py:329
  73.6 4.0 %collective-permute-done.13.refs_6_.refs_5_ = bf16[512,512]{1,0:T(8,128)(2,1)S(1)} collective-permute-done((bf16[512,512]{1,0:T(8,128)(2,1)S(1)}, bf16[512,512]{1,0:T(8,128)(2,1)S(1)}, u32[]{:S(2)}, u32[]{:S(2)}) %collective-permute-start.13) | collective-permute-done | bytes 524320 | tf_op jit(solution)/shard_map/row1/ppermute | solution.py:317
  77.6 2.8 %collective-permute-done.11.refs_4_ = bf16[256,512]{1,0:T(8,128)(2,1)S(1)} collective-permute-done((bf16[256,512]{1,0:T(8,128)(2,1)S(1)}, bf16[256,512]{1,0:T(8,128)(2,1)S(1)}, u32[]{:S(2)}, u32[]{:S(2)}) %collective-permute-start.11) | collective-permute-done | bytes 262176 | tf_op jit(solution)/shard_map/extra_z1/ppermute | solution.py:317
  80.4 0.9 %settle_extra.1 = (bf16[256,512]{1,0:T(8,128)(2,1)S(1)}, bf16[256,512]{1,0:T(8,128)(2,1)S(1)}) custom-call(s32[2,3]{1,0:T(2,128)S(1)} %copy-done.2, bf16[2,512,512]{2,1,0:T(8,128)(2,1)S(1)} %copy-done, bf16[256,512]{1,0:T(8,128)(2,1)S(1)} %extra_here.1.refs_5_.refs_0_.refs_2_, bf16[256,512]{1,0:T(8,128)(2,1)S(1)} %collective-permute-done.8.refs_1_.refs_3_, ...), custom_call_target="tpu_custom_call" | custom-call | flops 134217728 | bytes 1835032 | tf_op jit(solution)/shard_map/settle_extra/pallas_call | solution.py:299
  82.0 1.0 %collective-permute-done.14.refs_10_.refs_2_ = bf16[256,512]{1,0:T(8,128)(2,1)S(1)} collective-permute-done((bf16[256,512]{1,0:T(8,128)(2,1)S(1)}, bf16[256,512]{1,0:T(8,128)(2,1)S(1)}, u32[]{:S(2)}, u32[]{:S(2)}) %collective-permute-start.14) | collective-permute-done | bytes 262176 | tf_op jit(solution)/shard_map/sib_l/ppermute | solution.py:321
  83.4 2.6 %multiply.1.refs_6_.refs_3_ = bf16[2,3,256,512]{3,2,1,0:T(8,128)(2,1)S(1)} custom-call(s32[2,3]{1,0:T(2,128)S(1)} %copy-done.2, bf16[2,512,512]{2,1,0:T(8,128)(2,1)S(1)} %copy-done, bf16[256,512]{1,0:T(8,128)(2,1)S(1)} %get-tuple-element.34.refs_2_, bf16[256,512]{1,0:T(8,128)(2,1)S(1)} %collective-permute-done.15.refs_3_, ...), custom_call_target="tpu_custom_call" | custom-call | flops 1207959552 | bytes 5242904 | tf_op jit(solution)/shard_map/multiply/pallas_call | solution.py:299
  86.1 1.1 %settle_rows.1 = (bf16[2,512,512]{2,1,0:T(8,128)(2,1)S(1)}, bf16[512,512]{1,0:T(8,128)(2,1)S(1)}) custom-call(s32[2,3]{1,0:T(2,128)S(1)} %copy-done.2, bf16[256,512]{1,0:T(8,128)(2,1)S(1)} %get-tuple-element.33.refs_1_, bf16[256,512]{1,0:T(8,128)(2,1)S(1)} %collective-permute-done.14.refs_10_.refs_2_, ...), custom_call_target="tpu_custom_call" | custom-call | flops 268435456 | bytes 2097176 | tf_op jit(solution)/shard_map/settle_rows/pallas_call | solution.py:299
  87.2 2.2 %collective-permute-done.17.refs_4_ = bf16[2,3,256,512]{3,2,1,0:T(8,128)(2,1)S(1)} collective-permute-done((bf16[2,3,256,512]{3,2,1,0:T(8,128)(2,1)S(1)}, bf16[2,3,256,512]{3,2,1,0:T(8,128)(2,1)S(1)}, u32[]{:S(2)}, u32[]{:S(2)}) %collective-permute-start.17) | collective-permute-done | bytes 1572896 | tf_op jit(solution)/shard_map/sib_mine/ppermute | solution.py:321
  89.4 4.4 %finish.1 = bf16[3,512,512]{2,1,0:T(8,128)(2,1)} custom-call(s32[2,3]{1,0:T(2,128)S(1)} %copy-done.2, bf16[2,512,512]{2,1,0:T(8,128)(2,1)S(1)} %get-tuple-element.35.refs_1_, bf16[512,512]{1,0:T(8,128)(2,1)S(1)} %get-tuple-element.36.refs_2_, bf16[2,3,256,512]{3,2,1,0:T(8,128)(2,1)S(1)} %multiply.1.refs_6_.refs_3_, ...), custom_call_target="tpu_custom_call" | custom-call | flops 1610612736 | bytes 6815768 | tf_op jit(solution)/shard_map/finish/pallas_call | solution.py:299
  (32 shorter events, 8.4 us)
Async XLA Ops:
  0.0 1.4 %copy-start.1 = (bf16[3,512,1,512]{3,1,2,0:T(8,128)(2,1)S(1)}, bf16[3,512,1,512]{3,1,2,0:T(8,128)(2,1)}, u32[]{:S(2)}) copy-start(bf16[3,512,1,512]{3,1,2,0:T(8,128)(2,1)} %param.4) | copy-start | bytes 4718596
  1.4 0.7 copy-start.2
  2.1 0.7 copy-start.3
  3.6 4.2 %collective-permute-start = (bf16[3,256,512]{2,1,0:T(8,128)(2,1)S(1)}, bf16[3,256,512]{2,1,0:T(8,128)(2,1)S(1)}, u32[]{:S(2)}, u32[]{:S(2)}) collective-permute-start(bf16[3,256,512]{2,1,0:T(8,128)(2,1)S(1)} %get-tuple-element.22), channel_id=1, source_target_pairs={{0,1},{1,0},{2,3},{3,2},{4,5},{5,4},{6,7},{7,6},{8,9},{9,8},{10,11... | collective-permute-start | bytes 2359304 | tf_op jit(solution)/shard_map/sib_early/ppermute | solution.py:321
  4.1 27.4 %collective-permute-start.6 = (bf16[512,512]{1,0:T(8,128)(2,1)S(1)}, bf16[512,512]{1,0:T(8,128)(2,1)S(1)}, u32[]{:S(2)}, u32[]{:S(2)}) collective-permute-start(bf16[512,512]{1,0:T(8,128)(2,1)S(1)} %get-tuple-element.28.refs_0_.refs_3_), channel_id=1, source_target_pairs={{0,16},{24,8},{16,0},{8,24},{1,17},{25,9},{17,1},{9,25},{2,18},{26... | collective-permute-start | bytes 1572872 | tf_op jit(solution)/shard_map/swap/ppermute | solution.py:317
  8.5 24.6 %collective-permute-start.1 = (bf16[256,512]{1,0:T(8,128)(2,1)S(1)}, bf16[256,512]{1,0:T(8,128)(2,1)S(1)}, u32[]{:S(2)}, u32[]{:S(2)}) collective-permute-start(bf16[256,512]{1,0:T(8,128)(2,1)S(1)} %get-tuple-element.23.refs_1_), channel_id=1, source_target_pairs={{0,2},{1,5},{2,0},{3,7},{4,6},{5,1},{6,4},{7,3},{8,10},{9,13},{10,... | collective-permute-start | bytes 786440 | tf_op jit(solution)/shard_map/stays0/ppermute | solution.py:329
  10.0 23.1 %collective-permute-start.2 = (bf16[256,512]{1,0:T(8,128)(2,1)S(1)}, bf16[256,512]{1,0:T(8,128)(2,1)S(1)}, u32[]{:S(2)}, u32[]{:S(2)}) collective-permute-start(bf16[256,512]{1,0:T(8,128)(2,1)S(1)} %get-tuple-element.24.refs_2_), channel_id=1, source_target_pairs={{0,2},{1,5},{2,0},{3,7},{4,6},{5,1},{6,4},{7,3},{8,10},{9,13},{10,... | collective-permute-start | bytes 786440 | tf_op jit(solution)/shard_map/stays0/ppermute | solution.py:329
  10.6 22.5 %collective-permute-start.3 = (bf16[256,512]{1,0:T(8,128)(2,1)S(1)}, bf16[256,512]{1,0:T(8,128)(2,1)S(1)}, u32[]{:S(2)}, u32[]{:S(2)}) collective-permute-start(bf16[256,512]{1,0:T(8,128)(2,1)S(1)} %get-tuple-element.25.refs_3_), channel_id=1, source_target_pairs={{0,2},{1,5},{2,0},{3,7},{4,6},{5,1},{6,4},{7,3},{8,10},{9,13},{10,... | collective-permute-start | bytes 786440 | tf_op jit(solution)/shard_map/stays0/ppermute | solution.py:329
  12.1 21.1 %collective-permute-start.4 = (bf16[256,512]{1,0:T(8,128)(2,1)S(1)}, bf16[256,512]{1,0:T(8,128)(2,1)S(1)}, u32[]{:S(2)}, u32[]{:S(2)}) collective-permute-start(bf16[256,512]{1,0:T(8,128)(2,1)S(1)} %get-tuple-element.26.refs_4_), channel_id=1, source_target_pairs={{0,2},{1,5},{2,0},{3,7},{4,6},{5,1},{6,4},{7,3},{8,10},{9,13},{10,... | collective-permute-start | bytes 786440 | tf_op jit(solution)/shard_map/stays0/ppermute | solution.py:329
  31.6 6.4 %collective-permute-start.5 = (bf16[256,512]{1,0:T(8,128)(2,1)S(1)}, bf16[256,512]{1,0:T(8,128)(2,1)S(1)}, u32[]{:S(2)}, u32[]{:S(2)}) collective-permute-start(bf16[256,512]{1,0:T(8,128)(2,1)S(1)} %get-tuple-element.27.refs_5_), channel_id=1, source_target_pairs={{0,2},{1,5},{2,0},{3,7},{4,6},{5,1},{6,4},{7,3},{8,10},{9,13},{10,... | collective-permute-start | bytes 786440 | tf_op jit(solution)/shard_map/stays0/ppermute | solution.py:329
  38.7 12.1 %collective-permute-start.7 = (bf16[3,256,512]{2,1,0:T(8,128)(2,1)S(1)}, bf16[3,256,512]{2,1,0:T(8,128)(2,1)S(1)}, u32[]{:S(2)}, u32[]{:S(2)}) collective-permute-start(bf16[3,256,512]{2,1,0:T(8,128)(2,1)S(1)} %get-tuple-element.30.refs_1_.refs_4_), channel_id=1, source_target_pairs={{0,4},{1,3},{2,6},{3,1},{4,0},{5,7},{6,2},{7,5},{8,12},{9,11},{10,... | collective-permute-start | bytes 2359304 | tf_op jit(solution)/shard_map/stays1/ppermute | solution.py:329
  40.3 16.0 %collective-permute-start.10 = (bf16[2,256,512]{2,1,0:T(8,128)(2,1)S(1)}, bf16[2,256,512]{2,1,0:T(8,128)(2,1)S(1)}, u32[]{:S(2)}, u32[]{:S(2)}) collective-permute-start(bf16[2,256,512]{2,1,0:T(8,128)(2,1)S(1)} %get-tuple-element.32.refs_5_), channel_id=1, source_target_pairs={{0,4},{1,3},{2,6},{3,1},{4,0},{5,7},{6,2},{7,5},{8,12},{9,11},{10,... | collective-permute-start | bytes 1572872 | tf_op jit(solution)/shard_map/stays1/ppermute | solution.py:329
  40.8 10.6 %collective-permute-start.9 = (bf16[256,512]{1,0:T(8,128)(2,1)S(1)}, bf16[256,512]{1,0:T(8,128)(2,1)S(1)}, u32[]{:S(2)}, u32[]{:S(2)}) collective-permute-start(bf16[256,512]{1,0:T(8,128)(2,1)S(1)} %get-tuple-element.31), channel_id=1, source_target_pairs={{0,1},{1,0},{2,3},{3,2},{4,5},{5,4},{6,7},{7,6},{8,9},{9,8},{10,11... | collective-permute-start | bytes 786440 | tf_op jit(solution)/shard_map/sib_moved/ppermute | solution.py:321
  57.0 23.5 %copy-start = (bf16[2,512,512]{2,1,0:T(8,128)(2,1)S(1)}, bf16[2,512,512]{2,1,0:T(8,128)(2,1)}, u32[]{:S(2)}) copy-start(bf16[2,512,512]{2,1,0:T(8,128)(2,1)} %refs_1_.3) | copy-start | bytes 3145732
  57.0 14.4 %collective-permute-start.12 = (bf16[2,1,256,512]{3,2,1,0:T(8,128)(2,1)S(1)}, bf16[2,1,256,512]{3,2,1,0:T(8,128)(2,1)S(1)}, u32[]{:S(2)}, u32[]{:S(2)}) collective-permute-start(bf16[2,1,256,512]{3,2,1,0:T(8,128)(2,1)S(1)} %pick_third.1.refs_2_.refs_1_), channel_id=1, source_target_pairs={{0,2},{1,5},{2,0},{3,7},{4,6},{5,1},{6,4},{7,3},{8,10},{9,13},{10,... | collective-permute-start | bytes 1572872 | tf_op jit(solution)/shard_map/third0/ppermute | solution.py:329
  58.6 8.2 %collective-permute-start.8 = (bf16[256,512]{1,0:T(8,128)(2,1)S(1)}, bf16[256,512]{1,0:T(8,128)(2,1)S(1)}, u32[]{:S(2)}, u32[]{:S(2)}) collective-permute-start(bf16[256,512]{1,0:T(8,128)(2,1)S(1)} %extra_here.1.refs_5_.refs_0_.refs_2_), channel_id=1, source_target_pairs={{0,16},{24,8},{1,17},{25,9},{2,18},{26,10},{3,19},{27,11},{4,20},{... | collective-permute-start | bytes 786440 | tf_op jit(solution)/shard_map/extra_z2/ppermute | solution.py:317
  60.1 17.6 %collective-permute-start.13 = (bf16[512,512]{1,0:T(8,128)(2,1)S(1)}, bf16[512,512]{1,0:T(8,128)(2,1)S(1)}, u32[]{:S(2)}, u32[]{:S(2)}) collective-permute-start(bf16[512,512]{1,0:T(8,128)(2,1)S(1)} %get-tuple-element.29.refs_11_), channel_id=1, source_target_pairs={{0,8},{24,16},{16,24},{8,0},{1,9},{25,17},{17,25},{9,1},{2,10},{26... | collective-permute-start | bytes 1572872 | tf_op jit(solution)/shard_map/row1/ppermute | solution.py:317
  66.8 13.6 %collective-permute-start.11 = (bf16[256,512]{1,0:T(8,128)(2,1)S(1)}, bf16[256,512]{1,0:T(8,128)(2,1)S(1)}, u32[]{:S(2)}, u32[]{:S(2)}) collective-permute-start(bf16[256,512]{1,0:T(8,128)(2,1)S(1)} %hand_on.1), channel_id=1, source_target_pairs={{0,8},{24,16},{16,24},{8,0},{1,9},{25,17},{17,25},{9,1},{2,10},{26... | collective-permute-start | bytes 786440 | tf_op jit(solution)/shard_map/extra_z1/ppermute | solution.py:317
  72.0 11.3 %collective-permute-start.16 = (bf16[2,1,256,512]{3,2,1,0:T(8,128)(2,1)S(1)}, bf16[2,1,256,512]{3,2,1,0:T(8,128)(2,1)S(1)}, u32[]{:S(2)}, u32[]{:S(2)}) collective-permute-start(bf16[2,1,256,512]{3,2,1,0:T(8,128)(2,1)S(1)} %forward_third.1.refs_5_.refs_8_), channel_id=1, source_target_pairs={{0,4},{1,3},{2,6},{3,1},{4,0},{5,7},{6,2},{7,5},{8,12},{9,11},{10,... | collective-permute-start | bytes 1572872 | tf_op jit(solution)/shard_map/third1/ppermute | solution.py:329
  81.4 1.6 %collective-permute-start.14 = (bf16[256,512]{1,0:T(8,128)(2,1)S(1)}, bf16[256,512]{1,0:T(8,128)(2,1)S(1)}, u32[]{:S(2)}, u32[]{:S(2)}) collective-permute-start(bf16[256,512]{1,0:T(8,128)(2,1)S(1)} %get-tuple-element.33.refs_1_), channel_id=1, source_target_pairs={{0,1},{1,0},{2,3},{3,2},{4,5},{5,4},{6,7},{7,6},{8,9},{9,8},{10,11... | collective-permute-start | bytes 786440 | tf_op jit(solution)/shard_map/sib_l/ppermute | solution.py:321
  81.5 1.9 %collective-permute-start.15 = (bf16[256,512]{1,0:T(8,128)(2,1)S(1)}, bf16[256,512]{1,0:T(8,128)(2,1)S(1)}, u32[]{:S(2)}, u32[]{:S(2)}) collective-permute-start(bf16[256,512]{1,0:T(8,128)(2,1)S(1)} %get-tuple-element.34.refs_2_), channel_id=1, source_target_pairs={{0,1},{1,0},{2,3},{3,2},{4,5},{5,4},{6,7},{7,6},{8,9},{9,8},{10,11... | collective-permute-start | bytes 786440 | tf_op jit(solution)/shard_map/sib_v/ppermute | solution.py:321
  85.9 3.5 %collective-permute-start.17 = (bf16[2,3,256,512]{3,2,1,0:T(8,128)(2,1)S(1)}, bf16[2,3,256,512]{3,2,1,0:T(8,128)(2,1)S(1)}, u32[]{:S(2)}, u32[]{:S(2)}) collective-permute-start(bf16[2,3,256,512]{3,2,1,0:T(8,128)(2,1)S(1)} %multiply.1.refs_6_.refs_3_), channel_id=1, source_target_pairs={{0,1},{1,0},{2,3},{3,2},{4,5},{5,4},{6,7},{7,6},{8,9},{9,8},{10,11... | collective-permute-start | bytes 4718600 | tf_op jit(solution)/shard_map/sib_mine/ppermute | solution.py:321

commit v10 on v9

--- a/solution.py
+++ b/solution.py
@@ -65,9 +65,11 @@
 
 
 def views(refs, rb):
-    if len(refs) == 2:
-        refs = [refs[0].at[k] for k in range(rb)] + [refs[1].at[k] for k in range(rb - 1)]
-    return refs[0], refs[1:rb], refs[rb:]
+    if refs[0].shape[0] == rb:
+        one = [refs[0].at[k] for k in range(rb)] + [refs[1].at[k] for k in range(rb - 1)]
+        return one[0], one[1:rb], one[rb:]
+    one = [ref.at[0] for ref in refs]
+    return refs[-1].at[1], one[: rb - 1], one[rb - 1 :]
 
 
 def pick(n, m, piv, raw, sib, *pieces):
@@ -348,7 +350,8 @@
         return pairs
 
     hand = lambda stride: lambda _n, _m, *refs: hand_on(n, m, stride, *refs)
-    panel = call(pick, [strip] * (2 * rb - 1), "s", pivots, raw, early)
+    pieces = [(1, *strip)] * (2 * rb - 3) + [(2, *strip)]
+    panel = call(pick, pieces, "s", pivots, raw, early)
     got = [across("stays0", 0, piece) for piece in panel]
     step = lambda _n, _m, *refs: relay(n, m, n // 2, *refs)
     other_moved, send = call(
@@ -383,7 +386,7 @@
         early,
         moved,
         sib_moved,
-        after=[extra_here, stays[-1]],
+        after=[extra_here],
     )
     third_got = across("third0", 0, third)
 
@@ -403,7 +406,7 @@
         got = along("extra_z" + str(stride), split(stride), send)
         came.append(got)
         if stride > 1:
-            send = call(hand(stride), [strip], "", send, got, name="hand_on", after=[third])
+            send = call(hand(stride), [strip], "", send, got, name="hand_on", after=[third, stays[-1]])
         stride //= 2
     for s in range(stages - 1):
         step = lambda _n, _m, *refs: forward(n, m, s, stages, *refs)

time: 94.3 us -> 83.8 us (0.89)
  waiting for transfers between devices: 55.3 us -> 45.9 us
  starting transfers between devices: 22.6 us -> 21.4 us
    ppermute x9 -> x8, waiting for transfers between devices: 19.8 us -> 12.9 us  [across(): return lax.ppermute(value, 'pcol', pairs)]
    ppermute x4, waiting for transfers between devices: 31.9 us -> 29.4 us  [along(): return lax.ppermute(value, 'prow', pairs)]
    ppermute x9 -> x8, starting transfers between devices: 11 us -> 9.84 us  [across(): return lax.ppermute(value, 'pcol', pairs)]
  transfers between devices with their start and end apart: 18 -> 17, of which waited for: 10 -> 9; matrix products, arithmetic and copies ran while one was open for 0% -> 0% of each run, Pallas kernels for 4% -> 5%
where the time goes in v10:
time: 83.8 us; the launch traced here: 83.3 us
  waiting for transfers between devices  45.9 us (55%)
  starting transfers between devices  21.4 us (26%)
  Pallas kernels  13.1 us (16%)
  local copies, waits for them, and re-layouts  2.78 us (3%)
    ppermute x4, waiting for transfers between devices, along(): return lax.ppermute(value, 'prow', pairs)  29.4 us
    pallas_call x12, Pallas kernels, call(): pl.pallas_call(body, out_shape=outs, in_specs=specs, out_specs=[place] *...  13.1 us
    ppermute x8, waiting for transfers between devices, across(): return lax.ppermute(value, 'pcol', pairs)  12.9 us
    ppermute x4, starting transfers between devices, along(): return lax.ppermute(value, 'prow', pairs)  10.3 us
    ppermute x8, starting transfers between devices, across(): return lax.ppermute(value, 'pcol', pairs)  9.84 us
    ppermute x5, waiting for transfers between devices, sibling(): return lax.ppermute(value, 'pcol', [(i, i ^ 1) for i in range(m)])  3.56 us
    unnamed x8, local copies, waits for them, and re-layouts  2.78 us
  transfers between devices with their start and end apart: 17, of which 9 were waited for; matrix products, arithmetic and copies ran while one was open for 0% of the time, Pallas kernels for 5%

profile of v10, /device:TPU:0, one launch (start us, length us, event | category | flops | bytes accessed | tf_op | source)
XLA Modules:
  0.0 83.3 jit_solution(7182656809809900617)
XLA Ops:
  0.0 1.4 %copy-done.1 = bf16[3,512,1,512]{3,1,2,0:T(8,128)(2,1)S(1)} copy-done((bf16[3,512,1,512]{3,1,2,0:T(8,128)(2,1)S(1)}, bf16[3,512,1,512]{3,1,2,0:T(8,128)(2,1)}, u32[]{:S(2)}) %copy-start.1) | copy-done | bytes 1572888
  2.1 0.7 copy-done.3
  2.8 0.8 %prepare.1 = (bf16[3,512,512]{2,1,0:T(8,128)(2,1)S(1)}, bf16[512,512]{1,0:T(8,128)(2,1)S(1)}, bf16[3,256,512]{2,1,0:T(8,128)(2,1)S(1)}) custom-call(s32[2,3]{1,0:T(2,128)S(1)} %copy-done.2, s32[8,12]{1,0:T(8,128)S(1)} %bitcast.6, bf16[3,512,512]{2,1,0:T(8,128)(2,1)S(1)} %bitcast.5), custom_call_target="tpu_custom_call" | custom-call | bytes 1573272 | tf_op jit(solution)/shard_map/prepare/pallas_call | solution.py:301
  4.1 3.7 %collective-permute-start.5 = (bf16[512,512]{1,0:T(8,128)(2,1)S(1)}, bf16[512,512]{1,0:T(8,128)(2,1)S(1)}, u32[]{:S(2)}, u32[]{:S(2)}) collective-permute-start(bf16[512,512]{1,0:T(8,128)(2,1)S(1)} %get-tuple-element.26.refs_0_.refs_3_), channel_id=1, source_target_pairs={{0,16},{24,8},{16,0},{8,24},{1,17},{25,9},{17,1},{9,25},{2,18},{26... | collective-permute-start | bytes 1572872 | tf_op jit(solution)/shard_map/swap/ppermute | solution.py:319
  8.5 1.6 %collective-permute-start.4 = (bf16[2,256,512]{2,1,0:T(8,128)(2,1)S(1)}, bf16[2,256,512]{2,1,0:T(8,128)(2,1)S(1)}, u32[]{:S(2)}, u32[]{:S(2)}) collective-permute-start(bf16[2,256,512]{2,1,0:T(8,128)(2,1)S(1)} %get-tuple-element.25.refs_4_), channel_id=1, source_target_pairs={{0,2},{1,5},{2,0},{3,7},{4,6},{5,1},{6,4},{7,3},{8,10},{9,13},{10,... | collective-permute-start | bytes 1572872 | tf_op jit(solution)/shard_map/stays0/ppermute | solution.py:331
  10.6 1.5 %collective-permute-start.2 = (bf16[1,256,512]{2,1,0:T(8,128)(2,1)S(1)}, bf16[1,256,512]{2,1,0:T(8,128)(2,1)S(1)}, u32[]{:S(2)}, u32[]{:S(2)}) collective-permute-start(bf16[1,256,512]{2,1,0:T(8,128)(2,1)S(1)} %get-tuple-element.23.refs_2_), channel_id=1, source_target_pairs={{0,2},{1,5},{2,0},{3,7},{4,6},{5,1},{6,4},{7,3},{8,10},{9,13},{10,... | collective-permute-start | bytes 786440 | tf_op jit(solution)/shard_map/stays0/ppermute | solution.py:331
  12.6 19.0 %collective-permute-done.5.refs_1_.refs_3_.refs_4_.refs_6_ = bf16[512,512]{1,0:T(8,128)(2,1)S(1)} collective-permute-done((bf16[512,512]{1,0:T(8,128)(2,1)S(1)}, bf16[512,512]{1,0:T(8,128)(2,1)S(1)}, u32[]{:S(2)}, u32[]{:S(2)}) %collective-permute-start.5) | collective-permute-done | bytes 524320 | tf_op jit(solution)/shard_map/swap/ppermute | solution.py:319
  32.3 1.6 %collective-permute-start.6 = (bf16[3,256,512]{2,1,0:T(8,128)(2,1)S(1)}, bf16[3,256,512]{2,1,0:T(8,128)(2,1)S(1)}, u32[]{:S(2)}, u32[]{:S(2)}) collective-permute-start(bf16[3,256,512]{2,1,0:T(8,128)(2,1)S(1)} %get-tuple-element.28.refs_1_.refs_4_), channel_id=1, source_target_pairs={{0,4},{1,3},{2,6},{3,1},{4,0},{5,7},{6,2},{7,5},{8,12},{9,11},{10,... | collective-permute-start | bytes 2359304 | tf_op jit(solution)/shard_map/stays1/ppermute | solution.py:331
  34.0 0.9 %collective-permute-start.9 = (bf16[2,256,512]{2,1,0:T(8,128)(2,1)S(1)}, bf16[2,256,512]{2,1,0:T(8,128)(2,1)S(1)}, u32[]{:S(2)}, u32[]{:S(2)}) collective-permute-start(bf16[2,256,512]{2,1,0:T(8,128)(2,1)S(1)} %get-tuple-element.30.refs_5_), channel_id=1, source_target_pairs={{0,4},{1,3},{2,6},{3,1},{4,0},{5,7},{6,2},{7,5},{8,12},{9,11},{10,... | collective-permute-start | bytes 1572872 | tf_op jit(solution)/shard_map/stays1/ppermute | solution.py:331
  34.9 9.5 %collective-permute-done.6.refs_2_.refs_6_ = bf16[3,256,512]{2,1,0:T(8,128)(2,1)S(1)} collective-permute-done((bf16[3,256,512]{2,1,0:T(8,128)(2,1)S(1)}, bf16[3,256,512]{2,1,0:T(8,128)(2,1)S(1)}, u32[]{:S(2)}, u32[]{:S(2)}) %collective-permute-start.6) | collective-permute-done | bytes 786464 | tf_op jit(solution)/shard_map/stays1/ppermute | solution.py:331
  45.6 1.6 %collective-permute-start.11 = (bf16[2,1,256,512]{3,2,1,0:T(8,128)(2,1)S(1)}, bf16[2,1,256,512]{3,2,1,0:T(8,128)(2,1)S(1)}, u32[]{:S(2)}, u32[]{:S(2)}) collective-permute-start(bf16[2,1,256,512]{3,2,1,0:T(8,128)(2,1)S(1)} %pick_third.1.refs_2_.refs_1_), channel_id=1, source_target_pairs={{0,2},{1,5},{2,0},{3,7},{4,6},{5,1},{6,4},{7,3},{8,10},{9,13},{10,... | collective-permute-start | bytes 1572872 | tf_op jit(solution)/shard_map/third0/ppermute | solution.py:331
  47.2 1.5 %collective-permute-start.7 = (bf16[256,512]{1,0:T(8,128)(2,1)S(1)}, bf16[256,512]{1,0:T(8,128)(2,1)S(1)}, u32[]{:S(2)}, u32[]{:S(2)}) collective-permute-start(bf16[256,512]{1,0:T(8,128)(2,1)S(1)} %extra_here.1.refs_5_.refs_0_.refs_2_), channel_id=1, source_target_pairs={{0,16},{24,8},{1,17},{25,9},{2,18},{26,10},{3,19},{27,11},{4,20},{... | collective-permute-start | bytes 786440 | tf_op jit(solution)/shard_map/extra_z2/ppermute | solution.py:319
  49.3 3.4 %collective-permute-done.9.refs_3_.refs_7_ = bf16[2,256,512]{2,1,0:T(8,128)(2,1)S(1)} collective-permute-done((bf16[2,256,512]{2,1,0:T(8,128)(2,1)S(1)}, bf16[2,256,512]{2,1,0:T(8,128)(2,1)S(1)}, u32[]{:S(2)}, u32[]{:S(2)}) %collective-permute-start.9) | collective-permute-done | bytes 524320 | tf_op jit(solution)/shard_map/stays1/ppermute | solution.py:331
  52.7 2.8 %collective-permute-done.7.refs_1_.refs_3_ = bf16[256,512]{1,0:T(8,128)(2,1)S(1)} collective-permute-done((bf16[256,512]{1,0:T(8,128)(2,1)S(1)}, bf16[256,512]{1,0:T(8,128)(2,1)S(1)}, u32[]{:S(2)}, u32[]{:S(2)}) %collective-permute-start.7) | collective-permute-done | bytes 262176 | tf_op jit(solution)/shard_map/extra_z2/ppermute | solution.py:319
  55.5 4.6 %collective-permute-start.10 = (bf16[256,512]{1,0:T(8,128)(2,1)S(1)}, bf16[256,512]{1,0:T(8,128)(2,1)S(1)}, u32[]{:S(2)}, u32[]{:S(2)}) collective-permute-start(bf16[256,512]{1,0:T(8,128)(2,1)S(1)} %hand_on.1), channel_id=1, source_target_pairs={{0,8},{24,16},{16,24},{8,0},{1,9},{25,17},{17,25},{9,1},{2,10},{26... | collective-permute-start | bytes 786440 | tf_op jit(solution)/shard_map/extra_z1/ppermute | solution.py:319
  60.7 1.6 %collective-permute-start.15 = (bf16[2,1,256,512]{3,2,1,0:T(8,128)(2,1)S(1)}, bf16[2,1,256,512]{3,2,1,0:T(8,128)(2,1)S(1)}, u32[]{:S(2)}, u32[]{:S(2)}) collective-permute-start(bf16[2,1,256,512]{3,2,1,0:T(8,128)(2,1)S(1)} %forward_third.1.refs_5_.refs_8_), channel_id=1, source_target_pairs={{0,4},{1,3},{2,6},{3,1},{4,0},{5,7},{6,2},{7,5},{8,12},{9,11},{10,... | collective-permute-start | bytes 1572872 | tf_op jit(solution)/shard_map/third1/ppermute | solution.py:331
  62.3 4.4 %collective-permute-done.12.refs_6_.refs_5_ = bf16[512,512]{1,0:T(8,128)(2,1)S(1)} collective-permute-done((bf16[512,512]{1,0:T(8,128)(2,1)S(1)}, bf16[512,512]{1,0:T(8,128)(2,1)S(1)}, u32[]{:S(2)}, u32[]{:S(2)}) %collective-permute-start.12) | collective-permute-done | bytes 524320 | tf_op jit(solution)/shard_map/row1/ppermute | solution.py:319
  66.7 3.3 %collective-permute-done.10.refs_4_ = bf16[256,512]{1,0:T(8,128)(2,1)S(1)} collective-permute-done((bf16[256,512]{1,0:T(8,128)(2,1)S(1)}, bf16[256,512]{1,0:T(8,128)(2,1)S(1)}, u32[]{:S(2)}, u32[]{:S(2)}) %collective-permute-start.10) | collective-permute-done | bytes 262176 | tf_op jit(solution)/shard_map/extra_z1/ppermute | solution.py:319
  69.9 0.9 %settle_extra.1 = (bf16[256,512]{1,0:T(8,128)(2,1)S(1)}, bf16[256,512]{1,0:T(8,128)(2,1)S(1)}) custom-call(s32[2,3]{1,0:T(2,128)S(1)} %copy-done.2, bf16[2,512,512]{2,1,0:T(8,128)(2,1)S(1)} %copy-done, bf16[256,512]{1,0:T(8,128)(2,1)S(1)} %extra_here.1.refs_5_.refs_0_.refs_2_, bf16[256,512]{1,0:T(8,128)(2,1)S(1)} %collective-permute-done.7.refs_1_.refs_3_, ...), custom_call_target="tpu_custom_call" | custom-call | flops 134217728 | bytes 1835032 | tf_op jit(solution)/shard_map/settle_extra/pallas_call | solution.py:301
  71.5 1.0 %collective-permute-done.13.refs_10_.refs_2_ = bf16[256,512]{1,0:T(8,128)(2,1)S(1)} collective-permute-done((bf16[256,512]{1,0:T(8,128)(2,1)S(1)}, bf16[256,512]{1,0:T(8,128)(2,1)S(1)}, u32[]{:S(2)}, u32[]{:S(2)}) %collective-permute-start.13) | collective-permute-done | bytes 262176 | tf_op jit(solution)/shard_map/sib_l/ppermute | solution.py:323
  72.9 2.5 %multiply.1.refs_6_.refs_3_ = bf16[2,3,256,512]{3,2,1,0:T(8,128)(2,1)S(1)} custom-call(s32[2,3]{1,0:T(2,128)S(1)} %copy-done.2, bf16[2,512,512]{2,1,0:T(8,128)(2,1)S(1)} %copy-done, bf16[256,512]{1,0:T(8,128)(2,1)S(1)} %get-tuple-element.32.refs_2_, bf16[256,512]{1,0:T(8,128)(2,1)S(1)} %collective-permute-done.14.refs_3_, ...), custom_call_target="tpu_custom_call" | custom-call | flops 1207959552 | bytes 5242904 | tf_op jit(solution)/shard_map/multiply/pallas_call | solution.py:301
  75.6 1.1 %settle_rows.1 = (bf16[2,512,512]{2,1,0:T(8,128)(2,1)S(1)}, bf16[512,512]{1,0:T(8,128)(2,1)S(1)}) custom-call(s32[2,3]{1,0:T(2,128)S(1)} %copy-done.2, bf16[256,512]{1,0:T(8,128)(2,1)S(1)} %get-tuple-element.31.refs_1_, bf16[256,512]{1,0:T(8,128)(2,1)S(1)} %collective-permute-done.13.refs_10_.refs_2_, ...), custom_call_target="tpu_custom_call" | custom-call | flops 268435456 | bytes 2097176 | tf_op jit(solution)/shard_map/settle_rows/pallas_call | solution.py:301
  76.7 2.2 %collective-permute-done.16.refs_4_ = bf16[2,3,256,512]{3,2,1,0:T(8,128)(2,1)S(1)} collective-permute-done((bf16[2,3,256,512]{3,2,1,0:T(8,128)(2,1)S(1)}, bf16[2,3,256,512]{3,2,1,0:T(8,128)(2,1)S(1)}, u32[]{:S(2)}, u32[]{:S(2)}) %collective-permute-start.16) | collective-permute-done | bytes 1572896 | tf_op jit(solution)/shard_map/sib_mine/ppermute | solution.py:323
  78.9 4.4 %finish.1 = bf16[3,512,512]{2,1,0:T(8,128)(2,1)} custom-call(s32[2,3]{1,0:T(2,128)S(1)} %copy-done.2, bf16[2,512,512]{2,1,0:T(8,128)(2,1)S(1)} %get-tuple-element.33.refs_1_, bf16[512,512]{1,0:T(8,128)(2,1)S(1)} %get-tuple-element.34.refs_2_, bf16[2,3,256,512]{3,2,1,0:T(8,128)(2,1)S(1)} %multiply.1.refs_6_.refs_3_, ...), custom_call_target="tpu_custom_call" | custom-call | flops 1610612736 | bytes 6815768 | tf_op jit(solution)/shard_map/finish/pallas_call | solution.py:301
  (30 shorter events, 7.2 us)
Async XLA Ops:
  0.0 1.4 %copy-start.1 = (bf16[3,512,1,512]{3,1,2,0:T(8,128)(2,1)S(1)}, bf16[3,512,1,512]{3,1,2,0:T(8,128)(2,1)}, u32[]{:S(2)}) copy-start(bf16[3,512,1,512]{3,1,2,0:T(8,128)(2,1)} %param.4) | copy-start | bytes 4718596
  1.4 0.7 copy-start.2
  2.1 0.7 copy-start.3
  3.6 4.2 %collective-permute-start = (bf16[3,256,512]{2,1,0:T(8,128)(2,1)S(1)}, bf16[3,256,512]{2,1,0:T(8,128)(2,1)S(1)}, u32[]{:S(2)}, u32[]{:S(2)}) collective-permute-start(bf16[3,256,512]{2,1,0:T(8,128)(2,1)S(1)} %get-tuple-element.21), channel_id=1, source_target_pairs={{0,1},{1,0},{2,3},{3,2},{4,5},{5,4},{6,7},{7,6},{8,9},{9,8},{10,11... | collective-permute-start | bytes 2359304 | tf_op jit(solution)/shard_map/sib_early/ppermute | solution.py:323
  4.1 27.4 %collective-permute-start.5 = (bf16[512,512]{1,0:T(8,128)(2,1)S(1)}, bf16[512,512]{1,0:T(8,128)(2,1)S(1)}, u32[]{:S(2)}, u32[]{:S(2)}) collective-permute-start(bf16[512,512]{1,0:T(8,128)(2,1)S(1)} %get-tuple-element.26.refs_0_.refs_3_), channel_id=1, source_target_pairs={{0,16},{24,8},{16,0},{8,24},{1,17},{25,9},{17,1},{9,25},{2,18},{26... | collective-permute-start | bytes 1572872 | tf_op jit(solution)/shard_map/swap/ppermute | solution.py:319
  8.5 23.1 %collective-permute-start.4 = (bf16[2,256,512]{2,1,0:T(8,128)(2,1)S(1)}, bf16[2,256,512]{2,1,0:T(8,128)(2,1)S(1)}, u32[]{:S(2)}, u32[]{:S(2)}) collective-permute-start(bf16[2,256,512]{2,1,0:T(8,128)(2,1)S(1)} %get-tuple-element.25.refs_4_), channel_id=1, source_target_pairs={{0,2},{1,5},{2,0},{3,7},{4,6},{5,1},{6,4},{7,3},{8,10},{9,13},{10,... | collective-permute-start | bytes 1572872 | tf_op jit(solution)/shard_map/stays0/ppermute | solution.py:331
  10.0 21.5 %collective-permute-start.1 = (bf16[1,256,512]{2,1,0:T(8,128)(2,1)S(1)}, bf16[1,256,512]{2,1,0:T(8,128)(2,1)S(1)}, u32[]{:S(2)}, u32[]{:S(2)}) collective-permute-start(bf16[1,256,512]{2,1,0:T(8,128)(2,1)S(1)} %get-tuple-element.22.refs_1_), channel_id=1, source_target_pairs={{0,2},{1,5},{2,0},{3,7},{4,6},{5,1},{6,4},{7,3},{8,10},{9,13},{10,... | collective-permute-start | bytes 786440 | tf_op jit(solution)/shard_map/stays0/ppermute | solution.py:331
  10.6 21.0 %collective-permute-start.2 = (bf16[1,256,512]{2,1,0:T(8,128)(2,1)S(1)}, bf16[1,256,512]{2,1,0:T(8,128)(2,1)S(1)}, u32[]{:S(2)}, u32[]{:S(2)}) collective-permute-start(bf16[1,256,512]{2,1,0:T(8,128)(2,1)S(1)} %get-tuple-element.23.refs_2_), channel_id=1, source_target_pairs={{0,2},{1,5},{2,0},{3,7},{4,6},{5,1},{6,4},{7,3},{8,10},{9,13},{10,... | collective-permute-start | bytes 786440 | tf_op jit(solution)/shard_map/stays0/ppermute | solution.py:331
  12.1 19.5 %collective-permute-start.3 = (bf16[1,256,512]{2,1,0:T(8,128)(2,1)S(1)}, bf16[1,256,512]{2,1,0:T(8,128)(2,1)S(1)}, u32[]{:S(2)}, u32[]{:S(2)}) collective-permute-start(bf16[1,256,512]{2,1,0:T(8,128)(2,1)S(1)} %get-tuple-element.24.refs_3_), channel_id=1, source_target_pairs={{0,2},{1,5},{2,0},{3,7},{4,6},{5,1},{6,4},{7,3},{8,10},{9,13},{10,... | collective-permute-start | bytes 786440 | tf_op jit(solution)/shard_map/stays0/ppermute | solution.py:331
  32.3 12.1 %collective-permute-start.6 = (bf16[3,256,512]{2,1,0:T(8,128)(2,1)S(1)}, bf16[3,256,512]{2,1,0:T(8,128)(2,1)S(1)}, u32[]{:S(2)}, u32[]{:S(2)}) collective-permute-start(bf16[3,256,512]{2,1,0:T(8,128)(2,1)S(1)} %get-tuple-element.28.refs_1_.refs_4_), channel_id=1, source_target_pairs={{0,4},{1,3},{2,6},{3,1},{4,0},{5,7},{6,2},{7,5},{8,12},{9,11},{10,... | collective-permute-start | bytes 2359304 | tf_op jit(solution)/shard_map/stays1/ppermute | solution.py:331
  34.0 11.0 %collective-permute-start.8 = (bf16[256,512]{1,0:T(8,128)(2,1)S(1)}, bf16[256,512]{1,0:T(8,128)(2,1)S(1)}, u32[]{:S(2)}, u32[]{:S(2)}) collective-permute-start(bf16[256,512]{1,0:T(8,128)(2,1)S(1)} %get-tuple-element.29), channel_id=1, source_target_pairs={{0,1},{1,0},{2,3},{3,2},{4,5},{5,4},{6,7},{7,6},{8,9},{9,8},{10,11... | collective-permute-start | bytes 786440 | tf_op jit(solution)/shard_map/sib_moved/ppermute | solution.py:323
  34.0 18.7 %collective-permute-start.9 = (bf16[2,256,512]{2,1,0:T(8,128)(2,1)S(1)}, bf16[2,256,512]{2,1,0:T(8,128)(2,1)S(1)}, u32[]{:S(2)}, u32[]{:S(2)}) collective-permute-start(bf16[2,256,512]{2,1,0:T(8,128)(2,1)S(1)} %get-tuple-element.30.refs_5_), channel_id=1, source_target_pairs={{0,4},{1,3},{2,6},{3,1},{4,0},{5,7},{6,2},{7,5},{8,12},{9,11},{10,... | collective-permute-start | bytes 1572872 | tf_op jit(solution)/shard_map/stays1/ppermute | solution.py:331
  45.6 24.3 %copy-start = (bf16[2,512,512]{2,1,0:T(8,128)(2,1)S(1)}, bf16[2,512,512]{2,1,0:T(8,128)(2,1)}, u32[]{:S(2)}) copy-start(bf16[2,512,512]{2,1,0:T(8,128)(2,1)} %refs_1_.3) | copy-start | bytes 3145732
  45.6 14.4 %collective-permute-start.11 = (bf16[2,1,256,512]{3,2,1,0:T(8,128)(2,1)S(1)}, bf16[2,1,256,512]{3,2,1,0:T(8,128)(2,1)S(1)}, u32[]{:S(2)}, u32[]{:S(2)}) collective-permute-start(bf16[2,1,256,512]{3,2,1,0:T(8,128)(2,1)S(1)} %pick_third.1.refs_2_.refs_1_), channel_id=1, source_target_pairs={{0,2},{1,5},{2,0},{3,7},{4,6},{5,1},{6,4},{7,3},{8,10},{9,13},{10,... | collective-permute-start | bytes 1572872 | tf_op jit(solution)/shard_map/third0/ppermute | solution.py:331
  47.2 8.2 %collective-permute-start.7 = (bf16[256,512]{1,0:T(8,128)(2,1)S(1)}, bf16[256,512]{1,0:T(8,128)(2,1)S(1)}, u32[]{:S(2)}, u32[]{:S(2)}) collective-permute-start(bf16[256,512]{1,0:T(8,128)(2,1)S(1)} %extra_here.1.refs_5_.refs_0_.refs_2_), channel_id=1, source_target_pairs={{0,16},{24,8},{1,17},{25,9},{2,18},{26,10},{3,19},{27,11},{4,20},{... | collective-permute-start | bytes 786440 | tf_op jit(solution)/shard_map/extra_z2/ppermute | solution.py:319
  48.7 18.0 %collective-permute-start.12 = (bf16[512,512]{1,0:T(8,128)(2,1)S(1)}, bf16[512,512]{1,0:T(8,128)(2,1)S(1)}, u32[]{:S(2)}, u32[]{:S(2)}) collective-permute-start(bf16[512,512]{1,0:T(8,128)(2,1)S(1)} %get-tuple-element.27.refs_9_), channel_id=1, source_target_pairs={{0,8},{24,16},{16,24},{8,0},{1,9},{25,17},{17,25},{9,1},{2,10},{26... | collective-permute-start | bytes 1572872 | tf_op jit(solution)/shard_map/row1/ppermute | solution.py:319
  55.5 14.5 %collective-permute-start.10 = (bf16[256,512]{1,0:T(8,128)(2,1)S(1)}, bf16[256,512]{1,0:T(8,128)(2,1)S(1)}, u32[]{:S(2)}, u32[]{:S(2)}) collective-permute-start(bf16[256,512]{1,0:T(8,128)(2,1)S(1)} %hand_on.1), channel_id=1, source_target_pairs={{0,8},{24,16},{16,24},{8,0},{1,9},{25,17},{17,25},{9,1},{2,10},{26... | collective-permute-start | bytes 786440 | tf_op jit(solution)/shard_map/extra_z1/ppermute | solution.py:319
  60.7 12.2 %collective-permute-start.15 = (bf16[2,1,256,512]{3,2,1,0:T(8,128)(2,1)S(1)}, bf16[2,1,256,512]{3,2,1,0:T(8,128)(2,1)S(1)}, u32[]{:S(2)}, u32[]{:S(2)}) collective-permute-start(bf16[2,1,256,512]{3,2,1,0:T(8,128)(2,1)S(1)} %forward_third.1.refs_5_.refs_8_), channel_id=1, source_target_pairs={{0,4},{1,3},{2,6},{3,1},{4,0},{5,7},{6,2},{7,5},{8,12},{9,11},{10,... | collective-permute-start | bytes 1572872 | tf_op jit(solution)/shard_map/third1/ppermute | solution.py:331
  70.9 1.6 %collective-permute-start.13 = (bf16[256,512]{1,0:T(8,128)(2,1)S(1)}, bf16[256,512]{1,0:T(8,128)(2,1)S(1)}, u32[]{:S(2)}, u32[]{:S(2)}) collective-permute-start(bf16[256,512]{1,0:T(8,128)(2,1)S(1)} %get-tuple-element.31.refs_1_), channel_id=1, source_target_pairs={{0,1},{1,0},{2,3},{3,2},{4,5},{5,4},{6,7},{7,6},{8,9},{9,8},{10,11... | collective-permute-start | bytes 786440 | tf_op jit(solution)/shard_map/sib_l/ppermute | solution.py:323
  71.0 1.9 %collective-permute-start.14 = (bf16[256,512]{1,0:T(8,128)(2,1)S(1)}, bf16[256,512]{1,0:T(8,128)(2,1)S(1)}, u32[]{:S(2)}, u32[]{:S(2)}) collective-permute-start(bf16[256,512]{1,0:T(8,128)(2,1)S(1)} %get-tuple-element.32.refs_2_), channel_id=1, source_target_pairs={{0,1},{1,0},{2,3},{3,2},{4,5},{5,4},{6,7},{7,6},{8,9},{9,8},{10,11... | collective-permute-start | bytes 786440 | tf_op jit(solution)/shard_map/sib_v/ppermute | solution.py:323
  75.4 3.5 %collective-permute-start.16 = (bf16[2,3,256,512]{3,2,1,0:T(8,128)(2,1)S(1)}, bf16[2,3,256,512]{3,2,1,0:T(8,128)(2,1)S(1)}, u32[]{:S(2)}, u32[]{:S(2)}) collective-permute-start(bf16[2,3,256,512]{3,2,1,0:T(8,128)(2,1)S(1)} %multiply.1.refs_6_.refs_3_), channel_id=1, source_target_pairs={{0,1},{1,0},{2,3},{3,2},{4,5},{5,4},{6,7},{7,6},{8,9},{9,8},{10,11... | collective-permute-start | bytes 4718600 | tf_op jit(solution)/shard_map/sib_mine/ppermute | solution.py:323

commit v11 on v10

--- a/solution.py
+++ b/solution.py
@@ -101,10 +101,10 @@
             either(hit, panel.at[q, 0], lambda: raw[rb - 1, cut, :], lambda: sib[rb - 1])
 
 
-def relay(n, m, stride, leaving, moved, other, send):
+def relay(n, m, moved, other, send):
     core = lax.axis_index("pcol").astype(jnp.int32) & 1
     other[...] = moved[rows(1 - core, moved.shape[0] // 2), :]
-    hand_on(n, m, stride, leaving, moved, send)
+    send[...] = moved[...]
 
 
 def bit_of(f, column, stage, stages):
@@ -204,9 +204,8 @@
         place = r if which == 0 else n - 1 - r
         slot = jnp.where(f["low_first"], which, 1 - which)
         for s in range(len(came)):
-            here = place == 0 if s == 0 else (place & (2 * (n >> s) - 1)) == (n >> s)
-
-            @pl.when(here)
+
+            @pl.when(place == s)
             def _():
                 upper[slot] = came[s][...]
 
@@ -340,7 +339,7 @@
         blocks,
     )
     early = sibling("sib_early", other)
-    exchange = [(0, n // 2), (n - 1, n // 2 - 1), (n // 2, 0), (n // 2 - 1, n - 1)]
+    exchange = [(0, 1), (n - 1, n - 2), (n // 2, 0), (n // 2 - 1, n - 1)]
     moved = along("swap", exchange, leaving)
 
     def split(stride):
@@ -353,10 +352,7 @@
     pieces = [(1, *strip)] * (2 * rb - 3) + [(2, *strip)]
     panel = call(pick, pieces, "s", pivots, raw, early)
     got = [across("stays0", 0, piece) for piece in panel]
-    step = lambda _n, _m, *refs: relay(n, m, n // 2, *refs)
-    other_moved, send = call(
-        step, [strip, square], "", leaving, moved, name="relay", after=got
-    )
+    other_moved, send = call(relay, [strip, square], "", moved, name="relay", after=got)
     for s in range(stages - 1):
         step = lambda _n, _m, *refs: forward_all(n, m, rb, s, stages, *refs)
         panel = call(
@@ -391,13 +387,9 @@
     third_got = across("third0", 0, third)
 
     arrived = [leaving, moved]
-    stride = n // 4
-    while stride:
-        got = along("row" + str(stride), split(stride), send)
-        arrived.append(got)
-        if stride > 1:
-            send = call(hand(stride), [square], "", send, got, name="hand_on_row")
-        stride //= 2
+    for h in range(1, n - 1):
+        send = along("row" + str(h), [(h, h + 1), (n - 1 - h, n - 2 - h)], send)
+        arrived.append(send)
 
     came = [extra_here]
     send = extra_here
@@ -406,7 +398,7 @@
         got = along("extra_z" + str(stride), split(stride), send)
         came.append(got)
         if stride > 1:
-            send = call(hand(stride), [strip], "", send, got, name="hand_on", after=[third, stays[-1]])
+            send = call(hand(stride), [strip], "", send, got, name="hand_on", after=[third, stays[-1], arrived[2]])
         stride //= 2
     for s in range(stages - 1):
         step = lambda _n, _m, *refs: forward(n, m, s, stages, *refs)
@@ -422,7 +414,7 @@
         inverses,
         *came,
         products=0.5,
-        after=[third, arrived[2]],
+        after=[third, arrived[3]],
     )
     sib_v = sibling("sib_v", v_half)
     sib_l = sibling("sib_l", l_half)

time: 83.8 us -> 78.7 us (0.939)
  waiting for transfers between devices: 45.9 us -> 38.2 us
  starting transfers between devices: 21.4 us -> 24.3 us
    ppermute x4 -> x5, waiting for transfers between devices: 29.4 us -> 21 us  [along(): return lax.ppermute(value, 'prow', pairs)]
    ppermute x4 -> x5, starting transfers between devices: 10.3 us -> 11.9 us  [along(): return lax.ppermute(value, 'prow', pairs)]
    ppermute x8, starting transfers between devices: 9.84 us -> 11 us  [across(): return lax.ppermute(value, 'pcol', pairs)]
  transfers between devices with their start and end apart: 17 -> 18, of which waited for: 9 -> 10; matrix products, arithmetic and copies ran while one was open for 0% -> 0% of each run, Pallas kernels for 5% -> 6%
where the time goes in v11:
time: 78.7 us; the launch traced here: 78.5 us
  waiting for transfers between devices  38.2 us (49%)
  starting transfers between devices  24.3 us (31%)
  Pallas kernels  13.1 us (17%)
  local copies, waits for them, and re-layouts  2.78 us (4%)
    ppermute x5, waiting for transfers between devices, along(): return lax.ppermute(value, 'prow', pairs)  21 us
    ppermute x8, waiting for transfers between devices, across(): return lax.ppermute(value, 'pcol', pairs)  13.6 us
    pallas_call x12, Pallas kernels, call(): pl.pallas_call(body, out_shape=outs, in_specs=specs, out_specs=[place] *...  13.1 us
    ppermute x5, starting transfers between devices, along(): return lax.ppermute(value, 'prow', pairs)  11.9 us
    ppermute x8, starting transfers between devices, across(): return lax.ppermute(value, 'pcol', pairs)  11 us
    ppermute x5, waiting for transfers between devices, sibling(): return lax.ppermute(value, 'pcol', [(i, i ^ 1) for i in range(m)])  3.56 us
    unnamed x8, local copies, waits for them, and re-layouts  2.78 us
  transfers between devices with their start and end apart: 18, of which 10 were waited for; matrix products, arithmetic and copies ran while one was open for 0% of the time, Pallas kernels for 6%

profile of v11, /device:TPU:0, one launch (start us, length us, event | category | flops | bytes accessed | tf_op | source)
XLA Modules:
  0.0 78.5 jit_solution(6850509909335427370)
XLA Ops:
  0.0 1.4 %copy-done.1 = bf16[3,512,1,512]{3,1,2,0:T(8,128)(2,1)S(1)} copy-done((bf16[3,512,1,512]{3,1,2,0:T(8,128)(2,1)S(1)}, bf16[3,512,1,512]{3,1,2,0:T(8,128)(2,1)}, u32[]{:S(2)}) %copy-start.1) | copy-done | bytes 1572888
  2.8 0.8 %prepare.1 = (bf16[3,512,512]{2,1,0:T(8,128)(2,1)S(1)}, bf16[512,512]{1,0:T(8,128)(2,1)S(1)}, bf16[3,256,512]{2,1,0:T(8,128)(2,1)S(1)}) custom-call(s32[2,3]{1,0:T(2,128)S(1)} %copy-done.2, s32[8,12]{1,0:T(8,128)S(1)} %bitcast.6, bf16[3,512,512]{2,1,0:T(8,128)(2,1)S(1)} %bitcast.5), custom_call_target="tpu_custom_call" | custom-call | bytes 1573272 | tf_op jit(solution)/shard_map/prepare/pallas_call | solution.py:300
  4.1 2.6 %collective-permute-start.5 = (bf16[512,512]{1,0:T(8,128)(2,1)S(1)}, bf16[512,512]{1,0:T(8,128)(2,1)S(1)}, u32[]{:S(2)}, u32[]{:S(2)}) collective-permute-start(bf16[512,512]{1,0:T(8,128)(2,1)S(1)} %get-tuple-element.26.refs_3_), channel_id=1, source_target_pairs={{0,8},{24,16},{16,0},{8,24},{1,9},{25,17},{17,1},{9,25},{2,10},{26... | collective-permute-start | bytes 1572872 | tf_op jit(solution)/shard_map/swap/ppermute | solution.py:318
  7.5 2.2 %collective-permute-start.4 = (bf16[2,256,512]{2,1,0:T(8,128)(2,1)S(1)}, bf16[2,256,512]{2,1,0:T(8,128)(2,1)S(1)}, u32[]{:S(2)}, u32[]{:S(2)}) collective-permute-start(bf16[2,256,512]{2,1,0:T(8,128)(2,1)S(1)} %get-tuple-element.25.refs_4_), channel_id=1, source_target_pairs={{0,2},{1,5},{2,0},{3,7},{4,6},{5,1},{6,4},{7,3},{8,10},{9,13},{10,... | collective-permute-start | bytes 1572872 | tf_op jit(solution)/shard_map/stays0/ppermute | solution.py:330
  9.7 1.9 %collective-permute-start.2 = (bf16[1,256,512]{2,1,0:T(8,128)(2,1)S(1)}, bf16[1,256,512]{2,1,0:T(8,128)(2,1)S(1)}, u32[]{:S(2)}, u32[]{:S(2)}) collective-permute-start(bf16[1,256,512]{2,1,0:T(8,128)(2,1)S(1)} %get-tuple-element.23.refs_2_), channel_id=1, source_target_pairs={{0,2},{1,5},{2,0},{3,7},{4,6},{5,1},{6,4},{7,3},{8,10},{9,13},{10,... | collective-permute-start | bytes 786440 | tf_op jit(solution)/shard_map/stays0/ppermute | solution.py:330
  11.8 8.6 %collective-permute-done.5.refs_0_.refs_3_.refs_4_.refs_6_ = bf16[512,512]{1,0:T(8,128)(2,1)S(1)} collective-permute-done((bf16[512,512]{1,0:T(8,128)(2,1)S(1)}, bf16[512,512]{1,0:T(8,128)(2,1)S(1)}, u32[]{:S(2)}, u32[]{:S(2)}) %collective-permute-start.5) | collective-permute-done | bytes 524320 | tf_op jit(solution)/shard_map/swap/ppermute | solution.py:318
  20.3 2.1 %collective-permute-done.2.refs_2_.refs_6_ = bf16[1,256,512]{2,1,0:T(8,128)(2,1)S(1)} collective-permute-done((bf16[1,256,512]{2,1,0:T(8,128)(2,1)S(1)}, bf16[1,256,512]{2,1,0:T(8,128)(2,1)S(1)}, u32[]{:S(2)}, u32[]{:S(2)}) %collective-permute-start.2) | collective-permute-done | bytes 262176 | tf_op jit(solution)/shard_map/stays0/ppermute | solution.py:330
  22.4 2.8 %collective-permute-done.3.refs_3_.refs_7_ = bf16[1,256,512]{2,1,0:T(8,128)(2,1)S(1)} collective-permute-done((bf16[1,256,512]{2,1,0:T(8,128)(2,1)S(1)}, bf16[1,256,512]{2,1,0:T(8,128)(2,1)S(1)}, u32[]{:S(2)}, u32[]{:S(2)}) %collective-permute-start.3) | collective-permute-done | bytes 262176 | tf_op jit(solution)/shard_map/stays0/ppermute | solution.py:330
  26.0 2.1 %collective-permute-start.6 = (bf16[3,256,512]{2,1,0:T(8,128)(2,1)S(1)}, bf16[3,256,512]{2,1,0:T(8,128)(2,1)S(1)}, u32[]{:S(2)}, u32[]{:S(2)}) collective-permute-start(bf16[3,256,512]{2,1,0:T(8,128)(2,1)S(1)} %get-tuple-element.28.refs_1_.refs_4_), channel_id=1, source_target_pairs={{0,4},{1,3},{2,6},{3,1},{4,0},{5,7},{6,2},{7,5},{8,12},{9,11},{10,... | collective-permute-start | bytes 2359304 | tf_op jit(solution)/shard_map/stays1/ppermute | solution.py:330
  29.3 8.7 %collective-permute-done.6.refs_2_.refs_6_ = bf16[3,256,512]{2,1,0:T(8,128)(2,1)S(1)} collective-permute-done((bf16[3,256,512]{2,1,0:T(8,128)(2,1)S(1)}, bf16[3,256,512]{2,1,0:T(8,128)(2,1)S(1)}, u32[]{:S(2)}, u32[]{:S(2)}) %collective-permute-start.6) | collective-permute-done | bytes 786464 | tf_op jit(solution)/shard_map/stays1/ppermute | solution.py:330
  39.3 2.1 %collective-permute-start.12 = (bf16[2,1,256,512]{3,2,1,0:T(8,128)(2,1)S(1)}, bf16[2,1,256,512]{3,2,1,0:T(8,128)(2,1)S(1)}, u32[]{:S(2)}, u32[]{:S(2)}) collective-permute-start(bf16[2,1,256,512]{3,2,1,0:T(8,128)(2,1)S(1)} %pick_third.1.refs_2_.refs_1_), channel_id=1, source_target_pairs={{0,2},{1,5},{2,0},{3,7},{4,6},{5,1},{6,4},{7,3},{8,10},{9,13},{10,... | collective-permute-start | bytes 1572872 | tf_op jit(solution)/shard_map/third0/ppermute | solution.py:330
  41.4 4.5 %collective-permute-start.7 = (bf16[256,512]{1,0:T(8,128)(2,1)S(1)}, bf16[256,512]{1,0:T(8,128)(2,1)S(1)}, u32[]{:S(2)}, u32[]{:S(2)}) collective-permute-start(bf16[256,512]{1,0:T(8,128)(2,1)S(1)} %extra_here.1.refs_5_.refs_0_.refs_2_), channel_id=1, source_target_pairs={{0,16},{24,8},{1,17},{25,9},{2,18},{26,10},{3,19},{27,11},{4,20},{... | collective-permute-start | bytes 786440 | tf_op jit(solution)/shard_map/extra_z2/ppermute | solution.py:318
  45.9 1.3 %collective-permute-start.13 = (bf16[512,512]{1,0:T(8,128)(2,1)S(1)}, bf16[512,512]{1,0:T(8,128)(2,1)S(1)}, u32[]{:S(2)}, u32[]{:S(2)}) collective-permute-start(bf16[512,512]{1,0:T(8,128)(2,1)S(1)} %collective-permute-done.10.refs_4_.refs_5_), channel_id=1, source_target_pairs={{16,24},{8,0},{17,25},{9,1},{18,26},{10,2},{19,27},{11,3},{20,28},... | collective-permute-start | bytes 1572872 | tf_op jit(solution)/shard_map/row2/ppermute | solution.py:318
  47.2 2.5 %collective-permute-done.7.refs_1_.refs_3_ = bf16[256,512]{1,0:T(8,128)(2,1)S(1)} collective-permute-done((bf16[256,512]{1,0:T(8,128)(2,1)S(1)}, bf16[256,512]{1,0:T(8,128)(2,1)S(1)}, u32[]{:S(2)}, u32[]{:S(2)}) %collective-permute-start.7) | collective-permute-done | bytes 262176 | tf_op jit(solution)/shard_map/extra_z2/ppermute | solution.py:318
  49.8 2.8 %collective-permute-start.11 = (bf16[256,512]{1,0:T(8,128)(2,1)S(1)}, bf16[256,512]{1,0:T(8,128)(2,1)S(1)}, u32[]{:S(2)}, u32[]{:S(2)}) collective-permute-start(bf16[256,512]{1,0:T(8,128)(2,1)S(1)} %hand_on.1), channel_id=1, source_target_pairs={{0,8},{24,16},{16,24},{8,0},{1,9},{25,17},{17,25},{9,1},{2,10},{26... | collective-permute-start | bytes 786440 | tf_op jit(solution)/shard_map/extra_z1/ppermute | solution.py:318
  53.2 2.0 %collective-permute-start.16 = (bf16[2,1,256,512]{3,2,1,0:T(8,128)(2,1)S(1)}, bf16[2,1,256,512]{3,2,1,0:T(8,128)(2,1)S(1)}, u32[]{:S(2)}, u32[]{:S(2)}) collective-permute-start(bf16[2,1,256,512]{3,2,1,0:T(8,128)(2,1)S(1)} %forward_third.1.refs_5_.refs_8_), channel_id=1, source_target_pairs={{0,4},{1,3},{2,6},{3,1},{4,0},{5,7},{6,2},{7,5},{8,12},{9,11},{10,... | collective-permute-start | bytes 1572872 | tf_op jit(solution)/shard_map/third1/ppermute | solution.py:330
  55.2 7.1 %collective-permute-done.13.refs_6_ = bf16[512,512]{1,0:T(8,128)(2,1)S(1)} collective-permute-done((bf16[512,512]{1,0:T(8,128)(2,1)S(1)}, bf16[512,512]{1,0:T(8,128)(2,1)S(1)}, u32[]{:S(2)}, u32[]{:S(2)}) %collective-permute-start.13) | collective-permute-done | bytes 524320 | tf_op jit(solution)/shard_map/row2/ppermute | solution.py:318
  62.3 2.8 %collective-permute-done.11.refs_4_ = bf16[256,512]{1,0:T(8,128)(2,1)S(1)} collective-permute-done((bf16[256,512]{1,0:T(8,128)(2,1)S(1)}, bf16[256,512]{1,0:T(8,128)(2,1)S(1)}, u32[]{:S(2)}, u32[]{:S(2)}) %collective-permute-start.11) | collective-permute-done | bytes 262176 | tf_op jit(solution)/shard_map/extra_z1/ppermute | solution.py:318
  65.1 0.9 %settle_extra.1 = (bf16[256,512]{1,0:T(8,128)(2,1)S(1)}, bf16[256,512]{1,0:T(8,128)(2,1)S(1)}) custom-call(s32[2,3]{1,0:T(2,128)S(1)} %copy-done.2, bf16[2,512,512]{2,1,0:T(8,128)(2,1)S(1)} %copy-done, bf16[256,512]{1,0:T(8,128)(2,1)S(1)} %extra_here.1.refs_5_.refs_0_.refs_2_, bf16[256,512]{1,0:T(8,128)(2,1)S(1)} %collective-permute-done.7.refs_1_.refs_3_, ...), custom_call_target="tpu_custom_call" | custom-call | flops 134217728 | bytes 1835032 | tf_op jit(solution)/shard_map/settle_extra/pallas_call | solution.py:300
  66.6 1.0 %collective-permute-done.14.refs_10_.refs_2_ = bf16[256,512]{1,0:T(8,128)(2,1)S(1)} collective-permute-done((bf16[256,512]{1,0:T(8,128)(2,1)S(1)}, bf16[256,512]{1,0:T(8,128)(2,1)S(1)}, u32[]{:S(2)}, u32[]{:S(2)}) %collective-permute-start.14) | collective-permute-done | bytes 262176 | tf_op jit(solution)/shard_map/sib_l/ppermute | solution.py:322
  68.0 2.6 %multiply.1.refs_7_.refs_3_ = bf16[2,3,256,512]{3,2,1,0:T(8,128)(2,1)S(1)} custom-call(s32[2,3]{1,0:T(2,128)S(1)} %copy-done.2, bf16[2,512,512]{2,1,0:T(8,128)(2,1)S(1)} %copy-done, bf16[256,512]{1,0:T(8,128)(2,1)S(1)} %get-tuple-element.32.refs_2_, bf16[256,512]{1,0:T(8,128)(2,1)S(1)} %collective-permute-done.15.refs_3_, ...), custom_call_target="tpu_custom_call" | custom-call | flops 1207959552 | bytes 5242904 | tf_op jit(solution)/shard_map/multiply/pallas_call | solution.py:300
  70.8 1.1 %settle_rows.1 = (bf16[2,512,512]{2,1,0:T(8,128)(2,1)S(1)}, bf16[512,512]{1,0:T(8,128)(2,1)S(1)}) custom-call(s32[2,3]{1,0:T(2,128)S(1)} %copy-done.2, bf16[256,512]{1,0:T(8,128)(2,1)S(1)} %get-tuple-element.31.refs_1_, bf16[256,512]{1,0:T(8,128)(2,1)S(1)} %collective-permute-done.14.refs_10_.refs_2_, bf16[512,512]{1,0:T(8,128)(2,1)S(1)} %get-tuple-element.26.refs_3_, ...), custom_call_target="tpu_custom_call" | custom-call | flops 268435456 | bytes 2621464 | tf_op jit(solution)/shard_map/settle_rows/pallas_call | solution.py:300
  71.9 2.2 %collective-permute-done.17.refs_4_ = bf16[2,3,256,512]{3,2,1,0:T(8,128)(2,1)S(1)} collective-permute-done((bf16[2,3,256,512]{3,2,1,0:T(8,128)(2,1)S(1)}, bf16[2,3,256,512]{3,2,1,0:T(8,128)(2,1)S(1)}, u32[]{:S(2)}, u32[]{:S(2)}) %collective-permute-start.17) | collective-permute-done | bytes 1572896 | tf_op jit(solution)/shard_map/sib_mine/ppermute | solution.py:322
  74.1 4.4 %finish.1 = bf16[3,512,512]{2,1,0:T(8,128)(2,1)} custom-call(s32[2,3]{1,0:T(2,128)S(1)} %copy-done.2, bf16[2,512,512]{2,1,0:T(8,128)(2,1)S(1)} %get-tuple-element.33.refs_1_, bf16[512,512]{1,0:T(8,128)(2,1)S(1)} %get-tuple-element.34.refs_2_, bf16[2,3,256,512]{3,2,1,0:T(8,128)(2,1)S(1)} %multiply.1.refs_7_.refs_3_, ...), custom_call_target="tpu_custom_call" | custom-call | flops 1610612736 | bytes 6815768 | tf_op jit(solution)/shard_map/finish/pallas_call | solution.py:300
  (32 shorter events, 7.6 us)
Async XLA Ops:
  0.0 1.4 %copy-start.1 = (bf16[3,512,1,512]{3,1,2,0:T(8,128)(2,1)S(1)}, bf16[3,512,1,512]{3,1,2,0:T(8,128)(2,1)}, u32[]{:S(2)}) copy-start(bf16[3,512,1,512]{3,1,2,0:T(8,128)(2,1)} %param.4) | copy-start | bytes 4718596
  1.4 0.7 copy-start.2
  2.1 0.7 copy-start.3
  3.6 3.2 %collective-permute-start = (bf16[3,256,512]{2,1,0:T(8,128)(2,1)S(1)}, bf16[3,256,512]{2,1,0:T(8,128)(2,1)S(1)}, u32[]{:S(2)}, u32[]{:S(2)}) collective-permute-start(bf16[3,256,512]{2,1,0:T(8,128)(2,1)S(1)} %get-tuple-element.21), channel_id=1, source_target_pairs={{0,1},{1,0},{2,3},{3,2},{4,5},{5,4},{6,7},{7,6},{8,9},{9,8},{10,11... | collective-permute-start | bytes 2359304 | tf_op jit(solution)/shard_map/sib_early/ppermute | solution.py:322
  4.1 16.2 %collective-permute-start.5 = (bf16[512,512]{1,0:T(8,128)(2,1)S(1)}, bf16[512,512]{1,0:T(8,128)(2,1)S(1)}, u32[]{:S(2)}, u32[]{:S(2)}) collective-permute-start(bf16[512,512]{1,0:T(8,128)(2,1)S(1)} %get-tuple-element.26.refs_3_), channel_id=1, source_target_pairs={{0,8},{24,16},{16,0},{8,24},{1,9},{25,17},{17,1},{9,25},{2,10},{26... | collective-permute-start | bytes 1572872 | tf_op jit(solution)/shard_map/swap/ppermute | solution.py:318
  7.5 17.8 %collective-permute-start.4 = (bf16[2,256,512]{2,1,0:T(8,128)(2,1)S(1)}, bf16[2,256,512]{2,1,0:T(8,128)(2,1)S(1)}, u32[]{:S(2)}, u32[]{:S(2)}) collective-permute-start(bf16[2,256,512]{2,1,0:T(8,128)(2,1)S(1)} %get-tuple-element.25.refs_4_), channel_id=1, source_target_pairs={{0,2},{1,5},{2,0},{3,7},{4,6},{5,1},{6,4},{7,3},{8,10},{9,13},{10,... | collective-permute-start | bytes 1572872 | tf_op jit(solution)/shard_map/stays0/ppermute | solution.py:330
  9.7 10.7 %collective-permute-start.1 = (bf16[1,256,512]{2,1,0:T(8,128)(2,1)S(1)}, bf16[1,256,512]{2,1,0:T(8,128)(2,1)S(1)}, u32[]{:S(2)}, u32[]{:S(2)}) collective-permute-start(bf16[1,256,512]{2,1,0:T(8,128)(2,1)S(1)} %get-tuple-element.22.refs_1_), channel_id=1, source_target_pairs={{0,2},{1,5},{2,0},{3,7},{4,6},{5,1},{6,4},{7,3},{8,10},{9,13},{10,... | collective-permute-start | bytes 786440 | tf_op jit(solution)/shard_map/stays0/ppermute | solution.py:330
  9.7 12.7 %collective-permute-start.2 = (bf16[1,256,512]{2,1,0:T(8,128)(2,1)S(1)}, bf16[1,256,512]{2,1,0:T(8,128)(2,1)S(1)}, u32[]{:S(2)}, u32[]{:S(2)}) collective-permute-start(bf16[1,256,512]{2,1,0:T(8,128)(2,1)S(1)} %get-tuple-element.23.refs_2_), channel_id=1, source_target_pairs={{0,2},{1,5},{2,0},{3,7},{4,6},{5,1},{6,4},{7,3},{8,10},{9,13},{10,... | collective-permute-start | bytes 786440 | tf_op jit(solution)/shard_map/stays0/ppermute | solution.py:330
  11.7 13.6 %collective-permute-start.3 = (bf16[1,256,512]{2,1,0:T(8,128)(2,1)S(1)}, bf16[1,256,512]{2,1,0:T(8,128)(2,1)S(1)}, u32[]{:S(2)}, u32[]{:S(2)}) collective-permute-start(bf16[1,256,512]{2,1,0:T(8,128)(2,1)S(1)} %get-tuple-element.24.refs_3_), channel_id=1, source_target_pairs={{0,2},{1,5},{2,0},{3,7},{4,6},{5,1},{6,4},{7,3},{8,10},{9,13},{10,... | collective-permute-start | bytes 786440 | tf_op jit(solution)/shard_map/stays0/ppermute | solution.py:330
  26.0 12.1 %collective-permute-start.6 = (bf16[3,256,512]{2,1,0:T(8,128)(2,1)S(1)}, bf16[3,256,512]{2,1,0:T(8,128)(2,1)S(1)}, u32[]{:S(2)}, u32[]{:S(2)}) collective-permute-start(bf16[3,256,512]{2,1,0:T(8,128)(2,1)S(1)} %get-tuple-element.28.refs_1_.refs_4_), channel_id=1, source_target_pairs={{0,4},{1,3},{2,6},{3,1},{4,0},{5,7},{6,2},{7,5},{8,12},{9,11},{10,... | collective-permute-start | bytes 2359304 | tf_op jit(solution)/shard_map/stays1/ppermute | solution.py:330
  28.1 17.8 %collective-permute-start.10 = (bf16[512,512]{1,0:T(8,128)(2,1)S(1)}, bf16[512,512]{1,0:T(8,128)(2,1)S(1)}, u32[]{:S(2)}, u32[]{:S(2)}) collective-permute-start(bf16[512,512]{1,0:T(8,128)(2,1)S(1)} %get-tuple-element.27.refs_9_), channel_id=1, source_target_pairs={{8,16},{16,8},{9,17},{17,9},{10,18},{18,10},{11,19},{19,11},{12,20... | collective-permute-start | bytes 1572872 | tf_op jit(solution)/shard_map/row1/ppermute | solution.py:318
  28.8 9.9 %collective-permute-start.8 = (bf16[256,512]{1,0:T(8,128)(2,1)S(1)}, bf16[256,512]{1,0:T(8,128)(2,1)S(1)}, u32[]{:S(2)}, u32[]{:S(2)}) collective-permute-start(bf16[256,512]{1,0:T(8,128)(2,1)S(1)} %get-tuple-element.29), channel_id=1, source_target_pairs={{0,1},{1,0},{2,3},{3,2},{4,5},{5,4},{6,7},{7,6},{8,9},{9,8},{10,11... | collective-permute-start | bytes 786440 | tf_op jit(solution)/shard_map/sib_moved/ppermute | solution.py:322
  28.9 18.3 %collective-permute-start.9 = (bf16[2,256,512]{2,1,0:T(8,128)(2,1)S(1)}, bf16[2,256,512]{2,1,0:T(8,128)(2,1)S(1)}, u32[]{:S(2)}, u32[]{:S(2)}) collective-permute-start(bf16[2,256,512]{2,1,0:T(8,128)(2,1)S(1)} %get-tuple-element.30.refs_5_), channel_id=1, source_target_pairs={{0,4},{1,3},{2,6},{3,1},{4,0},{5,7},{6,2},{7,5},{8,12},{9,11},{10,... | collective-permute-start | bytes 1572872 | tf_op jit(solution)/shard_map/stays1/ppermute | solution.py:330
  39.3 25.8 %copy-start = (bf16[2,512,512]{2,1,0:T(8,128)(2,1)S(1)}, bf16[2,512,512]{2,1,0:T(8,128)(2,1)}, u32[]{:S(2)}) copy-start(bf16[2,512,512]{2,1,0:T(8,128)(2,1)} %refs_1_.3) | copy-start | bytes 3145732
  39.3 13.3 %collective-permute-start.12 = (bf16[2,1,256,512]{3,2,1,0:T(8,128)(2,1)S(1)}, bf16[2,1,256,512]{3,2,1,0:T(8,128)(2,1)S(1)}, u32[]{:S(2)}, u32[]{:S(2)}) collective-permute-start(bf16[2,1,256,512]{3,2,1,0:T(8,128)(2,1)S(1)} %pick_third.1.refs_2_.refs_1_), channel_id=1, source_target_pairs={{0,2},{1,5},{2,0},{3,7},{4,6},{5,1},{6,4},{7,3},{8,10},{9,13},{10,... | collective-permute-start | bytes 1572872 | tf_op jit(solution)/shard_map/third0/ppermute | solution.py:330
  41.4 8.4 %collective-permute-start.7 = (bf16[256,512]{1,0:T(8,128)(2,1)S(1)}, bf16[256,512]{1,0:T(8,128)(2,1)S(1)}, u32[]{:S(2)}, u32[]{:S(2)}) collective-permute-start(bf16[256,512]{1,0:T(8,128)(2,1)S(1)} %extra_here.1.refs_5_.refs_0_.refs_2_), channel_id=1, source_target_pairs={{0,16},{24,8},{1,17},{25,9},{2,18},{26,10},{3,19},{27,11},{4,20},{... | collective-permute-start | bytes 786440 | tf_op jit(solution)/shard_map/extra_z2/ppermute | solution.py:318
  45.9 16.4 %collective-permute-start.13 = (bf16[512,512]{1,0:T(8,128)(2,1)S(1)}, bf16[512,512]{1,0:T(8,128)(2,1)S(1)}, u32[]{:S(2)}, u32[]{:S(2)}) collective-permute-start(bf16[512,512]{1,0:T(8,128)(2,1)S(1)} %collective-permute-done.10.refs_4_.refs_5_), channel_id=1, source_target_pairs={{16,24},{8,0},{17,25},{9,1},{18,26},{10,2},{19,27},{11,3},{20,28},... | collective-permute-start | bytes 1572872 | tf_op jit(solution)/shard_map/row2/ppermute | solution.py:318
  49.8 15.4 %collective-permute-start.11 = (bf16[256,512]{1,0:T(8,128)(2,1)S(1)}, bf16[256,512]{1,0:T(8,128)(2,1)S(1)}, u32[]{:S(2)}, u32[]{:S(2)}) collective-permute-start(bf16[256,512]{1,0:T(8,128)(2,1)S(1)} %hand_on.1), channel_id=1, source_target_pairs={{0,8},{24,16},{16,24},{8,0},{1,9},{25,17},{17,25},{9,1},{2,10},{26... | collective-permute-start | bytes 786440 | tf_op jit(solution)/shard_map/extra_z1/ppermute | solution.py:318
  53.2 14.8 %collective-permute-start.16 = (bf16[2,1,256,512]{3,2,1,0:T(8,128)(2,1)S(1)}, bf16[2,1,256,512]{3,2,1,0:T(8,128)(2,1)S(1)}, u32[]{:S(2)}, u32[]{:S(2)}) collective-permute-start(bf16[2,1,256,512]{3,2,1,0:T(8,128)(2,1)S(1)} %forward_third.1.refs_5_.refs_8_), channel_id=1, source_target_pairs={{0,4},{1,3},{2,6},{3,1},{4,0},{5,7},{6,2},{7,5},{8,12},{9,11},{10,... | collective-permute-start | bytes 1572872 | tf_op jit(solution)/shard_map/third1/ppermute | solution.py:330
  66.1 1.6 %collective-permute-start.14 = (bf16[256,512]{1,0:T(8,128)(2,1)S(1)}, bf16[256,512]{1,0:T(8,128)(2,1)S(1)}, u32[]{:S(2)}, u32[]{:S(2)}) collective-permute-start(bf16[256,512]{1,0:T(8,128)(2,1)S(1)} %get-tuple-element.31.refs_1_), channel_id=1, source_target_pairs={{0,1},{1,0},{2,3},{3,2},{4,5},{5,4},{6,7},{7,6},{8,9},{9,8},{10,11... | collective-permute-start | bytes 786440 | tf_op jit(solution)/shard_map/sib_l/ppermute | solution.py:322
  66.1 1.9 %collective-permute-start.15 = (bf16[256,512]{1,0:T(8,128)(2,1)S(1)}, bf16[256,512]{1,0:T(8,128)(2,1)S(1)}, u32[]{:S(2)}, u32[]{:S(2)}) collective-permute-start(bf16[256,512]{1,0:T(8,128)(2,1)S(1)} %get-tuple-element.32.refs_2_), channel_id=1, source_target_pairs={{0,1},{1,0},{2,3},{3,2},{4,5},{5,4},{6,7},{7,6},{8,9},{9,8},{10,11... | collective-permute-start | bytes 786440 | tf_op jit(solution)/shard_map/sib_v/ppermute | solution.py:322
  70.6 3.5 %collective-permute-start.17 = (bf16[2,3,256,512]{3,2,1,0:T(8,128)(2,1)S(1)}, bf16[2,3,256,512]{3,2,1,0:T(8,128)(2,1)S(1)}, u32[]{:S(2)}, u32[]{:S(2)}) collective-permute-start(bf16[2,3,256,512]{3,2,1,0:T(8,128)(2,1)S(1)} %multiply.1.refs_7_.refs_3_), channel_id=1, source_target_pairs={{0,1},{1,0},{2,3},{3,2},{4,5},{5,4},{6,7},{7,6},{8,9},{9,8},{10,11... | collective-permute-start | bytes 4718600 | tf_op jit(solution)/shard_map/sib_mine/ppermute | solution.py:322
